TPU v7x, 256 devices: a whole 4x4x8 slice. The times are simulated.
256 devices in a mesh: context: 64 (over y_hi, z, x), tensor: 4 (over y_lo, core).
Axes of the slice: x: 4, y: 4 (y_hi: 2, y_lo: 2; y = y_hi * 2 + y_lo), z: 8, core: 2. Of those that a mesh axis runs over, the one named last changes fastest.
Arguments:
- mixer_values: bfloat16 [8192, 8192], P('context', 'tensor'), may hold values from -6 to 6
- gate_values: bfloat16 [8192, 8192], P('context', 'tensor'), may hold values from -6 to 6
- input_coefs: bfloat16 [8192, 512], P('context', 'tensor'), may hold values from -6 to 6
- output_coefs: bfloat16 [8192, 512], P('context', 'tensor'), may hold values from -0.5 to 0.5
- step_raw: bfloat16 [8192, 128], P('context', 'tensor')
- step_bias: float32 [128], P('tensor')
- decay_log: float32 [128], P('tensor'), as said below
- skip_gain: float32 [128], P('tensor'), may hold values from 0.5 to 1.5
- group_gain: float32 [8192], P('tensor'), may hold values from 0.5 to 1.5
- carry_state: float32 [128, 64, 128], P('tensor'), may hold values from -5 to 5
- out_weight: bfloat16 [8192, 4096], P('tensor', 'context'), may hold values from -0.0625 to 0.0625
- residual: bfloat16 [8192, 4096], P(('context', 'tensor')), may hold values from -6 to 6
- final_gain: float32 [4096], replicated, may hold values from 0.5 to 1.5
Outputs:
- layer_output: bfloat16 [8192, 4096], P('context')
Inputs may be any that keep to these rules, and one draw needn't show every extreme that they name: Every head's decay coefficient exp(decay_log) is below one.
All inputs are finite; a program needn't handle non-finite values.
Results may differ from a plain program's by a relative error of at most 0.0042.
Values may be sent and summed in bfloat16 or wider, within the bound.
No kernel may reach another device: no remote copies, remote signals or barrier semaphores. Data moves between devices by JAX's collectives and lax.ppermute only.
A program may use at most 192 MiB of HBM per device.

v0:
```python
import jax
import jax.numpy as jnp
from jax import lax
from jax.sharding import PartitionSpec as P

STATE = 128
NORM_GROUPS = 4
SPAN = 128


EPSILON = 1e-05
HIGHEST = lax.Precision.HIGHEST


def carried_in(part, axis, combine, identity):
    place = lax.axis_index(axis)
    gathered = jax.tree.map(lambda a: lax.all_gather(a, axis), part)
    state = jax.tree.map(lambda a, e: jnp.zeros_like(a) + jnp.asarray(e, a.dtype), part, identity)

    def one(turn, state):
        return combine(
            state, jax.tree.map(lambda a: lax.dynamic_index_in_dim(a, turn, 0, False), gathered)
        )

    return lax.fori_loop(0, place, one, state)


def combine_pairs(earlier, later):
    return (earlier[0] * later[0], later[0][:, None, None] * earlier[1] + later[1])


def finish(row_block, summed, gain_row):
    combined = row_block.astype(jnp.float32) + summed
    output = (
        combined
        * lax.rsqrt(jnp.mean(combined * combined, axis=-1, keepdims=True) + EPSILON)
        * gain_row
    )
    return output.astype(jnp.bfloat16)


def on_device(
    mixer_values,
    gate_values,
    input_coefs,
    output_coefs,
    step_raw,
    step_bias,
    decay_log,
    skip_gain,
    group_gain,
    carry_state,
    out_weight,
    residual,
    final_gain,
):
    tokens = mixer_values.shape[0]
    inner_width = mixer_values.shape[1]
    head_count = step_raw.shape[1]
    head_width = inner_width // head_count
    groups = input_coefs.shape[1] // STATE
    repeat = head_count // groups
    blocks = tokens // SPAN
    step_size = jax.nn.softplus(step_raw.astype(jnp.float32) + step_bias)
    cumulative = jnp.cumsum(
        (-jnp.exp(decay_log) * step_size).reshape(blocks, SPAN, head_count), axis=1
    )
    values = mixer_values.astype(jnp.float32).reshape(blocks, SPAN, groups, repeat, head_width)
    incoming_raw = input_coefs.reshape(blocks, SPAN, groups, STATE)
    outgoing_raw = output_coefs.reshape(blocks, SPAN, groups, STATE)
    incoming = incoming_raw.astype(jnp.float32)
    outgoing = outgoing_raw.astype(jnp.float32)
    steps_grouped = step_size.reshape(blocks, SPAN, groups, repeat)
    scores = jnp.einsum(
        "cign,cjgn->cgij", outgoing_raw, incoming_raw, preferred_element_type=jnp.float32
    )
    by_head = jnp.transpose(cumulative, (0, 2, 1)).reshape(blocks, groups, repeat, SPAN)
    log_gaps = by_head[..., :, None] - by_head[..., None, :]
    causal = jnp.arange(SPAN)[:, None] >= jnp.arange(SPAN)[None, :]
    within = jnp.exp(jnp.where(causal, log_gaps, -jnp.inf))
    weights = (
        scores[:, :, None] * within * jnp.transpose(steps_grouped, (0, 2, 3, 1))[:, :, :, None, :]
    )
    diagonal = jnp.einsum("cgrij,cjgrp->cigrp", weights, values, precision=HIGHEST)
    block_log = cumulative[:, -1, :]
    to_end = jnp.exp(block_log[:, None, :] - cumulative).reshape(blocks, SPAN, groups, repeat)
    fresh_terms = jnp.einsum(
        "cjgrp,cjgn->cgrpn",
        values * (steps_grouped * to_end)[..., None],
        incoming,
        precision=HIGHEST,
    )
    fresh_terms = fresh_terms.reshape(blocks, head_count, head_width, STATE)

    def advance(running, pieces):
        block_decay, update = pieces
        return (block_decay[:, None, None] * running + update, running)

    zero_state = jnp.zeros((head_count, head_width, STATE), jnp.float32)
    local_final, local_enter = lax.scan(advance, zero_state, (jnp.exp(block_log), fresh_terms))
    device_decay = jnp.exp(jnp.sum(block_log, axis=0))
    identity = (jnp.ones_like(device_decay), jnp.zeros_like(local_final))
    prefix_decay, prefix_state = carried_in(
        (device_decay, local_final), "context", combine_pairs, identity
    )
    entering = prefix_state + prefix_decay[:, None, None] * carry_state
    before = jnp.exp(jnp.cumsum(block_log, axis=0) - block_log)
    starts = (local_enter + before[:, :, None, None] * entering[None]).reshape(
        blocks, groups, repeat, head_width, STATE
    )
    carried = jnp.einsum("cign,cgrpn->cigrp", outgoing, starts, precision=HIGHEST)
    carried = carried * jnp.exp(cumulative).reshape(blocks, SPAN, groups, repeat)[..., None]
    mixer_out = (
        diagonal + carried + skip_gain.reshape(groups, repeat)[:, :, None] * values
    ).reshape(tokens, inner_width)
    gated_out = mixer_out * jax.nn.silu(gate_values.astype(jnp.float32))
    grouped = gated_out.reshape(tokens, NORM_GROUPS // lax.axis_size("tensor"), -1)
    normed = grouped * lax.rsqrt(jnp.mean(grouped * grouped, axis=-1, keepdims=True) + EPSILON)
    normed = (normed.reshape(tokens, inner_width) * group_gain).astype(jnp.bfloat16)
    whole_weight = lax.all_gather(out_weight, "context", axis=1, tiled=True)
    partial_sums = jnp.dot(normed, whole_weight, preferred_element_type=jnp.float32)
    summed = lax.psum_scatter(partial_sums, "tensor", scatter_dimension=0, tiled=True)
    output_part = finish(residual, summed, final_gain)
    return lax.all_gather(output_part, "tensor", axis=0, tiled=True)


def solution(mesh):
    return jax.shard_map(
        on_device,
        mesh=mesh,
        in_specs=(
            P("context", "tensor"),
            P("context", "tensor"),
            P("context", "tensor"),
            P("context", "tensor"),
            P("context", "tensor"),
            P("tensor"),
            P("tensor"),
            P("tensor"),
            P("tensor"),
            P("tensor", None, None),
            P("tensor", "context"),
            P(("context", "tensor"), None),
            P(),
        ),
        out_specs=P("context", None),
        check_vma=False,
    )
```

profile of v0, /device:TPU:1, one launch (start us, length us, event | category | flops | bytes accessed | tf_op | source)
XLA Modules:
  0.0 865.0 jit_solution(11635607177599342622)
XLA Ops:
  6.5 0.7 exponential_negate_fusion
  7.2 0.8 multiply_bitcast_fusion
  8.1 0.2 reduce_window_sum.19
  8.4 1.3 copy.44
  9.7 0.8 bitcast_exponential_fusion
  10.6 1.6 convolution_add_fusion
  12.3 0.7 all-gather.6.cloned.1.call-update
  13.1 156.7 %all-gather = f32[64,1,32]{2,1,0:T(1,128)S(1)} all-gather(f32[1,1,32]{2,1,0:T(1,128)S(1)} %get-tuple-element.73), channel_id=2, replica_groups=mesh['context'=64,'tensor'=4] {'context'}, dimensions={0}, use_global_device_ids=true | all-gather | bytes 8320 | tf_op jit(solution)/shard_map/all_gather | solution.py:17
  169.8 0.1 fusion.38
  169.9 3.5 fusion.6
  173.4 414.0 %all-gather.10.cloned.1.call-done = f32[2048,64,128]{2,1,0:T(8,128)} async-done(((f32[32,64,128]{2,1,0:T(8,128)}), f32[2048,64,128]{2,1,0:T(8,128)}) %all-gather.10.cloned.1.call-update) | async-done | bytes 67108880 | tf_op jit(solution)/shard_map/all_gather | solution.py:17
  587.4 0.1 broadcast.96
  587.6 0.6 copy-done.5
  588.2 2.3 fusion.11
  590.6 0.3 copy.47
  590.9 0.7 copy-done.2
  591.6 0.4 multiply_reduce_fusion
  592.0 195.3 %all-gather.6.cloned.1.call-done = bf16[2048,4096]{0,1:T(8,128)(2,1)} async-done(((bf16[2048,64]{0,1:T(8,128)(2,1)}), bf16[2048,4096]{0,1:T(8,128)(2,1)}) %all-gather.6.cloned.1.call-update) | async-done | bytes 16777232 | tf_op jit(solution)/shard_map/all_gather | solution.py:120
  787.3 12.8 %fusion.25 = f32[128,4096]{1,0:T(8,128)} fusion(bf16[2048,4096]{0,1:T(8,128)(2,1)} %all-gather.6.cloned.1.call-done, f32[2048]{0:T(1024)S(1)} %copy-done.6, f32[128]{0:T(128)S(1)} %add_rsqrt_fusion.1, f32[128,2048]{1,0:T(8,128)S(1)} %copy.47, bf16[128,2048]{1,0:T(8,128)(2,1)S(1)} %copy-done.2), kind=kOutput, calls=%fused_computation.32 | convolution fusion | flops 2149842944 | bytes 20455936 | tf_op jit(solution)/shard_map/dot_general | solution.py:121
  800.1 28.4 %reduce-scatter.2.cloned.1.call-done = f32[32,4096]{1,0:T(8,128)} async-done(((f32[128,4096]{1,0:T(8,128)}), f32[32,4096]{1,0:T(8,128)}) %reduce-scatter.2.cloned.1.call-update) | async-done | bytes 524304 | tf_op jit(solution)/shard_map/reduce_scatter | solution.py:122
  828.5 1.2 multiply_reduce_fusion.1
  829.7 1.9 multiply_convert_fusion.2
  831.6 24.5 %all-gather.8.cloned.1.call-done = bf16[128,4096]{1,0:T(8,128)(2,1)} async-done(((bf16[32,4096]{1,0:T(8,128)(2,1)}), bf16[128,4096]{1,0:T(8,128)(2,1)}) %all-gather.8.cloned.1.call-update) | async-done | bytes 1048592 | tf_op jit(solution)/shard_map/all_gather | solution.py:124
  856.2 2.3 copy.58
  (30 shorter events, 0.6 us)
Async XLA Ops:
  6.5 4.1 copy-start
  6.5 580.9 %all-gather.10.cloned.1.call-start = ((), (), s32[]{:S(2)}) async-start(), calls=%async_computation.4 | async-start | bytes 68157440 | tf_op jit(solution)/shard_map/all_gather | solution.py:17
  10.6 159.2 %copy-start.3 = (bf16[128,128]{1,0:T(8,128)(2,1)S(1)}, bf16[128,128]{1,0:T(8,128)(2,1)}, u32[]{:S(2)}) copy-start(bf16[128,128]{1,0:T(8,128)(2,1)} %param.18) | copy-start | bytes 98308
  12.2 775.1 %all-gather.6.cloned.1.call-start = ((), (), s32[]{:S(2)}) async-start(), calls=%async_computation.1 | async-start | bytes 17039360 | tf_op jit(solution)/shard_map/all_gather | solution.py:120
  13.0 815.5 %reduce-scatter.2.cloned.1.call-start = ((), (), s32[]{:S(2)}) async-start(), calls=%async_computation.2 | async-start | bytes 2621440 | tf_op jit(solution)/shard_map/reduce_scatter | solution.py:122
  587.5 0.7 copy-start.5
  590.5 1.0 copy-start.2
  590.5 196.7 %copy-start.6 = (f32[2048]{0:T(1024)S(1)}, f32[2048]{0:T(1024)}, u32[]{:S(2)}) copy-start(f32[2048]{0:T(1024)} %param.23) | copy-start | bytes 24580
  800.1 28.4 %copy-start.1 = (bf16[32,4096]{1,0:T(8,128)(2,1)S(1)}, bf16[32,4096]{1,0:T(8,128)(2,1)}, u32[]{:S(2)}) copy-start(bf16[32,4096]{1,0:T(8,128)(2,1)} %param.26) | copy-start | bytes 786436
  800.1 29.7 %copy-start.4 = (f32[4096]{0:T(1024)S(1)}, f32[4096]{0:T(1024)}, u32[]{:S(2)}) copy-start(f32[4096]{0:T(1024)} %param.27) | copy-start | bytes 49156
  800.1 56.1 %all-gather.8.cloned.1.call-start = ((), (), s32[]{:S(2)}) async-start(), calls=%async_computation.3 | async-start | bytes 1310720 | tf_op jit(solution)/shard_map/all_gather | solution.py:124
Sparse Core Ops, SparseCore 0:
  12.3 575.0 all-gather.9
  591.1 196.1 all-gather.5
  800.2 28.2 reduce-scatter.1
  831.7 24.3 all-gather.7
where the time goes:
time: 868 us; the launch traced here: 865 us
  waiting for transfers between devices  663 us (76%)
  blocking collectives  157 us (18%)
  matrix products  20.3 us (2%)
  between operations  13.3 us (2%)
    all_gather x1, waiting for transfers between devices, carried_in(): gathered = jax.tree.map(lambda a: lax.all_gather(a, axis), part)  414 us
    all_gather x1, waiting for transfers between devices, on_device(): whole_weight = lax.all_gather(out_weight, 'context', axis=1, tiled=True)  195 us
    all_gather x1, blocking collectives, carried_in(): gathered = jax.tree.map(lambda a: lax.all_gather(a, axis), part)  157 us
    reduce_scatter x1, waiting for transfers between devices, on_device(): lax.psum_scatter(partial_sums, 'tensor', scatter_dimension=0, tiled=True)  28.4 us
    all_gather x1, waiting for transfers between devices, on_device(): return lax.all_gather(output_part, 'tensor', axis=0, tiled=True)  24.5 us
  transfers between devices with their start and end apart: 4, of which 4 were waited for; matrix products, arithmetic and copies ran while one was open for 1% of the time, Pallas kernels for 0%

commit v1 on v0

v1 whole, which is shorter than its diff:
```python
import functools

import jax
import jax.numpy as jnp
from jax import lax
from jax.experimental import pallas as pl
from jax.experimental.pallas import tpu as pltpu
from jax.sharding import Mesh, PartitionSpec as P

EPSILON = 1e-05
HIGHEST = lax.Precision.HIGHEST
SPAN = 128
STATE = 128
HEAD_DIM = 64
EXTRA = 8
BF16, F32 = jnp.bfloat16, jnp.float32
CONTEXT = ("yh", "z", "x")
TENSOR = ("yl", "core")
SLICES = ("z", "x")
VMEM_LIMIT = 48 * 2**20


def call(kernel, outs, *, scratch=(), flops=0, smem=0, args=()):
    specs = [pl.BlockSpec(memory_space=pltpu.SMEM)] * smem
    specs += [pl.BlockSpec(memory_space=pltpu.VMEM)] * (len(args) - smem)
    moved = sum(a.size * a.dtype.itemsize for a in (*args, *jax.tree.leaves(outs)))
    return pl.pallas_call(
        kernel,
        out_shape=outs,
        in_specs=specs,
        out_specs=jax.tree.map(lambda _: pl.BlockSpec(memory_space=pltpu.VMEM), outs),
        scratch_shapes=scratch,
        compiler_params=pltpu.CompilerParams(vmem_limit_bytes=VMEM_LIMIT),
        cost_estimate=pl.CostEstimate(flops=flops, bytes_accessed=moved, transcendentals=0),
    )(*args)


def dot(a, b, precision=None):
    return lax.dot_general(
        a, b, (((1,), (0,)), ((), ())), precision=precision, preferred_element_type=F32
    )


def steps_of(raw, bias, decay_log):
    v = raw.astype(F32) + bias
    step = jnp.maximum(v, 0.0) + jnp.log1p(jnp.exp(-jnp.abs(v)))
    rows = lax.broadcasted_iota(jnp.int32, (SPAN, SPAN), 0)
    columns = lax.broadcasted_iota(jnp.int32, (SPAN, SPAN), 1)
    lower = jnp.where(rows >= columns, 1.0, 0.0).astype(F32)
    cumulative = dot(lower, -jnp.exp(decay_log) * step, HIGHEST)
    return step, cumulative


def split(a):
    high = a.astype(BF16)
    return high, (a - high.astype(F32)).astype(BF16)


def first_lanes(shape):
    return lax.broadcasted_iota(jnp.int32, shape, len(shape) - 1) < HEAD_DIM


def column(a, h):
    return jnp.broadcast_to(a[:, h : h + 1], (a.shape[0], 2 * HEAD_DIM))


def states_kernel(x_ref, b_ref, raw_ref, bias_ref, decay_ref, out_ref):
    step, cumulative = steps_of(raw_ref[...], bias_ref[...], decay_ref[...])
    last = cumulative[SPAN - 1 : SPAN, :]
    weight = step * jnp.exp(last - cumulative)
    b_t = jnp.transpose(b_ref[...])
    b_twice = jnp.concatenate([b_t, b_t], axis=1)
    low = first_lanes((SPAN, SPAN))
    for pair in range(step.shape[1] // 2):
        lanes = slice(pair * SPAN, (pair + 1) * SPAN)
        scale = jnp.where(low, column(weight, 2 * pair), column(weight, 2 * pair + 1))
        scaled = x_ref[:, lanes].astype(F32) * scale
        state = dot(b_twice, jnp.concatenate(split(scaled), axis=0))
        log = jnp.where(
            low[:1], column(last, 2 * pair), column(last, 2 * pair + 1)
        )
        for half in range(2):
            rows = slice(half * (STATE // 2), (half + 1) * (STATE // 2))
            out_ref[2 * pair + half, : STATE // 2, :] = state[rows]
            out_ref[2 * pair + half, STATE // 2 :, :] = jnp.broadcast_to(log, (EXTRA, SPAN))


def decay_and_state(parts_ref, k):
    decay = jnp.exp(parts_ref[k, STATE // 2 : STATE // 2 + 1, :])
    return decay, parts_ref[k, : STATE // 2, :]


def end_kernel(parts_ref, carry_ref, out_ref):
    run = carry_ref[...]
    for k in range(parts_ref.shape[0]):
        decay, state = decay_and_state(parts_ref, k)
        run = decay * run + state
    out_ref[...] = run


def enter_kernel(late_ref, parts_ref, carry_ref, sent_ref, out_ref):
    run = jnp.where(late_ref[0] > 0, sent_ref[...], carry_ref[...])
    for k in range(parts_ref.shape[0]):
        out_ref[k] = run
        decay, state = decay_and_state(parts_ref, k)
        run = decay * run + state


def mix_kernel(
    x_ref, gate_ref, b_ref, c_ref, raw_ref, bias_ref, decay_ref, skip_ref, gain_ref, state_ref, out_ref, gated_ref
):
    step, cumulative = steps_of(raw_ref[...], bias_ref[...], decay_ref[...])
    step_t, cumulative_t = jnp.transpose(step), jnp.transpose(cumulative)
    scores = lax.dot_general(
        c_ref[...], b_ref[...], (((1,), (1,)), ((), ())), preferred_element_type=F32
    )
    rows = lax.broadcasted_iota(jnp.int32, (SPAN, SPAN), 0)
    columns = lax.broadcasted_iota(jnp.int32, (SPAN, SPAN), 1)
    causal = rows >= columns
    low = first_lanes((SPAN, SPAN))
    c_twice = jnp.concatenate([c_ref[...], c_ref[...]], axis=1)
    squares = jnp.zeros((SPAN, SPAN), F32)
    pairs = step.shape[1] // 2
    for pair in range(pairs):
        lanes = slice(pair * SPAN, (pair + 1) * SPAN)
        x = x_ref[:, lanes]
        at, weights = [], []
        for h in (2 * pair, 2 * pair + 1):
            here = column(cumulative, h)
            within = jnp.exp(jnp.where(causal, here - cumulative_t[h : h + 1, :], -jnp.inf))
            at.append(here)
            weights.append(jnp.concatenate(split(scores * within * step_t[h : h + 1, :]), axis=1))
        both = dot(jnp.concatenate(weights, axis=0), jnp.concatenate([x, x], axis=0))
        carried = dot(c_twice, jnp.concatenate(split(state_ref[lanes, :]), axis=0))
        mixed = (
            jnp.where(low, both[:SPAN], both[SPAN:])
            + carried * jnp.exp(jnp.where(low, at[0], at[1]))
            + skip_ref[:, lanes] * x.astype(F32)
        )
        gate = gate_ref[:, lanes].astype(F32)
        gated = mixed * (gate / (1.0 + jnp.exp(-gate)))
        gated_ref[:, lanes] = gated
        squares += gated * gated
    width = pairs * SPAN
    root = lax.rsqrt(jnp.sum(squares, axis=-1, keepdims=True) / width + EPSILON)
    for pair in range(pairs):
        lanes = slice(pair * SPAN, (pair + 1) * SPAN)
        out_ref[:, lanes] = (gated_ref[:, lanes] * root * gain_ref[:, lanes]).astype(BF16)


def project_kernel(place_ref, own_ref, left_ref, right_ref, far_a_ref, far_b_ref, weight_ref, out_ref):
    def one(a, row):
        product = lax.dot_general(
            a, weight_ref[...], (((1,), (1,)), ((), ())), preferred_element_type=F32
        )
        out_ref[pl.ds(pl.multiple_of(row, SPAN // 2), a.shape[0]), :] = product.astype(BF16)

    one(own_ref[...], place_ref[0] * SPAN)
    one(left_ref[...], place_ref[1] * SPAN)
    one(right_ref[...], place_ref[2] * SPAN)
    one(far_a_ref[...], place_ref[3] * SPAN)
    one(far_b_ref[...], place_ref[3] * SPAN + SPAN // 2)


def finish_kernel(late_ref, parts_ref, residual_ref, gain_ref, out_ref, combined_ref, *, n_x, n_t, n_z):
    late = late_ref[0] > 0
    tokens = residual_ref.shape[0]
    sums = []
    for x in range(n_x):
        total = parts_ref[x * n_t].astype(F32)
        for t in range(1, n_t):
            total += parts_ref[x * n_t + t].astype(F32)
        sums.append(total)
    squares = jnp.zeros((tokens, 2 * HEAD_DIM), F32)
    for z in range(n_z):
        piece = slice(z * 2 * HEAD_DIM, (z + 1) * 2 * HEAD_DIM)
        own = [total[:, piece] for total in sums]
        swapped = [jnp.concatenate([a[:, HEAD_DIM:], a[:, :HEAD_DIM]], axis=1) for a in own]
        ordered = [jnp.where(late, b, a) for a, b in zip(own, swapped)]
        for yh in range(2):
            for x in range(0, n_x, 2):
                block = ((yh * n_z + z) * n_x + x) // 2
                lanes = slice(block * 2 * HEAD_DIM, (block + 1) * 2 * HEAD_DIM)
                half = slice(yh * HEAD_DIM, (yh + 1) * HEAD_DIM)
                both = jnp.concatenate([ordered[x][:, half], ordered[x + 1][:, half]], axis=1)
                combined = residual_ref[:, lanes].astype(F32) + both
                combined_ref[:, lanes] = combined
                squares += combined * combined
    root = lax.rsqrt(jnp.sum(squares, axis=-1, keepdims=True) / combined_ref.shape[1] + EPSILON)
    out_ref[...] = (combined_ref[...] * root * gain_ref[...]).astype(BF16)


def ring(n, by):
    return [(i, (i + by) % n) for i in range(n)]


def on_device(
    mixer_values,
    gate_values,
    input_coefs,
    output_coefs,
    step_raw,
    step_bias,
    decay_log,
    skip_gain,
    group_gain,
    carry_state,
    out_weight,
    residual,
    final_gain,
):
    tokens, inner = mixer_values.shape
    heads = step_raw.shape[1]
    n_z, n_x = lax.axis_size("z"), lax.axis_size("x")
    n_t = lax.axis_size("yl") * lax.axis_size("core")
    slices = n_z * n_x
    at_x = lax.axis_index("x")
    late = lax.axis_index("yh").astype(jnp.int32).reshape(1)
    bias, decay = step_bias.reshape(1, heads), decay_log.reshape(1, heads)
    skip = jnp.repeat(skip_gain, HEAD_DIM).reshape(1, inner)

    weight = out_weight.T
    weight = jnp.concatenate([weight, lax.ppermute(weight, "yh", ring(2, 1))], axis=0)
    weight = lax.all_gather(weight, "z", axis=0, tiled=True)

    half = STATE // 2
    states = call(
        states_kernel,
        jax.ShapeDtypeStruct((slices, half + EXTRA, 2 * HEAD_DIM), F32),
        flops=2 * tokens * inner * STATE * 2,
        args=(mixer_values, input_coefs, step_raw, bias, decay),
    )
    parts = lax.all_to_all(states, SLICES, 0, 0, tiled=True)

    mine = lax.axis_index(SLICES)
    pair = lax.dynamic_index_in_dim(carry_state.reshape(heads // 2, 2 * HEAD_DIM, STATE), mine // 2, 0, False)
    carry = lax.dynamic_slice_in_dim(pair.T, (mine % 2) * half, half, 0)
    ends = call(
        end_kernel, jax.ShapeDtypeStruct(carry.shape, F32), flops=10**6, args=(parts, carry)
    )
    sent = lax.ppermute(ends, "yh", [(0, 1)])
    entering = call(
        enter_kernel,
        jax.ShapeDtypeStruct((slices, half, 2 * HEAD_DIM), F32),
        flops=10**6,
        smem=1,
        args=(late, parts, carry, sent),
    )
    entering = lax.all_to_all(entering, SLICES, 0, 0, tiled=True).reshape(slices * half, 2 * HEAD_DIM)

    normed = call(
        mix_kernel,
        jax.ShapeDtypeStruct((tokens, inner), BF16),
        scratch=[pltpu.VMEM((tokens, inner), F32)],
        flops=2 * tokens * inner * tokens * 4,
        args=(
            mixer_values,
            gate_values,
            input_coefs,
            output_coefs,
            step_raw,
            bias,
            decay,
            skip,
            group_gain.reshape(1, inner),
            entering,
        ),
    )
    left = lax.ppermute(normed, "x", ring(n_x, 1))
    right = lax.ppermute(normed, "x", ring(n_x, -1))
    far_a = lax.ppermute(left[: tokens // 2], "x", ring(n_x, 1))
    far_b = lax.ppermute(right[tokens // 2 :], "x", ring(n_x, -1))
    place = (at_x + jnp.array([0, n_x - 1, 1, 2], jnp.int32)) % n_x
    partial = call(
        project_kernel,
        jax.ShapeDtypeStruct((n_x * tokens, weight.shape[0]), BF16),
        flops=2 * n_x * tokens * inner * weight.shape[0],
        smem=1,
        args=(place, normed, left, right, far_a, far_b, weight),
    )
    partial = lax.all_to_all(partial, ("x", *TENSOR), 0, 0, tiled=True)
    rows = residual.shape[0]
    done = call(
        functools.partial(finish_kernel, n_x=n_x, n_t=n_t, n_z=n_z),
        jax.ShapeDtypeStruct(residual.shape, BF16),
        scratch=[pltpu.VMEM(residual.shape, F32)],
        flops=10**6,
        smem=1,
        args=(late, partial.reshape(n_x * n_t, rows, weight.shape[0]), residual, final_gain.reshape(1, -1)),
    )
    across = lax.ppermute(done, "yl", ring(2, 1))
    mine_two = jnp.stack([done, across])
    theirs_two = lax.ppermute(mine_two, "core", ring(2, 1))
    first_y, first_core = lax.axis_index("yl") == 0, lax.axis_index("core") == 0
    even = jnp.where(first_core, mine_two, theirs_two)
    odd = jnp.where(first_core, theirs_two, mine_two)
    low = jnp.where(first_y, jnp.stack([even[0], odd[0]]), jnp.stack([even[1], odd[1]]))
    high = jnp.where(first_y, jnp.stack([even[1], odd[1]]), jnp.stack([even[0], odd[0]]))
    return jnp.concatenate([low, high]).reshape(tokens, residual.shape[1])


def solution(mesh):
    fine = Mesh(mesh.devices.reshape(2, 8, 4, 2, 2), (*CONTEXT, *TENSOR))
    return jax.shard_map(
        on_device,
        mesh=fine,
        in_specs=(
            P(CONTEXT, TENSOR),
            P(CONTEXT, TENSOR),
            P(CONTEXT, TENSOR),
            P(CONTEXT, TENSOR),
            P(CONTEXT, TENSOR),
            P(TENSOR),
            P(TENSOR),
            P(TENSOR),
            P(TENSOR),
            P(TENSOR, None, None),
            P(TENSOR, CONTEXT),
            P((*CONTEXT, *TENSOR), None),
            P(),
        ),
        out_specs=P(CONTEXT, None),
        check_vma=False,
    )
```

time: 868 us -> 199 us (0.23)
  waiting for transfers between devices: 663 us -> 102 us
  blocking collectives: 157 us -> 25.3 us
  starting transfers between devices: 0.12 us -> 37.5 us
  matrix products: 20.3 us -> 0 us
  Pallas kernels: 0 us -> 15.2 us
    all_gather x3 -> x1, waiting for transfers between devices: 634 us -> 0.01 us  [on_device(): weight = lax.all_gather(weight, 'z', axis=0, tiled=True)]
    all_gather x1 -> x0, blocking collectives: 157 us -> none  [carried_in(): gathered = jax.tree.map(lambda a: lax.all_gather(a, axis), part)]
    all_to_all x0 -> x2, waiting for transfers between devices: none -> 76 us  [the longest x1 39.1 us: on_device(): parts = lax.all_to_all(states, SLICES, 0, 0, tiled=True)]
    reduce_scatter x1 -> x0, waiting for transfers between devices: 28.4 us -> none  [on_device(): lax.psum_scatter(partial_sums, 'tensor', scatter_dimension=0, tiled=True)]
    ppermute x0 -> x8, waiting for transfers between devices: none -> 25.5 us  [the longest x1 7.58 us: on_device(): left = lax.ppermute(normed, 'x', ring(n_x, 1))]
    all_to_all x0 -> x1, blocking collectives: none -> 25.3 us  [on_device(): partial = lax.all_to_all(partial, ('x', *TENSOR), 0, 0, tiled=True)]
    dot_general x5 -> x0, matrix products: 20.3 us -> none  [the longest x1 12.8 us: on_device(): jnp.dot(normed, whole_weight, preferred_element_type=jnp.float32)]
    ppermute x0 -> x8, starting transfers between devices: none -> 18.9 us  [the longest x1 5.45 us: on_device(): sent = lax.ppermute(ends, 'yh', [(0, 1)])]
  transfers between devices with their start and end apart: 4 -> 11, of which waited for: 4 -> 9; matrix products, arithmetic and copies ran while one was open for 1% -> 0% of each run, Pallas kernels for 0% -> 3%
where the time goes in v1:
time: 199 us
  waiting for transfers between devices  102 us (51%)
  starting transfers between devices  37.5 us (19%)
  blocking collectives  25.3 us (13%)
  Pallas kernels  15.2 us (8%)
  between operations  13.6 us (7%)
  other arithmetic  3.06 us (2%)
  local copies, waits for them, and re-layouts  2.42 us (1%)
    all_to_all x1, waiting for transfers between devices, on_device(): parts = lax.all_to_all(states, SLICES, 0, 0, tiled=True)  39.1 us
    all_to_all x1, waiting for transfers between devices, on_device(): lax.all_to_all(entering, SLICES, 0, 0, tiled=True)  36.8 us
    all_to_all x1, blocking collectives, on_device(): partial = lax.all_to_all(partial, ('x', *TENSOR), 0, 0, tiled=True)  25.3 us
    pallas_call x6, Pallas kernels, call(): pl.pallas_call(kernel, out_shape=outs, in_specs=specs, out_specs=jax.tree...  15.2 us
    all_to_all x1, starting transfers between devices, on_device(): parts = lax.all_to_all(states, SLICES, 0, 0, tiled=True)  11.7 us
    ppermute x1, waiting for transfers between devices, on_device(): left = lax.ppermute(normed, 'x', ring(n_x, 1))  7.58 us
    all_to_all x1, starting transfers between devices, on_device(): lax.all_to_all(entering, SLICES, 0, 0, tiled=True)  6.86 us
    ppermute x1, waiting for transfers between devices, on_device(): across = lax.ppermute(done, 'yl', ring(2, 1))  5.5 us
  transfers between devices with their start and end apart: 11, of which 9 were waited for; matrix products, arithmetic and copies ran while one was open for 0% of the time, Pallas kernels for 3%

profile of v1, /device:TPU:1, one launch (start us, length us, event | category | flops | bytes accessed | tf_op | source)
XLA Modules:
  0.0 198.7 jit_solution(15424949268580879780)
XLA Ops:
  6.6 3.8 %collective-permute-start.5 = (bf16[64,2048]{1,0:T(8,128)(2,1)}, bf16[64,2048]{1,0:T(8,128)(2,1)S(1)}, u32[]{:S(2)}, u32[]{:S(2)}) collective-permute-start(bf16[64,2048]{1,0:T(8,128)(2,1)} %bitcast.30), channel_id=1, source_target_pairs={{0,128},{128,0},{1,129},{129,1},{2,130},{130,2},{3,131},{131,3},{4... | collective-permute-start | bytes 786440 | tf_op jit(solution)/shard_map/ppermute | solution.py:223
  10.4 5.3 %collective-permute-done.5 = bf16[64,2048]{1,0:T(8,128)(2,1)S(1)} collective-permute-done((bf16[64,2048]{1,0:T(8,128)(2,1)}, bf16[64,2048]{1,0:T(8,128)(2,1)S(1)}, u32[]{:S(2)}, u32[]{:S(2)}) %collective-permute-start.5) | collective-permute-done | bytes 262176 | tf_op jit(solution)/shard_map/ppermute | solution.py:223
  15.7 1.8 pad_maximum_fusion.1
  17.7 2.3 %shard_map.136 = f32[32,72,128]{2,1,0:T(8,128)} custom-call(bf16[128,2048]{1,0:T(8,128)(2,1)S(1)} %copy-done.1, bf16[128,128]{1,0:T(8,128)(2,1)S(1)} %copy-done.6, bf16[128,32]{1,0:T(8,128)(2,1)S(1)} %copy.17.raw_ref, f32[1,32]{1,0:T(1,128)S(1)} %bitcast.24, f32[1,32]{1,0:T(1,128)S(1)} %bitcast.26), custom_call_target="tpu_custom_call" | custom-call | flops 134217728 | bytes 1745152 | tf_op jit(solution)/shard_map/pallas_call | solution.py:27
  20.0 11.7 %all-to-all-start = ((f32[32,72,128]{2,1,0:T(8,128)}), f32[32,72,128]{2,1,0:T(8,128)S(1)}, u32[]{:S(2)}, u32[]{:S(2)}) async-start(f32[32,72,128]{2,1,0:T(8,128)} %shard_map.136), calls=%async_computation | async-start | bytes 2359296 | tf_op jit(solution)/shard_map/all_to_all | solution.py:233
  31.9 39.1 %all-to-all-done.parts_ref = f32[32,72,128]{2,1,0:T(8,128)S(1)} async-done(((f32[32,72,128]{2,1,0:T(8,128)}), f32[32,72,128]{2,1,0:T(8,128)S(1)}, u32[]{:S(2)}, u32[]{:S(2)}) %all-to-all-start) | async-done | bytes 1179680 | tf_op jit(solution)/shard_map/all_to_all | solution.py:233
  71.1 5.5 %collective-permute-start = (f32[64,128]{1,0:T(8,128)S(1)}, f32[64,128]{1,0:T(8,128)S(1)}, u32[]{:S(2)}, u32[]{:S(2)}) collective-permute-start(f32[64,128]{1,0:T(8,128)S(1)} %shard_map.137), channel_id=1, source_target_pairs={{0,128},{1,129},{2,130},{3,131},{4,132},{5,133},{6,134},{7,135},{8... | collective-permute-start | bytes 98312 | tf_op jit(solution)/shard_map/ppermute | solution.py:241
  77.6 1.1 shard_map.138
  78.7 6.9 %all-to-all-start.1 = ((f32[32,64,128]{2,1,0:T(8,128)}), f32[32,64,128]{2,1,0:T(8,128)S(1)}, u32[]{:S(2)}, u32[]{:S(2)}) async-start(f32[32,64,128]{2,1,0:T(8,128)} %shard_map.138), calls=%async_computation.1 | async-start | bytes 2097152 | tf_op jit(solution)/shard_map/all_to_all | solution.py:249
  85.7 36.8 %all-to-all-done.1 = f32[32,64,128]{2,1,0:T(8,128)S(1)} async-done(((f32[32,64,128]{2,1,0:T(8,128)}), f32[32,64,128]{2,1,0:T(8,128)S(1)}, u32[]{:S(2)}, u32[]{:S(2)}) %all-to-all-start.1) | async-done | bytes 1048608 | tf_op jit(solution)/shard_map/all_to_all | solution.py:249
  122.6 2.2 %shard_map.139.own_ref = bf16[128,2048]{1,0:T(8,128)(2,1)S(1)} custom-call(bf16[128,2048]{1,0:T(8,128)(2,1)S(1)} %copy-done.1, bf16[128,2048]{1,0:T(8,128)(2,1)S(1)} %copy-done.2, bf16[128,128]{1,0:T(8,128)(2,1)S(1)} %copy-done.6, bf16[128,128]{1,0:T(8,128)(2,1)S(1)} %copy-done.7, bf16[128,32]{1,0:T(8,128)(2,1)S(1)} %copy.17.raw_ref, f32[1,32]{1,0:T(1,128)S(1)} %bitcast.25, ...), custom_call_target="tpu_custom_call" | custom-call | flops 268435456 | bytes 2711808 | tf_op jit(solution)/shard_map/pallas_call | solution.py:27
  124.8 2.1 %collective-permute-start.1 = (bf16[128,2048]{1,0:T(8,128)(2,1)S(1)}, bf16[128,2048]{1,0:T(8,128)(2,1)S(1)}, u32[]{:S(2)}, u32[]{:S(2)}) collective-permute-start(bf16[128,2048]{1,0:T(8,128)(2,1)S(1)} %shard_map.139.own_ref), channel_id=1, source_target_pairs={{0,4},{4,8},{8,12},{12,0},{1,5},{5,9},{9,13},{13,1},{2,6},{6,10},{... | collective-permute-start | bytes 1572872 | tf_op jit(solution)/shard_map/ppermute | solution.py:269
  128.7 7.6 %collective-permute-done.1.left_ref = bf16[128,2048]{1,0:T(8,128)(2,1)S(1)} collective-permute-done((bf16[128,2048]{1,0:T(8,128)(2,1)S(1)}, bf16[128,2048]{1,0:T(8,128)(2,1)S(1)}, u32[]{:S(2)}, u32[]{:S(2)}) %collective-permute-start.1) | collective-permute-done | bytes 524320 | tf_op jit(solution)/shard_map/ppermute | solution.py:269
  136.3 2.2 %collective-permute-start.3 = (bf16[64,2048]{1,0:T(8,128)(2,1)S(1)}, bf16[64,2048]{1,0:T(8,128)(2,1)S(1)}, u32[]{:S(2)}, u32[]{:S(2)}) collective-permute-start(bf16[64,2048]{1,0:T(8,128)(2,1)S(1)} %slice.28), channel_id=1, source_target_pairs={{0,4},{4,8},{8,12},{12,0},{1,5},{5,9},{9,13},{13,1},{2,6},{6,10},{... | collective-permute-start | bytes 786440 | tf_op jit(solution)/shard_map/ppermute | solution.py:271
  139.4 3.4 %collective-permute-done.3.far_a_ref = bf16[64,2048]{1,0:T(8,128)(2,1)S(1)} collective-permute-done((bf16[64,2048]{1,0:T(8,128)(2,1)S(1)}, bf16[64,2048]{1,0:T(8,128)(2,1)S(1)}, u32[]{:S(2)}, u32[]{:S(2)}) %collective-permute-start.3) | collective-permute-done | bytes 262176 | tf_op jit(solution)/shard_map/ppermute | solution.py:271
  142.9 1.2 collective-permute-done.4.far_b_ref
  144.1 1.0 copy-done.4
  145.1 8.9 %shard_map.140 = bf16[512,1024]{1,0:T(8,128)(2,1)S(1)} custom-call(s32[4]{0:T(128)S(1)} %and_select_fusion.place_ref, bf16[128,2048]{1,0:T(8,128)(2,1)S(1)} %copy-done.4, bf16[128,2048]{1,0:T(8,128)(2,1)S(1)} %collective-permute-done.1.left_ref, bf16[128,2048]{1,0:T(8,128)(2,1)S(1)} %collective-permute-done.2.right_ref, ...), custom_call_target="tpu_custom_call" | custom-call | flops 2147483648 | bytes 7340048 | tf_op jit(solution)/shard_map/pallas_call | solution.py:27
  154.0 25.3 %all_to_all.19.parts_ref = bf16[16,32,1024]{2,1,0:T(8,128)(2,1)S(1)} all-to-all(bf16[16,32,1024]{2,1,0:T(8,128)(2,1)S(1)} %bitcast.19), channel_id=1, replica_groups=mesh['yh'=2,'z'=8,'x'=4,'yl'=2,'core'=2] {'x','yl','core'}, dimensions={0} | all-to-all | bytes 2097152 | tf_op jit(solution)/shard_map/all_to_all | solution.py:281
  180.0 1.3 collective-permute-start.6
  181.3 5.5 %collective-permute-done.6 = bf16[32,4096]{1,0:T(8,128)(2,1)S(1)} collective-permute-done((bf16[32,4096]{1,0:T(8,128)(2,1)S(1)}, bf16[32,4096]{1,0:T(8,128)(2,1)S(1)}, u32[]{:S(2)}, u32[]{:S(2)}) %collective-permute-start.6) | collective-permute-done | bytes 262176 | tf_op jit(solution)/shard_map/ppermute | solution.py:291
  186.9 2.1 %collective-permute-start.7 = (bf16[2,32,4096]{2,1,0:T(8,128)(2,1)S(1)}, bf16[2,32,4096]{2,1,0:T(8,128)(2,1)S(1)}, u32[]{:S(2)}, u32[]{:S(2)}) collective-permute-start(bf16[2,32,4096]{2,1,0:T(8,128)(2,1)S(1)} %pad_maximum_fusion.2), channel_id=1, source_target_pairs={{0,1},{1,0},{2,3},{3,2},{4,5},{5,4},{6,7},{7,6},{8,9},{9,8},{10,11... | collective-permute-start | bytes 1572872 | tf_op jit(solution)/shard_map/ppermute | solution.py:293
  189.0 1.5 collective-permute-done.7
  190.8 1.1 pad_maximum_fusion
  (50 shorter events, 5.3 us)
Async XLA Ops:
  6.5 25.2 %copy-start = (f32[32,64,128]{2,1,0:T(8,128)S(1)}, f32[32,64,128]{2,1,0:T(8,128)}, u32[]{:S(2)}) copy-start(f32[32,64,128]{2,1,0:T(8,128)} %param.23) | copy-start | bytes 3145732
  6.5 11.0 %copy-start.12 = (bf16[128,32]{0,1:T(8,128)(2,1)S(1)}, bf16[128,32]{0,1:T(8,128)(2,1)}, u32[]{:S(2)}) copy-start(bf16[128,32]{0,1:T(8,128)(2,1)} %param.18) | copy-start | bytes 24580
  6.5 11.1 %copy-start.10 = (f32[32]{0:T(128)S(1)}, f32[32]{0:T(128)}, u32[]{:S(2)}) copy-start(f32[32]{0:T(128)} %param.19) | copy-start | bytes 388
  6.5 11.1 %copy-start.11 = (f32[32]{0:T(128)S(1)}, f32[32]{0:T(128)}, u32[]{:S(2)}) copy-start(f32[32]{0:T(128)} %param.20) | copy-start | bytes 388
  6.5 11.1 %copy-start.1 = (bf16[128,2048]{1,0:T(8,128)(2,1)S(1)}, bf16[128,2048]{1,0:T(8,128)(2,1)}, u32[]{:S(2)}) copy-start(bf16[128,2048]{1,0:T(8,128)(2,1)} %x_ref.3) | copy-start | bytes 1572868
  6.5 11.1 %copy-start.6 = (bf16[128,128]{1,0:T(8,128)(2,1)S(1)}, bf16[128,128]{1,0:T(8,128)(2,1)}, u32[]{:S(2)}) copy-start(bf16[128,128]{1,0:T(8,128)(2,1)} %b_ref.3) | copy-start | bytes 98308
  6.6 137.5 %all-gather.2.cloned.1.call-start = ((), (), s32[]{:S(2)}) async-start(), calls=%async_computation.3 | async-start | bytes 4718592 | tf_op jit(solution)/shard_map/all_gather | solution.py:224
  6.6 9.1 %collective-permute-start.5 = (bf16[64,2048]{1,0:T(8,128)(2,1)}, bf16[64,2048]{1,0:T(8,128)(2,1)S(1)}, u32[]{:S(2)}, u32[]{:S(2)}) collective-permute-start(bf16[64,2048]{1,0:T(8,128)(2,1)} %bitcast.30), channel_id=1, source_target_pairs={{0,128},{128,0},{1,129},{129,1},{2,130},{130,2},{3,131},{131,3},{4... | collective-permute-start | bytes 786440 | tf_op jit(solution)/shard_map/ppermute | solution.py:223
  20.0 51.1 %all-to-all-start = ((f32[32,72,128]{2,1,0:T(8,128)}), f32[32,72,128]{2,1,0:T(8,128)S(1)}, u32[]{:S(2)}, u32[]{:S(2)}) async-start(f32[32,72,128]{2,1,0:T(8,128)} %shard_map.136), calls=%async_computation | async-start | bytes 2359296 | tf_op jit(solution)/shard_map/all_to_all | solution.py:233
  71.1 6.5 %collective-permute-start = (f32[64,128]{1,0:T(8,128)S(1)}, f32[64,128]{1,0:T(8,128)S(1)}, u32[]{:S(2)}, u32[]{:S(2)}) collective-permute-start(f32[64,128]{1,0:T(8,128)S(1)} %shard_map.137), channel_id=1, source_target_pairs={{0,128},{1,129},{2,130},{3,131},{4,132},{5,133},{6,134},{7,135},{8... | collective-permute-start | bytes 98312 | tf_op jit(solution)/shard_map/ppermute | solution.py:241
  78.7 6.9 %copy-start.13 = (f32[32]{0:T(128)S(1)}, f32[32]{0:T(128)}, u32[]{:S(2)}) copy-start(f32[32]{0:T(128)} %param.21) | copy-start | bytes 388
  78.7 43.9 %copy-start.2 = (bf16[128,2048]{1,0:T(8,128)(2,1)S(1)}, bf16[128,2048]{1,0:T(8,128)(2,1)}, u32[]{:S(2)}) copy-start(bf16[128,2048]{1,0:T(8,128)(2,1)} %gate_ref.1) | copy-start | bytes 1572868
  78.7 43.9 %copy-start.7 = (bf16[128,128]{1,0:T(8,128)(2,1)S(1)}, bf16[128,128]{1,0:T(8,128)(2,1)}, u32[]{:S(2)}) copy-start(bf16[128,128]{1,0:T(8,128)(2,1)} %c_ref.1) | copy-start | bytes 98308
  78.7 43.9 %copy-start.9 = (f32[2048]{0:T(1024)S(1)}, f32[2048]{0:T(1024)}, u32[]{:S(2)}) copy-start(f32[2048]{0:T(1024)} %param.22) | copy-start | bytes 24580
  78.7 43.9 %all-to-all-start.1 = ((f32[32,64,128]{2,1,0:T(8,128)}), f32[32,64,128]{2,1,0:T(8,128)S(1)}, u32[]{:S(2)}, u32[]{:S(2)}) async-start(f32[32,64,128]{2,1,0:T(8,128)} %shard_map.138), calls=%async_computation.1 | async-start | bytes 2097152 | tf_op jit(solution)/shard_map/all_to_all | solution.py:249
  122.6 16.9 %copy-start.14 = (s32[4]{0:T(128)S(1)}, s32[4]{0:T(128)}, u32[]{:S(2)}) copy-start(s32[4]{0:T(128)} %constant.87.clone) | copy-start | bytes 52
  124.8 11.5 %collective-permute-start.1 = (bf16[128,2048]{1,0:T(8,128)(2,1)S(1)}, bf16[128,2048]{1,0:T(8,128)(2,1)S(1)}, u32[]{:S(2)}, u32[]{:S(2)}) collective-permute-start(bf16[128,2048]{1,0:T(8,128)(2,1)S(1)} %shard_map.139.own_ref), channel_id=1, source_target_pairs={{0,4},{4,8},{8,12},{12,0},{1,5},{5,9},{9,13},{13,1},{2,6},{6,10},{... | collective-permute-start | bytes 1572872 | tf_op jit(solution)/shard_map/ppermute | solution.py:269
  126.9 11.6 %collective-permute-start.2 = (bf16[128,2048]{1,0:T(8,128)(2,1)S(1)}, bf16[128,2048]{1,0:T(8,128)(2,1)S(1)}, u32[]{:S(2)}, u32[]{:S(2)}) collective-permute-start(bf16[128,2048]{1,0:T(8,128)(2,1)S(1)} %shard_map.139.own_ref), channel_id=1, source_target_pairs={{0,12},{4,0},{8,4},{12,8},{1,13},{5,1},{9,5},{13,9},{2,14},{6,2},{... | collective-permute-start | bytes 1572872 | tf_op jit(solution)/shard_map/ppermute | solution.py:270
  136.3 6.6 %collective-permute-start.3 = (bf16[64,2048]{1,0:T(8,128)(2,1)S(1)}, bf16[64,2048]{1,0:T(8,128)(2,1)S(1)}, u32[]{:S(2)}, u32[]{:S(2)}) collective-permute-start(bf16[64,2048]{1,0:T(8,128)(2,1)S(1)} %slice.28), channel_id=1, source_target_pairs={{0,4},{4,8},{8,12},{12,0},{1,5},{5,9},{9,13},{13,1},{2,6},{6,10},{... | collective-permute-start | bytes 786440 | tf_op jit(solution)/shard_map/ppermute | solution.py:271
  138.5 5.5 %collective-permute-start.4 = (bf16[64,2048]{1,0:T(8,128)(2,1)S(1)}, bf16[64,2048]{1,0:T(8,128)(2,1)S(1)}, u32[]{:S(2)}, u32[]{:S(2)}) collective-permute-start(bf16[64,2048]{1,0:T(8,128)(2,1)S(1)} %slice.29), channel_id=1, source_target_pairs={{0,12},{4,0},{8,4},{12,8},{1,13},{5,1},{9,5},{13,9},{2,14},{6,2},{... | collective-permute-start | bytes 786440 | tf_op jit(solution)/shard_map/ppermute | solution.py:272
  154.0 25.3 %copy-start.5 = (bf16[32,4096]{1,0:T(8,128)(2,1)S(1)}, bf16[32,4096]{1,0:T(8,128)(2,1)}, u32[]{:S(2)}) copy-start(bf16[32,4096]{1,0:T(8,128)(2,1)} %residual_ref.1) | copy-start | bytes 786436
  154.0 25.3 %copy-start.8 = (f32[4096]{0:T(1024)S(1)}, f32[4096]{0:T(1024)}, u32[]{:S(2)}) copy-start(f32[4096]{0:T(1024)} %param.26) | copy-start | bytes 49156
  180.0 6.8 %collective-permute-start.6 = (bf16[32,4096]{1,0:T(8,128)(2,1)S(1)}, bf16[32,4096]{1,0:T(8,128)(2,1)S(1)}, u32[]{:S(2)}, u32[]{:S(2)}) collective-permute-start(bf16[32,4096]{1,0:T(8,128)(2,1)S(1)} %shard_map.141), channel_id=1, source_target_pairs={{0,2},{2,0},{1,3},{3,1},{4,6},{6,4},{5,7},{7,5},{8,10},{10,8},{9,1... | collective-permute-start | bytes 786440 | tf_op jit(solution)/shard_map/ppermute | solution.py:291
  186.9 3.6 %collective-permute-start.7 = (bf16[2,32,4096]{2,1,0:T(8,128)(2,1)S(1)}, bf16[2,32,4096]{2,1,0:T(8,128)(2,1)S(1)}, u32[]{:S(2)}, u32[]{:S(2)}) collective-permute-start(bf16[2,32,4096]{2,1,0:T(8,128)(2,1)S(1)} %pad_maximum_fusion.2), channel_id=1, source_target_pairs={{0,1},{1,0},{2,3},{3,2},{4,5},{5,4},{6,7},{7,6},{8,9},{9,8},{10,11... | collective-permute-start | bytes 1572872 | tf_op jit(solution)/shard_map/ppermute | solution.py:293
  (2 other events, 1.8 us)
Sparse Core Ops, SparseCore 0:
  17.6 102.6 all-gather.1

commit v2 on v1

v2 whole, which is shorter than its diff:
```python
import functools

import jax
import jax.numpy as jnp
from jax import lax
from jax.experimental import pallas as pl
from jax.experimental.pallas import tpu as pltpu
from jax.sharding import Mesh, PartitionSpec as P

EPSILON = 1e-05
HIGHEST = lax.Precision.HIGHEST
SPAN = 128
STATE = 128
HEAD_DIM = 64
EXTRA = 8
BF16, F32 = jnp.bfloat16, jnp.float32
CONTEXT = ("yh", "z", "x")
TENSOR = ("yl", "core")
GROUPS = ("yh", "z")
VMEM_LIMIT = 14 * 2**20


def call(kernel, outs, *, scratch=(), flops=0, smem=0, hbm=0, args=()):
    specs = [pl.BlockSpec(memory_space=pltpu.SMEM)] * smem
    specs += [pl.BlockSpec(memory_space=pltpu.VMEM)] * (len(args) - smem - hbm)
    specs += [pl.BlockSpec(memory_space=pl.ANY)] * hbm
    moved = sum(a.size * a.dtype.itemsize for a in (*args, *jax.tree.leaves(outs)))
    return pl.pallas_call(
        kernel,
        out_shape=outs,
        in_specs=specs,
        out_specs=jax.tree.map(lambda _: pl.BlockSpec(memory_space=pltpu.VMEM), outs),
        scratch_shapes=scratch,
        compiler_params=pltpu.CompilerParams(vmem_limit_bytes=VMEM_LIMIT),
        cost_estimate=pl.CostEstimate(flops=flops, bytes_accessed=moved, transcendentals=0),
    )(*args)


def dot(a, b, precision=None):
    return lax.dot_general(
        a, b, (((1,), (0,)), ((), ())), precision=precision, preferred_element_type=F32
    )


def steps_of(raw, bias, decay_log):
    v = raw.astype(F32) + bias
    step = jnp.maximum(v, 0.0) + jnp.log1p(jnp.exp(-jnp.abs(v)))
    rows = lax.broadcasted_iota(jnp.int32, (SPAN, SPAN), 0)
    columns = lax.broadcasted_iota(jnp.int32, (SPAN, SPAN), 1)
    lower = jnp.where(rows >= columns, 1.0, 0.0).astype(F32)
    cumulative = dot(lower, -jnp.exp(decay_log) * step, HIGHEST)
    return step, cumulative


def split(a):
    high = a.astype(BF16)
    return high, (a - high.astype(F32)).astype(BF16)


def first_lanes(shape):
    return lax.broadcasted_iota(jnp.int32, shape, len(shape) - 1) < HEAD_DIM


def column(a, h):
    return jnp.broadcast_to(a[:, h : h + 1], (a.shape[0], 2 * HEAD_DIM))


def group_columns(ref):
    inner = (ref.shape[1] - 3 * SPAN) // 2
    x, gate = ref.at[:, :inner], ref.at[:, inner : 2 * inner]
    b, c, raw = (ref.at[:, 2 * inner + i * SPAN : 2 * inner + (i + 1) * SPAN] for i in range(3))
    return x, gate, b, c, raw


def fresh_states(x_ref, b, step, cumulative):
    last = cumulative[SPAN - 1 : SPAN, :]
    weight = step * jnp.exp(last - cumulative)
    b_t = jnp.transpose(b)
    b_twice = jnp.concatenate([b_t, b_t], axis=1)
    low = first_lanes((SPAN, SPAN))
    for pair in range(x_ref.shape[1] // SPAN):
        lanes = slice(pair * SPAN, (pair + 1) * SPAN)
        scale = jnp.where(low, column(weight, 2 * pair), column(weight, 2 * pair + 1))
        scaled = x_ref[:, lanes].astype(F32) * scale
        state = dot(b_twice, jnp.concatenate(split(scaled), axis=0))
        log = jnp.where(low[:1], column(last, 2 * pair), column(last, 2 * pair + 1))
        yield pair, state, log


def states_kernel(x_ref, b_ref, raw_ref, bias_ref, decay_ref, out_ref):
    step, cumulative = steps_of(raw_ref[...], bias_ref[...], decay_ref[...])
    each = out_ref.shape[1] // SPAN
    for pair, state, log in fresh_states(x_ref, b_ref[...], step, cumulative):
        member, at = divmod(pair, each)
        out_ref[member, at * STATE : (at + 1) * STATE, :] = state
        out_ref[member, each * STATE + at : each * STATE + at + 1, :] = log


def group_kernel(parts_ref, out_ref):
    members, rows, _ = parts_ref.shape
    pairs = rows // STATE
    slices, size = out_ref.shape[0], out_ref.shape[1] - EXTRA
    for pair in range(pairs):
        here = slice(pair * STATE, (pair + 1) * STATE)
        at = pairs * STATE + pair
        log = parts_ref[0, at : at + 1, :]
        state = parts_ref[0, here, :]
        for member in range(1, members):
            more = parts_ref[member, at : at + 1, :]
            state = jnp.exp(more) * state + parts_ref[member, here, :]
            log = log + more
        for i in range(STATE // size):
            out_ref[pair * (STATE // size) + i, :size, :] = state[i * size : (i + 1) * size]
            out_ref[pair * (STATE // size) + i, size:, :] = jnp.broadcast_to(log, (EXTRA, SPAN))


def enter_kernel(parts_ref, carry_ref, out_ref):
    size = out_ref.shape[1]
    run = carry_ref[...]
    for k in range(parts_ref.shape[0]):
        out_ref[k] = run
        run = jnp.exp(parts_ref[k, size : size + 1, :]) * run + parts_ref[k, :size, :]


def local_kernel(block_ref, bias_ref, decay_ref, skip_ref, mixed_ref, state_ref, log_ref):
    x_ref, _, b_ref, c_ref, raw_ref = group_columns(block_ref)
    heads = bias_ref.shape[1]
    step, cumulative = steps_of(raw_ref[...][:, :heads], bias_ref[...], decay_ref[...])
    step_t, cumulative_t = jnp.transpose(step), jnp.transpose(cumulative)
    scores = lax.dot_general(
        c_ref[...], b_ref[...], (((1,), (1,)), ((), ())), preferred_element_type=F32
    )
    rows = lax.broadcasted_iota(jnp.int32, (SPAN, SPAN), 0)
    columns = lax.broadcasted_iota(jnp.int32, (SPAN, SPAN), 1)
    causal = rows >= columns
    low = first_lanes((SPAN, SPAN))
    for pair, state, log in fresh_states(x_ref, b_ref[...], step, cumulative):
        lanes = slice(pair * SPAN, (pair + 1) * SPAN)
        state_ref[lanes, :] = state
        log_ref[pair : pair + 1, :] = log
        x = x_ref[:, lanes]
        weights = []
        for h in (2 * pair, 2 * pair + 1):
            gap = column(cumulative, h) - cumulative_t[h : h + 1, :]
            within = jnp.exp(jnp.where(causal, gap, -jnp.inf))
            weights.append(jnp.concatenate(split(scores * within * step_t[h : h + 1, :]), axis=1))
        both = dot(jnp.concatenate(weights, axis=0), jnp.concatenate([x, x], axis=0))
        mixed_ref[:, lanes] = jnp.where(low, both[:SPAN], both[SPAN:]) + skip_ref[:, lanes] * x.astype(F32)


def mix_kernel(place_ref, entering_ref, bias_ref, decay_ref, gain_ref, *refs):
    operands, (out_ref, enter_ref, logs_ref, mixed_ref, gated_ref, semaphores) = refs[:-6], refs[-6:]
    n = len(operands) // 4
    blocks, logs, states, mixed = (operands[i * n : (i + 1) * n] for i in range(4))
    pairs = entering_ref.shape[0] // SPAN
    state_copies = [
        pltpu.make_async_copy(states[i], enter_ref.at[place_ref[i]], semaphores.at[i]) for i in range(n)
    ]
    mixed_copies = [
        pltpu.make_async_copy(mixed[i], mixed_ref.at[i], semaphores.at[n + i]) for i in range(n)
    ]
    for copy in (*state_copies, *mixed_copies):
        copy.start()
    for i in range(n):
        logs_ref[place_ref[i]] = logs[i][...]
    for copy in state_copies:
        copy.wait()
    for pair in range(pairs):
        lanes = slice(pair * SPAN, (pair + 1) * SPAN)
        run = entering_ref[lanes, :]
        for p in range(n):
            fresh = enter_ref[p, lanes, :]
            enter_ref[p, lanes, :] = run
            run = jnp.exp(logs_ref[p, pair : pair + 1, :]) * run + fresh
    heads = bias_ref.shape[1]
    low = first_lanes((SPAN, SPAN))
    for i, block_ref in enumerate(blocks):
        mixed_copies[i].wait()
        _, gate_ref, _, c_ref, raw_ref = group_columns(block_ref)
        _, cumulative = steps_of(raw_ref[...][:, :heads], bias_ref[...], decay_ref[...])
        c_twice = jnp.concatenate([c_ref[...], c_ref[...]], axis=1)
        squares = jnp.zeros((SPAN, SPAN), F32)
        place = place_ref[i]
        for pair in range(pairs):
            lanes = slice(pair * SPAN, (pair + 1) * SPAN)
            at = jnp.where(low, column(cumulative, 2 * pair), column(cumulative, 2 * pair + 1))
            carried = dot(c_twice, jnp.concatenate(split(enter_ref[place, lanes, :]), axis=0))
            mixed = mixed_ref[i, :, lanes] + carried * jnp.exp(at)
            gate = gate_ref[:, lanes].astype(F32)
            gated = mixed * (gate / (1.0 + jnp.exp(-gate)))
            gated_ref[:, lanes] = gated
            squares += gated * gated
        root = lax.rsqrt(jnp.sum(squares, axis=-1, keepdims=True) / (pairs * SPAN) + EPSILON)
        to = pl.ds(pl.multiple_of(place * SPAN, SPAN), SPAN)
        for pair in range(pairs):
            lanes = slice(pair * SPAN, (pair + 1) * SPAN)
            out_ref[to, lanes] = (gated_ref[:, lanes] * root * gain_ref[:, lanes]).astype(BF16)


def project_kernel(tokens_ref, weight_ref, out_ref):
    product = lax.dot_general(
        tokens_ref[...], weight_ref[...], (((1,), (1,)), ((), ())), preferred_element_type=F32
    )
    out_ref[...] = product.astype(BF16)


def project(tokens, weight, tile=256):
    rows, depth = tokens.shape
    columns = weight.shape[0]
    return pl.pallas_call(
        project_kernel,
        grid=(columns // tile,),
        out_shape=jax.ShapeDtypeStruct((rows, columns), BF16),
        in_specs=[pl.BlockSpec((rows, depth), lambda i: (0, 0)), pl.BlockSpec((tile, depth), lambda i: (i, 0))],
        out_specs=pl.BlockSpec((rows, tile), lambda i: (0, i)),
        compiler_params=pltpu.CompilerParams(vmem_limit_bytes=VMEM_LIMIT),
        cost_estimate=pl.CostEstimate(
            flops=2 * rows * depth * columns, bytes_accessed=weight.size * 2, transcendentals=0
        ),
    )(tokens, weight)


def finish_kernel(late_ref, parts_ref, residual_ref, gain_ref, out_ref, combined_ref, *, n_x, n_t, n_z):
    late = late_ref[0] > 0
    tokens = residual_ref.shape[0]
    sums = []
    for x in range(n_x):
        total = parts_ref[x * n_t].astype(F32)
        for t in range(1, n_t):
            total += parts_ref[x * n_t + t].astype(F32)
        sums.append(total)
    squares = jnp.zeros((tokens, 2 * HEAD_DIM), F32)
    for z in range(n_z):
        piece = slice(z * 2 * HEAD_DIM, (z + 1) * 2 * HEAD_DIM)
        own = [total[:, piece] for total in sums]
        swapped = [jnp.concatenate([a[:, HEAD_DIM:], a[:, :HEAD_DIM]], axis=1) for a in own]
        ordered = [jnp.where(late, b, a) for a, b in zip(own, swapped)]
        for yh in range(2):
            for x in range(0, n_x, 2):
                block = ((yh * n_z + z) * n_x + x) // 2
                lanes = slice(block * 2 * HEAD_DIM, (block + 1) * 2 * HEAD_DIM)
                half = slice(yh * HEAD_DIM, (yh + 1) * HEAD_DIM)
                both = jnp.concatenate([ordered[x][:, half], ordered[x + 1][:, half]], axis=1)
                combined = residual_ref[:, lanes].astype(F32) + both
                combined_ref[:, lanes] = combined
                squares += combined * combined
    root = lax.rsqrt(jnp.sum(squares, axis=-1, keepdims=True) / combined_ref.shape[1] + EPSILON)
    out_ref[...] = (combined_ref[...] * root * gain_ref[...]).astype(BF16)


def ring(n, by):
    return [(i, (i + by) % n) for i in range(n)]


def on_device(
    mixer_values,
    gate_values,
    input_coefs,
    output_coefs,
    step_raw,
    step_bias,
    decay_log,
    skip_gain,
    group_gain,
    carry_state,
    out_weight,
    residual,
    final_gain,
):
    tokens, inner = mixer_values.shape
    heads = step_raw.shape[1]
    n_z, n_x = lax.axis_size("z"), lax.axis_size("x")
    n_t = lax.axis_size("yl") * lax.axis_size("core")
    groups = 2 * n_z
    at_x = lax.axis_index("x")
    late = lax.axis_index("yh").astype(jnp.int32).reshape(1)
    bias, decay = step_bias.reshape(1, heads), decay_log.reshape(1, heads)
    skip = jnp.repeat(skip_gain, HEAD_DIM).reshape(1, inner)
    pairs = heads // 2
    quarter = inner // n_x
    size = quarter // groups

    states = call(
        states_kernel,
        jax.ShapeDtypeStruct((n_x, quarter + EXTRA, SPAN), F32),
        flops=2 * tokens * inner * STATE * 2,
        args=(mixer_values, input_coefs, step_raw, bias, decay),
    )
    parts = lax.all_to_all(states, "x", 0, 0, tiled=True)

    weight = out_weight.T
    across = lax.ppermute(weight, "yh", ring(2, 1))
    across, parts = lax.optimization_barrier((across, parts))
    weight = jnp.concatenate([weight, across], axis=0)
    weight = lax.all_gather(weight, "z", axis=0, tiled=True)

    own = jnp.concatenate(
        [mixer_values, gate_values, input_coefs, output_coefs, jnp.pad(step_raw, ((0, 0), (0, SPAN - heads)))], axis=1
    )
    own, parts = lax.optimization_barrier((own, parts))
    left = lax.ppermute(own, "x", ring(n_x, 1))
    right = lax.ppermute(own, "x", ring(n_x, -1))
    far = jnp.concatenate(
        [
            lax.ppermute(left[: tokens // 2], "x", ring(n_x, 1)),
            lax.ppermute(right[tokens // 2 :], "x", ring(n_x, -1)),
        ]
    )
    place = (at_x + jnp.array([0, n_x - 1, 1, 2], jnp.int32)) % n_x

    grouped = call(
        group_kernel, jax.ShapeDtypeStruct((groups, size + EXTRA, SPAN), F32), flops=10**6, args=(parts,)
    )
    parts = lax.all_to_all(grouped, GROUPS, 0, 0, tiled=True)
    mine = lax.axis_index(GROUPS)
    each = STATE // size
    carry = lax.dynamic_index_in_dim(
        carry_state.reshape(pairs, SPAN, STATE), at_x * (pairs // n_x) + mine // each, 0, False
    )
    carry = lax.dynamic_slice_in_dim(carry.T, (mine % each) * size, size, 0)
    entering = call(
        enter_kernel, jax.ShapeDtypeStruct((groups, size, SPAN), F32), flops=10**6, args=(parts, carry)
    )
    entering = lax.all_to_all(entering, GROUPS, 0, 0, tiled=True).reshape(1, quarter, SPAN)
    entering = lax.all_to_all(jnp.broadcast_to(entering, (n_x, quarter, SPAN)), "x", 0, 0, tiled=True)

    blocks = (own, left, right, far)
    locals_ = []
    for block in blocks:
        outs = call(
            local_kernel,
            [
                jax.ShapeDtypeStruct((tokens, inner), F32),
                jax.ShapeDtypeStruct((inner, SPAN), F32),
                jax.ShapeDtypeStruct((pairs, SPAN), F32),
            ],
            flops=2 * tokens * inner * tokens * 6,
            args=(block, bias, decay, skip),
        )
        locals_.append(outs)
    mixed, fresh, logs = zip(*locals_)
    normed = call(
        mix_kernel,
        jax.ShapeDtypeStruct((n_x * tokens, inner), BF16),
        scratch=[
            pltpu.VMEM((n_x, inner, SPAN), F32),
            pltpu.VMEM((n_x, pairs, SPAN), F32),
            pltpu.VMEM((n_x, tokens, inner), F32),
            pltpu.VMEM((tokens, inner), F32),
            pltpu.SemaphoreType.DMA((2 * n_x,)),
        ],
        flops=2 * n_x * tokens * inner * STATE * 2,
        smem=1,
        hbm=2 * n_x,
        args=(
            place,
            entering.reshape(inner, SPAN),
            bias,
            decay,
            group_gain.reshape(1, inner),
            *blocks,
            *logs,
            *fresh,
            *mixed,
        ),
    )
    partial = project(normed, weight)
    partial = lax.all_to_all(partial, ("x", *TENSOR), 0, 0, tiled=True)
    rows = residual.shape[0]
    done = call(
        functools.partial(finish_kernel, n_x=n_x, n_t=n_t, n_z=n_z),
        jax.ShapeDtypeStruct(residual.shape, BF16),
        scratch=[pltpu.VMEM(residual.shape, F32)],
        flops=10**6,
        smem=1,
        args=(late, partial.reshape(n_x * n_t, rows, weight.shape[0]), residual, final_gain.reshape(1, -1)),
    )
    across = lax.ppermute(done, "yl", ring(2, 1))
    mine_two = jnp.stack([done, across])
    theirs_two = lax.ppermute(mine_two, "core", ring(2, 1))
    first_y, first_core = lax.axis_index("yl") == 0, lax.axis_index("core") == 0
    even = jnp.where(first_core, mine_two, theirs_two)
    odd = jnp.where(first_core, theirs_two, mine_two)
    low = jnp.where(first_y, jnp.stack([even[0], odd[0]]), jnp.stack([even[1], odd[1]]))
    high = jnp.where(first_y, jnp.stack([even[1], odd[1]]), jnp.stack([even[0], odd[0]]))
    return jnp.concatenate([low, high]).reshape(tokens, residual.shape[1])


def solution(mesh):
    fine = Mesh(mesh.devices.reshape(2, 8, 4, 2, 2), (*CONTEXT, *TENSOR))
    return jax.shard_map(
        on_device,
        mesh=fine,
        in_specs=(
            P(CONTEXT, TENSOR),
            P(CONTEXT, TENSOR),
            P(CONTEXT, TENSOR),
            P(CONTEXT, TENSOR),
            P(CONTEXT, TENSOR),
            P(TENSOR),
            P(TENSOR),
            P(TENSOR),
            P(TENSOR),
            P(TENSOR, None, None),
            P(TENSOR, CONTEXT),
            P((*CONTEXT, *TENSOR), None),
            P(),
        ),
        out_specs=P(CONTEXT, None),
        check_vma=False,
    )
```

time: 199 us -> 194 us (0.975)
  waiting for transfers between devices: 102 us -> 48.5 us
  local copies, waits for them, and re-layouts: 2.42 us -> 37.6 us
  Pallas kernels: 15.2 us -> 24.8 us
  starting transfers between devices: 37.5 us -> 40.8 us
    all_to_all x2 -> x4, waiting for transfers between devices: 76 us -> 18.5 us  [the longest x1 8.04 us: on_device(): lax.all_to_all(entering, GROUPS, 0, 0, tiled=True).reshape(1, quarter, SPAN)]
    unnamed x32 -> x83, local copies, waits for them, and re-layouts: 2.08 us -> 33.6 us
    all_to_all x2 -> x4, starting transfers between devices: 18.6 us -> 28.8 us  [the longest x1 11.9 us: on_device(): parts = lax.all_to_all(grouped, GROUPS, 0, 0, tiled=True)]
    ppermute x6 -> x5, starting transfers between devices: 15.5 us -> 8.62 us  [the longest x1 3 us: on_device(): across = lax.ppermute(weight, 'yh', ring(2, 1))]
    pallas_call x6 -> x9, Pallas kernels: 15.2 us -> 21.7 us  [call(): pl.pallas_call(kernel, out_shape=outs, in_specs=specs, out_specs=jax.tree...]
    ppermute x6 -> x5, waiting for transfers between devices: 18.5 us -> 23 us  [the longest x1 10 us: on_device(): left = lax.ppermute(own, 'x', ring(n_x, 1))]
    pallas_call x0 -> x1, Pallas kernels: none -> 3.08 us  [project(): pl.pallas_call(project_kernel, grid=(columns // tile,), out_shape=jax.Sha...]
  transfers between devices with their start and end apart: 11 -> 12, of which waited for: 9 -> 8; matrix products, arithmetic and copies ran while one was open for 0% -> 4% of each run, Pallas kernels for 3% -> 10%
where the time goes in v2:
time: 194 us; the launch traced here: 192 us
  waiting for transfers between devices  48.5 us (25%)
  starting transfers between devices  40.8 us (21%)
  local copies, waits for them, and re-layouts  37.6 us (19%)
  Pallas kernels  24.8 us (13%)
  blocking collectives  23.9 us (12%)
  between operations  13.8 us (7%)
  other arithmetic  3.09 us (2%)
    unnamed x83, local copies, waits for them, and re-layouts  33.6 us
    all_to_all x1, blocking collectives, on_device(): partial = lax.all_to_all(partial, ('x', *TENSOR), 0, 0, tiled=True)  23.9 us
    pallas_call x9, Pallas kernels, call(): pl.pallas_call(kernel, out_shape=outs, in_specs=specs, out_specs=jax.tree...  21.7 us
    all_to_all x1, starting transfers between devices, on_device(): parts = lax.all_to_all(grouped, GROUPS, 0, 0, tiled=True)  11.9 us
    ppermute x1, waiting for transfers between devices, on_device(): left = lax.ppermute(own, 'x', ring(n_x, 1))  10 us
    ppermute x1, waiting for transfers between devices, on_device(): lax.ppermute(right[tokens // 2:], 'x', ring(n_x, -1))  8.34 us
    all_to_all x1, starting transfers between devices, on_device(): lax.all_to_all(entering, GROUPS, 0, 0, tiled=True).reshape(1, quarter, SPAN)  8.15 us
    all_to_all x1, waiting for transfers between devices, on_device(): lax.all_to_all(entering, GROUPS, 0, 0, tiled=True).reshape(1, quarter, SPAN)  8.04 us
  transfers between devices with their start and end apart: 12, of which 8 were waited for; matrix products, arithmetic and copies ran while one was open for 4% of the time, Pallas kernels for 10%

profile of v2, /device:TPU:1, one launch (start us, length us, event | category | flops | bytes accessed | tf_op | source)
XLA Modules:
  0.0 192.5 jit_solution(16790744606315146819)
XLA Ops:
  10.6 2.3 %shard_map.136 = f32[4,520,128]{2,1,0:T(8,128)} custom-call(bf16[128,2048]{1,0:T(8,128)(2,1)S(1)} %copy-done.5, bf16[128,128]{1,0:T(8,128)(2,1)S(1)} %copy-done.25, bf16[128,32]{1,0:T(8,128)(2,1)S(1)} %copy.15.raw_ref, f32[1,32]{1,0:T(1,128)S(1)} %bitcast.24, f32[1,32]{1,0:T(1,128)S(1)} %bitcast.30), custom_call_target="tpu_custom_call" | custom-call | flops 134217728 | bytes 1630464 | tf_op jit(solution)/shard_map/pallas_call | solution.py:28
  12.8 5.0 %all-to-all-start = ((f32[4,520,128]{2,1,0:T(8,128)}), f32[4,520,128]{2,1,0:T(8,128)S(1)}, u32[]{:S(2)}, u32[]{:S(2)}) async-start(f32[4,520,128]{2,1,0:T(8,128)} %shard_map.136), calls=%async_computation | async-start | bytes 2129920 | tf_op jit(solution)/shard_map/all_to_all | solution.py:289
  17.8 3.0 %collective-permute-start = (bf16[64,2048]{1,0:T(8,128)(2,1)S(1)}, bf16[64,2048]{1,0:T(8,128)(2,1)}, u32[]{:S(2)}, u32[]{:S(2)}) collective-permute-start(bf16[64,2048]{1,0:T(8,128)(2,1)S(1)} %bitcast.39), channel_id=1, source_target_pairs={{0,128},{128,0},{1,129},{129,1},{2,130},{130,2},{3,131},{131,3},{4... | collective-permute-start | bytes 786440 | tf_op jit(solution)/shard_map/ppermute | solution.py:292
  20.8 4.7 %collective-permute-done = bf16[64,2048]{1,0:T(8,128)(2,1)} collective-permute-done((bf16[64,2048]{1,0:T(8,128)(2,1)S(1)}, bf16[64,2048]{1,0:T(8,128)(2,1)}, u32[]{:S(2)}, u32[]{:S(2)}) %collective-permute-start) | collective-permute-done | bytes 262176 | tf_op jit(solution)/shard_map/ppermute | solution.py:292
  25.5 5.7 %all-to-all-done.parts_ref = f32[4,520,128]{2,1,0:T(8,128)S(1)} async-done(((f32[4,520,128]{2,1,0:T(8,128)}), f32[4,520,128]{2,1,0:T(8,128)S(1)}, u32[]{:S(2)}, u32[]{:S(2)}) %all-to-all-start) | async-done | bytes 1064992 | tf_op jit(solution)/shard_map/all_to_all | solution.py:289
  37.0 2.4 %collective-permute-start.2 = (bf16[128,4480]{1,0:T(8,128)(2,1)}, bf16[128,4480]{1,0:T(8,128)(2,1)}, u32[]{:S(2)}, u32[]{:S(2)}) collective-permute-start(bf16[128,4480]{1,0:T(8,128)(2,1)} %pad_dynamic-update-slice_fusion.block_ref.refs_0_), channel_id=1, source_target_pairs={{0,12},{4,0},{8,4},{12,8},{1,13},{5,1},{9,5},{13,9},{2,14},{6,2},{... | collective-permute-start | bytes 3440648 | tf_op jit(solution)/shard_map/ppermute | solution.py:302
  40.2 11.9 %all-to-all-start.1 = ((f32[16,40,128]{2,1,0:T(8,128)}), f32[16,40,128]{2,1,0:T(8,128)S(1)}, u32[]{:S(2)}, u32[]{:S(2)}) async-start(f32[16,40,128]{2,1,0:T(8,128)} %copy-done.7), calls=%async_computation.1 | async-start | bytes 655360 | tf_op jit(solution)/shard_map/all_to_all | solution.py:314
  52.1 10.0 %collective-permute-done.1.block_ref.refs_1_ = bf16[128,4480]{1,0:T(8,128)(2,1)S(1)} collective-permute-done((bf16[128,4480]{1,0:T(8,128)(2,1)}, bf16[128,4480]{1,0:T(8,128)(2,1)S(1)}, u32[]{:S(2)}, u32[]{:S(2)}) %collective-permute-start.1) | collective-permute-done | bytes 1146912 | tf_op jit(solution)/shard_map/ppermute | solution.py:301
  63.2 4.7 %all-to-all-done.1.parts_ref = f32[16,40,128]{2,1,0:T(8,128)S(1)} async-done(((f32[16,40,128]{2,1,0:T(8,128)}), f32[16,40,128]{2,1,0:T(8,128)S(1)}, u32[]{:S(2)}, u32[]{:S(2)}) %all-to-all-start.1) | async-done | bytes 327712 | tf_op jit(solution)/shard_map/all_to_all | solution.py:314
  68.6 8.2 %all-to-all-start.2 = ((f32[16,32,128]{2,1,0:T(8,128)}), f32[16,32,128]{2,1,0:T(8,128)S(1)}, u32[]{:S(2)}, u32[]{:S(2)}) async-start(f32[16,32,128]{2,1,0:T(8,128)} %shard_map.138), calls=%async_computation.2 | async-start | bytes 524288 | tf_op jit(solution)/shard_map/all_to_all | solution.py:324
  77.0 3.3 %shard_map.139 = (f32[128,2048]{1,0:T(8,128)S(1)}, f32[2048,128]{1,0:T(8,128)S(1)}, f32[16,128]{1,0:T(8,128)S(1)}) custom-call(bf16[128,4480]{1,0:T(8,128)(2,1)} %pad_dynamic-update-slice_fusion.block_ref.refs_0_, f32[1,32]{1,0:T(1,128)S(1)} %bitcast.25, f32[1,32]{1,0:T(1,128)S(1)} %bitcast.31, f32[1,2048]{1,0:T(1,128)S(1)} %reshape_reshape.3.skip_ref), custom_call_target="tpu_custom_call" | custom-call | flops 402653184 | bytes 3260672 | tf_op jit(solution)/shard_map/pallas_call | solution.py:28
  82.3 8.0 %all-to-all-done.2 = f32[16,32,128]{2,1,0:T(8,128)S(1)} async-done(((f32[16,32,128]{2,1,0:T(8,128)}), f32[16,32,128]{2,1,0:T(8,128)S(1)}, u32[]{:S(2)}, u32[]{:S(2)}) %all-to-all-start.2) | async-done | bytes 262176 | tf_op jit(solution)/shard_map/all_to_all | solution.py:324
  91.3 3.8 %all-to-all-start.3 = ((f32[4,512,128]{2,1,0:T(8,128)}), f32[4,512,128]{2,1,0:T(8,128)S(1)}, u32[]{:S(2)}, u32[]{:S(2)}) async-start(f32[4,512,128]{2,1,0:T(8,128)} %broadcast_in_dim.11), calls=%async_computation.3 | async-start | bytes 2097152 | tf_op jit(solution)/shard_map/all_to_all | solution.py:325
  96.3 2.9 %collective-permute-start.4 = (bf16[64,4480]{1,0:T(8,128)(2,1)S(1)}, bf16[64,4480]{1,0:T(8,128)(2,1)S(1)}, u32[]{:S(2)}, u32[]{:S(2)}) collective-permute-start(bf16[64,4480]{1,0:T(8,128)(2,1)S(1)} %slice.29), channel_id=1, source_target_pairs={{0,12},{4,0},{8,4},{12,8},{1,13},{5,1},{9,5},{13,9},{2,14},{6,2},{... | collective-permute-start | bytes 1720328 | tf_op jit(solution)/shard_map/ppermute | solution.py:306
  99.2 2.0 %shard_map.140 = (f32[128,2048]{1,0:T(8,128)S(1)}, f32[2048,128]{1,0:T(8,128)S(1)}, f32[16,128]{1,0:T(8,128)S(1)}) custom-call(bf16[128,4480]{1,0:T(8,128)(2,1)S(1)} %collective-permute-done.1.block_ref.refs_1_, f32[1,32]{1,0:T(1,128)S(1)} %bitcast.26, f32[1,32]{1,0:T(1,128)S(1)} %bitcast.32, f32[1,2048]{1,0:T(1,128)S(1)} %reshape_reshape.3.skip_ref), custom_call_target="tpu_custom_call" | custom-call | flops 402653184 | bytes 3260672 | tf_op jit(solution)/shard_map/pallas_call | solution.py:28
  103.2 3.2 %shard_map.141 = (f32[128,2048]{1,0:T(8,128)S(1)}, f32[2048,128]{1,0:T(8,128)S(1)}, f32[16,128]{1,0:T(8,128)S(1)}) custom-call(bf16[128,4480]{1,0:T(8,128)(2,1)} %collective-permute-done.2.block_ref.refs_2_, f32[1,32]{1,0:T(1,128)S(1)} %bitcast.27, f32[1,32]{1,0:T(1,128)S(1)} %bitcast.33, f32[1,2048]{1,0:T(1,128)S(1)} %reshape_reshape.3.skip_ref), custom_call_target="tpu_custom_call" | custom-call | flops 402653184 | bytes 3260672 | tf_op jit(solution)/shard_map/pallas_call | solution.py:28
  109.0 8.3 %collective-permute-done.4 = bf16[64,4480]{1,0:T(8,128)(2,1)S(1)} collective-permute-done((bf16[64,4480]{1,0:T(8,128)(2,1)S(1)}, bf16[64,4480]{1,0:T(8,128)(2,1)S(1)}, u32[]{:S(2)}, u32[]{:S(2)}) %collective-permute-start.4) | collective-permute-done | bytes 573472 | tf_op jit(solution)/shard_map/ppermute | solution.py:306
  117.4 2.0 %shard_map.142 = (f32[128,2048]{1,0:T(8,128)S(1)}, f32[2048,128]{1,0:T(8,128)S(1)}, f32[16,128]{1,0:T(8,128)S(1)}) custom-call(bf16[128,4480]{1,0:T(8,128)(2,1)S(1)} %constant_dynamic-update-slice_fusion.4.block_ref.refs_3_, f32[1,32]{1,0:T(1,128)S(1)} %bitcast.28, f32[1,32]{1,0:T(1,128)S(1)} %bitcast.34, f32[1,2048]{1,0:T(1,128)S(1)} %reshape_reshape.3.skip_ref), custom_call_target="tpu_custom_call" | custom-call | flops 402653184 | bytes 3260672 | tf_op jit(solution)/shard_map/pallas_call | solution.py:28
  133.5 7.5 %shard_map.143.tokens_ref = bf16[512,2048]{1,0:T(8,128)(2,1)S(1)} custom-call(s32[4]{0:T(128)S(1)} %and_select_fusion.place_ref, f32[2048,128]{1,0:T(8,128)S(1)} %bitcast.17, f32[1,32]{1,0:T(1,128)S(1)} %bitcast.29, f32[1,32]{1,0:T(1,128)S(1)} %bitcast.35, f32[1,2048]{1,0:T(1,128)S(1)} %bitcast.23, ...), custom_call_target="tpu_custom_call" | custom-call | flops 536870912 | bytes 16163088 | tf_op jit(solution)/shard_map/pallas_call | solution.py:28
  143.9 2.2 %copy-done.32 = bf16[1024,2048]{1,0:T(8,128)(2,1)S(1)} copy-done((bf16[1024,2048]{1,0:T(8,128)(2,1)S(1)}, bf16[1024,2048]{1,0:T(8,128)(2,1)}, u32[]{:S(2)}) %copy-start.32) | copy-done | bytes 4194328
  146.1 3.1 %shard_map.144 = bf16[512,1024]{1,0:T(8,128)(2,1)S(1)} custom-call(bf16[512,2048]{1,0:T(8,128)(2,1)S(1)} %copy-done.4, bf16[1024,2048]{1,0:T(8,128)(2,1)S(1)} %copy-done.32), custom_call_target="tpu_custom_call" | custom-call | flops 2147483648 | bytes 4194304 | tf_op jit(solution)/shard_map/pallas_call | solution.py:210
  149.2 23.9 %all_to_all.29.parts_ref = bf16[16,32,1024]{2,1,0:T(8,128)(2,1)S(1)} all-to-all(bf16[16,32,1024]{2,1,0:T(8,128)(2,1)S(1)} %bitcast.20), channel_id=1, replica_groups=mesh['yh'=2,'z'=8,'x'=4,'yl'=2,'core'=2] {'x','yl','core'}, dimensions={0} | all-to-all | bytes 2097152 | tf_op jit(solution)/shard_map/all_to_all | solution.py:368
  175.1 5.5 %collective-permute-done.5 = bf16[32,4096]{1,0:T(8,128)(2,1)S(1)} collective-permute-done((bf16[32,4096]{1,0:T(8,128)(2,1)S(1)}, bf16[32,4096]{1,0:T(8,128)(2,1)S(1)}, u32[]{:S(2)}, u32[]{:S(2)}) %collective-permute-start.5) | collective-permute-done | bytes 262176 | tf_op jit(solution)/shard_map/ppermute | solution.py:378
  180.7 2.1 %collective-permute-start.6 = (bf16[2,32,4096]{2,1,0:T(8,128)(2,1)S(1)}, bf16[2,32,4096]{2,1,0:T(8,128)(2,1)S(1)}, u32[]{:S(2)}, u32[]{:S(2)}) collective-permute-start(bf16[2,32,4096]{2,1,0:T(8,128)(2,1)S(1)} %pad_maximum_fusion.2), channel_id=1, source_target_pairs={{0,1},{1,0},{2,3},{3,2},{4,5},{5,4},{6,7},{7,6},{8,9},{9,8},{10,11... | collective-permute-start | bytes 1572872 | tf_op jit(solution)/shard_map/ppermute | solution.py:380
  (110 shorter events, 43.1 us)
Async XLA Ops:
  6.5 56.5 %copy-start = (f32[32,64,128]{2,1,0:T(8,128)S(1)}, f32[32,64,128]{2,1,0:T(8,128)}, u32[]{:S(2)}) copy-start(f32[32,64,128]{2,1,0:T(8,128)} %param.23) | copy-start | bytes 3145732
  12.8 5.0 %copy-start.34 = (bf16[2048,64]{0,1:T(8,128)(2,1)S(1)}, bf16[2048,64]{0,1:T(8,128)(2,1)}, u32[]{:S(2)}) copy-start(bf16[2048,64]{0,1:T(8,128)(2,1)} %param.24) | copy-start | bytes 786436
  12.8 18.4 %all-to-all-start = ((f32[4,520,128]{2,1,0:T(8,128)}), f32[4,520,128]{2,1,0:T(8,128)S(1)}, u32[]{:S(2)}, u32[]{:S(2)}) async-start(f32[4,520,128]{2,1,0:T(8,128)} %shard_map.136), calls=%async_computation | async-start | bytes 2129920 | tf_op jit(solution)/shard_map/all_to_all | solution.py:289
  17.8 15.2 %copy-start.6 = (bf16[128,2048]{1,0:T(8,128)(2,1)S(1)}, bf16[128,2048]{1,0:T(8,128)(2,1)}, u32[]{:S(2)}) copy-start(bf16[128,2048]{1,0:T(8,128)(2,1)} %x_ref.1) | copy-start | bytes 1572868
  17.8 124.6 %all-gather.2.cloned.1.call-start = ((), (), s32[]{:S(2)}) async-start(), calls=%async_computation.5 | async-start | bytes 4718592 | tf_op jit(solution)/shard_map/all_gather | solution.py:295
  17.8 16.2 %copy-start.33 = (bf16[128,2048]{1,0:T(8,128)(2,1)S(1)}, bf16[128,2048]{1,0:T(8,128)(2,1)}, u32[]{:S(2)}) copy-start(bf16[128,2048]{1,0:T(8,128)(2,1)} %param.15) | copy-start | bytes 1572868
  17.8 7.7 %collective-permute-start = (bf16[64,2048]{1,0:T(8,128)(2,1)S(1)}, bf16[64,2048]{1,0:T(8,128)(2,1)}, u32[]{:S(2)}, u32[]{:S(2)}) collective-permute-start(bf16[64,2048]{1,0:T(8,128)(2,1)S(1)} %bitcast.39), channel_id=1, source_target_pairs={{0,128},{128,0},{1,129},{129,1},{2,130},{130,2},{3,131},{131,3},{4... | collective-permute-start | bytes 786440 | tf_op jit(solution)/shard_map/ppermute | solution.py:292
  33.0 2.4 %copy-start.35 = (bf16[128,128]{1,0:T(8,128)(2,1)S(1)}, bf16[128,128]{1,0:T(8,128)(2,1)}, u32[]{:S(2)}) copy-start(bf16[128,128]{1,0:T(8,128)(2,1)} %param.17) | copy-start | bytes 98308
  36.7 25.5 %collective-permute-start.1 = (bf16[128,4480]{1,0:T(8,128)(2,1)}, bf16[128,4480]{1,0:T(8,128)(2,1)S(1)}, u32[]{:S(2)}, u32[]{:S(2)}) collective-permute-start(bf16[128,4480]{1,0:T(8,128)(2,1)} %pad_dynamic-update-slice_fusion.block_ref.refs_0_), channel_id=1, source_target_pairs={{0,4},{4,8},{8,12},{12,0},{1,5},{5,9},{9,13},{13,1},{2,6},{6,10},{... | collective-permute-start | bytes 3440648 | tf_op jit(solution)/shard_map/ppermute | solution.py:301
  37.0 58.2 %collective-permute-start.2 = (bf16[128,4480]{1,0:T(8,128)(2,1)}, bf16[128,4480]{1,0:T(8,128)(2,1)}, u32[]{:S(2)}, u32[]{:S(2)}) collective-permute-start(bf16[128,4480]{1,0:T(8,128)(2,1)} %pad_dynamic-update-slice_fusion.block_ref.refs_0_), channel_id=1, source_target_pairs={{0,12},{4,0},{8,4},{12,8},{1,13},{5,1},{9,5},{13,9},{2,14},{6,2},{... | collective-permute-start | bytes 3440648 | tf_op jit(solution)/shard_map/ppermute | solution.py:302
  40.2 27.7 %all-to-all-start.1 = ((f32[16,40,128]{2,1,0:T(8,128)}), f32[16,40,128]{2,1,0:T(8,128)S(1)}, u32[]{:S(2)}, u32[]{:S(2)}) async-start(f32[16,40,128]{2,1,0:T(8,128)} %copy-done.7), calls=%async_computation.1 | async-start | bytes 655360 | tf_op jit(solution)/shard_map/all_to_all | solution.py:314
  52.1 24.7 %copy-start.36 = (f32[32]{0:T(128)S(1)}, f32[32]{0:T(128)}, u32[]{:S(2)}) copy-start(f32[32]{0:T(128)} %param.21) | copy-start | bytes 388
  52.1 24.8 %copy-start.37 = (s32[4]{0:T(128)S(1)}, s32[4]{0:T(128)}, u32[]{:S(2)}) copy-start(s32[4]{0:T(128)} %constant.88.clone) | copy-start | bytes 52
  52.1 24.8 %copy-start.29 = (f32[32]{0:T(128)S(1)}, f32[32]{0:T(128)}, u32[]{:S(2)}) copy-start(f32[32]{0:T(128)} %param.19) | copy-start | bytes 388
  52.1 24.8 %copy-start.31 = (f32[32]{0:T(128)S(1)}, f32[32]{0:T(128)}, u32[]{:S(2)}) copy-start(f32[32]{0:T(128)} %param.20) | copy-start | bytes 388
  63.0 44.5 %collective-permute-start.3 = (bf16[64,4480]{1,0:T(8,128)(2,1)}, bf16[64,4480]{1,0:T(8,128)(2,1)}, u32[]{:S(2)}, u32[]{:S(2)}) collective-permute-start(bf16[64,4480]{1,0:T(8,128)(2,1)} %slice.28), channel_id=1, source_target_pairs={{0,4},{4,8},{8,12},{12,0},{1,5},{5,9},{9,13},{13,1},{2,6},{6,10},{... | collective-permute-start | bytes 1720328 | tf_op jit(solution)/shard_map/ppermute | solution.py:305
  68.6 21.7 %all-to-all-start.2 = ((f32[16,32,128]{2,1,0:T(8,128)}), f32[16,32,128]{2,1,0:T(8,128)S(1)}, u32[]{:S(2)}, u32[]{:S(2)}) async-start(f32[16,32,128]{2,1,0:T(8,128)} %shard_map.138), calls=%async_computation.2 | async-start | bytes 524288 | tf_op jit(solution)/shard_map/all_to_all | solution.py:324
  91.3 31.1 %all-to-all-start.3 = ((f32[4,512,128]{2,1,0:T(8,128)}), f32[4,512,128]{2,1,0:T(8,128)S(1)}, u32[]{:S(2)}, u32[]{:S(2)}) async-start(f32[4,512,128]{2,1,0:T(8,128)} %broadcast_in_dim.11), calls=%async_computation.3 | async-start | bytes 2097152 | tf_op jit(solution)/shard_map/all_to_all | solution.py:325
  96.3 21.1 %collective-permute-start.4 = (bf16[64,4480]{1,0:T(8,128)(2,1)S(1)}, bf16[64,4480]{1,0:T(8,128)(2,1)S(1)}, u32[]{:S(2)}, u32[]{:S(2)}) collective-permute-start(bf16[64,4480]{1,0:T(8,128)(2,1)S(1)} %slice.29), channel_id=1, source_target_pairs={{0,12},{4,0},{8,4},{12,8},{1,13},{5,1},{9,5},{13,9},{2,14},{6,2},{... | collective-permute-start | bytes 1720328 | tf_op jit(solution)/shard_map/ppermute | solution.py:306
  109.0 13.4 %copy-start.27 = (f32[2048]{0:T(1024)S(1)}, f32[2048]{0:T(1024)}, u32[]{:S(2)}) copy-start(f32[2048]{0:T(1024)} %param.22) | copy-start | bytes 24580
  149.2 23.9 %copy-start.24 = (bf16[32,4096]{1,0:T(8,128)(2,1)S(1)}, bf16[32,4096]{1,0:T(8,128)(2,1)}, u32[]{:S(2)}) copy-start(bf16[32,4096]{1,0:T(8,128)(2,1)} %residual_ref.1) | copy-start | bytes 786436
  149.2 23.9 %copy-start.26 = (f32[4096]{0:T(1024)S(1)}, f32[4096]{0:T(1024)}, u32[]{:S(2)}) copy-start(f32[4096]{0:T(1024)} %param.26) | copy-start | bytes 49156
  173.8 6.8 %collective-permute-start.5 = (bf16[32,4096]{1,0:T(8,128)(2,1)S(1)}, bf16[32,4096]{1,0:T(8,128)(2,1)S(1)}, u32[]{:S(2)}, u32[]{:S(2)}) collective-permute-start(bf16[32,4096]{1,0:T(8,128)(2,1)S(1)} %shard_map.145), channel_id=1, source_target_pairs={{0,2},{2,0},{1,3},{3,1},{4,6},{6,4},{5,7},{7,5},{8,10},{10,8},{9,1... | collective-permute-start | bytes 786440 | tf_op jit(solution)/shard_map/ppermute | solution.py:378
  180.7 3.6 %collective-permute-start.6 = (bf16[2,32,4096]{2,1,0:T(8,128)(2,1)S(1)}, bf16[2,32,4096]{2,1,0:T(8,128)(2,1)S(1)}, u32[]{:S(2)}, u32[]{:S(2)}) collective-permute-start(bf16[2,32,4096]{2,1,0:T(8,128)(2,1)S(1)} %pad_maximum_fusion.2), channel_id=1, source_target_pairs={{0,1},{1,0},{2,3},{3,2},{4,5},{5,4},{6,7},{7,6},{8,9},{9,8},{10,11... | collective-permute-start | bytes 1572872 | tf_op jit(solution)/shard_map/ppermute | solution.py:380
  (26 other events, 29.6 us)
Sparse Core Ops, SparseCore 0:
  33.2 70.6 all-gather.1

commit v3 on v2

v3 whole, which is shorter than its diff:
```python
import functools

import jax
import jax.numpy as jnp
from jax import lax
from jax.experimental import pallas as pl
from jax.experimental.pallas import tpu as pltpu
from jax.sharding import Mesh, PartitionSpec as P

EPSILON = 1e-05
HIGHEST = lax.Precision.HIGHEST
SPAN = 128
STATE = 128
HEAD_DIM = 64
EXTRA = 8
BF16, F32 = jnp.bfloat16, jnp.float32
CONTEXT = ("yh", "z", "x")
TENSOR = ("yl", "core")
GROUPS = ("yh", "z")
VMEM_LIMIT = 14 * 2**20
VMEM_MOST = 61 * 2**20


def call(kernel, outs, *, scratch=(), flops=0, smem=0, vmem=0, hbm_outs=0, args=()):
    specs = [pl.BlockSpec(memory_space=pltpu.SMEM)] * smem
    specs += [pl.BlockSpec(memory_space=pltpu.VMEM)] * vmem
    specs += [pl.BlockSpec(memory_space=pltpu.HBM)] * (len(args) - smem - vmem)
    places = [pltpu.VMEM] * (len(outs) - hbm_outs) + [pltpu.HBM] * hbm_outs
    moved = sum(a.size * a.dtype.itemsize for a in (*args, *outs))
    return pl.pallas_call(
        kernel,
        out_shape=list(outs),
        in_specs=specs,
        out_specs=[pl.BlockSpec(memory_space=m) for m in places],
        scratch_shapes=scratch,
        compiler_params=pltpu.CompilerParams(
            vmem_limit_bytes=VMEM_MOST if len(args) > smem + vmem else VMEM_LIMIT
        ),
        cost_estimate=pl.CostEstimate(flops=flops, bytes_accessed=moved, transcendentals=0),
    )(*args)


def copies(pairs, semaphores, first=0):
    started = [pltpu.make_async_copy(a, b, semaphores.at[first + i]) for i, (a, b) in enumerate(pairs)]
    for copy in started:
        copy.start()
    return started


def dot(a, b, precision=None):
    return lax.dot_general(
        a, b, (((1,), (0,)), ((), ())), precision=precision, preferred_element_type=F32
    )


def steps_of(raw_t, bias, decay_log):
    v = raw_t.astype(F32) + bias
    step = jnp.maximum(v, 0.0) + jnp.log1p(jnp.exp(-jnp.abs(v)))
    rows = lax.broadcasted_iota(jnp.int32, (SPAN, SPAN), 0)
    columns = lax.broadcasted_iota(jnp.int32, (SPAN, SPAN), 1)
    upper = jnp.where(rows <= columns, 1.0, 0.0).astype(F32)
    return step, dot(-jnp.exp(decay_log) * step, upper, HIGHEST)


def split(a):
    high = a.astype(BF16)
    return high, (a - high.astype(F32)).astype(BF16)


def first_lanes(shape):
    return lax.broadcasted_iota(jnp.int32, shape, len(shape) - 1) < HEAD_DIM


def column(a, h):
    return jnp.broadcast_to(a[:, h : h + 1], (a.shape[0], 2 * HEAD_DIM))


def fresh_states(x_ref, b, step_t, cumulative_t):
    last = cumulative_t[:, SPAN - 1 : SPAN]
    weight = jnp.transpose(step_t * jnp.exp(last - cumulative_t))
    b_t = jnp.transpose(b)
    b_twice = jnp.concatenate([b_t, b_t], axis=1)
    low = first_lanes((SPAN, SPAN))
    for pair in range(x_ref.shape[1] // SPAN):
        lanes = slice(pair * SPAN, (pair + 1) * SPAN)
        scale = jnp.where(low, column(weight, 2 * pair), column(weight, 2 * pair + 1))
        scaled = x_ref[:, lanes].astype(F32) * scale
        state = dot(b_twice, jnp.concatenate(split(scaled), axis=0))
        log = jnp.where(
            low[:1], column(last[2 * pair : 2 * pair + 1], 0), column(last[2 * pair + 1 : 2 * pair + 2], 0)
        )
        yield pair, state, log


def states_kernel(x_hbm, gate_hbm, b_hbm, c_hbm, raw_hbm, bias_hbm, decay_hbm, out_ref, packed_hbm, *scratch):
    packed_ref, bias_ref, decay_ref, semaphores = scratch
    inner, heads = x_hbm.shape[1], raw_hbm.shape[0]
    at = 2 * inner
    x_ref = packed_ref.at[:, :inner]
    gets = copies(
        [
            (raw_hbm, packed_ref.at[:heads, at + 2 * SPAN :]),
            (bias_hbm, bias_ref),
            (decay_hbm, decay_ref),
            (b_hbm, packed_ref.at[:, at : at + SPAN]),
            (x_hbm, x_ref),
            (c_hbm, packed_ref.at[:, at + SPAN : at + 2 * SPAN]),
            (gate_hbm, packed_ref.at[:, inner:at]),
        ],
        semaphores,
    )
    packed_ref[heads:, at + 2 * SPAN :] = jnp.zeros((SPAN - heads, SPAN), BF16)
    for copy in gets[:3]:
        copy.wait()
    step, cumulative = steps_of(packed_ref[:heads, at + 2 * SPAN :], bias_ref[...], decay_ref[...])
    for copy in gets[3:]:
        copy.wait()
    (put,) = copies([(packed_ref, packed_hbm)], semaphores, len(gets))
    each = out_ref.shape[1] // SPAN
    for pair, state, log in fresh_states(x_ref, packed_ref[:, at : at + SPAN], step, cumulative):
        member, place = divmod(pair, each)
        out_ref[member, place * STATE : (place + 1) * STATE, :] = state
        out_ref[member, each * STATE + place : each * STATE + place + 1, :] = log
    put.wait()


def group_kernel(parts_ref, out_ref):
    members, rows, _ = parts_ref.shape
    pairs = rows // STATE
    slices, size = out_ref.shape[0], out_ref.shape[1] - EXTRA
    for pair in range(pairs):
        here = slice(pair * STATE, (pair + 1) * STATE)
        at = pairs * STATE + pair
        log = parts_ref[0, at : at + 1, :]
        state = parts_ref[0, here, :]
        for member in range(1, members):
            more = parts_ref[member, at : at + 1, :]
            state = jnp.exp(more) * state + parts_ref[member, here, :]
            log = log + more
        for i in range(STATE // size):
            out_ref[pair * (STATE // size) + i, :size, :] = state[i * size : (i + 1) * size]
            out_ref[pair * (STATE // size) + i, size:, :] = jnp.broadcast_to(log, (EXTRA, SPAN))


def enter_kernel(parts_ref, carry_ref, out_ref):
    size = out_ref.shape[1]
    run = carry_ref[...]
    for k in range(parts_ref.shape[0]):
        out_ref[k] = run
        run = jnp.exp(parts_ref[k, size : size + 1, :]) * run + parts_ref[k, :size, :]


def local_kernel(bias_ref, decay_ref, skip_ref, block_hbm, log_ref, mixed_hbm, state_hbm, *scratch):
    x_ref, coefs_ref, mixed_ref, state_ref, semaphores = scratch
    inner, heads = x_ref.shape[1], bias_ref.shape[0]
    for copy in copies(
        [(block_hbm.at[:, :inner], x_ref), (block_hbm.at[:, 2 * inner :], coefs_ref)], semaphores
    ):
        copy.wait()
    b, c = coefs_ref[:, :SPAN], coefs_ref[:, SPAN : 2 * SPAN]
    step_t, cumulative_t = steps_of(coefs_ref[:heads, 2 * SPAN :], bias_ref[...], decay_ref[...])
    cumulative = jnp.transpose(cumulative_t)
    scores = lax.dot_general(c, b, (((1,), (1,)), ((), ())), preferred_element_type=F32)
    rows = lax.broadcasted_iota(jnp.int32, (SPAN, SPAN), 0)
    columns = lax.broadcasted_iota(jnp.int32, (SPAN, SPAN), 1)
    causal = rows >= columns
    low = first_lanes((SPAN, SPAN))
    for pair, state, log in fresh_states(x_ref, b, step_t, cumulative_t):
        lanes = slice(pair * SPAN, (pair + 1) * SPAN)
        state_ref[lanes, :] = state
        log_ref[pair : pair + 1, :] = log
        x = x_ref[:, lanes]
        weights = []
        for h in (2 * pair, 2 * pair + 1):
            gap = column(cumulative, h) - cumulative_t[h : h + 1, :]
            within = jnp.exp(jnp.where(causal, gap, -jnp.inf))
            weights.append(jnp.concatenate(split(scores * within * step_t[h : h + 1, :]), axis=1))
        both = dot(jnp.concatenate(weights, axis=0), jnp.concatenate([x, x], axis=0))
        mixed_ref[:, lanes] = jnp.where(low, both[:SPAN], both[SPAN:]) + skip_ref[:, lanes] * x.astype(F32)
    for copy in copies([(state_ref, state_hbm), (mixed_ref, mixed_hbm)], semaphores, 2):
        copy.wait()


def mix_kernel(n, place_ref, entering_ref, bias_ref, decay_ref, gain_ref, *refs):
    logs, operands = refs[:n], refs[n : 4 * n + 1]
    out_ref, enter_ref, logs_ref, mixed_ref, block_ref, gated_ref, normed_ref, weight_ref, semaphores = refs[4 * n + 1 :]
    states, mixed, blocks, weight_hbm = operands[:n], operands[n : 2 * n], operands[2 * n : 3 * n], operands[3 * n]
    inner, heads = gated_ref.shape[1], bias_ref.shape[0]
    pairs = inner // SPAN
    state_copies = copies([(states[i], enter_ref.at[place_ref[i]]) for i in range(n)], semaphores)
    block_copies = copies([(blocks[i].at[:, inner:], block_ref.at[i]) for i in range(n)], semaphores, n)
    mixed_copies = copies([(mixed[i], mixed_ref.at[i]) for i in range(n)], semaphores, 2 * n)
    (weight_copy,) = copies([(weight_hbm, weight_ref)], semaphores, 3 * n)
    for i in range(n):
        logs_ref[place_ref[i]] = logs[i][...]
    for copy in state_copies:
        copy.wait()
    for pair in range(pairs):
        lanes = slice(pair * SPAN, (pair + 1) * SPAN)
        run = entering_ref[lanes, :]
        for p in range(n):
            fresh = enter_ref[p, lanes, :]
            enter_ref[p, lanes, :] = run
            run = jnp.exp(logs_ref[p, pair : pair + 1, :]) * run + fresh
    low = first_lanes((SPAN, SPAN))
    for i in range(n):
        block_copies[i].wait()
        mixed_copies[i].wait()
        raw_t = block_ref[i, :heads, inner + 2 * SPAN :]
        _, cumulative_t = steps_of(raw_t, bias_ref[...], decay_ref[...])
        cumulative = jnp.transpose(cumulative_t)
        c = block_ref[i, :, inner + SPAN : inner + 2 * SPAN]
        c_twice = jnp.concatenate([c, c], axis=1)
        squares = jnp.zeros((SPAN, SPAN), F32)
        place = place_ref[i]
        for pair in range(pairs):
            lanes = slice(pair * SPAN, (pair + 1) * SPAN)
            at = jnp.where(low, column(cumulative, 2 * pair), column(cumulative, 2 * pair + 1))
            carried = dot(c_twice, jnp.concatenate(split(enter_ref[place, lanes, :]), axis=0))
            mixer_out = mixed_ref[i, :, lanes] + carried * jnp.exp(at)
            gate = block_ref[i, :, lanes].astype(F32)
            gated = mixer_out * (gate / (1.0 + jnp.exp(-gate)))
            gated_ref[:, lanes] = gated
            squares += gated * gated
        root = lax.rsqrt(jnp.sum(squares, axis=-1, keepdims=True) / inner + EPSILON)
        to = pl.ds(pl.multiple_of(place * SPAN, SPAN), SPAN)
        for pair in range(pairs):
            lanes = slice(pair * SPAN, (pair + 1) * SPAN)
            normed_ref[to, lanes] = (gated_ref[:, lanes] * root * gain_ref[:, lanes]).astype(BF16)
    weight_copy.wait()
    for tile in range(weight_ref.shape[0] // (2 * SPAN)):
        columns = slice(2 * tile * SPAN, 2 * (tile + 1) * SPAN)
        product = lax.dot_general(
            normed_ref[...], weight_ref[columns, :], (((1,), (1,)), ((), ())), preferred_element_type=F32
        )
        out_ref[:, columns] = product.astype(BF16)


def finish_kernel(late_ref, parts_ref, residual_ref, gain_ref, out_ref, combined_ref, *, n_x, n_t, n_z):
    late = late_ref[0] > 0
    tokens = residual_ref.shape[0]
    sums = []
    for x in range(n_x):
        total = parts_ref[x * n_t].astype(F32)
        for t in range(1, n_t):
            total += parts_ref[x * n_t + t].astype(F32)
        sums.append(total)
    squares = jnp.zeros((tokens, 2 * HEAD_DIM), F32)
    for z in range(n_z):
        piece = slice(z * 2 * HEAD_DIM, (z + 1) * 2 * HEAD_DIM)
        own = [total[:, piece] for total in sums]
        swapped = [jnp.concatenate([a[:, HEAD_DIM:], a[:, :HEAD_DIM]], axis=1) for a in own]
        ordered = [jnp.where(late, b, a) for a, b in zip(own, swapped)]
        for yh in range(2):
            for x in range(0, n_x, 2):
                block = ((yh * n_z + z) * n_x + x) // 2
                lanes = slice(block * 2 * HEAD_DIM, (block + 1) * 2 * HEAD_DIM)
                half = slice(yh * HEAD_DIM, (yh + 1) * HEAD_DIM)
                both = jnp.concatenate([ordered[x][:, half], ordered[x + 1][:, half]], axis=1)
                combined = residual_ref[:, lanes].astype(F32) + both
                combined_ref[:, lanes] = combined
                squares += combined * combined
    root = lax.rsqrt(jnp.sum(squares, axis=-1, keepdims=True) / combined_ref.shape[1] + EPSILON)
    out_ref[...] = (combined_ref[...] * root * gain_ref[...]).astype(BF16)


def ring(n, by):
    return [(i, (i + by) % n) for i in range(n)]


def on_device(
    mixer_values,
    gate_values,
    input_coefs,
    output_coefs,
    step_raw,
    step_bias,
    decay_log,
    skip_gain,
    group_gain,
    carry_state,
    out_weight,
    residual,
    final_gain,
):
    tokens, inner = mixer_values.shape
    heads = step_raw.shape[1]
    n_z, n_x = lax.axis_size("z"), lax.axis_size("x")
    n_t = lax.axis_size("yl") * lax.axis_size("core")
    groups = 2 * n_z
    at_x = lax.axis_index("x")
    late = lax.axis_index("yh").astype(jnp.int32).reshape(1)
    bias, decay = step_bias.reshape(heads, 1), decay_log.reshape(heads, 1)
    skip = jnp.repeat(skip_gain, HEAD_DIM).reshape(1, inner)
    pairs = heads // 2
    quarter = inner // n_x
    size = quarter // groups
    packed = 2 * inner + 3 * SPAN

    states, own = call(
        states_kernel,
        [
            jax.ShapeDtypeStruct((n_x, quarter + EXTRA, SPAN), F32),
            jax.ShapeDtypeStruct((tokens, packed), BF16),
        ],
        scratch=[
            pltpu.VMEM((tokens, packed), BF16),
            pltpu.VMEM((heads, 1), F32),
            pltpu.VMEM((heads, 1), F32),
            pltpu.SemaphoreType.DMA((8,)),
        ],
        flops=2 * tokens * inner * STATE * 2,
        hbm_outs=1,
        args=(mixer_values, gate_values, input_coefs, output_coefs, step_raw.T, bias, decay),
    )
    parts = lax.all_to_all(states, "x", 0, 0, tiled=True)

    weight = out_weight.T
    across = lax.ppermute(weight, "yh", ring(2, 1))
    across, parts, own = lax.optimization_barrier((across, parts, own))
    weight = jnp.concatenate([weight, across], axis=0)
    weight = lax.all_gather(weight, "z", axis=0, tiled=True)

    left = lax.ppermute(own, "x", ring(n_x, 1))
    right = lax.ppermute(own, "x", ring(n_x, -1))

    (grouped,) = call(
        group_kernel,
        [jax.ShapeDtypeStruct((groups, size + EXTRA, SPAN), F32)],
        flops=10**6,
        vmem=1,
        args=(parts,),
    )
    parts = lax.all_to_all(grouped, GROUPS, 0, 0, tiled=True)
    parts, left, right = lax.optimization_barrier((parts, left, right))
    onward, back, parts = lax.optimization_barrier((left[: tokens // 2], right[tokens // 2 :], parts))
    far = jnp.concatenate([lax.ppermute(onward, "x", ring(n_x, 1)), lax.ppermute(back, "x", ring(n_x, -1))])
    place = (at_x + jnp.array([0, n_x - 1, 1, 2], jnp.int32)) % n_x
    mine = lax.axis_index(GROUPS)
    each = STATE // size
    carry = lax.dynamic_index_in_dim(
        carry_state.reshape(pairs, SPAN, STATE), at_x * (pairs // n_x) + mine // each, 0, False
    )
    carry = lax.dynamic_slice_in_dim(carry.T, (mine % each) * size, size, 0)
    (entering,) = call(
        enter_kernel,
        [jax.ShapeDtypeStruct((groups, size, SPAN), F32)],
        flops=10**6,
        vmem=2,
        args=(parts, carry),
    )
    entering = lax.all_to_all(entering, GROUPS, 0, 0, tiled=True).reshape(1, quarter, SPAN)
    entering = lax.all_to_all(jnp.broadcast_to(entering, (n_x, quarter, SPAN)), "x", 0, 0, tiled=True)

    blocks = (own, left, right, far)
    locals_ = []
    for block in blocks:
        outs = call(
            local_kernel,
            [
                jax.ShapeDtypeStruct((pairs, SPAN), F32),
                jax.ShapeDtypeStruct((tokens, inner), F32),
                jax.ShapeDtypeStruct((inner, SPAN), F32),
            ],
            scratch=[
                pltpu.VMEM((tokens, inner), BF16),
                pltpu.VMEM((tokens, 3 * SPAN), BF16),
                pltpu.VMEM((tokens, inner), F32),
                pltpu.VMEM((inner, SPAN), F32),
                pltpu.SemaphoreType.DMA((4,)),
            ],
            flops=2 * tokens * inner * tokens * 6,
            vmem=3,
            hbm_outs=2,
            args=(bias, decay, skip, block),
        )
        locals_.append(outs)
    logs, mixed, fresh = zip(*locals_)
    (partial,) = call(
        functools.partial(mix_kernel, n_x),
        [jax.ShapeDtypeStruct((n_x * tokens, weight.shape[0]), BF16)],
        scratch=[
            pltpu.VMEM((n_x, inner, SPAN), F32),
            pltpu.VMEM((n_x, pairs, SPAN), F32),
            pltpu.VMEM((n_x, tokens, inner), F32),
            pltpu.VMEM((n_x, tokens, packed - inner), BF16),
            pltpu.VMEM((tokens, inner), F32),
            pltpu.VMEM((n_x * tokens, inner), BF16),
            pltpu.VMEM(weight.shape, BF16),
            pltpu.SemaphoreType.DMA((3 * n_x + 1,)),
        ],
        flops=2 * n_x * tokens * inner * (STATE * 2 + weight.shape[0]),
        smem=1,
        vmem=4 + n_x,
        args=(
            place,
            entering.reshape(inner, SPAN),
            bias,
            decay,
            group_gain.reshape(1, inner),
            *logs,
            *fresh,
            *mixed,
            *blocks,
            weight,
        ),
    )
    partial = lax.all_to_all(partial, ("x", *TENSOR), 0, 0, tiled=True)
    rows = residual.shape[0]
    (done,) = call(
        functools.partial(finish_kernel, n_x=n_x, n_t=n_t, n_z=n_z),
        [jax.ShapeDtypeStruct(residual.shape, BF16)],
        scratch=[pltpu.VMEM(residual.shape, F32)],
        flops=10**6,
        smem=1,
        vmem=3,
        args=(late, partial.reshape(n_x * n_t, rows, weight.shape[0]), residual, final_gain.reshape(1, -1)),
    )
    across = lax.ppermute(done, "yl", ring(2, 1))
    mine_two = jnp.stack([done, across])
    theirs_two = lax.ppermute(mine_two, "core", ring(2, 1))
    first_y, first_core = lax.axis_index("yl") == 0, lax.axis_index("core") == 0
    even = jnp.where(first_core, mine_two, theirs_two)
    odd = jnp.where(first_core, theirs_two, mine_two)
    low = jnp.where(first_y, jnp.stack([even[0], odd[0]]), jnp.stack([even[1], odd[1]]))
    high = jnp.where(first_y, jnp.stack([even[1], odd[1]]), jnp.stack([even[0], odd[0]]))
    return jnp.concatenate([low, high]).reshape(tokens, residual.shape[1])


def solution(mesh):
    fine = Mesh(mesh.devices.reshape(2, 8, 4, 2, 2), (*CONTEXT, *TENSOR))
    return jax.shard_map(
        on_device,
        mesh=fine,
        in_specs=(
            P(CONTEXT, TENSOR),
            P(CONTEXT, TENSOR),
            P(CONTEXT, TENSOR),
            P(CONTEXT, TENSOR),
            P(CONTEXT, TENSOR),
            P(TENSOR),
            P(TENSOR),
            P(TENSOR),
            P(TENSOR),
            P(TENSOR, None, None),
            P(TENSOR, CONTEXT),
            P((*CONTEXT, *TENSOR), None),
            P(),
        ),
        out_specs=P(CONTEXT, None),
        check_vma=False,
    )
```

time: 194 us -> 169 us (0.87)
  local copies, waits for them, and re-layouts: 37.6 us -> 11.8 us
  Pallas kernels: 24.8 us -> 42.5 us
  waiting for transfers between devices: 48.5 us -> 34.2 us
    unnamed x83 -> x18, local copies, waits for them, and re-layouts: 33.6 us -> 3.01 us
    pallas_call x10 -> x9, Pallas kernels: 24.8 us -> 42.5 us  [call(): pl.pallas_call(kernel, out_shape=list(outs), in_specs=specs, out_specs=[p...]
    all_to_all x1, waiting for transfers between devices: 4.69 us -> 15.3 us  [on_device(): parts = lax.all_to_all(grouped, GROUPS, 0, 0, tiled=True)]
    ppermute x1, waiting for transfers between devices: 10 us -> 0.01 us  [on_device(): left = lax.ppermute(own, 'x', ring(n_x, 1))]
    ppermute x2, waiting for transfers between devices: 8.34 us -> 0.01 us  [the longest x1 0.01 us: on_device(): lax.ppermute(back, 'x', ring(n_x, -1))]
    all_to_all x1, waiting for transfers between devices: 8.04 us -> 0.01 us  [on_device(): lax.all_to_all(entering, GROUPS, 0, 0, tiled=True).reshape(1, quarter, SPAN)]
    reshape x0 -> x2, local copies, waits for them, and re-layouts: none -> 2.76 us  [on_device(): bias, decay = (step_bias.reshape(heads, 1), decay_log.reshape(heads, 1))]
  transfers between devices with their start and end apart: 12 -> 12, of which waited for: 8 -> 6; matrix products, arithmetic and copies ran while one was open for 4% -> 5% of each run, Pallas kernels for 10% -> 15%
where the time goes in v3:
time: 169 us; the launch traced here: 168 us
  Pallas kernels  42.5 us (25%)
  starting transfers between devices  40.1 us (24%)
  waiting for transfers between devices  34.2 us (20%)
  blocking collectives  23.6 us (14%)
  between operations  13.6 us (8%)
  local copies, waits for them, and re-layouts  11.8 us (7%)
  other arithmetic  2.64 us (2%)
    pallas_call x9, Pallas kernels, call(): pl.pallas_call(kernel, out_shape=list(outs), in_specs=specs, out_specs=[p...  42.5 us
    all_to_all x1, blocking collectives, on_device(): partial = lax.all_to_all(partial, ('x', *TENSOR), 0, 0, tiled=True)  23.6 us
    all_to_all x1, waiting for transfers between devices, on_device(): parts = lax.all_to_all(grouped, GROUPS, 0, 0, tiled=True)  15.3 us
    all_to_all x1, starting transfers between devices, on_device(): parts = lax.all_to_all(grouped, GROUPS, 0, 0, tiled=True)  11.9 us
    all_to_all x1, starting transfers between devices, on_device(): lax.all_to_all(entering, GROUPS, 0, 0, tiled=True).reshape(1, quarter, SPAN)  7.56 us
    all_to_all x1, waiting for transfers between devices, on_device(): parts = lax.all_to_all(states, 'x', 0, 0, tiled=True)  5.76 us
    ppermute x1, waiting for transfers between devices, on_device(): across = lax.ppermute(done, 'yl', ring(2, 1))  5.5 us
    all_to_all x1, starting transfers between devices, on_device(): parts = lax.all_to_all(states, 'x', 0, 0, tiled=True)  4.99 us
  transfers between devices with their start and end apart: 12, of which 6 were waited for; matrix products, arithmetic and copies ran while one was open for 5% of the time, Pallas kernels for 15%

profile of v3, /device:TPU:1, one launch (start us, length us, event | category | flops | bytes accessed | tf_op | source)
XLA Modules:
  0.0 168.3 jit_solution(9789580722318706193)
XLA Ops:
  6.5 1.4 copy.15.bias_hbm.bias_ref
  9.3 3.5 %shard_map.136 = (f32[4,520,128]{2,1,0:T(8,128)}, bf16[128,4480]{1,0:T(8,128)(2,1)}) custom-call(bf16[128,2048]{1,0:T(8,128)(2,1)} %x_hbm.1, bf16[128,2048]{1,0:T(8,128)(2,1)} %gate_hbm.1, bf16[128,128]{1,0:T(8,128)(2,1)} %b_hbm.1, bf16[128,128]{1,0:T(8,128)(2,1)} %c_hbm.1, bf16[32,128]{1,0:T(8,128)(2,1)} %bitcast.30, f32[32,1]{1,0:T(8,128)} %copy.15.bias_hbm.bias_ref, ...), custom_call_target="tpu_custom_call" | custom-call | flops 134217728 | bytes 3334400 | tf_op jit(solution)/shard_map/pallas_call | solution.py:30
  12.8 5.0 %all-to-all-start = ((f32[4,520,128]{2,1,0:T(8,128)}), f32[4,520,128]{2,1,0:T(8,128)S(1)}, u32[]{:S(2)}, u32[]{:S(2)}) async-start(f32[4,520,128]{2,1,0:T(8,128)} %get-tuple-element.28), calls=%async_computation | async-start | bytes 2129920 | tf_op jit(solution)/shard_map/all_to_all | solution.py:316
  17.8 3.0 %collective-permute-start = (bf16[64,2048]{1,0:T(8,128)(2,1)S(1)}, bf16[64,2048]{1,0:T(8,128)(2,1)S(1)}, u32[]{:S(2)}, u32[]{:S(2)}) collective-permute-start(bf16[64,2048]{1,0:T(8,128)(2,1)S(1)} %bitcast.27), channel_id=1, source_target_pairs={{0,128},{128,0},{1,129},{129,1},{2,130},{130,2},{3,131},{131,3},{4... | collective-permute-start | bytes 786440 | tf_op jit(solution)/shard_map/ppermute | solution.py:319
  20.8 4.7 %collective-permute-done = bf16[64,2048]{1,0:T(8,128)(2,1)S(1)} collective-permute-done((bf16[64,2048]{1,0:T(8,128)(2,1)S(1)}, bf16[64,2048]{1,0:T(8,128)(2,1)S(1)}, u32[]{:S(2)}, u32[]{:S(2)}) %collective-permute-start) | collective-permute-done | bytes 262176 | tf_op jit(solution)/shard_map/ppermute | solution.py:319
  25.4 5.8 %all-to-all-done.parts_ref = f32[4,520,128]{2,1,0:T(8,128)S(1)} async-done(((f32[4,520,128]{2,1,0:T(8,128)}), f32[4,520,128]{2,1,0:T(8,128)S(1)}, u32[]{:S(2)}, u32[]{:S(2)}) %all-to-all-start) | async-done | bytes 1064992 | tf_op jit(solution)/shard_map/all_to_all | solution.py:316
  32.4 2.4 %collective-permute-start.2 = (bf16[128,4480]{1,0:T(8,128)(2,1)}, bf16[128,4480]{1,0:T(8,128)(2,1)}, u32[]{:S(2)}, u32[]{:S(2)}) collective-permute-start(bf16[128,4480]{1,0:T(8,128)(2,1)} %get-tuple-element.31.block_hbm.refs_12_), channel_id=1, source_target_pairs={{0,12},{4,0},{8,4},{12,8},{1,13},{5,1},{9,5},{13,9},{2,14},{6,2},{... | collective-permute-start | bytes 3440648 | tf_op jit(solution)/shard_map/ppermute | solution.py:325
  35.6 11.9 %all-to-all-start.1 = ((f32[16,40,128]{2,1,0:T(8,128)}), f32[16,40,128]{2,1,0:T(8,128)S(1)}, u32[]{:S(2)}, u32[]{:S(2)}) async-start(f32[16,40,128]{2,1,0:T(8,128)} %shard_map.137), calls=%async_computation.1 | async-start | bytes 655360 | tf_op jit(solution)/shard_map/all_to_all | solution.py:334
  47.5 15.3 %all-to-all-done.1.parts_ref = f32[16,40,128]{2,1,0:T(8,128)S(1)} async-done(((f32[16,40,128]{2,1,0:T(8,128)}), f32[16,40,128]{2,1,0:T(8,128)S(1)}, u32[]{:S(2)}, u32[]{:S(2)}) %all-to-all-start.1) | async-done | bytes 327712 | tf_op jit(solution)/shard_map/all_to_all | solution.py:334
  66.0 7.6 %all-to-all-start.2 = ((f32[16,32,128]{2,1,0:T(8,128)}), f32[16,32,128]{2,1,0:T(8,128)S(1)}, u32[]{:S(2)}, u32[]{:S(2)}) async-start(f32[16,32,128]{2,1,0:T(8,128)} %shard_map.138), calls=%async_computation.2 | async-start | bytes 524288 | tf_op jit(solution)/shard_map/all_to_all | solution.py:352
  74.8 5.8 %shard_map.139 = (f32[16,128]{1,0:T(8,128)}, f32[128,2048]{1,0:T(8,128)}, f32[2048,128]{1,0:T(8,128)}) custom-call(f32[32,1]{1,0:T(8,128)} %copy.15.bias_hbm.bias_ref, f32[32,1]{1,0:T(8,128)} %copy.16.decay_hbm.decay_ref, f32[1,2048]{1,0:T(1,128)} %reshape_reshape.3.skip_ref, bf16[128,4480]{1,0:T(8,128)(2,1)} %get-tuple-element.31.block_hbm.refs_12_), custom_call_target="tpu_custom_call" | custom-call | flops 402653184 | bytes 3260672 | tf_op jit(solution)/shard_map/pallas_call | solution.py:30
  80.6 2.7 %collective-permute-start.4 = (bf16[64,4480]{1,0:T(8,128)(2,1)S(1)}, bf16[64,4480]{1,0:T(8,128)(2,1)}, u32[]{:S(2)}, u32[]{:S(2)}) collective-permute-start(bf16[64,4480]{1,0:T(8,128)(2,1)S(1)} %slice.23), channel_id=1, source_target_pairs={{0,12},{4,0},{8,4},{12,8},{1,13},{5,1},{9,5},{13,9},{2,14},{6,2},{... | collective-permute-start | bytes 1720328 | tf_op jit(solution)/shard_map/ppermute | solution.py:337
  83.3 5.9 %shard_map.140 = (f32[16,128]{1,0:T(8,128)}, f32[128,2048]{1,0:T(8,128)}, f32[2048,128]{1,0:T(8,128)}) custom-call(f32[32,1]{1,0:T(8,128)} %copy.15.bias_hbm.bias_ref, f32[32,1]{1,0:T(8,128)} %copy.16.decay_hbm.decay_ref, f32[1,2048]{1,0:T(1,128)} %reshape_reshape.3.skip_ref, bf16[128,4480]{1,0:T(8,128)(2,1)} %copy-done.4), custom_call_target="tpu_custom_call" | custom-call | flops 402653184 | bytes 3260672 | tf_op jit(solution)/shard_map/pallas_call | solution.py:30
  89.2 5.8 %shard_map.141 = (f32[16,128]{1,0:T(8,128)}, f32[128,2048]{1,0:T(8,128)}, f32[2048,128]{1,0:T(8,128)}) custom-call(f32[32,1]{1,0:T(8,128)} %copy.15.bias_hbm.bias_ref, f32[32,1]{1,0:T(8,128)} %copy.16.decay_hbm.decay_ref, f32[1,2048]{1,0:T(1,128)} %reshape_reshape.3.skip_ref, bf16[128,4480]{1,0:T(8,128)(2,1)} %collective-permute-done.2.block_hbm.refs_14_), custom_call_target="tpu_custom_call" | custom-call | flops 402653184 | bytes 3260672 | tf_op jit(solution)/shard_map/pallas_call | solution.py:30
  96.1 3.7 %all-to-all-start.3 = ((f32[4,512,128]{2,1,0:T(8,128)}), f32[4,512,128]{2,1,0:T(8,128)S(1)}, u32[]{:S(2)}, u32[]{:S(2)}) async-start(f32[4,512,128]{2,1,0:T(8,128)} %broadcast_in_dim.11), calls=%async_computation.3 | async-start | bytes 2097152 | tf_op jit(solution)/shard_map/all_to_all | solution.py:353
  99.8 1.9 %constant_dynamic-update-slice_fusion.1 = bf16[128,4480]{1,0:T(8,128)(2,1)} fusion(bf16[64,4480]{1,0:T(8,128)(2,1)} %collective-permute-done.3), kind=kLoop, calls=%fused_computation.10 | loop fusion | bytes 1146880
  101.8 2.0 %constant_dynamic-update-slice_fusion.block_hbm.refs_15_ = bf16[128,4480]{1,0:T(8,128)(2,1)} fusion(bf16[128,4480]{1,0:T(8,128)(2,1)} %constant_dynamic-update-slice_fusion.1, bf16[64,4480]{1,0:T(8,128)(2,1)} %collective-permute-done.4), kind=kLoop, calls=%fused_computation.9 | loop fusion | bytes 1146880 | tf_op jit(solution)/shard_map/concatenate | solution.py:337
  103.7 5.8 %shard_map.142 = (f32[16,128]{1,0:T(8,128)}, f32[128,2048]{1,0:T(8,128)}, f32[2048,128]{1,0:T(8,128)}) custom-call(f32[32,1]{1,0:T(8,128)} %copy.15.bias_hbm.bias_ref, f32[32,1]{1,0:T(8,128)} %copy.16.decay_hbm.decay_ref, f32[1,2048]{1,0:T(1,128)} %reshape_reshape.3.skip_ref, bf16[128,4480]{1,0:T(8,128)(2,1)} %constant_dynamic-update-slice_fusion.block_hbm.refs_15_), custom_call_target="tpu_custom_call" | custom-call | flops 402653184 | bytes 3260672 | tf_op jit(solution)/shard_map/pallas_call | solution.py:30
  109.5 1.3 all-to-all-done.3
  111.8 13.5 %shard_map.143 = bf16[512,1024]{1,0:T(8,128)(2,1)} custom-call(s32[4]{0:T(128)} %and_select_fusion.place_ref, f32[2048,128]{1,0:T(8,128)} %bitcast.22, f32[32,1]{1,0:T(8,128)} %copy.15.bias_hbm.bias_ref, f32[32,1]{1,0:T(8,128)} %copy.16.decay_hbm.decay_ref, f32[1,2048]{1,0:T(1,128)} %bitcast.29, f32[16,128]{1,0:T(8,128)} %get-tuple-element.36.refs_0_, ...), custom_call_target="tpu_custom_call" | custom-call | flops 2684354560 | bytes 19308816 | tf_op jit(solution)/shard_map/pallas_call | solution.py:30
  125.4 23.6 %all_to_all.29.parts_ref = bf16[16,32,1024]{2,1,0:T(8,128)(2,1)S(1)} all-to-all(bf16[16,32,1024]{2,1,0:T(8,128)(2,1)} %bitcast.23), channel_id=1, replica_groups=mesh['yh'=2,'z'=8,'x'=4,'yl'=2,'core'=2] {'x','yl','core'}, dimensions={0} | all-to-all | bytes 2097152 | tf_op jit(solution)/shard_map/all_to_all | solution.py:408
  151.0 5.5 %collective-permute-done.5 = bf16[32,4096]{1,0:T(8,128)(2,1)S(1)} collective-permute-done((bf16[32,4096]{1,0:T(8,128)(2,1)S(1)}, bf16[32,4096]{1,0:T(8,128)(2,1)S(1)}, u32[]{:S(2)}, u32[]{:S(2)}) %collective-permute-start.5) | collective-permute-done | bytes 262176 | tf_op jit(solution)/shard_map/ppermute | solution.py:419
  156.5 2.1 %collective-permute-start.6 = (bf16[2,32,4096]{2,1,0:T(8,128)(2,1)S(1)}, bf16[2,32,4096]{2,1,0:T(8,128)(2,1)S(1)}, u32[]{:S(2)}, u32[]{:S(2)}) collective-permute-start(bf16[2,32,4096]{2,1,0:T(8,128)(2,1)S(1)} %pad_maximum_fusion.2), channel_id=1, source_target_pairs={{0,1},{1,0},{2,3},{3,2},{4,5},{5,4},{6,7},{7,6},{8,9},{9,8},{10,11... | collective-permute-start | bytes 1572872 | tf_op jit(solution)/shard_map/ppermute | solution.py:421
  158.6 1.5 collective-permute-done.6
  (45 shorter events, 13.0 us)
Async XLA Ops:
  6.5 58.5 %copy-start = (f32[32,64,128]{2,1,0:T(8,128)S(1)}, f32[32,64,128]{2,1,0:T(8,128)}, u32[]{:S(2)}) copy-start(f32[32,64,128]{2,1,0:T(8,128)} %param.23) | copy-start | bytes 3145732
  12.8 5.0 %copy-start.5 = (bf16[2048,64]{0,1:T(8,128)(2,1)S(1)}, bf16[2048,64]{0,1:T(8,128)(2,1)}, u32[]{:S(2)}) copy-start(bf16[2048,64]{0,1:T(8,128)(2,1)} %param.24) | copy-start | bytes 786436
  12.8 18.4 %all-to-all-start = ((f32[4,520,128]{2,1,0:T(8,128)}), f32[4,520,128]{2,1,0:T(8,128)S(1)}, u32[]{:S(2)}, u32[]{:S(2)}) async-start(f32[4,520,128]{2,1,0:T(8,128)} %get-tuple-element.28), calls=%async_computation | async-start | bytes 2129920 | tf_op jit(solution)/shard_map/all_to_all | solution.py:316
  17.8 93.1 %all-gather.2.cloned.1.call-start = ((), (), s32[]{:S(2)}) async-start(), calls=%async_computation.5 | async-start | bytes 4718592 | tf_op jit(solution)/shard_map/all_gather | solution.py:322
  17.8 7.6 %collective-permute-start = (bf16[64,2048]{1,0:T(8,128)(2,1)S(1)}, bf16[64,2048]{1,0:T(8,128)(2,1)S(1)}, u32[]{:S(2)}, u32[]{:S(2)}) collective-permute-start(bf16[64,2048]{1,0:T(8,128)(2,1)S(1)} %bitcast.27), channel_id=1, source_target_pairs={{0,128},{128,0},{1,129},{129,1},{2,130},{130,2},{3,131},{131,3},{4... | collective-permute-start | bytes 786440 | tf_op jit(solution)/shard_map/ppermute | solution.py:319
  32.0 30.8 %collective-permute-start.1 = (bf16[128,4480]{1,0:T(8,128)(2,1)}, bf16[128,4480]{1,0:T(8,128)(2,1)S(1)}, u32[]{:S(2)}, u32[]{:S(2)}) collective-permute-start(bf16[128,4480]{1,0:T(8,128)(2,1)} %get-tuple-element.31.block_hbm.refs_12_), channel_id=1, source_target_pairs={{0,4},{4,8},{8,12},{12,0},{1,5},{5,9},{9,13},{13,1},{2,6},{6,10},{... | collective-permute-start | bytes 3440648 | tf_op jit(solution)/shard_map/ppermute | solution.py:324
  32.4 30.5 %collective-permute-start.2 = (bf16[128,4480]{1,0:T(8,128)(2,1)}, bf16[128,4480]{1,0:T(8,128)(2,1)}, u32[]{:S(2)}, u32[]{:S(2)}) collective-permute-start(bf16[128,4480]{1,0:T(8,128)(2,1)} %get-tuple-element.31.block_hbm.refs_12_), channel_id=1, source_target_pairs={{0,12},{4,0},{8,4},{12,8},{1,13},{5,1},{9,5},{13,9},{2,14},{6,2},{... | collective-permute-start | bytes 3440648 | tf_op jit(solution)/shard_map/ppermute | solution.py:325
  35.6 27.2 %all-to-all-start.1 = ((f32[16,40,128]{2,1,0:T(8,128)}), f32[16,40,128]{2,1,0:T(8,128)S(1)}, u32[]{:S(2)}, u32[]{:S(2)}) async-start(f32[16,40,128]{2,1,0:T(8,128)} %shard_map.137), calls=%async_computation.1 | async-start | bytes 655360 | tf_op jit(solution)/shard_map/all_to_all | solution.py:334
  62.8 2.1 %copy-start.4 = (bf16[128,4480]{1,0:T(8,128)(2,1)}, bf16[128,4480]{1,0:T(8,128)(2,1)S(1)}, u32[]{:S(2)}) copy-start(bf16[128,4480]{1,0:T(8,128)(2,1)S(1)} %collective-permute-done.1.block_hbm.refs_13_) | copy-start | bytes 3440644
  63.8 9.7 %copy-start.6 = (f32[32]{0:T(128)S(1)}, f32[32]{0:T(128)}, u32[]{:S(2)}) copy-start(f32[32]{0:T(128)} %param.21) | copy-start | bytes 388
  63.8 10.5 %copy-start.7 = (s32[4]{0:T(128)S(1)}, s32[4]{0:T(128)}, u32[]{:S(2)}) copy-start(s32[4]{0:T(128)} %constant.86.clone) | copy-start | bytes 52
  64.9 34.9 %collective-permute-start.3 = (bf16[64,4480]{1,0:T(8,128)(2,1)}, bf16[64,4480]{1,0:T(8,128)(2,1)}, u32[]{:S(2)}, u32[]{:S(2)}) collective-permute-start(bf16[64,4480]{1,0:T(8,128)(2,1)} %slice.22), channel_id=1, source_target_pairs={{0,4},{4,8},{8,12},{12,0},{1,5},{5,9},{9,13},{13,1},{2,6},{6,10},{... | collective-permute-start | bytes 1720328 | tf_op jit(solution)/shard_map/ppermute | solution.py:337
  66.0 29.1 %all-to-all-start.2 = ((f32[16,32,128]{2,1,0:T(8,128)}), f32[16,32,128]{2,1,0:T(8,128)S(1)}, u32[]{:S(2)}, u32[]{:S(2)}) async-start(f32[16,32,128]{2,1,0:T(8,128)} %shard_map.138), calls=%async_computation.2 | async-start | bytes 524288 | tf_op jit(solution)/shard_map/all_to_all | solution.py:352
  80.6 21.2 %collective-permute-start.4 = (bf16[64,4480]{1,0:T(8,128)(2,1)S(1)}, bf16[64,4480]{1,0:T(8,128)(2,1)}, u32[]{:S(2)}, u32[]{:S(2)}) collective-permute-start(bf16[64,4480]{1,0:T(8,128)(2,1)S(1)} %slice.23), channel_id=1, source_target_pairs={{0,12},{4,0},{8,4},{12,8},{1,13},{5,1},{9,5},{13,9},{2,14},{6,2},{... | collective-permute-start | bytes 1720328 | tf_op jit(solution)/shard_map/ppermute | solution.py:337
  96.1 14.8 %all-to-all-start.3 = ((f32[4,512,128]{2,1,0:T(8,128)}), f32[4,512,128]{2,1,0:T(8,128)S(1)}, u32[]{:S(2)}, u32[]{:S(2)}) async-start(f32[4,512,128]{2,1,0:T(8,128)} %broadcast_in_dim.11), calls=%async_computation.3 | async-start | bytes 2097152 | tf_op jit(solution)/shard_map/all_to_all | solution.py:353
  110.9 1.0 copy-start.3
  125.3 23.7 %copy-start.1 = (bf16[32,4096]{1,0:T(8,128)(2,1)S(1)}, bf16[32,4096]{1,0:T(8,128)(2,1)}, u32[]{:S(2)}) copy-start(bf16[32,4096]{1,0:T(8,128)(2,1)} %residual_ref.1) | copy-start | bytes 786436
  125.4 23.6 %copy-start.2 = (f32[4096]{0:T(1024)S(1)}, f32[4096]{0:T(1024)}, u32[]{:S(2)}) copy-start(f32[4096]{0:T(1024)} %param.26) | copy-start | bytes 49156
  149.7 6.8 %collective-permute-start.5 = (bf16[32,4096]{1,0:T(8,128)(2,1)S(1)}, bf16[32,4096]{1,0:T(8,128)(2,1)S(1)}, u32[]{:S(2)}, u32[]{:S(2)}) collective-permute-start(bf16[32,4096]{1,0:T(8,128)(2,1)S(1)} %shard_map.144), channel_id=1, source_target_pairs={{0,2},{2,0},{1,3},{3,1},{4,6},{6,4},{5,7},{7,5},{8,10},{10,8},{9,1... | collective-permute-start | bytes 786440 | tf_op jit(solution)/shard_map/ppermute | solution.py:419
  156.5 3.6 %collective-permute-start.6 = (bf16[2,32,4096]{2,1,0:T(8,128)(2,1)S(1)}, bf16[2,32,4096]{2,1,0:T(8,128)(2,1)S(1)}, u32[]{:S(2)}, u32[]{:S(2)}) collective-permute-start(bf16[2,32,4096]{2,1,0:T(8,128)(2,1)S(1)} %pad_maximum_fusion.2), channel_id=1, source_target_pairs={{0,1},{1,0},{2,3},{3,2},{4,5},{5,4},{6,7},{7,6},{8,9},{9,8},{10,11... | collective-permute-start | bytes 1572872 | tf_op jit(solution)/shard_map/ppermute | solution.py:421
Sparse Core Ops, SparseCore 0:
  32.2 70.6 all-gather.1

commit v4 on v3

--- a/solution.py
+++ b/solution.py
@@ -53,13 +53,19 @@
     )
 
 
+def as_column(row):
+    square = (row.shape[1], row.shape[1])
+    same = lax.broadcasted_iota(jnp.int32, square, 0) == lax.broadcasted_iota(jnp.int32, square, 1)
+    return jnp.sum(jnp.where(same, jnp.broadcast_to(row, square), 0.0), axis=1, keepdims=True)
+
+
 def steps_of(raw_t, bias, decay_log):
-    v = raw_t.astype(F32) + bias
+    v = raw_t.astype(F32) + as_column(bias)
     step = jnp.maximum(v, 0.0) + jnp.log1p(jnp.exp(-jnp.abs(v)))
     rows = lax.broadcasted_iota(jnp.int32, (SPAN, SPAN), 0)
     columns = lax.broadcasted_iota(jnp.int32, (SPAN, SPAN), 1)
     upper = jnp.where(rows <= columns, 1.0, 0.0).astype(F32)
-    return step, dot(-jnp.exp(decay_log) * step, upper, HIGHEST)
+    return step, dot(-jnp.exp(as_column(decay_log)) * step, upper, HIGHEST)
 
 
 def split(a):
@@ -75,24 +81,30 @@
     return jnp.broadcast_to(a[:, h : h + 1], (a.shape[0], 2 * HEAD_DIM))
 
 
-def fresh_states(x_ref, b, step_t, cumulative_t):
+def pair_row(a, pair):
+    low = first_lanes((1, 2 * HEAD_DIM))
+    return jnp.where(low, column(a[2 * pair : 2 * pair + 1], 0), column(a[2 * pair + 1 : 2 * pair + 2], 0))
+
+
+def fresh_states(x_ref, b, step_t, cumulative_t, x_in=()):
     last = cumulative_t[:, SPAN - 1 : SPAN]
     weight = jnp.transpose(step_t * jnp.exp(last - cumulative_t))
     b_t = jnp.transpose(b)
     b_twice = jnp.concatenate([b_t, b_t], axis=1)
     low = first_lanes((SPAN, SPAN))
-    for pair in range(x_ref.shape[1] // SPAN):
+    pairs = x_ref.shape[1] // SPAN
+    for pair in range(pairs):
+        if x_in and pair % (pairs // len(x_in)) == 0:
+            for copy in x_in[pair // (pairs // len(x_in))]:
+                copy.wait()
         lanes = slice(pair * SPAN, (pair + 1) * SPAN)
         scale = jnp.where(low, column(weight, 2 * pair), column(weight, 2 * pair + 1))
         scaled = x_ref[:, lanes].astype(F32) * scale
         state = dot(b_twice, jnp.concatenate(split(scaled), axis=0))
-        log = jnp.where(
-            low[:1], column(last[2 * pair : 2 * pair + 1], 0), column(last[2 * pair + 1 : 2 * pair + 2], 0)
-        )
-        yield pair, state, log
-
-
-def states_kernel(x_hbm, gate_hbm, b_hbm, c_hbm, raw_hbm, bias_hbm, decay_hbm, out_ref, packed_hbm, *scratch):
+        yield pair, state, pair_row(last, pair)
+
+
+def states_kernel(x_hbm, gate_hbm, b_hbm, c_hbm, raw_hbm, bias_hbm, decay_hbm, out_ref, top_hbm, bottom_hbm, *scratch):
     packed_ref, bias_ref, decay_ref, semaphores = scratch
     inner, heads = x_hbm.shape[1], raw_hbm.shape[0]
     at = 2 * inner
@@ -115,13 +127,15 @@
     step, cumulative = steps_of(packed_ref[:heads, at + 2 * SPAN :], bias_ref[...], decay_ref[...])
     for copy in gets[3:]:
         copy.wait()
-    (put,) = copies([(packed_ref, packed_hbm)], semaphores, len(gets))
+    half = SPAN // 2
+    puts = copies([(packed_ref.at[:half], top_hbm), (packed_ref.at[half:], bottom_hbm)], semaphores, len(gets))
     each = out_ref.shape[1] // SPAN
     for pair, state, log in fresh_states(x_ref, packed_ref[:, at : at + SPAN], step, cumulative):
         member, place = divmod(pair, each)
         out_ref[member, place * STATE : (place + 1) * STATE, :] = state
         out_ref[member, each * STATE + place : each * STATE + place + 1, :] = log
-    put.wait()
+    for put in puts:
+        put.wait()
 
 
 def group_kernel(parts_ref, out_ref):
@@ -150,12 +164,22 @@
         run = jnp.exp(parts_ref[k, size : size + 1, :]) * run + parts_ref[k, :size, :]
 
 
-def local_kernel(bias_ref, decay_ref, skip_ref, block_hbm, log_ref, mixed_hbm, state_hbm, *scratch):
-    x_ref, coefs_ref, mixed_ref, state_ref, semaphores = scratch
-    inner, heads = x_ref.shape[1], bias_ref.shape[0]
-    for copy in copies(
-        [(block_hbm.at[:, :inner], x_ref), (block_hbm.at[:, 2 * inner :], coefs_ref)], semaphores
-    ):
+def halves(pieces, columns, ref):
+    half = SPAN // 2
+    return [(pieces[0].at[:, columns], ref.at[:half]), (pieces[1].at[:, columns], ref.at[half:])]
+
+
+def local_kernel(bias_ref, decay_ref, skip_ref, top_hbm, bottom_hbm, mixed_hbm, state_hbm, *scratch):
+    x_ref, coefs_ref, mixed_ref, state_ref, gets, puts = scratch
+    inner, heads = x_ref.shape[1], bias_ref.shape[1]
+    step = inner // 4
+    pieces = (top_hbm, bottom_hbm)
+    coefs_in = copies(halves(pieces, slice(2 * inner, None), coefs_ref), gets)
+    x_in = [
+        copies(halves(pieces, pl.ds(i * step, step), x_ref.at[:, pl.ds(i * step, step)]), gets, 2 + 2 * i)
+        for i in range(4)
+    ]
+    for copy in coefs_in:
         copy.wait()
     b, c = coefs_ref[:, :SPAN], coefs_ref[:, SPAN : 2 * SPAN]
     step_t, cumulative_t = steps_of(coefs_ref[:heads, 2 * SPAN :], bias_ref[...], decay_ref[...])
@@ -165,10 +189,11 @@
     columns = lax.broadcasted_iota(jnp.int32, (SPAN, SPAN), 1)
     causal = rows >= columns
     low = first_lanes((SPAN, SPAN))
-    for pair, state, log in fresh_states(x_ref, b, step_t, cumulative_t):
+    each = step // SPAN
+    out = []
+    for pair, state, _ in fresh_states(x_ref, b, step_t, cumulative_t, x_in):
         lanes = slice(pair * SPAN, (pair + 1) * SPAN)
         state_ref[lanes, :] = state
-        log_ref[pair : pair + 1, :] = log
         x = x_ref[:, lanes]
         weights = []
         for h in (2 * pair, 2 * pair + 1):
@@ -177,57 +202,114 @@
             weights.append(jnp.concatenate(split(scores * within * step_t[h : h + 1, :]), axis=1))
         both = dot(jnp.concatenate(weights, axis=0), jnp.concatenate([x, x], axis=0))
         mixed_ref[:, lanes] = jnp.where(low, both[:SPAN], both[SPAN:]) + skip_ref[:, lanes] * x.astype(F32)
-    for copy in copies([(state_ref, state_hbm), (mixed_ref, mixed_hbm)], semaphores, 2):
-        copy.wait()
-
-
-def mix_kernel(n, place_ref, entering_ref, bias_ref, decay_ref, gain_ref, *refs):
-    logs, operands = refs[:n], refs[n : 4 * n + 1]
-    out_ref, enter_ref, logs_ref, mixed_ref, block_ref, gated_ref, normed_ref, weight_ref, semaphores = refs[4 * n + 1 :]
-    states, mixed, blocks, weight_hbm = operands[:n], operands[n : 2 * n], operands[2 * n : 3 * n], operands[3 * n]
-    inner, heads = gated_ref.shape[1], bias_ref.shape[0]
+        if pair % each == each - 1:
+            part = pl.ds(pair // each * step, step)
+            out += copies(
+                [
+                    (state_ref.at[part], state_hbm.at[part]),
+                    (mixed_ref.at[:, part], mixed_hbm.at[:, part]),
+                ],
+                puts,
+                len(out),
+            )
+    for copy in out:
+        copy.wait()
+
+
+def fold_kernel(n, place_ref, bias_ref, decay_ref, *refs):
+    states, mixed, blocks = refs[:n], refs[n : 2 * n], refs[2 * n : 4 * n]
+    out, (enter_ref, logs_ref, mixed_ref, coefs_ref, gets, puts) = refs[4 * n : 5 * n], refs[5 * n :]
+    inner, heads = mixed_ref.shape[2], bias_ref.shape[1]
     pairs = inner // SPAN
-    state_copies = copies([(states[i], enter_ref.at[place_ref[i]]) for i in range(n)], semaphores)
-    block_copies = copies([(blocks[i].at[:, inner:], block_ref.at[i]) for i in range(n)], semaphores, n)
-    mixed_copies = copies([(mixed[i], mixed_ref.at[i]) for i in range(n)], semaphores, 2 * n)
-    (weight_copy,) = copies([(weight_hbm, weight_ref)], semaphores, 3 * n)
-    for i in range(n):
-        logs_ref[place_ref[i]] = logs[i][...]
-    for copy in state_copies:
+    coefs_in, state_in, mixed_in = [], [], []
+    for i in range(n):
+        coefs_in += copies(
+            halves(blocks[2 * i : 2 * i + 2], slice(2 * inner, None), coefs_ref.at[i]), gets, 2 * i
+        )
+    for i in range(n):
+        state_in += copies([(states[i], enter_ref.at[place_ref[i]])], gets, 2 * n + i)
+    for i in range(n):
+        mixed_in += copies([(mixed[i], mixed_ref.at[i])], gets, 3 * n + i)
+    for copy in coefs_in:
+        copy.wait()
+    for i in range(n):
+        raw_t = coefs_ref[i, :heads, 2 * SPAN :]
+        logs_ref[place_ref[i]] = steps_of(raw_t, bias_ref[...], decay_ref[...])[1]
+    for copy in state_in:
         copy.wait()
     for pair in range(pairs):
         lanes = slice(pair * SPAN, (pair + 1) * SPAN)
-        run = entering_ref[lanes, :]
+        run = jnp.zeros((SPAN, SPAN), F32)
         for p in range(n):
             fresh = enter_ref[p, lanes, :]
             enter_ref[p, lanes, :] = run
-            run = jnp.exp(logs_ref[p, pair : pair + 1, :]) * run + fresh
+            run = jnp.exp(pair_row(logs_ref[p, :, SPAN - 1 :], pair)) * run + fresh
     low = first_lanes((SPAN, SPAN))
-    for i in range(n):
-        block_copies[i].wait()
-        mixed_copies[i].wait()
-        raw_t = block_ref[i, :heads, inner + 2 * SPAN :]
-        _, cumulative_t = steps_of(raw_t, bias_ref[...], decay_ref[...])
-        cumulative = jnp.transpose(cumulative_t)
-        c = block_ref[i, :, inner + SPAN : inner + 2 * SPAN]
+    out_copies = []
+    for i in range(n):
+        mixed_in[i].wait()
+        place = place_ref[i]
+        cumulative = jnp.transpose(logs_ref[place])
+        c = coefs_ref[i, :, SPAN : 2 * SPAN]
         c_twice = jnp.concatenate([c, c], axis=1)
-        squares = jnp.zeros((SPAN, SPAN), F32)
-        place = place_ref[i]
         for pair in range(pairs):
             lanes = slice(pair * SPAN, (pair + 1) * SPAN)
             at = jnp.where(low, column(cumulative, 2 * pair), column(cumulative, 2 * pair + 1))
             carried = dot(c_twice, jnp.concatenate(split(enter_ref[place, lanes, :]), axis=0))
+            mixed_ref[i, :, lanes] += carried * jnp.exp(at)
+        out_copies += copies([(mixed_ref.at[i], out[i])], puts, i)
+    for copy in out_copies:
+        copy.wait()
+
+
+def mix_kernel(n, place_ref, bias_ref, decay_ref, gain_ref, *refs):
+    entering_hbm, mixed, blocks, weight_hbm = refs[0], refs[1 : n + 1], refs[n + 1 : 3 * n + 1], refs[3 * n + 1]
+    out_ref, enter_ref, logs_ref, mixed_ref, block_ref, normed_ref, weight_ref, semaphores = refs[3 * n + 2 :]
+    inner, heads = mixed_ref.shape[2], bias_ref.shape[1]
+    pairs = inner // SPAN
+    block_in, mixed_in = [], []
+    for i in range(n):
+        block_in += copies(
+            halves(blocks[2 * i : 2 * i + 2], slice(inner, None), block_ref.at[i]), semaphores, 2 * i
+        )
+        if i == 0:
+            (enter_in,) = copies([(entering_hbm, enter_ref)], semaphores, 3 * n)
+        mixed_in += copies([(mixed[i], mixed_ref.at[i])], semaphores, 2 * n + i)
+    (weight_in,) = copies([(weight_hbm, weight_ref)], semaphores, 3 * n + 1)
+    for i in range(n):
+        for copy in block_in[2 * i : 2 * i + 2]:
+            copy.wait()
+        raw_t = block_ref[i, :heads, inner + 2 * SPAN :]
+        logs_ref[place_ref[i]] = steps_of(raw_t, bias_ref[...], decay_ref[...])[1]
+    before = jnp.zeros((heads, 1), F32)
+    for p in range(n):
+        here = logs_ref[p]
+        logs_ref[p] = here + before
+        before = before + here[:, SPAN - 1 :]
+    enter_in.wait()
+    low = first_lanes((SPAN, SPAN))
+    for i in range(n):
+        mixed_in[i].wait()
+        place = place_ref[i]
+        cumulative = jnp.transpose(logs_ref[place])
+        c = block_ref[i, :, inner + SPAN : inner + 2 * SPAN]
+        c_twice = jnp.concatenate([c, c], axis=1)
+        squares = jnp.zeros((SPAN, SPAN), F32)
+        for pair in range(pairs):
+            lanes = slice(pair * SPAN, (pair + 1) * SPAN)
+            at = jnp.where(low, column(cumulative, 2 * pair), column(cumulative, 2 * pair + 1))
+            carried = dot(c_twice, jnp.concatenate(split(enter_ref[lanes, :]), axis=0))
             mixer_out = mixed_ref[i, :, lanes] + carried * jnp.exp(at)
             gate = block_ref[i, :, lanes].astype(F32)
             gated = mixer_out * (gate / (1.0 + jnp.exp(-gate)))
-            gated_ref[:, lanes] = gated
+            mixed_ref[i, :, lanes] = gated
             squares += gated * gated
         root = lax.rsqrt(jnp.sum(squares, axis=-1, keepdims=True) / inner + EPSILON)
         to = pl.ds(pl.multiple_of(place * SPAN, SPAN), SPAN)
         for pair in range(pairs):
             lanes = slice(pair * SPAN, (pair + 1) * SPAN)
-            normed_ref[to, lanes] = (gated_ref[:, lanes] * root * gain_ref[:, lanes]).astype(BF16)
-    weight_copy.wait()
+            normed_ref[to, lanes] = (mixed_ref[i, :, lanes] * root * gain_ref[:, lanes]).astype(BF16)
+    weight_in.wait()
     for tile in range(weight_ref.shape[0] // (2 * SPAN)):
         columns = slice(2 * tile * SPAN, 2 * (tile + 1) * SPAN)
         product = lax.dot_general(
@@ -290,39 +372,60 @@
     groups = 2 * n_z
     at_x = lax.axis_index("x")
     late = lax.axis_index("yh").astype(jnp.int32).reshape(1)
-    bias, decay = step_bias.reshape(heads, 1), decay_log.reshape(heads, 1)
+    bias, decay = step_bias.reshape(1, heads), decay_log.reshape(1, heads)
     skip = jnp.repeat(skip_gain, HEAD_DIM).reshape(1, inner)
     pairs = heads // 2
     quarter = inner // n_x
     size = quarter // groups
     packed = 2 * inner + 3 * SPAN
 
-    states, own = call(
+    half_block = jax.ShapeDtypeStruct((tokens // 2, packed), BF16)
+    values = jax.ShapeDtypeStruct((tokens, inner), F32)
+
+    weight = out_weight.T
+    across = lax.ppermute(weight, "yh", ring(2, 1))
+
+    states, top, bottom = call(
         states_kernel,
-        [
-            jax.ShapeDtypeStruct((n_x, quarter + EXTRA, SPAN), F32),
-            jax.ShapeDtypeStruct((tokens, packed), BF16),
-        ],
+        [jax.ShapeDtypeStruct((n_x, quarter + EXTRA, SPAN), F32), half_block, half_block],
         scratch=[
             pltpu.VMEM((tokens, packed), BF16),
-            pltpu.VMEM((heads, 1), F32),
-            pltpu.VMEM((heads, 1), F32),
-            pltpu.SemaphoreType.DMA((8,)),
+            pltpu.VMEM((1, heads), F32),
+            pltpu.VMEM((1, heads), F32),
+            pltpu.SemaphoreType.DMA((9,)),
         ],
         flops=2 * tokens * inner * STATE * 2,
-        hbm_outs=1,
+        hbm_outs=2,
         args=(mixer_values, gate_values, input_coefs, output_coefs, step_raw.T, bias, decay),
     )
+    across, states = lax.optimization_barrier((across, states))
     parts = lax.all_to_all(states, "x", 0, 0, tiled=True)
-
-    weight = out_weight.T
-    across = lax.ppermute(weight, "yh", ring(2, 1))
-    across, parts, own = lax.optimization_barrier((across, parts, own))
     weight = jnp.concatenate([weight, across], axis=0)
     weight = lax.all_gather(weight, "z", axis=0, tiled=True)
 
-    left = lax.ppermute(own, "x", ring(n_x, 1))
-    right = lax.ppermute(own, "x", ring(n_x, -1))
+    parts, top, bottom = lax.optimization_barrier((parts, top, bottom))
+    own = (top, bottom)
+    left = tuple(lax.ppermute(a, "x", ring(n_x, 1)) for a in own)
+    right = tuple(lax.ppermute(a, "x", ring(n_x, -1)) for a in (bottom, top))[::-1]
+    place = (at_x + jnp.array([0, n_x - 1, 1, 2], jnp.int32)) % n_x
+
+    def local(block):
+        return call(
+            local_kernel,
+            [values, jax.ShapeDtypeStruct((inner, SPAN), F32)],
+            scratch=[
+                pltpu.VMEM((tokens, inner), BF16),
+                pltpu.VMEM((tokens, 3 * SPAN), BF16),
+                pltpu.VMEM((tokens, inner), F32),
+                pltpu.VMEM((inner, SPAN), F32),
+                pltpu.SemaphoreType.DMA((10,)),
+                pltpu.SemaphoreType.DMA((8,)),
+            ],
+            flops=2 * tokens * inner * tokens * 6,
+            vmem=3,
+            hbm_outs=2,
+            args=(bias, decay, skip, *block),
+        )
 
     (grouped,) = call(
         group_kernel,
@@ -332,10 +435,9 @@
         args=(parts,),
     )
     parts = lax.all_to_all(grouped, GROUPS, 0, 0, tiled=True)
-    parts, left, right = lax.optimization_barrier((parts, left, right))
-    onward, back, parts = lax.optimization_barrier((left[: tokens // 2], right[tokens // 2 :], parts))
-    far = jnp.concatenate([lax.ppermute(onward, "x", ring(n_x, 1)), lax.ppermute(back, "x", ring(n_x, -1))])
-    place = (at_x + jnp.array([0, n_x - 1, 1, 2], jnp.int32)) % n_x
+    own_local, parts, onward, back = lax.optimization_barrier((local(own), parts, left[0], right[1]))
+    left, right = (onward, left[1]), (right[0], back)
+    far = (lax.ppermute(onward, "x", ring(n_x, 1)), lax.ppermute(back, "x", ring(n_x, -1)))
     mine = lax.axis_index(GROUPS)
     each = STATE // size
     carry = lax.dynamic_index_in_dim(
@@ -350,56 +452,49 @@
         args=(parts, carry),
     )
     entering = lax.all_to_all(entering, GROUPS, 0, 0, tiled=True).reshape(1, quarter, SPAN)
+    entering, left_local, right_local, far = lax.optimization_barrier((entering, local(left), local(right), far))
     entering = lax.all_to_all(jnp.broadcast_to(entering, (n_x, quarter, SPAN)), "x", 0, 0, tiled=True)
 
-    blocks = (own, left, right, far)
-    locals_ = []
-    for block in blocks:
-        outs = call(
-            local_kernel,
-            [
-                jax.ShapeDtypeStruct((pairs, SPAN), F32),
-                jax.ShapeDtypeStruct((tokens, inner), F32),
-                jax.ShapeDtypeStruct((inner, SPAN), F32),
-            ],
-            scratch=[
-                pltpu.VMEM((tokens, inner), BF16),
-                pltpu.VMEM((tokens, 3 * SPAN), BF16),
-                pltpu.VMEM((tokens, inner), F32),
-                pltpu.VMEM((inner, SPAN), F32),
-                pltpu.SemaphoreType.DMA((4,)),
-            ],
-            flops=2 * tokens * inner * tokens * 6,
-            vmem=3,
-            hbm_outs=2,
-            args=(bias, decay, skip, block),
-        )
-        locals_.append(outs)
-    logs, mixed, fresh = zip(*locals_)
+    mixed, fresh = zip(own_local, left_local, right_local, local(far))
+    blocks = (*own, *left, *right, *far)
+    mixed = call(
+        functools.partial(fold_kernel, n_x),
+        [values] * n_x,
+        scratch=[
+            pltpu.VMEM((n_x, inner, SPAN), F32),
+            pltpu.VMEM((n_x, heads, SPAN), F32),
+            pltpu.VMEM((n_x, tokens, inner), F32),
+            pltpu.VMEM((n_x, tokens, 3 * SPAN), BF16),
+            pltpu.SemaphoreType.DMA((4 * n_x,)),
+            pltpu.SemaphoreType.DMA((n_x,)),
+        ],
+        flops=2 * n_x * tokens * inner * STATE * 2,
+        smem=1,
+        vmem=2,
+        hbm_outs=n_x,
+        args=(place, bias, decay, *fresh, *mixed, *blocks),
+    )
     (partial,) = call(
         functools.partial(mix_kernel, n_x),
         [jax.ShapeDtypeStruct((n_x * tokens, weight.shape[0]), BF16)],
         scratch=[
-            pltpu.VMEM((n_x, inner, SPAN), F32),
-            pltpu.VMEM((n_x, pairs, SPAN), F32),
+            pltpu.VMEM((inner, SPAN), F32),
+            pltpu.VMEM((n_x, heads, SPAN), F32),
             pltpu.VMEM((n_x, tokens, inner), F32),
             pltpu.VMEM((n_x, tokens, packed - inner), BF16),
-            pltpu.VMEM((tokens, inner), F32),
             pltpu.VMEM((n_x * tokens, inner), BF16),
             pltpu.VMEM(weight.shape, BF16),
-            pltpu.SemaphoreType.DMA((3 * n_x + 1,)),
+            pltpu.SemaphoreType.DMA((3 * n_x + 2,)),
         ],
         flops=2 * n_x * tokens * inner * (STATE * 2 + weight.shape[0]),
         smem=1,
-        vmem=4 + n_x,
+        vmem=3,
         args=(
             place,
-            entering.reshape(inner, SPAN),
             bias,
             decay,
             group_gain.reshape(1, inner),
-            *logs,
-            *fresh,
+            entering.reshape(inner, SPAN),
             *mixed,
             *blocks,
             weight,

time: 169 us -> 164 us (0.970)
  blocking collectives: 23.6 us -> 46.3 us
  waiting for transfers between devices: 34.2 us -> 16.1 us
  local copies, waits for them, and re-layouts: 11.8 us -> 2.97 us
  starting transfers between devices: 40.1 us -> 34.6 us
  Pallas kernels: 42.5 us -> 47.1 us
    all_to_all x0 -> x1, blocking collectives: none -> 18 us  [on_device(): parts = lax.all_to_all(states, 'x', 0, 0, tiled=True)]
    all_to_all x1, waiting for transfers between devices: 15.3 us -> 2.83 us  [on_device(): parts = lax.all_to_all(grouped, GROUPS, 0, 0, tiled=True)]
    all_to_all x1 -> x0, waiting for transfers between devices: 5.76 us -> none  [on_device(): parts = lax.all_to_all(states, 'x', 0, 0, tiled=True)]
    all_to_all x1 -> x0, starting transfers between devices: 4.99 us -> none  [on_device(): parts = lax.all_to_all(states, 'x', 0, 0, tiled=True)]
    all_to_all x1, blocking collectives: 23.6 us -> 28.3 us  [on_device(): partial = lax.all_to_all(partial, ('x', *TENSOR), 0, 0, tiled=True)]
    pallas_call x9 -> x10, Pallas kernels: 42.5 us -> 47.1 us  [call(): pl.pallas_call(kernel, out_shape=list(outs), in_specs=specs, out_specs=[p...]
    ppermute x1, waiting for transfers between devices: 4.65 us -> 1.77 us  [on_device(): across = lax.ppermute(weight, 'yh', ring(2, 1))]
    reshape x2 -> x0, local copies, waits for them, and re-layouts: 2.76 us -> none  [on_device(): bias, decay = (step_bias.reshape(heads, 1), decay_log.reshape(heads, 1))]
  transfers between devices with their start and end apart: 12 -> 13, of which waited for: 6 -> 6; matrix products, arithmetic and copies ran while one was open for 5% -> 2% of each run, Pallas kernels for 15% -> 21%
where the time goes in v4:
time: 164 us; the launch traced here: 163 us
  Pallas kernels  47.1 us (29%)
  blocking collectives  46.3 us (28%)
  starting transfers between devices  34.6 us (21%)
  waiting for transfers between devices  16.1 us (10%)
  between operations  13.6 us (8%)
  local copies, waits for them, and re-layouts  2.97 us (2%)
  other arithmetic  2.69 us (2%)
    pallas_call x10, Pallas kernels, call(): pl.pallas_call(kernel, out_shape=list(outs), in_specs=specs, out_specs=[p...  47.1 us
    all_to_all x1, blocking collectives, on_device(): partial = lax.all_to_all(partial, ('x', *TENSOR), 0, 0, tiled=True)  28.3 us
    all_to_all x1, blocking collectives, on_device(): parts = lax.all_to_all(states, 'x', 0, 0, tiled=True)  18 us
    all_to_all x1, starting transfers between devices, on_device(): parts = lax.all_to_all(grouped, GROUPS, 0, 0, tiled=True)  10.9 us
    all_to_all x1, starting transfers between devices, on_device(): lax.all_to_all(entering, GROUPS, 0, 0, tiled=True).reshape(1, quarter, SPAN)  5.96 us
    ppermute x1, waiting for transfers between devices, on_device(): across = lax.ppermute(done, 'yl', ring(2, 1))  5.5 us
    ppermute x1, starting transfers between devices, on_device(): across = lax.ppermute(weight, 'yh', ring(2, 1))  3.74 us
    all_to_all x1, starting transfers between devices, on_device(): lax.all_to_all(jnp.broadcast_to(entering, (n_x, quarter, SPAN)), 'x', 0,...  3.65 us
  transfers between devices with their start and end apart: 13, of which 6 were waited for; matrix products, arithmetic and copies ran while one was open for 2% of the time, Pallas kernels for 21%

profile of v4, /device:TPU:1, one launch (start us, length us, event | category | flops | bytes accessed | tf_op | source)
XLA Modules:
  0.0 163.3 jit_solution(18136692736803582316)
XLA Ops:
  6.5 3.7 %collective-permute-start = (bf16[64,2048]{1,0:T(8,128)(2,1)}, bf16[64,2048]{1,0:T(8,128)(2,1)S(1)}, u32[]{:S(2)}, u32[]{:S(2)}) collective-permute-start(bf16[64,2048]{1,0:T(8,128)(2,1)} %bitcast.28), channel_id=1, source_target_pairs={{0,128},{128,0},{1,129},{129,1},{2,130},{130,2},{3,131},{131,3},{4... | collective-permute-start | bytes 786440 | tf_op jit(solution)/shard_map/ppermute | solution.py:386
  10.3 3.5 %shard_map.136 = (f32[4,520,128]{2,1,0:T(8,128)}, bf16[64,4480]{1,0:T(8,128)(2,1)}, bf16[64,4480]{1,0:T(8,128)(2,1)}) custom-call(bf16[128,2048]{1,0:T(8,128)(2,1)} %x_hbm.1, bf16[128,2048]{1,0:T(8,128)(2,1)} %gate_hbm.1, bf16[128,128]{1,0:T(8,128)(2,1)} %b_hbm.1, bf16[128,128]{1,0:T(8,128)(2,1)} %c_hbm.1, bf16[32,128]{1,0:T(8,128)(2,1)} %bitcast.30, ...), custom_call_target="tpu_custom_call" | custom-call | flops 134217728 | bytes 3334400 | tf_op jit(solution)/shard_map/pallas_call | solution.py:30
  13.8 1.8 %collective-permute-done = bf16[64,2048]{1,0:T(8,128)(2,1)S(1)} collective-permute-done((bf16[64,2048]{1,0:T(8,128)(2,1)}, bf16[64,2048]{1,0:T(8,128)(2,1)S(1)}, u32[]{:S(2)}, u32[]{:S(2)}) %collective-permute-start) | collective-permute-done | bytes 262176 | tf_op jit(solution)/shard_map/ppermute | solution.py:386
  16.5 18.0 %all_to_all.29.parts_ref = f32[4,520,128]{2,1,0:T(8,128)S(1)} all-to-all(f32[4,520,128]{2,1,0:T(8,128)S(1)} %copy-done.6), channel_id=1, replica_groups=mesh['yh'=2,'z'=8,'x'=4,'yl'=2,'core'=2] {'x'}, dimensions={0} | all-to-all | bytes 2129920 | tf_op jit(solution)/shard_map/all_to_all | solution.py:402
  35.2 10.9 %all-to-all-start.1 = ((f32[16,40,128]{2,1,0:T(8,128)}), f32[16,40,128]{2,1,0:T(8,128)S(1)}, u32[]{:S(2)}, u32[]{:S(2)}) async-start(f32[16,40,128]{2,1,0:T(8,128)} %shard_map.138), calls=%async_computation.1 | async-start | bytes 655360 | tf_op jit(solution)/shard_map/all_to_all | solution.py:437
  46.7 2.3 %collective-permute-start.2 = (bf16[64,4480]{1,0:T(8,128)(2,1)S(1)}, bf16[64,4480]{1,0:T(8,128)(2,1)}, u32[]{:S(2)}, u32[]{:S(2)}) collective-permute-start(bf16[64,4480]{1,0:T(8,128)(2,1)S(1)} %copy-done.5), channel_id=1, source_target_pairs={{0,12},{4,0},{8,4},{12,8},{1,13},{5,1},{9,5},{13,9},{2,14},{6,2},{... | collective-permute-start | bytes 1720328 | tf_op jit(solution)/shard_map/ppermute | solution.py:409
  49.7 1.4 collective-permute-start.3
  51.2 5.3 %shard_map.137 = (f32[128,2048]{1,0:T(8,128)}, f32[2048,128]{1,0:T(8,128)}) custom-call(f32[1,32]{1,0:T(1,128)} %bitcast.33, f32[1,32]{1,0:T(1,128)} %bitcast.40, f32[1,2048]{1,0:T(1,128)} %reshape_reshape.3.skip_ref, bf16[64,4480]{1,0:T(8,128)(2,1)} %get-tuple-element.41.top_hbm.refs_8_.refs_5_, bf16[64,4480]{1,0:T(8,128)(2,1)} %get-tuple-element.42.bottom_hbm.refs_9_.refs_6_), custom_call_target="tpu_custom_call" | custom-call | flops 402653184 | bytes 3252480 | tf_op jit(solution)/shard_map/pallas_call | solution.py:30
  56.5 2.6 %collective-permute-done.1.top_hbm.refs_10_.refs_7_ = bf16[64,4480]{1,0:T(8,128)(2,1)} collective-permute-done((bf16[64,4480]{1,0:T(8,128)(2,1)S(1)}, bf16[64,4480]{1,0:T(8,128)(2,1)}, u32[]{:S(2)}, u32[]{:S(2)}) %collective-permute-start.1) | collective-permute-done | bytes 573472 | tf_op jit(solution)/shard_map/ppermute | solution.py:408
  59.0 2.8 %all-to-all-done.1.parts_ref = f32[16,40,128]{2,1,0:T(8,128)S(1)} async-done(((f32[16,40,128]{2,1,0:T(8,128)}), f32[16,40,128]{2,1,0:T(8,128)S(1)}, u32[]{:S(2)}, u32[]{:S(2)}) %all-to-all-start.1) | async-done | bytes 327712 | tf_op jit(solution)/shard_map/all_to_all | solution.py:437
  62.3 2.2 %collective-permute-start.6 = (bf16[64,4480]{1,0:T(8,128)(2,1)}, bf16[64,4480]{1,0:T(8,128)(2,1)}, u32[]{:S(2)}, u32[]{:S(2)}) collective-permute-start(bf16[64,4480]{1,0:T(8,128)(2,1)} %collective-permute-done.2.bottom_hbm.refs_13_.refs_10_), channel_id=1, source_target_pairs={{0,12},{4,0},{8,4},{12,8},{1,13},{5,1},{9,5},{13,9},{2,14},{6,2},{... | collective-permute-start | bytes 1720328 | tf_op jit(solution)/shard_map/ppermute | solution.py:440
  65.5 6.0 %all-to-all-start.2 = ((f32[16,32,128]{2,1,0:T(8,128)}), f32[16,32,128]{2,1,0:T(8,128)S(1)}, u32[]{:S(2)}, u32[]{:S(2)}) async-start(f32[16,32,128]{2,1,0:T(8,128)} %shard_map.139), calls=%async_computation.2 | async-start | bytes 524288 | tf_op jit(solution)/shard_map/all_to_all | solution.py:454
  71.4 5.3 %shard_map.141 = (f32[128,2048]{1,0:T(8,128)}, f32[2048,128]{1,0:T(8,128)}) custom-call(f32[1,32]{1,0:T(1,128)} %bitcast.34, f32[1,32]{1,0:T(1,128)} %bitcast.41, f32[1,2048]{1,0:T(1,128)} %reshape_reshape.3.skip_ref, bf16[64,4480]{1,0:T(8,128)(2,1)} %collective-permute-done.4.top_hbm.refs_12_.refs_9_, ...), custom_call_target="tpu_custom_call" | custom-call | flops 402653184 | bytes 3252480 | tf_op jit(solution)/shard_map/pallas_call | solution.py:30
  76.7 5.3 %shard_map.140 = (f32[128,2048]{1,0:T(8,128)}, f32[2048,128]{1,0:T(8,128)}) custom-call(f32[1,32]{1,0:T(1,128)} %bitcast.35, f32[1,32]{1,0:T(1,128)} %bitcast.42, f32[1,2048]{1,0:T(1,128)} %reshape_reshape.3.skip_ref, bf16[64,4480]{1,0:T(8,128)(2,1)} %collective-permute-done.1.top_hbm.refs_10_.refs_7_, ...), custom_call_target="tpu_custom_call" | custom-call | flops 402653184 | bytes 3252480 | tf_op jit(solution)/shard_map/pallas_call | solution.py:30
  82.0 1.8 %all-to-all-done.2 = f32[16,32,128]{2,1,0:T(8,128)S(1)} async-done(((f32[16,32,128]{2,1,0:T(8,128)}), f32[16,32,128]{2,1,0:T(8,128)S(1)}, u32[]{:S(2)}, u32[]{:S(2)}) %all-to-all-start.2) | async-done | bytes 262176 | tf_op jit(solution)/shard_map/all_to_all | solution.py:454
  84.9 3.6 %all-to-all-start.3 = ((f32[4,512,128]{2,1,0:T(8,128)}), f32[4,512,128]{2,1,0:T(8,128)S(1)}, u32[]{:S(2)}, u32[]{:S(2)}) async-start(f32[4,512,128]{2,1,0:T(8,128)} %broadcast_in_dim.12), calls=%async_computation.3 | async-start | bytes 2097152 | tf_op jit(solution)/shard_map/all_to_all | solution.py:456
  89.1 5.3 %shard_map.142 = (f32[128,2048]{1,0:T(8,128)}, f32[2048,128]{1,0:T(8,128)}) custom-call(f32[1,32]{1,0:T(1,128)} %bitcast.36, f32[1,32]{1,0:T(1,128)} %bitcast.43, f32[1,2048]{1,0:T(1,128)} %reshape_reshape.3.skip_ref, bf16[64,4480]{1,0:T(8,128)(2,1)} %collective-permute-done.5.top_hbm.refs_14_.refs_11_, ...), custom_call_target="tpu_custom_call" | custom-call | flops 402653184 | bytes 3252480 | tf_op jit(solution)/shard_map/pallas_call | solution.py:30
  94.5 8.2 %shard_map.143 = (f32[128,2048]{1,0:T(8,128)}, f32[128,2048]{1,0:T(8,128)}, f32[128,2048]{1,0:T(8,128)}, f32[128,2048]{1,0:T(8,128)}) custom-call(s32[4]{0:T(128)} %and_select_fusion.place_ref, f32[1,32]{1,0:T(1,128)} %bitcast.37, f32[1,32]{1,0:T(1,128)} %bitcast.44, f32[2048,128]{1,0:T(8,128)} %get-tuple-element.54.refs_0_, ...), custom_call_target="tpu_custom_call" | custom-call | flops 536870912 | bytes 17170704 | tf_op jit(solution)/shard_map/pallas_call | solution.py:30
  103.7 11.9 %shard_map.144 = bf16[512,1024]{1,0:T(8,128)(2,1)} custom-call(s32[4]{0:T(128)} %and_select_fusion.place_ref, f32[1,32]{1,0:T(1,128)} %bitcast.38, f32[1,32]{1,0:T(1,128)} %bitcast.45, f32[1,2048]{1,0:T(1,128)} %bitcast.31, f32[2048,128]{1,0:T(8,128)} %bitcast.23, f32[128,2048]{1,0:T(8,128)} %get-tuple-element.64.refs_1_, ...), custom_call_target="tpu_custom_call" | custom-call | flops 2684354560 | bytes 15081744 | tf_op jit(solution)/shard_map/pallas_call | solution.py:30
  115.7 28.3 %all_to_all.30.parts_ref = bf16[16,32,1024]{2,1,0:T(8,128)(2,1)S(1)} all-to-all(bf16[16,32,1024]{2,1,0:T(8,128)(2,1)} %bitcast.24), channel_id=1, replica_groups=mesh['yh'=2,'z'=8,'x'=4,'yl'=2,'core'=2] {'x','yl','core'}, dimensions={0} | all-to-all | bytes 2097152 | tf_op jit(solution)/shard_map/all_to_all | solution.py:503
  144.7 1.3 collective-permute-start.7
  146.0 5.5 %collective-permute-done.7 = bf16[32,4096]{1,0:T(8,128)(2,1)S(1)} collective-permute-done((bf16[32,4096]{1,0:T(8,128)(2,1)S(1)}, bf16[32,4096]{1,0:T(8,128)(2,1)S(1)}, u32[]{:S(2)}, u32[]{:S(2)}) %collective-permute-start.7) | collective-permute-done | bytes 262176 | tf_op jit(solution)/shard_map/ppermute | solution.py:514
  151.5 2.1 %collective-permute-start.8 = (bf16[2,32,4096]{2,1,0:T(8,128)(2,1)S(1)}, bf16[2,32,4096]{2,1,0:T(8,128)(2,1)S(1)}, u32[]{:S(2)}, u32[]{:S(2)}) collective-permute-start(bf16[2,32,4096]{2,1,0:T(8,128)(2,1)S(1)} %pad_maximum_fusion.2), channel_id=1, source_target_pairs={{0,1},{1,0},{2,3},{3,2},{4,5},{5,4},{6,7},{7,6},{8,9},{9,8},{10,11... | collective-permute-start | bytes 1572872 | tf_op jit(solution)/shard_map/ppermute | solution.py:516
  153.6 1.5 collective-permute-done.8
  (47 shorter events, 8.9 us)
Async XLA Ops:
  6.5 58.0 %copy-start = (f32[32,64,128]{2,1,0:T(8,128)S(1)}, f32[32,64,128]{2,1,0:T(8,128)}, u32[]{:S(2)}) copy-start(f32[32,64,128]{2,1,0:T(8,128)} %param.23) | copy-start | bytes 3145732
  6.5 9.0 %copy-start.7 = (bf16[2048,64]{0,1:T(8,128)(2,1)S(1)}, bf16[2048,64]{0,1:T(8,128)(2,1)}, u32[]{:S(2)}) copy-start(bf16[2048,64]{0,1:T(8,128)(2,1)} %param.24) | copy-start | bytes 786436
  6.5 96.2 %all-gather.2.cloned.1.call-start = ((), (), s32[]{:S(2)}) async-start(), calls=%async_computation.5 | async-start | bytes 4718592 | tf_op jit(solution)/shard_map/all_gather | solution.py:404
  6.5 9.0 %collective-permute-start = (bf16[64,2048]{1,0:T(8,128)(2,1)}, bf16[64,2048]{1,0:T(8,128)(2,1)S(1)}, u32[]{:S(2)}, u32[]{:S(2)}) collective-permute-start(bf16[64,2048]{1,0:T(8,128)(2,1)} %bitcast.28), channel_id=1, source_target_pairs={{0,128},{128,0},{1,129},{129,1},{2,130},{130,2},{3,131},{131,3},{4... | collective-permute-start | bytes 786440 | tf_op jit(solution)/shard_map/ppermute | solution.py:386
  13.8 2.7 %copy-start.6 = (f32[4,520,128]{2,1,0:T(8,128)S(1)}, f32[4,520,128]{2,1,0:T(8,128)}, u32[]{:S(2)}) copy-start(f32[4,520,128]{2,1,0:T(8,128)} %get-tuple-element.38) | copy-start | bytes 3194884
  34.4 11.7 %copy-start.4 = (bf16[64,4480]{1,0:T(8,128)(2,1)S(1)}, bf16[64,4480]{1,0:T(8,128)(2,1)}, u32[]{:S(2)}) copy-start(bf16[64,4480]{1,0:T(8,128)(2,1)} %get-tuple-element.41.top_hbm.refs_8_.refs_5_) | copy-start | bytes 1720324
  34.4 12.2 %copy-start.5 = (bf16[64,4480]{1,0:T(8,128)(2,1)S(1)}, bf16[64,4480]{1,0:T(8,128)(2,1)}, u32[]{:S(2)}) copy-start(bf16[64,4480]{1,0:T(8,128)(2,1)} %get-tuple-element.42.bottom_hbm.refs_9_.refs_6_) | copy-start | bytes 1720324
  34.4 14.5 %copy-start.8 = (f32[32]{0:T(128)S(1)}, f32[32]{0:T(128)}, u32[]{:S(2)}) copy-start(f32[32]{0:T(128)} %param.21) | copy-start | bytes 388
  35.2 26.6 %all-to-all-start.1 = ((f32[16,40,128]{2,1,0:T(8,128)}), f32[16,40,128]{2,1,0:T(8,128)S(1)}, u32[]{:S(2)}, u32[]{:S(2)}) async-start(f32[16,40,128]{2,1,0:T(8,128)} %shard_map.138), calls=%async_computation.1 | async-start | bytes 655360 | tf_op jit(solution)/shard_map/all_to_all | solution.py:437
  46.2 12.8 %collective-permute-start.1 = (bf16[64,4480]{1,0:T(8,128)(2,1)S(1)}, bf16[64,4480]{1,0:T(8,128)(2,1)}, u32[]{:S(2)}, u32[]{:S(2)}) collective-permute-start(bf16[64,4480]{1,0:T(8,128)(2,1)S(1)} %copy-done.4), channel_id=1, source_target_pairs={{0,4},{4,8},{8,12},{12,0},{1,5},{5,9},{9,13},{13,1},{2,6},{6,10},{... | collective-permute-start | bytes 1720328 | tf_op jit(solution)/shard_map/ppermute | solution.py:408
  46.7 12.4 %collective-permute-start.2 = (bf16[64,4480]{1,0:T(8,128)(2,1)S(1)}, bf16[64,4480]{1,0:T(8,128)(2,1)}, u32[]{:S(2)}, u32[]{:S(2)}) collective-permute-start(bf16[64,4480]{1,0:T(8,128)(2,1)S(1)} %copy-done.5), channel_id=1, source_target_pairs={{0,12},{4,0},{8,4},{12,8},{1,13},{5,1},{9,5},{13,9},{2,14},{6,2},{... | collective-permute-start | bytes 1720328 | tf_op jit(solution)/shard_map/ppermute | solution.py:409
  48.9 22.5 %collective-permute-start.4 = (bf16[64,4480]{1,0:T(8,128)(2,1)S(1)}, bf16[64,4480]{1,0:T(8,128)(2,1)}, u32[]{:S(2)}, u32[]{:S(2)}) collective-permute-start(bf16[64,4480]{1,0:T(8,128)(2,1)S(1)} %copy-done.4), channel_id=1, source_target_pairs={{0,12},{4,0},{8,4},{12,8},{1,13},{5,1},{9,5},{13,9},{2,14},{6,2},{... | collective-permute-start | bytes 1720328 | tf_op jit(solution)/shard_map/ppermute | solution.py:409
  49.7 27.0 %collective-permute-start.3 = (bf16[64,4480]{1,0:T(8,128)(2,1)S(1)}, bf16[64,4480]{1,0:T(8,128)(2,1)}, u32[]{:S(2)}, u32[]{:S(2)}) collective-permute-start(bf16[64,4480]{1,0:T(8,128)(2,1)S(1)} %copy-done.5), channel_id=1, source_target_pairs={{0,4},{4,8},{8,12},{12,0},{1,5},{5,9},{9,13},{13,1},{2,6},{6,10},{... | collective-permute-start | bytes 1720328 | tf_op jit(solution)/shard_map/ppermute | solution.py:408
  61.9 22.0 %collective-permute-start.5 = (bf16[64,4480]{1,0:T(8,128)(2,1)}, bf16[64,4480]{1,0:T(8,128)(2,1)}, u32[]{:S(2)}, u32[]{:S(2)}) collective-permute-start(bf16[64,4480]{1,0:T(8,128)(2,1)} %collective-permute-done.1.top_hbm.refs_10_.refs_7_), channel_id=1, source_target_pairs={{0,4},{4,8},{8,12},{12,0},{1,5},{5,9},{9,13},{13,1},{2,6},{6,10},{... | collective-permute-start | bytes 1720328 | tf_op jit(solution)/shard_map/ppermute | solution.py:440
  62.3 21.6 %collective-permute-start.6 = (bf16[64,4480]{1,0:T(8,128)(2,1)}, bf16[64,4480]{1,0:T(8,128)(2,1)}, u32[]{:S(2)}, u32[]{:S(2)}) collective-permute-start(bf16[64,4480]{1,0:T(8,128)(2,1)} %collective-permute-done.2.bottom_hbm.refs_13_.refs_10_), channel_id=1, source_target_pairs={{0,12},{4,0},{8,4},{12,8},{1,13},{5,1},{9,5},{13,9},{2,14},{6,2},{... | collective-permute-start | bytes 1720328 | tf_op jit(solution)/shard_map/ppermute | solution.py:440
  65.5 18.4 %all-to-all-start.2 = ((f32[16,32,128]{2,1,0:T(8,128)}), f32[16,32,128]{2,1,0:T(8,128)S(1)}, u32[]{:S(2)}, u32[]{:S(2)}) async-start(f32[16,32,128]{2,1,0:T(8,128)} %shard_map.139), calls=%async_computation.2 | async-start | bytes 524288 | tf_op jit(solution)/shard_map/all_to_all | solution.py:454
  84.9 3.7 %copy-start.9 = (s32[4]{0:T(128)S(1)}, s32[4]{0:T(128)}, u32[]{:S(2)}) copy-start(s32[4]{0:T(128)} %constant.86.clone) | copy-start | bytes 52
  84.9 17.8 %all-to-all-start.3 = ((f32[4,512,128]{2,1,0:T(8,128)}), f32[4,512,128]{2,1,0:T(8,128)S(1)}, u32[]{:S(2)}, u32[]{:S(2)}) async-start(f32[4,512,128]{2,1,0:T(8,128)} %broadcast_in_dim.12), calls=%async_computation.3 | async-start | bytes 2097152 | tf_op jit(solution)/shard_map/all_to_all | solution.py:456
  102.7 1.0 copy-start.3
  115.6 28.4 %copy-start.1 = (bf16[32,4096]{1,0:T(8,128)(2,1)S(1)}, bf16[32,4096]{1,0:T(8,128)(2,1)}, u32[]{:S(2)}) copy-start(bf16[32,4096]{1,0:T(8,128)(2,1)} %residual_ref.1) | copy-start | bytes 786436
  115.7 28.4 %copy-start.2 = (f32[4096]{0:T(1024)S(1)}, f32[4096]{0:T(1024)}, u32[]{:S(2)}) copy-start(f32[4096]{0:T(1024)} %param.26) | copy-start | bytes 49156
  144.7 6.8 %collective-permute-start.7 = (bf16[32,4096]{1,0:T(8,128)(2,1)S(1)}, bf16[32,4096]{1,0:T(8,128)(2,1)S(1)}, u32[]{:S(2)}, u32[]{:S(2)}) collective-permute-start(bf16[32,4096]{1,0:T(8,128)(2,1)S(1)} %shard_map.145), channel_id=1, source_target_pairs={{0,2},{2,0},{1,3},{3,1},{4,6},{6,4},{5,7},{7,5},{8,10},{10,8},{9,1... | collective-permute-start | bytes 786440 | tf_op jit(solution)/shard_map/ppermute | solution.py:514
  151.5 3.6 %collective-permute-start.8 = (bf16[2,32,4096]{2,1,0:T(8,128)(2,1)S(1)}, bf16[2,32,4096]{2,1,0:T(8,128)(2,1)S(1)}, u32[]{:S(2)}, u32[]{:S(2)}) collective-permute-start(bf16[2,32,4096]{2,1,0:T(8,128)(2,1)S(1)} %pad_maximum_fusion.2), channel_id=1, source_target_pairs={{0,1},{1,0},{2,3},{3,2},{4,5},{5,4},{6,7},{7,6},{8,9},{9,8},{10,11... | collective-permute-start | bytes 1572872 | tf_op jit(solution)/shard_map/ppermute | solution.py:516
Sparse Core Ops, SparseCore 0:
  16.6 69.3 all-gather.1

commit v5 on v4

--- a/solution.py
+++ b/solution.py
@@ -262,9 +262,9 @@
         copy.wait()
 
 
-def mix_kernel(n, place_ref, bias_ref, decay_ref, gain_ref, *refs):
-    entering_hbm, mixed, blocks, weight_hbm = refs[0], refs[1 : n + 1], refs[n + 1 : 3 * n + 1], refs[3 * n + 1]
-    out_ref, enter_ref, logs_ref, mixed_ref, block_ref, normed_ref, weight_ref, semaphores = refs[3 * n + 2 :]
+def mix_kernel(n, place_ref, bias_ref, decay_ref, gain_ref, enter_ref, *refs):
+    mixed, blocks, weight_hbm = refs[:n], refs[n : 3 * n], refs[3 * n]
+    out_ref, logs_ref, mixed_ref, block_ref, normed_ref, weight_ref, semaphores = refs[3 * n + 1 :]
     inner, heads = mixed_ref.shape[2], bias_ref.shape[1]
     pairs = inner // SPAN
     block_in, mixed_in = [], []
@@ -272,10 +272,8 @@
         block_in += copies(
             halves(blocks[2 * i : 2 * i + 2], slice(inner, None), block_ref.at[i]), semaphores, 2 * i
         )
-        if i == 0:
-            (enter_in,) = copies([(entering_hbm, enter_ref)], semaphores, 3 * n)
         mixed_in += copies([(mixed[i], mixed_ref.at[i])], semaphores, 2 * n + i)
-    (weight_in,) = copies([(weight_hbm, weight_ref)], semaphores, 3 * n + 1)
+    (weight_in,) = copies([(weight_hbm, weight_ref)], semaphores, 3 * n)
     for i in range(n):
         for copy in block_in[2 * i : 2 * i + 2]:
             copy.wait()
@@ -286,7 +284,6 @@
         here = logs_ref[p]
         logs_ref[p] = here + before
         before = before + here[:, SPAN - 1 :]
-    enter_in.wait()
     low = first_lanes((SPAN, SPAN))
     for i in range(n):
         mixed_in[i].wait()
@@ -398,8 +395,8 @@
         hbm_outs=2,
         args=(mixer_values, gate_values, input_coefs, output_coefs, step_raw.T, bias, decay),
     )
-    across, states = lax.optimization_barrier((across, states))
     parts = lax.all_to_all(states, "x", 0, 0, tiled=True)
+    across, parts = lax.optimization_barrier((across, parts))
     weight = jnp.concatenate([weight, across], axis=0)
     weight = lax.all_gather(weight, "z", axis=0, tiled=True)
 
@@ -421,7 +418,7 @@
                 pltpu.SemaphoreType.DMA((10,)),
                 pltpu.SemaphoreType.DMA((8,)),
             ],
-            flops=2 * tokens * inner * tokens * 6,
+            flops=10**6,
             vmem=3,
             hbm_outs=2,
             args=(bias, decay, skip, *block),
@@ -478,17 +475,16 @@
         functools.partial(mix_kernel, n_x),
         [jax.ShapeDtypeStruct((n_x * tokens, weight.shape[0]), BF16)],
         scratch=[
-            pltpu.VMEM((inner, SPAN), F32),
             pltpu.VMEM((n_x, heads, SPAN), F32),
             pltpu.VMEM((n_x, tokens, inner), F32),
             pltpu.VMEM((n_x, tokens, packed - inner), BF16),
             pltpu.VMEM((n_x * tokens, inner), BF16),
             pltpu.VMEM(weight.shape, BF16),
-            pltpu.SemaphoreType.DMA((3 * n_x + 2,)),
+            pltpu.SemaphoreType.DMA((3 * n_x + 1,)),
         ],
         flops=2 * n_x * tokens * inner * (STATE * 2 + weight.shape[0]),
         smem=1,
-        vmem=3,
+        vmem=4,
         args=(
             place,
             bias,

time: 164 us -> 162 us (0.988)
  blocking collectives: 46.3 us -> 28.6 us
  starting transfers between devices: 34.6 us -> 42.7 us
  waiting for transfers between devices: 16.1 us -> 22.7 us
    all_to_all x1 -> x0, blocking collectives: 18 us -> none  [on_device(): parts = lax.all_to_all(states, 'x', 0, 0, tiled=True)]
    all_to_all x0 -> x1, waiting for transfers between devices: none -> 5.75 us  [on_device(): parts = lax.all_to_all(states, 'x', 0, 0, tiled=True)]
    all_to_all x0 -> x1, starting transfers between devices: none -> 4.99 us  [on_device(): parts = lax.all_to_all(states, 'x', 0, 0, tiled=True)]
    ppermute x1, waiting for transfers between devices: 1.77 us -> 4.66 us  [on_device(): across = lax.ppermute(weight, 'yh', ring(2, 1))]
    all_to_all x1, waiting for transfers between devices: 2.83 us -> 0.01 us  [on_device(): parts = lax.all_to_all(grouped, GROUPS, 0, 0, tiled=True)]
    all_to_all x1, starting transfers between devices: 5.96 us -> 8.79 us  [on_device(): lax.all_to_all(entering, GROUPS, 0, 0, tiled=True).reshape(1, quarter, SPAN)]
  transfers between devices with their start and end apart: 13 -> 14, of which waited for: 6 -> 6; matrix products, arithmetic and copies ran while one was open for 2% -> 2% of each run, Pallas kernels for 21% -> 19%
where the time goes in v5:
time: 162 us; the launch traced here: 161 us
  Pallas kernels  47.4 us (29%)
  starting transfers between devices  42.7 us (26%)
  blocking collectives  28.6 us (18%)
  waiting for transfers between devices  22.7 us (14%)
  between operations  13.6 us (8%)
  local copies, waits for them, and re-layouts  2.97 us (2%)
  other arithmetic  2.66 us (2%)
    pallas_call x10, Pallas kernels, call(): pl.pallas_call(kernel, out_shape=list(outs), in_specs=specs, out_specs=[p...  47.4 us
    all_to_all x1, blocking collectives, on_device(): partial = lax.all_to_all(partial, ('x', *TENSOR), 0, 0, tiled=True)  28.6 us
    all_to_all x1, starting transfers between devices, on_device(): parts = lax.all_to_all(grouped, GROUPS, 0, 0, tiled=True)  11.9 us
    all_to_all x1, starting transfers between devices, on_device(): lax.all_to_all(entering, GROUPS, 0, 0, tiled=True).reshape(1, quarter, SPAN)  8.79 us
    all_to_all x1, waiting for transfers between devices, on_device(): parts = lax.all_to_all(states, 'x', 0, 0, tiled=True)  5.75 us
    ppermute x1, waiting for transfers between devices, on_device(): across = lax.ppermute(done, 'yl', ring(2, 1))  5.5 us
    all_to_all x1, starting transfers between devices, on_device(): parts = lax.all_to_all(states, 'x', 0, 0, tiled=True)  4.99 us
    ppermute x1, waiting for transfers between devices, on_device(): across = lax.ppermute(weight, 'yh', ring(2, 1))  4.66 us
  transfers between devices with their start and end apart: 14, of which 6 were waited for; matrix products, arithmetic and copies ran while one was open for 2% of the time, Pallas kernels for 19%

profile of v5, /device:TPU:1, one launch (start us, length us, event | category | flops | bytes accessed | tf_op | source)
XLA Modules:
  0.0 160.6 jit_solution(1209907348233050057)
XLA Ops:
  6.5 3.5 %shard_map.136 = (f32[4,520,128]{2,1,0:T(8,128)}, bf16[64,4480]{1,0:T(8,128)(2,1)}, bf16[64,4480]{1,0:T(8,128)(2,1)}) custom-call(bf16[128,2048]{1,0:T(8,128)(2,1)} %x_hbm.1, bf16[128,2048]{1,0:T(8,128)(2,1)} %gate_hbm.1, bf16[128,128]{1,0:T(8,128)(2,1)} %b_hbm.1, bf16[128,128]{1,0:T(8,128)(2,1)} %c_hbm.1, bf16[32,128]{1,0:T(8,128)(2,1)} %bitcast.44, ...), custom_call_target="tpu_custom_call" | custom-call | flops 134217728 | bytes 3334400 | tf_op jit(solution)/shard_map/pallas_call | solution.py:30
  10.1 5.0 %all-to-all-start = ((f32[4,520,128]{2,1,0:T(8,128)}), f32[4,520,128]{2,1,0:T(8,128)S(1)}, u32[]{:S(2)}, u32[]{:S(2)}) async-start(f32[4,520,128]{2,1,0:T(8,128)} %get-tuple-element.37), calls=%async_computation | async-start | bytes 2129920 | tf_op jit(solution)/shard_map/all_to_all | solution.py:398
  15.1 3.0 %collective-permute-start = (bf16[64,2048]{1,0:T(8,128)(2,1)S(1)}, bf16[64,2048]{1,0:T(8,128)(2,1)S(1)}, u32[]{:S(2)}, u32[]{:S(2)}) collective-permute-start(bf16[64,2048]{1,0:T(8,128)(2,1)S(1)} %bitcast.28), channel_id=1, source_target_pairs={{0,128},{128,0},{1,129},{129,1},{2,130},{130,2},{3,131},{131,3},{4... | collective-permute-start | bytes 786440 | tf_op jit(solution)/shard_map/ppermute | solution.py:383
  18.1 4.7 %collective-permute-done = bf16[64,2048]{1,0:T(8,128)(2,1)S(1)} collective-permute-done((bf16[64,2048]{1,0:T(8,128)(2,1)S(1)}, bf16[64,2048]{1,0:T(8,128)(2,1)S(1)}, u32[]{:S(2)}, u32[]{:S(2)}) %collective-permute-start) | collective-permute-done | bytes 262176 | tf_op jit(solution)/shard_map/ppermute | solution.py:383
  22.7 5.8 %all-to-all-done.parts_ref = f32[4,520,128]{2,1,0:T(8,128)S(1)} async-done(((f32[4,520,128]{2,1,0:T(8,128)}), f32[4,520,128]{2,1,0:T(8,128)S(1)}, u32[]{:S(2)}, u32[]{:S(2)}) %all-to-all-start) | async-done | bytes 1064992 | tf_op jit(solution)/shard_map/all_to_all | solution.py:398
  30.2 11.9 %all-to-all-start.1 = ((f32[16,40,128]{2,1,0:T(8,128)}), f32[16,40,128]{2,1,0:T(8,128)S(1)}, u32[]{:S(2)}, u32[]{:S(2)}) async-start(f32[16,40,128]{2,1,0:T(8,128)} %shard_map.138), calls=%async_computation.1 | async-start | bytes 655360 | tf_op jit(solution)/shard_map/all_to_all | solution.py:434
  42.4 2.4 %collective-permute-start.2 = (bf16[64,4480]{1,0:T(8,128)(2,1)}, bf16[64,4480]{1,0:T(8,128)(2,1)}, u32[]{:S(2)}, u32[]{:S(2)}) collective-permute-start(bf16[64,4480]{1,0:T(8,128)(2,1)} %get-tuple-element.42.bottom_hbm.refs_9_.refs_5_), channel_id=1, source_target_pairs={{0,12},{4,0},{8,4},{12,8},{1,13},{5,1},{9,5},{13,9},{2,14},{6,2},{... | collective-permute-start | bytes 1720328 | tf_op jit(solution)/shard_map/ppermute | solution.py:406
  45.6 1.5 collective-permute-start.3
  47.0 5.3 %shard_map.137 = (f32[128,2048]{1,0:T(8,128)}, f32[2048,128]{1,0:T(8,128)}) custom-call(f32[1,32]{1,0:T(1,128)} %bitcast.31, f32[1,32]{1,0:T(1,128)} %bitcast.38, f32[1,2048]{1,0:T(1,128)} %reshape_reshape.3.skip_ref, bf16[64,4480]{1,0:T(8,128)(2,1)} %get-tuple-element.41.top_hbm.refs_8_.refs_4_, bf16[64,4480]{1,0:T(8,128)(2,1)} %get-tuple-element.42.bottom_hbm.refs_9_.refs_5_), custom_call_target="tpu_custom_call" | custom-call | flops 1000000 | bytes 3252480 | tf_op jit(solution)/shard_map/pallas_call | solution.py:30
  52.3 3.4 %collective-permute-done.1.top_hbm.refs_10_.refs_6_ = bf16[64,4480]{1,0:T(8,128)(2,1)S(1)} collective-permute-done((bf16[64,4480]{1,0:T(8,128)(2,1)S(1)}, bf16[64,4480]{1,0:T(8,128)(2,1)S(1)}, u32[]{:S(2)}, u32[]{:S(2)}) %collective-permute-start.1) | collective-permute-done | bytes 573472 | tf_op jit(solution)/shard_map/ppermute | solution.py:405
  55.9 2.7 %collective-permute-start.6 = (bf16[64,4480]{1,0:T(8,128)(2,1)}, bf16[64,4480]{1,0:T(8,128)(2,1)}, u32[]{:S(2)}, u32[]{:S(2)}) collective-permute-start(bf16[64,4480]{1,0:T(8,128)(2,1)} %collective-permute-done.2.bottom_hbm.refs_13_.refs_9_), channel_id=1, source_target_pairs={{0,12},{4,0},{8,4},{12,8},{1,13},{5,1},{9,5},{13,9},{2,14},{6,2},{... | collective-permute-start | bytes 1720328 | tf_op jit(solution)/shard_map/ppermute | solution.py:437
  59.5 8.8 %all-to-all-start.2 = ((f32[16,32,128]{2,1,0:T(8,128)}), f32[16,32,128]{2,1,0:T(8,128)S(1)}, u32[]{:S(2)}, u32[]{:S(2)}) async-start(f32[16,32,128]{2,1,0:T(8,128)} %shard_map.139), calls=%async_computation.2 | async-start | bytes 524288 | tf_op jit(solution)/shard_map/all_to_all | solution.py:451
  68.3 5.3 %shard_map.141 = (f32[128,2048]{1,0:T(8,128)}, f32[2048,128]{1,0:T(8,128)}) custom-call(f32[1,32]{1,0:T(1,128)} %bitcast.32, f32[1,32]{1,0:T(1,128)} %bitcast.39, f32[1,2048]{1,0:T(1,128)} %reshape_reshape.3.skip_ref, bf16[64,4480]{1,0:T(8,128)(2,1)} %collective-permute-done.4.top_hbm.refs_12_.refs_8_, ...), custom_call_target="tpu_custom_call" | custom-call | flops 1000000 | bytes 3252480 | tf_op jit(solution)/shard_map/pallas_call | solution.py:30
  73.6 5.3 %shard_map.140 = (f32[128,2048]{1,0:T(8,128)}, f32[2048,128]{1,0:T(8,128)}) custom-call(f32[1,32]{1,0:T(1,128)} %bitcast.33, f32[1,32]{1,0:T(1,128)} %bitcast.40, f32[1,2048]{1,0:T(1,128)} %reshape_reshape.3.skip_ref, bf16[64,4480]{1,0:T(8,128)(2,1)} %copy-done.4, bf16[64,4480]{1,0:T(8,128)(2,1)} %collective-permute-done.3.bottom_hbm.refs_11_.refs_7_), custom_call_target="tpu_custom_call" | custom-call | flops 1000000 | bytes 3252480 | tf_op jit(solution)/shard_map/pallas_call | solution.py:30
  78.9 1.8 %all-to-all-done.2 = f32[16,32,128]{2,1,0:T(8,128)S(1)} async-done(((f32[16,32,128]{2,1,0:T(8,128)}), f32[16,32,128]{2,1,0:T(8,128)S(1)}, u32[]{:S(2)}, u32[]{:S(2)}) %all-to-all-start.2) | async-done | bytes 262176 | tf_op jit(solution)/shard_map/all_to_all | solution.py:451
  81.8 3.7 %all-to-all-start.3 = ((f32[4,512,128]{2,1,0:T(8,128)}), f32[4,512,128]{2,1,0:T(8,128)S(1)}, u32[]{:S(2)}, u32[]{:S(2)}) async-start(f32[4,512,128]{2,1,0:T(8,128)} %broadcast_in_dim.12), calls=%async_computation.3 | async-start | bytes 2097152 | tf_op jit(solution)/shard_map/all_to_all | solution.py:453
  86.0 5.3 %shard_map.142 = (f32[128,2048]{1,0:T(8,128)}, f32[2048,128]{1,0:T(8,128)}) custom-call(f32[1,32]{1,0:T(1,128)} %bitcast.34, f32[1,32]{1,0:T(1,128)} %bitcast.41, f32[1,2048]{1,0:T(1,128)} %reshape_reshape.3.skip_ref, bf16[64,4480]{1,0:T(8,128)(2,1)} %collective-permute-done.5.top_hbm.refs_14_.refs_10_, ...), custom_call_target="tpu_custom_call" | custom-call | flops 1000000 | bytes 3252480 | tf_op jit(solution)/shard_map/pallas_call | solution.py:30
  91.3 8.3 %shard_map.143 = (f32[128,2048]{1,0:T(8,128)}, f32[128,2048]{1,0:T(8,128)}, f32[128,2048]{1,0:T(8,128)}, f32[128,2048]{1,0:T(8,128)}) custom-call(s32[4]{0:T(128)} %and_select_fusion.place_ref, f32[1,32]{1,0:T(1,128)} %bitcast.35, f32[1,32]{1,0:T(1,128)} %bitcast.42, f32[2048,128]{1,0:T(8,128)} %get-tuple-element.54.refs_0_, ...), custom_call_target="tpu_custom_call" | custom-call | flops 536870912 | bytes 17170704 | tf_op jit(solution)/shard_map/pallas_call | solution.py:30
  100.6 12.1 %shard_map.144 = bf16[512,1024]{1,0:T(8,128)(2,1)} custom-call(s32[4]{0:T(128)} %and_select_fusion.place_ref, f32[1,32]{1,0:T(1,128)} %bitcast.36, f32[1,32]{1,0:T(1,128)} %bitcast.43, f32[1,2048]{1,0:T(1,128)} %bitcast.45, f32[2048,128]{1,0:T(8,128)} %bitcast.23, f32[128,2048]{1,0:T(8,128)} %get-tuple-element.64.refs_0_, ...), custom_call_target="tpu_custom_call" | custom-call | flops 2684354560 | bytes 15081744 | tf_op jit(solution)/shard_map/pallas_call | solution.py:30
  112.7 28.6 %all_to_all.29.parts_ref = bf16[16,32,1024]{2,1,0:T(8,128)(2,1)S(1)} all-to-all(bf16[16,32,1024]{2,1,0:T(8,128)(2,1)} %bitcast.24), channel_id=1, replica_groups=mesh['yh'=2,'z'=8,'x'=4,'yl'=2,'core'=2] {'x','yl','core'}, dimensions={0} | all-to-all | bytes 2097152 | tf_op jit(solution)/shard_map/all_to_all | solution.py:499
  142.0 1.3 collective-permute-start.7
  143.3 5.5 %collective-permute-done.7 = bf16[32,4096]{1,0:T(8,128)(2,1)S(1)} collective-permute-done((bf16[32,4096]{1,0:T(8,128)(2,1)S(1)}, bf16[32,4096]{1,0:T(8,128)(2,1)S(1)}, u32[]{:S(2)}, u32[]{:S(2)}) %collective-permute-start.7) | collective-permute-done | bytes 262176 | tf_op jit(solution)/shard_map/ppermute | solution.py:510
  148.8 2.1 %collective-permute-start.8 = (bf16[2,32,4096]{2,1,0:T(8,128)(2,1)S(1)}, bf16[2,32,4096]{2,1,0:T(8,128)(2,1)S(1)}, u32[]{:S(2)}, u32[]{:S(2)}) collective-permute-start(bf16[2,32,4096]{2,1,0:T(8,128)(2,1)S(1)} %pad_maximum_fusion.2), channel_id=1, source_target_pairs={{0,1},{1,0},{2,3},{3,2},{4,5},{5,4},{6,7},{7,6},{8,9},{9,8},{10,11... | collective-permute-start | bytes 1572872 | tf_op jit(solution)/shard_map/ppermute | solution.py:512
  150.9 1.5 collective-permute-done.8
  (46 shorter events, 8.4 us)
Async XLA Ops:
  6.5 52.0 %copy-start = (f32[32,64,128]{2,1,0:T(8,128)S(1)}, f32[32,64,128]{2,1,0:T(8,128)}, u32[]{:S(2)}) copy-start(f32[32,64,128]{2,1,0:T(8,128)} %param.23) | copy-start | bytes 3145732
  10.1 5.0 %copy-start.6 = (bf16[2048,64]{0,1:T(8,128)(2,1)S(1)}, bf16[2048,64]{0,1:T(8,128)(2,1)}, u32[]{:S(2)}) copy-start(bf16[2048,64]{0,1:T(8,128)(2,1)} %param.24) | copy-start | bytes 786436
  10.1 18.4 %all-to-all-start = ((f32[4,520,128]{2,1,0:T(8,128)}), f32[4,520,128]{2,1,0:T(8,128)S(1)}, u32[]{:S(2)}, u32[]{:S(2)}) async-start(f32[4,520,128]{2,1,0:T(8,128)} %get-tuple-element.37), calls=%async_computation | async-start | bytes 2129920 | tf_op jit(solution)/shard_map/all_to_all | solution.py:398
  15.1 84.5 %all-gather.2.cloned.1.call-start = ((), (), s32[]{:S(2)}) async-start(), calls=%async_computation.5 | async-start | bytes 4718592 | tf_op jit(solution)/shard_map/all_gather | solution.py:401
  15.1 7.7 %collective-permute-start = (bf16[64,2048]{1,0:T(8,128)(2,1)S(1)}, bf16[64,2048]{1,0:T(8,128)(2,1)S(1)}, u32[]{:S(2)}, u32[]{:S(2)}) collective-permute-start(bf16[64,2048]{1,0:T(8,128)(2,1)S(1)} %bitcast.28), channel_id=1, source_target_pairs={{0,128},{128,0},{1,129},{129,1},{2,130},{130,2},{3,131},{131,3},{4... | collective-permute-start | bytes 786440 | tf_op jit(solution)/shard_map/ppermute | solution.py:383
  29.4 12.7 %copy-start.3 = (bf16[64,4480]{1,0:T(8,128)(2,1)S(1)}, bf16[64,4480]{1,0:T(8,128)(2,1)}, u32[]{:S(2)}) copy-start(bf16[64,4480]{1,0:T(8,128)(2,1)} %get-tuple-element.41.top_hbm.refs_8_.refs_4_) | copy-start | bytes 1720324
  29.4 15.5 %copy-start.7 = (f32[32]{0:T(128)S(1)}, f32[32]{0:T(128)}, u32[]{:S(2)}) copy-start(f32[32]{0:T(128)} %param.21) | copy-start | bytes 388
  30.2 25.6 %all-to-all-start.1 = ((f32[16,40,128]{2,1,0:T(8,128)}), f32[16,40,128]{2,1,0:T(8,128)S(1)}, u32[]{:S(2)}, u32[]{:S(2)}) async-start(f32[16,40,128]{2,1,0:T(8,128)} %shard_map.138), calls=%async_computation.1 | async-start | bytes 655360 | tf_op jit(solution)/shard_map/all_to_all | solution.py:434
  42.1 13.7 %collective-permute-start.1 = (bf16[64,4480]{1,0:T(8,128)(2,1)S(1)}, bf16[64,4480]{1,0:T(8,128)(2,1)S(1)}, u32[]{:S(2)}, u32[]{:S(2)}) collective-permute-start(bf16[64,4480]{1,0:T(8,128)(2,1)S(1)} %copy-done.3), channel_id=1, source_target_pairs={{0,4},{4,8},{8,12},{12,0},{1,5},{5,9},{9,13},{13,1},{2,6},{6,10},{... | collective-permute-start | bytes 1720328 | tf_op jit(solution)/shard_map/ppermute | solution.py:405
  42.4 13.4 %collective-permute-start.2 = (bf16[64,4480]{1,0:T(8,128)(2,1)}, bf16[64,4480]{1,0:T(8,128)(2,1)}, u32[]{:S(2)}, u32[]{:S(2)}) collective-permute-start(bf16[64,4480]{1,0:T(8,128)(2,1)} %get-tuple-element.42.bottom_hbm.refs_9_.refs_5_), channel_id=1, source_target_pairs={{0,12},{4,0},{8,4},{12,8},{1,13},{5,1},{9,5},{13,9},{2,14},{6,2},{... | collective-permute-start | bytes 1720328 | tf_op jit(solution)/shard_map/ppermute | solution.py:406
  45.6 22.7 %collective-permute-start.4 = (bf16[64,4480]{1,0:T(8,128)(2,1)S(1)}, bf16[64,4480]{1,0:T(8,128)(2,1)}, u32[]{:S(2)}, u32[]{:S(2)}) collective-permute-start(bf16[64,4480]{1,0:T(8,128)(2,1)S(1)} %copy-done.3), channel_id=1, source_target_pairs={{0,12},{4,0},{8,4},{12,8},{1,13},{5,1},{9,5},{13,9},{2,14},{6,2},{... | collective-permute-start | bytes 1720328 | tf_op jit(solution)/shard_map/ppermute | solution.py:406
  45.6 28.0 %collective-permute-start.3 = (bf16[64,4480]{1,0:T(8,128)(2,1)}, bf16[64,4480]{1,0:T(8,128)(2,1)}, u32[]{:S(2)}, u32[]{:S(2)}) collective-permute-start(bf16[64,4480]{1,0:T(8,128)(2,1)} %get-tuple-element.42.bottom_hbm.refs_9_.refs_5_), channel_id=1, source_target_pairs={{0,4},{4,8},{8,12},{12,0},{1,5},{5,9},{9,13},{13,1},{2,6},{6,10},{... | collective-permute-start | bytes 1720328 | tf_op jit(solution)/shard_map/ppermute | solution.py:405
  55.8 17.8 %copy-start.4 = (bf16[64,4480]{1,0:T(8,128)(2,1)}, bf16[64,4480]{1,0:T(8,128)(2,1)S(1)}, u32[]{:S(2)}) copy-start(bf16[64,4480]{1,0:T(8,128)(2,1)S(1)} %collective-permute-done.1.top_hbm.refs_10_.refs_6_) | copy-start | bytes 1720324
  55.8 24.9 %collective-permute-start.5 = (bf16[64,4480]{1,0:T(8,128)(2,1)S(1)}, bf16[64,4480]{1,0:T(8,128)(2,1)}, u32[]{:S(2)}, u32[]{:S(2)}) collective-permute-start(bf16[64,4480]{1,0:T(8,128)(2,1)S(1)} %collective-permute-done.1.top_hbm.refs_10_.refs_6_), channel_id=1, source_target_pairs={{0,4},{4,8},{8,12},{12,0},{1,5},{5,9},{9,13},{13,1},{2,6},{6,10},{... | collective-permute-start | bytes 1720328 | tf_op jit(solution)/shard_map/ppermute | solution.py:437
  55.9 24.8 %collective-permute-start.6 = (bf16[64,4480]{1,0:T(8,128)(2,1)}, bf16[64,4480]{1,0:T(8,128)(2,1)}, u32[]{:S(2)}, u32[]{:S(2)}) collective-permute-start(bf16[64,4480]{1,0:T(8,128)(2,1)} %collective-permute-done.2.bottom_hbm.refs_13_.refs_9_), channel_id=1, source_target_pairs={{0,12},{4,0},{8,4},{12,8},{1,13},{5,1},{9,5},{13,9},{2,14},{6,2},{... | collective-permute-start | bytes 1720328 | tf_op jit(solution)/shard_map/ppermute | solution.py:437
  59.5 21.2 %all-to-all-start.2 = ((f32[16,32,128]{2,1,0:T(8,128)}), f32[16,32,128]{2,1,0:T(8,128)S(1)}, u32[]{:S(2)}, u32[]{:S(2)}) async-start(f32[16,32,128]{2,1,0:T(8,128)} %shard_map.139), calls=%async_computation.2 | async-start | bytes 524288 | tf_op jit(solution)/shard_map/all_to_all | solution.py:451
  81.8 3.7 %copy-start.8 = (s32[4]{0:T(128)S(1)}, s32[4]{0:T(128)}, u32[]{:S(2)}) copy-start(s32[4]{0:T(128)} %constant.86.clone) | copy-start | bytes 52
  81.8 17.8 %all-to-all-start.3 = ((f32[4,512,128]{2,1,0:T(8,128)}), f32[4,512,128]{2,1,0:T(8,128)S(1)}, u32[]{:S(2)}, u32[]{:S(2)}) async-start(f32[4,512,128]{2,1,0:T(8,128)} %broadcast_in_dim.12), calls=%async_computation.3 | async-start | bytes 2097152 | tf_op jit(solution)/shard_map/all_to_all | solution.py:453
  99.6 1.0 copy-start.5
  112.7 28.6 %copy-start.1 = (bf16[32,4096]{1,0:T(8,128)(2,1)S(1)}, bf16[32,4096]{1,0:T(8,128)(2,1)}, u32[]{:S(2)}) copy-start(bf16[32,4096]{1,0:T(8,128)(2,1)} %residual_ref.1) | copy-start | bytes 786436
  112.7 28.6 %copy-start.2 = (f32[4096]{0:T(1024)S(1)}, f32[4096]{0:T(1024)}, u32[]{:S(2)}) copy-start(f32[4096]{0:T(1024)} %param.26) | copy-start | bytes 49156
  142.0 6.8 %collective-permute-start.7 = (bf16[32,4096]{1,0:T(8,128)(2,1)S(1)}, bf16[32,4096]{1,0:T(8,128)(2,1)S(1)}, u32[]{:S(2)}, u32[]{:S(2)}) collective-permute-start(bf16[32,4096]{1,0:T(8,128)(2,1)S(1)} %shard_map.145), channel_id=1, source_target_pairs={{0,2},{2,0},{1,3},{3,1},{4,6},{6,4},{5,7},{7,5},{8,10},{10,8},{9,1... | collective-permute-start | bytes 786440 | tf_op jit(solution)/shard_map/ppermute | solution.py:510
  148.8 3.6 %collective-permute-start.8 = (bf16[2,32,4096]{2,1,0:T(8,128)(2,1)S(1)}, bf16[2,32,4096]{2,1,0:T(8,128)(2,1)S(1)}, u32[]{:S(2)}, u32[]{:S(2)}) collective-permute-start(bf16[2,32,4096]{2,1,0:T(8,128)(2,1)S(1)} %pad_maximum_fusion.2), channel_id=1, source_target_pairs={{0,1},{1,0},{2,3},{3,2},{4,5},{5,4},{6,7},{7,6},{8,9},{9,8},{10,11... | collective-permute-start | bytes 1572872 | tf_op jit(solution)/shard_map/ppermute | solution.py:512
Sparse Core Ops, SparseCore 0:
  29.5 69.0 all-gather.1

commit v6 on v5

--- a/solution.py
+++ b/solution.py
@@ -169,18 +169,8 @@
     return [(pieces[0].at[:, columns], ref.at[:half]), (pieces[1].at[:, columns], ref.at[half:])]
 
 
-def local_kernel(bias_ref, decay_ref, skip_ref, top_hbm, bottom_hbm, mixed_hbm, state_hbm, *scratch):
-    x_ref, coefs_ref, mixed_ref, state_ref, gets, puts = scratch
-    inner, heads = x_ref.shape[1], bias_ref.shape[1]
-    step = inner // 4
-    pieces = (top_hbm, bottom_hbm)
-    coefs_in = copies(halves(pieces, slice(2 * inner, None), coefs_ref), gets)
-    x_in = [
-        copies(halves(pieces, pl.ds(i * step, step), x_ref.at[:, pl.ds(i * step, step)]), gets, 2 + 2 * i)
-        for i in range(4)
-    ]
-    for copy in coefs_in:
-        copy.wait()
+def local_block(x_ref, coefs_ref, bias_ref, decay_ref, skip_ref, mixed_ref, state_ref, x_in=(), after=None):
+    heads = bias_ref.shape[1]
     b, c = coefs_ref[:, :SPAN], coefs_ref[:, SPAN : 2 * SPAN]
     step_t, cumulative_t = steps_of(coefs_ref[:heads, 2 * SPAN :], bias_ref[...], decay_ref[...])
     cumulative = jnp.transpose(cumulative_t)
@@ -189,8 +179,6 @@
     columns = lax.broadcasted_iota(jnp.int32, (SPAN, SPAN), 1)
     causal = rows >= columns
     low = first_lanes((SPAN, SPAN))
-    each = step // SPAN
-    out = []
     for pair, state, _ in fresh_states(x_ref, b, step_t, cumulative_t, x_in):
         lanes = slice(pair * SPAN, (pair + 1) * SPAN)
         state_ref[lanes, :] = state
@@ -202,40 +190,67 @@
             weights.append(jnp.concatenate(split(scores * within * step_t[h : h + 1, :]), axis=1))
         both = dot(jnp.concatenate(weights, axis=0), jnp.concatenate([x, x], axis=0))
         mixed_ref[:, lanes] = jnp.where(low, both[:SPAN], both[SPAN:]) + skip_ref[:, lanes] * x.astype(F32)
+        if after is not None:
+            after(pair)
+    return cumulative_t
+
+
+def local_kernel(bias_ref, decay_ref, skip_ref, top_hbm, bottom_hbm, mixed_hbm, state_hbm, *scratch):
+    x_ref, coefs_ref, mixed_ref, state_ref, gets, puts = scratch
+    inner = x_ref.shape[1]
+    step = inner // 4
+    each = step // SPAN
+    pieces = (top_hbm, bottom_hbm)
+    coefs_in = copies(halves(pieces, slice(2 * inner, None), coefs_ref), gets)
+    x_in = [
+        copies(halves(pieces, pl.ds(i * step, step), x_ref.at[:, pl.ds(i * step, step)]), gets, 2 + 2 * i)
+        for i in range(4)
+    ]
+    for copy in coefs_in:
+        copy.wait()
+    out = []
+
+    def after(pair):
         if pair % each == each - 1:
             part = pl.ds(pair // each * step, step)
-            out += copies(
-                [
-                    (state_ref.at[part], state_hbm.at[part]),
-                    (mixed_ref.at[:, part], mixed_hbm.at[:, part]),
-                ],
-                puts,
-                len(out),
-            )
+            moves = [(state_ref.at[part], state_hbm.at[part]), (mixed_ref.at[:, part], mixed_hbm.at[:, part])]
+            out.extend(copies(moves, puts, len(out)))
+
+    local_block(x_ref, coefs_ref, bias_ref, decay_ref, skip_ref, mixed_ref, state_ref, x_in, after)
     for copy in out:
         copy.wait()
 
 
-def fold_kernel(n, place_ref, bias_ref, decay_ref, *refs):
-    states, mixed, blocks = refs[:n], refs[n : 2 * n], refs[2 * n : 4 * n]
-    out, (enter_ref, logs_ref, mixed_ref, coefs_ref, gets, puts) = refs[4 * n : 5 * n], refs[5 * n :]
+def fold_kernel(n, place_ref, bias_ref, decay_ref, skip_ref, state_hbm, own_hbm, *refs):
+    blocks, out = refs[: 2 * n], refs[2 * n : 3 * n]
+    x_ref, enter_ref, logs_ref, mixed_ref, coefs_ref, gets, puts = refs[3 * n :]
     inner, heads = mixed_ref.shape[2], bias_ref.shape[1]
     pairs = inner // SPAN
-    coefs_in, state_in, mixed_in = [], [], []
+    coefs_in, x_in = [], []
     for i in range(n):
-        coefs_in += copies(
-            halves(blocks[2 * i : 2 * i + 2], slice(2 * inner, None), coefs_ref.at[i]), gets, 2 * i
-        )
+        pieces = blocks[2 * i : 2 * i + 2]
+        coefs_in.append(copies(halves(pieces, slice(2 * inner, None), coefs_ref.at[i]), gets, 2 * i))
+        if i:
+            x_in.append(copies(halves(pieces, slice(0, inner), x_ref.at[i - 1]), gets, 2 * (n + i)))
+    own_in = copies([(state_hbm, enter_ref.at[place_ref[0]]), (own_hbm, mixed_ref.at[0])], gets, 2 * n)
     for i in range(n):
-        state_in += copies([(states[i], enter_ref.at[place_ref[i]])], gets, 2 * n + i)
-    for i in range(n):
-        mixed_in += copies([(mixed[i], mixed_ref.at[i])], gets, 3 * n + i)
-    for copy in coefs_in:
-        copy.wait()
-    for i in range(n):
-        raw_t = coefs_ref[i, :heads, 2 * SPAN :]
-        logs_ref[place_ref[i]] = steps_of(raw_t, bias_ref[...], decay_ref[...])[1]
-    for copy in state_in:
+        for copy in coefs_in[i]:
+            copy.wait()
+        place = place_ref[i]
+        if i:
+            logs_ref[place] = local_block(
+                x_ref.at[i - 1],
+                coefs_ref.at[i],
+                bias_ref,
+                decay_ref,
+                skip_ref,
+                mixed_ref.at[i],
+                enter_ref.at[place],
+                [x_in[i - 1]],
+            )
+        else:
+            logs_ref[place] = steps_of(coefs_ref[i, :heads, 2 * SPAN :], bias_ref[...], decay_ref[...])[1]
+    for copy in own_in:
         copy.wait()
     for pair in range(pairs):
         lanes = slice(pair * SPAN, (pair + 1) * SPAN)
@@ -247,7 +262,6 @@
     low = first_lanes((SPAN, SPAN))
     out_copies = []
     for i in range(n):
-        mixed_in[i].wait()
         place = place_ref[i]
         cumulative = jnp.transpose(logs_ref[place])
         c = coefs_ref[i, :, SPAN : 2 * SPAN]
@@ -402,27 +416,26 @@
 
     parts, top, bottom = lax.optimization_barrier((parts, top, bottom))
     own = (top, bottom)
-    left = tuple(lax.ppermute(a, "x", ring(n_x, 1)) for a in own)
-    right = tuple(lax.ppermute(a, "x", ring(n_x, -1)) for a in (bottom, top))[::-1]
+    left_top = lax.ppermute(top, "x", ring(n_x, 1))
+    right_bottom = lax.ppermute(bottom, "x", ring(n_x, -1))
     place = (at_x + jnp.array([0, n_x - 1, 1, 2], jnp.int32)) % n_x
 
-    def local(block):
-        return call(
-            local_kernel,
-            [values, jax.ShapeDtypeStruct((inner, SPAN), F32)],
-            scratch=[
-                pltpu.VMEM((tokens, inner), BF16),
-                pltpu.VMEM((tokens, 3 * SPAN), BF16),
-                pltpu.VMEM((tokens, inner), F32),
-                pltpu.VMEM((inner, SPAN), F32),
-                pltpu.SemaphoreType.DMA((10,)),
-                pltpu.SemaphoreType.DMA((8,)),
-            ],
-            flops=10**6,
-            vmem=3,
-            hbm_outs=2,
-            args=(bias, decay, skip, *block),
-        )
+    own_local = call(
+        local_kernel,
+        [values, jax.ShapeDtypeStruct((inner, SPAN), F32)],
+        scratch=[
+            pltpu.VMEM((tokens, inner), BF16),
+            pltpu.VMEM((tokens, 3 * SPAN), BF16),
+            pltpu.VMEM((tokens, inner), F32),
+            pltpu.VMEM((inner, SPAN), F32),
+            pltpu.SemaphoreType.DMA((10,)),
+            pltpu.SemaphoreType.DMA((8,)),
+        ],
+        flops=10**6,
+        vmem=3,
+        hbm_outs=2,
+        args=(bias, decay, skip, *own),
+    )
 
     (grouped,) = call(
         group_kernel,
@@ -432,9 +445,12 @@
         args=(parts,),
     )
     parts = lax.all_to_all(grouped, GROUPS, 0, 0, tiled=True)
-    own_local, parts, onward, back = lax.optimization_barrier((local(own), parts, left[0], right[1]))
-    left, right = (onward, left[1]), (right[0], back)
-    far = (lax.ppermute(onward, "x", ring(n_x, 1)), lax.ppermute(back, "x", ring(n_x, -1)))
+    (mixed, fresh), parts, left_top, right_bottom, top_later, bottom_later = lax.optimization_barrier(
+        (own_local, parts, left_top, right_bottom, top, bottom)
+    )
+    left = (left_top, lax.ppermute(bottom_later, "x", ring(n_x, 1)))
+    right = (lax.ppermute(top_later, "x", ring(n_x, -1)), right_bottom)
+    far = (lax.ppermute(left_top, "x", ring(n_x, 1)), lax.ppermute(right_bottom, "x", ring(n_x, -1)))
     mine = lax.axis_index(GROUPS)
     each = STATE // size
     carry = lax.dynamic_index_in_dim(
@@ -449,15 +465,15 @@
         args=(parts, carry),
     )
     entering = lax.all_to_all(entering, GROUPS, 0, 0, tiled=True).reshape(1, quarter, SPAN)
-    entering, left_local, right_local, far = lax.optimization_barrier((entering, local(left), local(right), far))
+    entering, left, right, far = lax.optimization_barrier((entering, left, right, far))
     entering = lax.all_to_all(jnp.broadcast_to(entering, (n_x, quarter, SPAN)), "x", 0, 0, tiled=True)
 
-    mixed, fresh = zip(own_local, left_local, right_local, local(far))
     blocks = (*own, *left, *right, *far)
     mixed = call(
         functools.partial(fold_kernel, n_x),
         [values] * n_x,
         scratch=[
+            pltpu.VMEM((n_x - 1, tokens, inner), BF16),
             pltpu.VMEM((n_x, inner, SPAN), F32),
             pltpu.VMEM((n_x, heads, SPAN), F32),
             pltpu.VMEM((n_x, tokens, inner), F32),
@@ -467,9 +483,9 @@
         ],
         flops=2 * n_x * tokens * inner * STATE * 2,
         smem=1,
-        vmem=2,
+        vmem=3,
         hbm_outs=n_x,
-        args=(place, bias, decay, *fresh, *mixed, *blocks),
+        args=(place, bias, decay, skip, fresh, mixed, *blocks),
     )
     (partial,) = call(
         functools.partial(mix_kernel, n_x),

time: 162 us -> 160 us (0.988)
  blocking collectives: 28.6 us -> 47.3 us
  Pallas kernels: 47.4 us -> 35.4 us
  starting transfers between devices: 42.7 us -> 35.3 us
    all_to_all x0 -> x1, blocking collectives: none -> 21.1 us  [on_device(): lax.all_to_all(entering, GROUPS, 0, 0, tiled=True).reshape(1, quarter, SPAN)]
    pallas_call x10 -> x7, Pallas kernels: 47.4 us -> 35.4 us  [call(): pl.pallas_call(kernel, out_shape=list(outs), in_specs=specs, out_specs=[p...]
    all_to_all x1 -> x0, starting transfers between devices: 8.79 us -> none  [on_device(): lax.all_to_all(entering, GROUPS, 0, 0, tiled=True).reshape(1, quarter, SPAN)]
    all_to_all x1, blocking collectives: 28.6 us -> 26.1 us  [on_device(): partial = lax.all_to_all(partial, ('x', *TENSOR), 0, 0, tiled=True)]
    all_to_all x1 -> x0, waiting for transfers between devices: 1.76 us -> none  [on_device(): lax.all_to_all(entering, GROUPS, 0, 0, tiled=True).reshape(1, quarter, SPAN)]
  transfers between devices with their start and end apart: 14 -> 13, of which waited for: 6 -> 5; matrix products, arithmetic and copies ran while one was open for 2% -> 2% of each run, Pallas kernels for 19% -> 12%
where the time goes in v6:
time: 160 us
  blocking collectives  47.3 us (30%)
  Pallas kernels  35.4 us (22%)
  starting transfers between devices  35.3 us (22%)
  waiting for transfers between devices  22.4 us (14%)
  between operations  13.6 us (8%)
  local copies, waits for them, and re-layouts  3.07 us (2%)
  other arithmetic  2.72 us (2%)
    pallas_call x7, Pallas kernels, call(): pl.pallas_call(kernel, out_shape=list(outs), in_specs=specs, out_specs=[p...  35.4 us
    all_to_all x1, blocking collectives, on_device(): partial = lax.all_to_all(partial, ('x', *TENSOR), 0, 0, tiled=True)  26.1 us
    all_to_all x1, blocking collectives, on_device(): lax.all_to_all(entering, GROUPS, 0, 0, tiled=True).reshape(1, quarter, SPAN)  21.1 us
    all_to_all x1, starting transfers between devices, on_device(): parts = lax.all_to_all(grouped, GROUPS, 0, 0, tiled=True)  12 us
    all_to_all x1, waiting for transfers between devices, on_device(): parts = lax.all_to_all(states, 'x', 0, 0, tiled=True)  5.75 us
    ppermute x1, waiting for transfers between devices, on_device(): across = lax.ppermute(done, 'yl', ring(2, 1))  5.5 us
    all_to_all x1, starting transfers between devices, on_device(): parts = lax.all_to_all(states, 'x', 0, 0, tiled=True)  4.99 us
    ppermute x1, waiting for transfers between devices, on_device(): left_top = lax.ppermute(top, 'x', ring(n_x, 1))  4.91 us
  transfers between devices with their start and end apart: 13, of which 5 were waited for; matrix products, arithmetic and copies ran while one was open for 2% of the time, Pallas kernels for 12%

profile of v6, /device:TPU:1, one launch (start us, length us, event | category | flops | bytes accessed | tf_op | source)
XLA Modules:
  0.0 159.8 jit_solution(1678188404038576970)
XLA Ops:
  6.5 3.6 %shard_map.136 = (f32[4,520,128]{2,1,0:T(8,128)}, bf16[64,4480]{1,0:T(8,128)(2,1)}, bf16[64,4480]{1,0:T(8,128)(2,1)}) custom-call(bf16[128,2048]{1,0:T(8,128)(2,1)} %x_hbm.1, bf16[128,2048]{1,0:T(8,128)(2,1)} %gate_hbm.1, bf16[128,128]{1,0:T(8,128)(2,1)} %b_hbm.1, bf16[128,128]{1,0:T(8,128)(2,1)} %c_hbm.1, bf16[32,128]{1,0:T(8,128)(2,1)} %bitcast.38, ...), custom_call_target="tpu_custom_call" | custom-call | flops 134217728 | bytes 3334400 | tf_op jit(solution)/shard_map/pallas_call | solution.py:30
  10.1 5.0 %all-to-all-start = ((f32[4,520,128]{2,1,0:T(8,128)}), f32[4,520,128]{2,1,0:T(8,128)S(1)}, u32[]{:S(2)}, u32[]{:S(2)}) async-start(f32[4,520,128]{2,1,0:T(8,128)} %get-tuple-element.33), calls=%async_computation | async-start | bytes 2129920 | tf_op jit(solution)/shard_map/all_to_all | solution.py:412
  15.1 3.0 %collective-permute-start = (bf16[64,2048]{1,0:T(8,128)(2,1)S(1)}, bf16[64,2048]{1,0:T(8,128)(2,1)S(1)}, u32[]{:S(2)}, u32[]{:S(2)}) collective-permute-start(bf16[64,2048]{1,0:T(8,128)(2,1)S(1)} %bitcast.28), channel_id=1, source_target_pairs={{0,128},{128,0},{1,129},{129,1},{2,130},{130,2},{3,131},{131,3},{4... | collective-permute-start | bytes 786440 | tf_op jit(solution)/shard_map/ppermute | solution.py:397
  18.1 4.7 %collective-permute-done = bf16[64,2048]{1,0:T(8,128)(2,1)S(1)} collective-permute-done((bf16[64,2048]{1,0:T(8,128)(2,1)S(1)}, bf16[64,2048]{1,0:T(8,128)(2,1)S(1)}, u32[]{:S(2)}, u32[]{:S(2)}) %collective-permute-start) | collective-permute-done | bytes 262176 | tf_op jit(solution)/shard_map/ppermute | solution.py:397
  22.8 5.8 %all-to-all-done.parts_ref = f32[4,520,128]{2,1,0:T(8,128)S(1)} async-done(((f32[4,520,128]{2,1,0:T(8,128)}), f32[4,520,128]{2,1,0:T(8,128)S(1)}, u32[]{:S(2)}, u32[]{:S(2)}) %all-to-all-start) | async-done | bytes 1064992 | tf_op jit(solution)/shard_map/all_to_all | solution.py:412
  28.5 0.9 pad_maximum_fusion.1
  30.2 12.0 %all-to-all-start.1 = ((f32[16,40,128]{2,1,0:T(8,128)}), f32[16,40,128]{2,1,0:T(8,128)S(1)}, u32[]{:S(2)}, u32[]{:S(2)}) async-start(f32[16,40,128]{2,1,0:T(8,128)} %shard_map.138), calls=%async_computation.1 | async-start | bytes 655360 | tf_op jit(solution)/shard_map/all_to_all | solution.py:447
  42.6 2.4 %collective-permute-start.2 = (bf16[64,4480]{1,0:T(8,128)(2,1)}, bf16[64,4480]{1,0:T(8,128)(2,1)}, u32[]{:S(2)}, u32[]{:S(2)}) collective-permute-start(bf16[64,4480]{1,0:T(8,128)(2,1)} %get-tuple-element.44.bottom_hbm.refs_1_.refs_5_), channel_id=1, source_target_pairs={{0,12},{4,0},{8,4},{12,8},{1,13},{5,1},{9,5},{13,9},{2,14},{6,2},{... | collective-permute-start | bytes 1720328 | tf_op jit(solution)/shard_map/ppermute | solution.py:420
  45.7 5.3 %shard_map.137 = (f32[128,2048]{1,0:T(8,128)}, f32[2048,128]{1,0:T(8,128)}) custom-call(f32[1,32]{1,0:T(1,128)} %bitcast.31, f32[1,32]{1,0:T(1,128)} %bitcast.35, f32[1,2048]{1,0:T(1,128)} %reshape_reshape.3.skip_ref, bf16[64,4480]{1,0:T(8,128)(2,1)} %get-tuple-element.45.top_hbm.refs_0_.refs_4_, bf16[64,4480]{1,0:T(8,128)(2,1)} %get-tuple-element.44.bottom_hbm.refs_1_.refs_5_), custom_call_target="tpu_custom_call" | custom-call | flops 1000000 | bytes 3252480 | tf_op jit(solution)/shard_map/pallas_call | solution.py:30
  51.0 4.9 %collective-permute-done.1.refs_2_.refs_6_ = bf16[64,4480]{1,0:T(8,128)(2,1)} collective-permute-done((bf16[64,4480]{1,0:T(8,128)(2,1)S(1)}, bf16[64,4480]{1,0:T(8,128)(2,1)}, u32[]{:S(2)}, u32[]{:S(2)}) %collective-permute-start.1) | collective-permute-done | bytes 573472 | tf_op jit(solution)/shard_map/ppermute | solution.py:419
  56.0 2.7 %collective-permute-start.4 = (bf16[64,4480]{1,0:T(8,128)(2,1)S(1)}, bf16[64,4480]{1,0:T(8,128)(2,1)}, u32[]{:S(2)}, u32[]{:S(2)}) collective-permute-start(bf16[64,4480]{1,0:T(8,128)(2,1)S(1)} %copy-done.4), channel_id=1, source_target_pairs={{0,12},{4,0},{8,4},{12,8},{1,13},{5,1},{9,5},{13,9},{2,14},{6,2},{... | collective-permute-start | bytes 1720328 | tf_op jit(solution)/shard_map/ppermute | solution.py:452
  58.7 2.7 %collective-permute-start.6 = (bf16[64,4480]{1,0:T(8,128)(2,1)}, bf16[64,4480]{1,0:T(8,128)(2,1)}, u32[]{:S(2)}, u32[]{:S(2)}) collective-permute-start(bf16[64,4480]{1,0:T(8,128)(2,1)} %collective-permute-done.2.refs_5_.refs_9_), channel_id=1, source_target_pairs={{0,12},{4,0},{8,4},{12,8},{1,13},{5,1},{9,5},{13,9},{2,14},{6,2},{... | collective-permute-start | bytes 1720328 | tf_op jit(solution)/shard_map/ppermute | solution.py:453
  61.5 21.1 %all_to_all.29 = f32[16,32,128]{2,1,0:T(8,128)S(1)} all-to-all(f32[16,32,128]{2,1,0:T(8,128)S(1)} %shard_map.139), channel_id=1, replica_groups=mesh['yh'=2,'z'=8,'x'=4,'yl'=2,'core'=2] {'yh','z'}, dimensions={0} | all-to-all | bytes 524288 | tf_op jit(solution)/shard_map/all_to_all | solution.py:467
  82.7 1.1 broadcast_in_dim.12
  83.8 3.8 %all-to-all-start.3 = ((f32[4,512,128]{2,1,0:T(8,128)}), f32[4,512,128]{2,1,0:T(8,128)S(1)}, u32[]{:S(2)}, u32[]{:S(2)}) async-start(f32[4,512,128]{2,1,0:T(8,128)} %broadcast_in_dim.12), calls=%async_computation.3 | async-start | bytes 2097152 | tf_op jit(solution)/shard_map/all_to_all | solution.py:469
  88.2 12.9 %shard_map.140 = (f32[128,2048]{1,0:T(8,128)}, f32[128,2048]{1,0:T(8,128)}, f32[128,2048]{1,0:T(8,128)}, f32[128,2048]{1,0:T(8,128)}) custom-call(s32[4]{0:T(128)} %and_select_fusion.place_ref, f32[1,32]{1,0:T(1,128)} %bitcast.32, f32[1,32]{1,0:T(1,128)} %bitcast.36, f32[1,2048]{1,0:T(1,128)} %reshape_reshape.3.skip_ref, ...), custom_call_target="tpu_custom_call" | custom-call | flops 536870912 | bytes 10887440 | tf_op jit(solution)/shard_map/pallas_call | solution.py:30
  101.2 0.9 copy-done.5
  102.1 12.1 %shard_map.141 = bf16[512,1024]{1,0:T(8,128)(2,1)} custom-call(s32[4]{0:T(128)} %and_select_fusion.place_ref, f32[1,32]{1,0:T(1,128)} %bitcast.33, f32[1,32]{1,0:T(1,128)} %bitcast.37, f32[1,2048]{1,0:T(1,128)} %bitcast.39, f32[2048,128]{1,0:T(8,128)} %bitcast.23, f32[128,2048]{1,0:T(8,128)} %get-tuple-element.56.refs_0_, ...), custom_call_target="tpu_custom_call" | custom-call | flops 2684354560 | bytes 15081744 | tf_op jit(solution)/shard_map/pallas_call | solution.py:30
  114.3 26.1 %all_to_all.30.parts_ref = bf16[16,32,1024]{2,1,0:T(8,128)(2,1)S(1)} all-to-all(bf16[16,32,1024]{2,1,0:T(8,128)(2,1)} %bitcast.24), channel_id=1, replica_groups=mesh['yh'=2,'z'=8,'x'=4,'yl'=2,'core'=2] {'x','yl','core'}, dimensions={0} | all-to-all | bytes 2097152 | tf_op jit(solution)/shard_map/all_to_all | solution.py:515
  141.1 1.3 collective-permute-start.7
  142.4 5.5 %collective-permute-done.7 = bf16[32,4096]{1,0:T(8,128)(2,1)S(1)} collective-permute-done((bf16[32,4096]{1,0:T(8,128)(2,1)S(1)}, bf16[32,4096]{1,0:T(8,128)(2,1)S(1)}, u32[]{:S(2)}, u32[]{:S(2)}) %collective-permute-start.7) | collective-permute-done | bytes 262176 | tf_op jit(solution)/shard_map/ppermute | solution.py:526
  148.0 2.1 %collective-permute-start.8 = (bf16[2,32,4096]{2,1,0:T(8,128)(2,1)S(1)}, bf16[2,32,4096]{2,1,0:T(8,128)(2,1)S(1)}, u32[]{:S(2)}, u32[]{:S(2)}) collective-permute-start(bf16[2,32,4096]{2,1,0:T(8,128)(2,1)S(1)} %pad_maximum_fusion.2), channel_id=1, source_target_pairs={{0,1},{1,0},{2,3},{3,2},{4,5},{5,4},{6,7},{7,6},{8,9},{9,8},{10,11... | collective-permute-start | bytes 1572872 | tf_op jit(solution)/shard_map/ppermute | solution.py:528
  150.1 1.5 collective-permute-done.8
  151.9 1.1 pad_maximum_fusion
  (44 shorter events, 3.8 us)
Async XLA Ops:
  6.5 54.8 %copy-start = (f32[32,64,128]{2,1,0:T(8,128)S(1)}, f32[32,64,128]{2,1,0:T(8,128)}, u32[]{:S(2)}) copy-start(f32[32,64,128]{2,1,0:T(8,128)} %param.23) | copy-start | bytes 3145732
  10.1 5.0 %copy-start.7 = (bf16[2048,64]{0,1:T(8,128)(2,1)S(1)}, bf16[2048,64]{0,1:T(8,128)(2,1)}, u32[]{:S(2)}) copy-start(bf16[2048,64]{0,1:T(8,128)(2,1)} %param.24) | copy-start | bytes 786436
  10.1 18.4 %all-to-all-start = ((f32[4,520,128]{2,1,0:T(8,128)}), f32[4,520,128]{2,1,0:T(8,128)S(1)}, u32[]{:S(2)}, u32[]{:S(2)}) async-start(f32[4,520,128]{2,1,0:T(8,128)} %get-tuple-element.33), calls=%async_computation | async-start | bytes 2129920 | tf_op jit(solution)/shard_map/all_to_all | solution.py:412
  15.1 86.1 %all-gather.2.cloned.1.call-start = ((), (), s32[]{:S(2)}) async-start(), calls=%async_computation.5 | async-start | bytes 4718592 | tf_op jit(solution)/shard_map/all_gather | solution.py:415
  15.1 7.7 %collective-permute-start = (bf16[64,2048]{1,0:T(8,128)(2,1)S(1)}, bf16[64,2048]{1,0:T(8,128)(2,1)S(1)}, u32[]{:S(2)}, u32[]{:S(2)}) collective-permute-start(bf16[64,2048]{1,0:T(8,128)(2,1)S(1)} %bitcast.28), channel_id=1, source_target_pairs={{0,128},{128,0},{1,129},{129,1},{2,130},{130,2},{3,131},{131,3},{4... | collective-permute-start | bytes 786440 | tf_op jit(solution)/shard_map/ppermute | solution.py:397
  29.4 12.8 %copy-start.3 = (bf16[64,4480]{1,0:T(8,128)(2,1)S(1)}, bf16[64,4480]{1,0:T(8,128)(2,1)}, u32[]{:S(2)}) copy-start(bf16[64,4480]{1,0:T(8,128)(2,1)} %get-tuple-element.45.top_hbm.refs_0_.refs_4_) | copy-start | bytes 1720324
  29.4 15.6 %copy-start.8 = (f32[32]{0:T(128)S(1)}, f32[32]{0:T(128)}, u32[]{:S(2)}) copy-start(f32[32]{0:T(128)} %param.21) | copy-start | bytes 388
  30.2 25.8 %copy-start.4 = (bf16[64,4480]{1,0:T(8,128)(2,1)S(1)}, bf16[64,4480]{1,0:T(8,128)(2,1)}, u32[]{:S(2)}) copy-start(bf16[64,4480]{1,0:T(8,128)(2,1)} %get-tuple-element.45.top_hbm.refs_0_.refs_4_) | copy-start | bytes 1720324
  30.2 25.7 %all-to-all-start.1 = ((f32[16,40,128]{2,1,0:T(8,128)}), f32[16,40,128]{2,1,0:T(8,128)S(1)}, u32[]{:S(2)}, u32[]{:S(2)}) async-start(f32[16,40,128]{2,1,0:T(8,128)} %shard_map.138), calls=%async_computation.1 | async-start | bytes 655360 | tf_op jit(solution)/shard_map/all_to_all | solution.py:447
  42.2 13.7 %collective-permute-start.1 = (bf16[64,4480]{1,0:T(8,128)(2,1)S(1)}, bf16[64,4480]{1,0:T(8,128)(2,1)}, u32[]{:S(2)}, u32[]{:S(2)}) collective-permute-start(bf16[64,4480]{1,0:T(8,128)(2,1)S(1)} %copy-done.3), channel_id=1, source_target_pairs={{0,4},{4,8},{8,12},{12,0},{1,5},{5,9},{9,13},{13,1},{2,6},{6,10},{... | collective-permute-start | bytes 1720328 | tf_op jit(solution)/shard_map/ppermute | solution.py:419
  42.6 13.4 %collective-permute-start.2 = (bf16[64,4480]{1,0:T(8,128)(2,1)}, bf16[64,4480]{1,0:T(8,128)(2,1)}, u32[]{:S(2)}, u32[]{:S(2)}) collective-permute-start(bf16[64,4480]{1,0:T(8,128)(2,1)} %get-tuple-element.44.bottom_hbm.refs_1_.refs_5_), channel_id=1, source_target_pairs={{0,12},{4,0},{8,4},{12,8},{1,13},{5,1},{9,5},{13,9},{2,14},{6,2},{... | collective-permute-start | bytes 1720328 | tf_op jit(solution)/shard_map/ppermute | solution.py:420
  56.0 26.7 %collective-permute-start.3 = (bf16[64,4480]{1,0:T(8,128)(2,1)}, bf16[64,4480]{1,0:T(8,128)(2,1)S(1)}, u32[]{:S(2)}, u32[]{:S(2)}) collective-permute-start(bf16[64,4480]{1,0:T(8,128)(2,1)} %get-tuple-element.44.bottom_hbm.refs_1_.refs_5_), channel_id=1, source_target_pairs={{0,4},{4,8},{8,12},{12,0},{1,5},{5,9},{9,13},{13,1},{2,6},{6,10},{... | collective-permute-start | bytes 1720328 | tf_op jit(solution)/shard_map/ppermute | solution.py:451
  56.0 26.7 %collective-permute-start.4 = (bf16[64,4480]{1,0:T(8,128)(2,1)S(1)}, bf16[64,4480]{1,0:T(8,128)(2,1)}, u32[]{:S(2)}, u32[]{:S(2)}) collective-permute-start(bf16[64,4480]{1,0:T(8,128)(2,1)S(1)} %copy-done.4), channel_id=1, source_target_pairs={{0,12},{4,0},{8,4},{12,8},{1,13},{5,1},{9,5},{13,9},{2,14},{6,2},{... | collective-permute-start | bytes 1720328 | tf_op jit(solution)/shard_map/ppermute | solution.py:452
  58.7 24.0 %collective-permute-start.5 = (bf16[64,4480]{1,0:T(8,128)(2,1)}, bf16[64,4480]{1,0:T(8,128)(2,1)}, u32[]{:S(2)}, u32[]{:S(2)}) collective-permute-start(bf16[64,4480]{1,0:T(8,128)(2,1)} %collective-permute-done.1.refs_2_.refs_6_), channel_id=1, source_target_pairs={{0,4},{4,8},{8,12},{12,0},{1,5},{5,9},{9,13},{13,1},{2,6},{6,10},{... | collective-permute-start | bytes 1720328 | tf_op jit(solution)/shard_map/ppermute | solution.py:453
  58.7 24.0 %collective-permute-start.6 = (bf16[64,4480]{1,0:T(8,128)(2,1)}, bf16[64,4480]{1,0:T(8,128)(2,1)}, u32[]{:S(2)}, u32[]{:S(2)}) collective-permute-start(bf16[64,4480]{1,0:T(8,128)(2,1)} %collective-permute-done.2.refs_5_.refs_9_), channel_id=1, source_target_pairs={{0,12},{4,0},{8,4},{12,8},{1,13},{5,1},{9,5},{13,9},{2,14},{6,2},{... | collective-permute-start | bytes 1720328 | tf_op jit(solution)/shard_map/ppermute | solution.py:453
  82.7 1.2 copy-start.6
  83.8 3.8 %copy-start.9 = (s32[4]{0:T(128)S(1)}, s32[4]{0:T(128)}, u32[]{:S(2)}) copy-start(s32[4]{0:T(128)} %constant.86.clone) | copy-start | bytes 52
  83.8 17.3 %all-to-all-start.3 = ((f32[4,512,128]{2,1,0:T(8,128)}), f32[4,512,128]{2,1,0:T(8,128)S(1)}, u32[]{:S(2)}, u32[]{:S(2)}) async-start(f32[4,512,128]{2,1,0:T(8,128)} %broadcast_in_dim.12), calls=%async_computation.3 | async-start | bytes 2097152 | tf_op jit(solution)/shard_map/all_to_all | solution.py:469
  101.2 1.0 copy-start.5
  114.3 26.2 %copy-start.1 = (bf16[32,4096]{1,0:T(8,128)(2,1)S(1)}, bf16[32,4096]{1,0:T(8,128)(2,1)}, u32[]{:S(2)}) copy-start(bf16[32,4096]{1,0:T(8,128)(2,1)} %residual_ref.1) | copy-start | bytes 786436
  114.3 26.2 %copy-start.2 = (f32[4096]{0:T(1024)S(1)}, f32[4096]{0:T(1024)}, u32[]{:S(2)}) copy-start(f32[4096]{0:T(1024)} %param.26) | copy-start | bytes 49156
  141.1 6.8 %collective-permute-start.7 = (bf16[32,4096]{1,0:T(8,128)(2,1)S(1)}, bf16[32,4096]{1,0:T(8,128)(2,1)S(1)}, u32[]{:S(2)}, u32[]{:S(2)}) collective-permute-start(bf16[32,4096]{1,0:T(8,128)(2,1)S(1)} %shard_map.142), channel_id=1, source_target_pairs={{0,2},{2,0},{1,3},{3,1},{4,6},{6,4},{5,7},{7,5},{8,10},{10,8},{9,1... | collective-permute-start | bytes 786440 | tf_op jit(solution)/shard_map/ppermute | solution.py:526
  148.0 3.6 %collective-permute-start.8 = (bf16[2,32,4096]{2,1,0:T(8,128)(2,1)S(1)}, bf16[2,32,4096]{2,1,0:T(8,128)(2,1)S(1)}, u32[]{:S(2)}, u32[]{:S(2)}) collective-permute-start(bf16[2,32,4096]{2,1,0:T(8,128)(2,1)S(1)} %pad_maximum_fusion.2), channel_id=1, source_target_pairs={{0,1},{1,0},{2,3},{3,2},{4,5},{5,4},{6,7},{7,6},{8,9},{9,8},{10,11... | collective-permute-start | bytes 1572872 | tf_op jit(solution)/shard_map/ppermute | solution.py:528
Sparse Core Ops, SparseCore 0:
  29.5 69.2 all-gather.1

commit v7 on v6

--- a/solution.py
+++ b/solution.py
@@ -278,7 +278,7 @@
 
 def mix_kernel(n, place_ref, bias_ref, decay_ref, gain_ref, enter_ref, *refs):
     mixed, blocks, weight_hbm = refs[:n], refs[n : 3 * n], refs[3 * n]
-    out_ref, logs_ref, mixed_ref, block_ref, normed_ref, weight_ref, semaphores = refs[3 * n + 1 :]
+    kept_ref, sent_ref, logs_ref, mixed_ref, block_ref, normed_ref, weight_ref, semaphores = refs[3 * n + 1 :]
     inner, heads = mixed_ref.shape[2], bias_ref.shape[1]
     pairs = inner // SPAN
     block_in, mixed_in = [], []
@@ -321,23 +321,28 @@
             lanes = slice(pair * SPAN, (pair + 1) * SPAN)
             normed_ref[to, lanes] = (mixed_ref[i, :, lanes] * root * gain_ref[:, lanes]).astype(BF16)
     weight_in.wait()
-    for tile in range(weight_ref.shape[0] // (2 * SPAN)):
-        columns = slice(2 * tile * SPAN, 2 * (tile + 1) * SPAN)
-        product = lax.dot_general(
-            normed_ref[...], weight_ref[columns, :], (((1,), (1,)), ((), ())), preferred_element_type=F32
-        )
-        out_ref[:, columns] = product.astype(BF16)
-
-
-def finish_kernel(late_ref, parts_ref, residual_ref, gain_ref, out_ref, combined_ref, *, n_x, n_t, n_z):
+    core, width = place_ref[n], kept_ref.shape[1]
+    for ref, side in ((sent_ref, 1 - core), (kept_ref, core)):
+        for tile in range(width // (2 * SPAN)):
+            columns = slice(2 * tile * SPAN, 2 * (tile + 1) * SPAN)
+            rows = pl.ds(pl.multiple_of(side * width + 2 * tile * SPAN, 2 * SPAN), 2 * SPAN)
+            ref[:, columns] = lax.dot_general(
+                normed_ref[...], weight_ref[rows, :], (((1,), (1,)), ((), ())), preferred_element_type=F32
+            )
+
+
+def finish_kernel(late_ref, parts_ref, residual_ref, gain_ref, out_ref, combined_ref, *, n_x, n_z):
     late = late_ref[0] > 0
     tokens = residual_ref.shape[0]
     sums = []
     for x in range(n_x):
-        total = parts_ref[x * n_t].astype(F32)
-        for t in range(1, n_t):
-            total += parts_ref[x * n_t + t].astype(F32)
-        sums.append(total)
+        cores = []
+        for core in range(parts_ref.shape[2]):
+            total = parts_ref[x, 0, core].astype(F32)
+            for y in range(1, parts_ref.shape[1]):
+                total += parts_ref[x, y, core].astype(F32)
+            cores.append(total)
+        sums.append(jnp.concatenate(cores, axis=1))
     squares = jnp.zeros((tokens, 2 * HEAD_DIM), F32)
     for z in range(n_z):
         piece = slice(z * 2 * HEAD_DIM, (z + 1) * 2 * HEAD_DIM)
@@ -419,6 +424,7 @@
     left_top = lax.ppermute(top, "x", ring(n_x, 1))
     right_bottom = lax.ppermute(bottom, "x", ring(n_x, -1))
     place = (at_x + jnp.array([0, n_x - 1, 1, 2], jnp.int32)) % n_x
+    place = jnp.concatenate([place, lax.axis_index("core").astype(jnp.int32).reshape(1)])
 
     own_local = call(
         local_kernel,
@@ -445,11 +451,13 @@
         args=(parts,),
     )
     parts = lax.all_to_all(grouped, GROUPS, 0, 0, tiled=True)
-    (mixed, fresh), parts, left_top, right_bottom, top_later, bottom_later = lax.optimization_barrier(
-        (own_local, parts, left_top, right_bottom, top, bottom)
-    )
-    left = (left_top, lax.ppermute(bottom_later, "x", ring(n_x, 1)))
-    right = (lax.ppermute(top_later, "x", ring(n_x, -1)), right_bottom)
+    own_local, top_later, bottom_later = lax.optimization_barrier((own_local, top, bottom))
+    left_bottom = lax.ppermute(bottom_later, "x", ring(n_x, 1))
+    right_top = lax.ppermute(top_later, "x", ring(n_x, -1))
+    (mixed, fresh), parts, left_top, right_bottom, place = lax.optimization_barrier(
+        (own_local, parts, left_top, right_bottom, place)
+    )
+    left, right = (left_top, left_bottom), (right_top, right_bottom)
     far = (lax.ppermute(left_top, "x", ring(n_x, 1)), lax.ppermute(right_bottom, "x", ring(n_x, -1)))
     mine = lax.axis_index(GROUPS)
     each = STATE // size
@@ -487,9 +495,9 @@
         hbm_outs=n_x,
         args=(place, bias, decay, skip, fresh, mixed, *blocks),
     )
-    (partial,) = call(
+    kept, sent = call(
         functools.partial(mix_kernel, n_x),
-        [jax.ShapeDtypeStruct((n_x * tokens, weight.shape[0]), BF16)],
+        [jax.ShapeDtypeStruct((n_x * tokens, weight.shape[0] // 2), F32)] * 2,
         scratch=[
             pltpu.VMEM((n_x, heads, SPAN), F32),
             pltpu.VMEM((n_x, tokens, inner), F32),
@@ -512,16 +520,17 @@
             weight,
         ),
     )
+    partial = (kept + lax.ppermute(sent, "core", ring(2, 1))).astype(BF16)
     partial = lax.all_to_all(partial, ("x", *TENSOR), 0, 0, tiled=True)
     rows = residual.shape[0]
     (done,) = call(
-        functools.partial(finish_kernel, n_x=n_x, n_t=n_t, n_z=n_z),
+        functools.partial(finish_kernel, n_x=n_x, n_z=n_z),
         [jax.ShapeDtypeStruct(residual.shape, BF16)],
         scratch=[pltpu.VMEM(residual.shape, F32)],
         flops=10**6,
         smem=1,
         vmem=3,
-        args=(late, partial.reshape(n_x * n_t, rows, weight.shape[0]), residual, final_gain.reshape(1, -1)),
+        args=(late, partial.reshape(n_x, n_t // 2, 2, rows, weight.shape[0] // 2), residual, final_gain.reshape(1, -1)),
     )
     across = lax.ppermute(done, "yl", ring(2, 1))
     mine_two = jnp.stack([done, across])

time: 160 us -> 159 us (level)
  blocking collectives: 47.3 us -> 14.6 us
  starting transfers between devices: 35.3 us -> 52.4 us
  waiting for transfers between devices: 22.4 us -> 34.2 us
    all_to_all x1 -> x0, blocking collectives: 21.1 us -> none  [on_device(): lax.all_to_all(entering, GROUPS, 0, 0, tiled=True).reshape(1, quarter, SPAN)]
    all_to_all x0 -> x1, waiting for transfers between devices: none -> 12.4 us  [on_device(): lax.all_to_all(entering, GROUPS, 0, 0, tiled=True).reshape(1, quarter, SPAN)]
    all_to_all x1, blocking collectives: 26.1 us -> 14.6 us  [on_device(): partial = lax.all_to_all(partial, ('x', *TENSOR), 0, 0, tiled=True)]
    all_to_all x0 -> x1, starting transfers between devices: none -> 8.78 us  [on_device(): lax.all_to_all(entering, GROUPS, 0, 0, tiled=True).reshape(1, quarter, SPAN)]
    ppermute x2 -> x3, starting transfers between devices: 2.67 us -> 11.1 us  [the longest x1 8.41 us: on_device(): partial = (kept + lax.ppermute(sent, 'core', ring(2, 1))).astype(BF16)]
    ppermute x1, waiting for transfers between devices: 4.91 us -> 1.57 us  [on_device(): left_top = lax.ppermute(top, 'x', ring(n_x, 1))]
    ppermute x2 -> x3, waiting for transfers between devices: 0.01 us -> 2.5 us  [the longest x1 2.5 us: on_device(): partial = (kept + lax.ppermute(sent, 'core', ring(2, 1))).astype(BF16)]
  transfers between devices with their start and end apart: 13 -> 15, of which waited for: 5 -> 8; matrix products, arithmetic and copies ran while one was open for 2% -> 2% of each run, Pallas kernels for 12% -> 13%
where the time goes in v7:
time: 159 us; the launch traced here: 158 us
  starting transfers between devices  52.4 us (33%)
  Pallas kernels  36 us (23%)
  waiting for transfers between devices  34.2 us (22%)
  blocking collectives  14.6 us (9%)
  between operations  13.6 us (9%)
  other arithmetic  4.09 us (3%)
  local copies, waits for them, and re-layouts  2.94 us (2%)
    pallas_call x7, Pallas kernels, call(): pl.pallas_call(kernel, out_shape=list(outs), in_specs=specs, out_specs=[p...  36 us
    all_to_all x1, blocking collectives, on_device(): partial = lax.all_to_all(partial, ('x', *TENSOR), 0, 0, tiled=True)  14.6 us
    all_to_all x1, waiting for transfers between devices, on_device(): lax.all_to_all(entering, GROUPS, 0, 0, tiled=True).reshape(1, quarter, SPAN)  12.4 us
    all_to_all x1, starting transfers between devices, on_device(): parts = lax.all_to_all(grouped, GROUPS, 0, 0, tiled=True)  12 us
    all_to_all x1, starting transfers between devices, on_device(): lax.all_to_all(entering, GROUPS, 0, 0, tiled=True).reshape(1, quarter, SPAN)  8.78 us
    ppermute x1, starting transfers between devices, on_device(): partial = (kept + lax.ppermute(sent, 'core', ring(2, 1))).astype(BF16)  8.41 us
    all_to_all x1, waiting for transfers between devices, on_device(): parts = lax.all_to_all(states, 'x', 0, 0, tiled=True)  5.75 us
    ppermute x1, waiting for transfers between devices, on_device(): across = lax.ppermute(done, 'yl', ring(2, 1))  5.5 us
  transfers between devices with their start and end apart: 15, of which 8 were waited for; matrix products, arithmetic and copies ran while one was open for 2% of the time, Pallas kernels for 13%

profile of v7, /device:TPU:1, one launch (start us, length us, event | category | flops | bytes accessed | tf_op | source)
XLA Modules:
  0.0 157.9 jit_solution(14918510758677505582)
XLA Ops:
  6.5 3.5 %shard_map.136 = (f32[4,520,128]{2,1,0:T(8,128)}, bf16[64,4480]{1,0:T(8,128)(2,1)}, bf16[64,4480]{1,0:T(8,128)(2,1)}) custom-call(bf16[128,2048]{1,0:T(8,128)(2,1)} %x_hbm.1, bf16[128,2048]{1,0:T(8,128)(2,1)} %gate_hbm.1, bf16[128,128]{1,0:T(8,128)(2,1)} %b_hbm.1, bf16[128,128]{1,0:T(8,128)(2,1)} %c_hbm.1, bf16[32,128]{1,0:T(8,128)(2,1)} %bitcast.41, ...), custom_call_target="tpu_custom_call" | custom-call | flops 134217728 | bytes 3334400 | tf_op jit(solution)/shard_map/pallas_call | solution.py:30
  10.1 5.0 %all-to-all-start = ((f32[4,520,128]{2,1,0:T(8,128)}), f32[4,520,128]{2,1,0:T(8,128)S(1)}, u32[]{:S(2)}, u32[]{:S(2)}) async-start(f32[4,520,128]{2,1,0:T(8,128)} %get-tuple-element.38), calls=%async_computation | async-start | bytes 2129920 | tf_op jit(solution)/shard_map/all_to_all | solution.py:417
  15.1 3.0 %collective-permute-start = (bf16[64,2048]{1,0:T(8,128)(2,1)S(1)}, bf16[64,2048]{1,0:T(8,128)(2,1)S(1)}, u32[]{:S(2)}, u32[]{:S(2)}) collective-permute-start(bf16[64,2048]{1,0:T(8,128)(2,1)S(1)} %bitcast.31), channel_id=1, source_target_pairs={{0,128},{128,0},{1,129},{129,1},{2,130},{130,2},{3,131},{131,3},{4... | collective-permute-start | bytes 786440 | tf_op jit(solution)/shard_map/ppermute | solution.py:402
  18.1 4.7 %collective-permute-done = bf16[64,2048]{1,0:T(8,128)(2,1)S(1)} collective-permute-done((bf16[64,2048]{1,0:T(8,128)(2,1)S(1)}, bf16[64,2048]{1,0:T(8,128)(2,1)S(1)}, u32[]{:S(2)}, u32[]{:S(2)}) %collective-permute-start) | collective-permute-done | bytes 262176 | tf_op jit(solution)/shard_map/ppermute | solution.py:402
  22.7 5.8 %all-to-all-done.parts_ref = f32[4,520,128]{2,1,0:T(8,128)S(1)} async-done(((f32[4,520,128]{2,1,0:T(8,128)}), f32[4,520,128]{2,1,0:T(8,128)S(1)}, u32[]{:S(2)}, u32[]{:S(2)}) %all-to-all-start) | async-done | bytes 1064992 | tf_op jit(solution)/shard_map/all_to_all | solution.py:417
  30.2 12.0 %all-to-all-start.1 = ((f32[16,40,128]{2,1,0:T(8,128)}), f32[16,40,128]{2,1,0:T(8,128)S(1)}, u32[]{:S(2)}, u32[]{:S(2)}) async-start(f32[16,40,128]{2,1,0:T(8,128)} %shard_map.138), calls=%async_computation.1 | async-start | bytes 655360 | tf_op jit(solution)/shard_map/all_to_all | solution.py:453
  42.6 2.4 %collective-permute-start.2 = (bf16[64,4480]{1,0:T(8,128)(2,1)}, bf16[64,4480]{1,0:T(8,128)(2,1)}, u32[]{:S(2)}, u32[]{:S(2)}) collective-permute-start(bf16[64,4480]{1,0:T(8,128)(2,1)} %get-tuple-element.52.bottom_hbm.refs_1_.refs_5_), channel_id=1, source_target_pairs={{0,12},{4,0},{8,4},{12,8},{1,13},{5,1},{9,5},{13,9},{2,14},{6,2},{... | collective-permute-start | bytes 1720328 | tf_op jit(solution)/shard_map/ppermute | solution.py:425
  46.3 5.3 %shard_map.137 = (f32[128,2048]{1,0:T(8,128)}, f32[2048,128]{1,0:T(8,128)}) custom-call(f32[1,32]{1,0:T(1,128)} %bitcast.34, f32[1,32]{1,0:T(1,128)} %bitcast.38, f32[1,2048]{1,0:T(1,128)} %reshape_reshape.3.skip_ref, bf16[64,4480]{1,0:T(8,128)(2,1)} %get-tuple-element.53.top_hbm.refs_0_.refs_4_, bf16[64,4480]{1,0:T(8,128)(2,1)} %get-tuple-element.52.bottom_hbm.refs_1_.refs_5_), custom_call_target="tpu_custom_call" | custom-call | flops 1000000 | bytes 3252480 | tf_op jit(solution)/shard_map/pallas_call | solution.py:30
  51.7 2.7 %collective-permute-start.4 = (bf16[64,4480]{1,0:T(8,128)(2,1)S(1)}, bf16[64,4480]{1,0:T(8,128)(2,1)}, u32[]{:S(2)}, u32[]{:S(2)}) collective-permute-start(bf16[64,4480]{1,0:T(8,128)(2,1)S(1)} %copy-done.4), channel_id=1, source_target_pairs={{0,12},{4,0},{8,4},{12,8},{1,13},{5,1},{9,5},{13,9},{2,14},{6,2},{... | collective-permute-start | bytes 1720328 | tf_op jit(solution)/shard_map/ppermute | solution.py:456
  54.4 1.6 collective-permute-done.1.refs_2_.refs_6_
  55.9 2.7 %collective-permute-start.6 = (bf16[64,4480]{1,0:T(8,128)(2,1)}, bf16[64,4480]{1,0:T(8,128)(2,1)}, u32[]{:S(2)}, u32[]{:S(2)}) collective-permute-start(bf16[64,4480]{1,0:T(8,128)(2,1)} %collective-permute-done.2.refs_5_.refs_9_), channel_id=1, source_target_pairs={{0,12},{4,0},{8,4},{12,8},{1,13},{5,1},{9,5},{13,9},{2,14},{6,2},{... | collective-permute-start | bytes 1720328 | tf_op jit(solution)/shard_map/ppermute | solution.py:461
  59.5 8.8 %all-to-all-start.2 = ((f32[16,32,128]{2,1,0:T(8,128)}), f32[16,32,128]{2,1,0:T(8,128)S(1)}, u32[]{:S(2)}, u32[]{:S(2)}) async-start(f32[16,32,128]{2,1,0:T(8,128)} %shard_map.139), calls=%async_computation.2 | async-start | bytes 524288 | tf_op jit(solution)/shard_map/all_to_all | solution.py:475
  68.3 12.4 %all-to-all-done.2 = f32[16,32,128]{2,1,0:T(8,128)S(1)} async-done(((f32[16,32,128]{2,1,0:T(8,128)}), f32[16,32,128]{2,1,0:T(8,128)S(1)}, u32[]{:S(2)}, u32[]{:S(2)}) %all-to-all-start.2) | async-done | bytes 262176 | tf_op jit(solution)/shard_map/all_to_all | solution.py:475
  81.9 3.7 %all-to-all-start.3 = ((f32[4,512,128]{2,1,0:T(8,128)}), f32[4,512,128]{2,1,0:T(8,128)S(1)}, u32[]{:S(2)}, u32[]{:S(2)}) async-start(f32[4,512,128]{2,1,0:T(8,128)} %broadcast_in_dim.12), calls=%async_computation.3 | async-start | bytes 2097152 | tf_op jit(solution)/shard_map/all_to_all | solution.py:477
  85.6 12.9 %shard_map.140 = (f32[128,2048]{1,0:T(8,128)}, f32[128,2048]{1,0:T(8,128)}, f32[128,2048]{1,0:T(8,128)}, f32[128,2048]{1,0:T(8,128)}) custom-call(s32[5]{0:T(128)} %pad_add_fusion.place_ref, f32[1,32]{1,0:T(1,128)} %bitcast.35, f32[1,32]{1,0:T(1,128)} %bitcast.39, f32[1,2048]{1,0:T(1,128)} %reshape_reshape.3.skip_ref, ...), custom_call_target="tpu_custom_call" | custom-call | flops 536870912 | bytes 10887444 | tf_op jit(solution)/shard_map/pallas_call | solution.py:30
  99.5 12.1 %shard_map.141 = (f32[512,512]{1,0:T(8,128)}, f32[512,512]{1,0:T(8,128)}) custom-call(s32[5]{0:T(128)} %pad_add_fusion.place_ref, f32[1,32]{1,0:T(1,128)} %bitcast.36, f32[1,32]{1,0:T(1,128)} %bitcast.40, f32[1,2048]{1,0:T(1,128)} %bitcast.42, f32[2048,128]{1,0:T(8,128)} %bitcast.26, f32[128,2048]{1,0:T(8,128)} %get-tuple-element.64.refs_0_, ...), custom_call_target="tpu_custom_call" | custom-call | flops 2684354560 | bytes 16130324 | tf_op jit(solution)/shard_map/pallas_call | solution.py:30
  111.6 8.4 %collective-permute-start.7 = (f32[512,512]{1,0:T(8,128)}, f32[512,512]{1,0:T(8,128)S(1)}, u32[]{:S(2)}, u32[]{:S(2)}) collective-permute-start(f32[512,512]{1,0:T(8,128)} %get-tuple-element.70), channel_id=1, source_target_pairs={{0,1},{1,0},{2,3},{3,2},{4,5},{5,4},{6,7},{7,6},{8,9},{9,8},{10,11... | collective-permute-start | bytes 3145736 | tf_op jit(solution)/shard_map/ppermute | solution.py:523
  120.1 2.5 %collective-permute-done.7 = f32[512,512]{1,0:T(8,128)S(1)} collective-permute-done((f32[512,512]{1,0:T(8,128)}, f32[512,512]{1,0:T(8,128)S(1)}, u32[]{:S(2)}, u32[]{:S(2)}) %collective-permute-start.7) | collective-permute-done | bytes 1048608 | tf_op jit(solution)/shard_map/ppermute | solution.py:523
  122.5 1.4 add_convert_fusion
  124.0 14.6 %all_to_all.29 = bf16[16,32,512]{2,1,0:T(8,128)(2,1)S(1)} all-to-all(bf16[16,32,512]{2,1,0:T(8,128)(2,1)S(1)} %bitcast.27), channel_id=1, replica_groups=mesh['yh'=2,'z'=8,'x'=4,'yl'=2,'core'=2] {'x','yl','core'}, dimensions={0} | all-to-all | bytes 1048576 | tf_op jit(solution)/shard_map/all_to_all | solution.py:524
  139.2 1.3 collective-permute-start.8
  140.5 5.5 %collective-permute-done.8 = bf16[32,4096]{1,0:T(8,128)(2,1)S(1)} collective-permute-done((bf16[32,4096]{1,0:T(8,128)(2,1)S(1)}, bf16[32,4096]{1,0:T(8,128)(2,1)S(1)}, u32[]{:S(2)}, u32[]{:S(2)}) %collective-permute-start.8) | collective-permute-done | bytes 262176 | tf_op jit(solution)/shard_map/ppermute | solution.py:535
  146.1 2.1 %collective-permute-start.9 = (bf16[2,32,4096]{2,1,0:T(8,128)(2,1)S(1)}, bf16[2,32,4096]{2,1,0:T(8,128)(2,1)S(1)}, u32[]{:S(2)}, u32[]{:S(2)}) collective-permute-start(bf16[2,32,4096]{2,1,0:T(8,128)(2,1)S(1)} %pad_maximum_fusion.2), channel_id=1, source_target_pairs={{0,1},{1,0},{2,3},{3,2},{4,5},{5,4},{6,7},{7,6},{8,9},{9,8},{10,11... | collective-permute-start | bytes 1572872 | tf_op jit(solution)/shard_map/ppermute | solution.py:537
  148.2 1.5 collective-permute-done.9
  (49 shorter events, 8.5 us)
Async XLA Ops:
  6.5 52.1 %copy-start = (f32[32,64,128]{2,1,0:T(8,128)S(1)}, f32[32,64,128]{2,1,0:T(8,128)}, u32[]{:S(2)}) copy-start(f32[32,64,128]{2,1,0:T(8,128)} %param.23) | copy-start | bytes 3145732
  10.1 5.0 %copy-start.7 = (bf16[2048,64]{0,1:T(8,128)(2,1)S(1)}, bf16[2048,64]{0,1:T(8,128)(2,1)}, u32[]{:S(2)}) copy-start(bf16[2048,64]{0,1:T(8,128)(2,1)} %param.24) | copy-start | bytes 786436
  10.1 18.4 %all-to-all-start = ((f32[4,520,128]{2,1,0:T(8,128)}), f32[4,520,128]{2,1,0:T(8,128)S(1)}, u32[]{:S(2)}, u32[]{:S(2)}) async-start(f32[4,520,128]{2,1,0:T(8,128)} %get-tuple-element.38), calls=%async_computation | async-start | bytes 2129920 | tf_op jit(solution)/shard_map/all_to_all | solution.py:417
  15.1 83.7 %all-gather.2.cloned.1.call-start = ((), (), s32[]{:S(2)}) async-start(), calls=%async_computation.5 | async-start | bytes 4718592 | tf_op jit(solution)/shard_map/all_gather | solution.py:420
  15.1 7.7 %collective-permute-start = (bf16[64,2048]{1,0:T(8,128)(2,1)S(1)}, bf16[64,2048]{1,0:T(8,128)(2,1)S(1)}, u32[]{:S(2)}, u32[]{:S(2)}) collective-permute-start(bf16[64,2048]{1,0:T(8,128)(2,1)S(1)} %bitcast.31), channel_id=1, source_target_pairs={{0,128},{128,0},{1,129},{129,1},{2,130},{130,2},{3,131},{131,3},{4... | collective-permute-start | bytes 786440 | tf_op jit(solution)/shard_map/ppermute | solution.py:402
  29.4 12.9 %copy-start.3 = (bf16[64,4480]{1,0:T(8,128)(2,1)S(1)}, bf16[64,4480]{1,0:T(8,128)(2,1)}, u32[]{:S(2)}) copy-start(bf16[64,4480]{1,0:T(8,128)(2,1)} %get-tuple-element.53.top_hbm.refs_0_.refs_4_) | copy-start | bytes 1720324
  29.4 15.6 %copy-start.8 = (f32[32]{0:T(128)S(1)}, f32[32]{0:T(128)}, u32[]{:S(2)}) copy-start(f32[32]{0:T(128)} %param.21) | copy-start | bytes 388
  29.4 16.4 %copy-start.9 = (s32[4]{0:T(128)S(1)}, s32[4]{0:T(128)}, u32[]{:S(2)}) copy-start(s32[4]{0:T(128)} %constant.86.clone) | copy-start | bytes 52
  30.2 21.5 %copy-start.4 = (bf16[64,4480]{1,0:T(8,128)(2,1)S(1)}, bf16[64,4480]{1,0:T(8,128)(2,1)}, u32[]{:S(2)}) copy-start(bf16[64,4480]{1,0:T(8,128)(2,1)} %get-tuple-element.53.top_hbm.refs_0_.refs_4_) | copy-start | bytes 1720324
  30.2 25.7 %all-to-all-start.1 = ((f32[16,40,128]{2,1,0:T(8,128)}), f32[16,40,128]{2,1,0:T(8,128)S(1)}, u32[]{:S(2)}, u32[]{:S(2)}) async-start(f32[16,40,128]{2,1,0:T(8,128)} %shard_map.138), calls=%async_computation.1 | async-start | bytes 655360 | tf_op jit(solution)/shard_map/all_to_all | solution.py:453
  42.2 13.7 %collective-permute-start.1 = (bf16[64,4480]{1,0:T(8,128)(2,1)S(1)}, bf16[64,4480]{1,0:T(8,128)(2,1)}, u32[]{:S(2)}, u32[]{:S(2)}) collective-permute-start(bf16[64,4480]{1,0:T(8,128)(2,1)S(1)} %copy-done.3), channel_id=1, source_target_pairs={{0,4},{4,8},{8,12},{12,0},{1,5},{5,9},{9,13},{13,1},{2,6},{6,10},{... | collective-permute-start | bytes 1720328 | tf_op jit(solution)/shard_map/ppermute | solution.py:424
  42.6 13.4 %collective-permute-start.2 = (bf16[64,4480]{1,0:T(8,128)(2,1)}, bf16[64,4480]{1,0:T(8,128)(2,1)}, u32[]{:S(2)}, u32[]{:S(2)}) collective-permute-start(bf16[64,4480]{1,0:T(8,128)(2,1)} %get-tuple-element.52.bottom_hbm.refs_1_.refs_5_), channel_id=1, source_target_pairs={{0,12},{4,0},{8,4},{12,8},{1,13},{5,1},{9,5},{13,9},{2,14},{6,2},{... | collective-permute-start | bytes 1720328 | tf_op jit(solution)/shard_map/ppermute | solution.py:425
  51.6 16.7 %collective-permute-start.3 = (bf16[64,4480]{1,0:T(8,128)(2,1)}, bf16[64,4480]{1,0:T(8,128)(2,1)}, u32[]{:S(2)}, u32[]{:S(2)}) collective-permute-start(bf16[64,4480]{1,0:T(8,128)(2,1)} %get-tuple-element.52.bottom_hbm.refs_1_.refs_5_), channel_id=1, source_target_pairs={{0,4},{4,8},{8,12},{12,0},{1,5},{5,9},{9,13},{13,1},{2,6},{6,10},{... | collective-permute-start | bytes 1720328 | tf_op jit(solution)/shard_map/ppermute | solution.py:455
  51.7 16.6 %collective-permute-start.4 = (bf16[64,4480]{1,0:T(8,128)(2,1)S(1)}, bf16[64,4480]{1,0:T(8,128)(2,1)}, u32[]{:S(2)}, u32[]{:S(2)}) collective-permute-start(bf16[64,4480]{1,0:T(8,128)(2,1)S(1)} %copy-done.4), channel_id=1, source_target_pairs={{0,12},{4,0},{8,4},{12,8},{1,13},{5,1},{9,5},{13,9},{2,14},{6,2},{... | collective-permute-start | bytes 1720328 | tf_op jit(solution)/shard_map/ppermute | solution.py:456
  55.9 24.8 %collective-permute-start.5 = (bf16[64,4480]{1,0:T(8,128)(2,1)}, bf16[64,4480]{1,0:T(8,128)(2,1)S(1)}, u32[]{:S(2)}, u32[]{:S(2)}) collective-permute-start(bf16[64,4480]{1,0:T(8,128)(2,1)} %collective-permute-done.1.refs_2_.refs_6_), channel_id=1, source_target_pairs={{0,4},{4,8},{8,12},{12,0},{1,5},{5,9},{9,13},{13,1},{2,6},{6,10},{... | collective-permute-start | bytes 1720328 | tf_op jit(solution)/shard_map/ppermute | solution.py:461
  55.9 24.8 %collective-permute-start.6 = (bf16[64,4480]{1,0:T(8,128)(2,1)}, bf16[64,4480]{1,0:T(8,128)(2,1)}, u32[]{:S(2)}, u32[]{:S(2)}) collective-permute-start(bf16[64,4480]{1,0:T(8,128)(2,1)} %collective-permute-done.2.refs_5_.refs_9_), channel_id=1, source_target_pairs={{0,12},{4,0},{8,4},{12,8},{1,13},{5,1},{9,5},{13,9},{2,14},{6,2},{... | collective-permute-start | bytes 1720328 | tf_op jit(solution)/shard_map/ppermute | solution.py:461
  59.5 21.2 %all-to-all-start.2 = ((f32[16,32,128]{2,1,0:T(8,128)}), f32[16,32,128]{2,1,0:T(8,128)S(1)}, u32[]{:S(2)}, u32[]{:S(2)}) async-start(f32[16,32,128]{2,1,0:T(8,128)} %shard_map.139), calls=%async_computation.2 | async-start | bytes 524288 | tf_op jit(solution)/shard_map/all_to_all | solution.py:475
  80.8 1.2 copy-start.6
  81.9 16.6 %all-to-all-start.3 = ((f32[4,512,128]{2,1,0:T(8,128)}), f32[4,512,128]{2,1,0:T(8,128)S(1)}, u32[]{:S(2)}, u32[]{:S(2)}) async-start(f32[4,512,128]{2,1,0:T(8,128)} %broadcast_in_dim.12), calls=%async_computation.3 | async-start | bytes 2097152 | tf_op jit(solution)/shard_map/all_to_all | solution.py:477
  111.6 10.9 %collective-permute-start.7 = (f32[512,512]{1,0:T(8,128)}, f32[512,512]{1,0:T(8,128)S(1)}, u32[]{:S(2)}, u32[]{:S(2)}) collective-permute-start(f32[512,512]{1,0:T(8,128)} %get-tuple-element.70), channel_id=1, source_target_pairs={{0,1},{1,0},{2,3},{3,2},{4,5},{5,4},{6,7},{7,6},{8,9},{9,8},{10,11... | collective-permute-start | bytes 3145736 | tf_op jit(solution)/shard_map/ppermute | solution.py:523
  123.9 14.7 %copy-start.1 = (bf16[32,4096]{1,0:T(8,128)(2,1)S(1)}, bf16[32,4096]{1,0:T(8,128)(2,1)}, u32[]{:S(2)}) copy-start(bf16[32,4096]{1,0:T(8,128)(2,1)} %residual_ref.1) | copy-start | bytes 786436
  123.9 14.6 %copy-start.2 = (f32[4096]{0:T(1024)S(1)}, f32[4096]{0:T(1024)}, u32[]{:S(2)}) copy-start(f32[4096]{0:T(1024)} %param.26) | copy-start | bytes 49156
  139.2 6.8 %collective-permute-start.8 = (bf16[32,4096]{1,0:T(8,128)(2,1)S(1)}, bf16[32,4096]{1,0:T(8,128)(2,1)S(1)}, u32[]{:S(2)}, u32[]{:S(2)}) collective-permute-start(bf16[32,4096]{1,0:T(8,128)(2,1)S(1)} %shard_map.142), channel_id=1, source_target_pairs={{0,2},{2,0},{1,3},{3,1},{4,6},{6,4},{5,7},{7,5},{8,10},{10,8},{9,1... | collective-permute-start | bytes 786440 | tf_op jit(solution)/shard_map/ppermute | solution.py:535
  146.1 3.6 %collective-permute-start.9 = (bf16[2,32,4096]{2,1,0:T(8,128)(2,1)S(1)}, bf16[2,32,4096]{2,1,0:T(8,128)(2,1)S(1)}, u32[]{:S(2)}, u32[]{:S(2)}) collective-permute-start(bf16[2,32,4096]{2,1,0:T(8,128)(2,1)S(1)} %pad_maximum_fusion.2), channel_id=1, source_target_pairs={{0,1},{1,0},{2,3},{3,2},{4,5},{5,4},{6,7},{7,6},{8,9},{9,8},{10,11... | collective-permute-start | bytes 1572872 | tf_op jit(solution)/shard_map/ppermute | solution.py:537
  (1 other events, 1.0 us)
Sparse Core Ops, SparseCore 0:
  29.5 69.2 all-gather.1

commit v8 on v7

--- a/solution.py
+++ b/solution.py
@@ -21,7 +21,7 @@
 VMEM_MOST = 61 * 2**20
 
 
-def call(kernel, outs, *, scratch=(), flops=0, smem=0, vmem=0, hbm_outs=0, args=()):
+def call(kernel, outs, *, scratch=(), flops=0, smem=0, vmem=0, hbm_outs=0, limit=VMEM_MOST, args=()):
     specs = [pl.BlockSpec(memory_space=pltpu.SMEM)] * smem
     specs += [pl.BlockSpec(memory_space=pltpu.VMEM)] * vmem
     specs += [pl.BlockSpec(memory_space=pltpu.HBM)] * (len(args) - smem - vmem)
@@ -34,7 +34,7 @@
         out_specs=[pl.BlockSpec(memory_space=m) for m in places],
         scratch_shapes=scratch,
         compiler_params=pltpu.CompilerParams(
-            vmem_limit_bytes=VMEM_MOST if len(args) > smem + vmem else VMEM_LIMIT
+            vmem_limit_bytes=limit if len(args) > smem + vmem else VMEM_LIMIT
         ),
         cost_estimate=pl.CostEstimate(flops=flops, bytes_accessed=moved, transcendentals=0),
     )(*args)
@@ -221,36 +221,32 @@
         copy.wait()
 
 
-def fold_kernel(n, place_ref, bias_ref, decay_ref, skip_ref, state_hbm, own_hbm, *refs):
+def fold_kernel(n, place_ref, bias_ref, decay_ref, skip_ref, *refs):
+    last = n - 1
+    states, given, refs = refs[:last], refs[last : 2 * last], refs[2 * last :]
     blocks, out = refs[: 2 * n], refs[2 * n : 3 * n]
     x_ref, enter_ref, logs_ref, mixed_ref, coefs_ref, gets, puts = refs[3 * n :]
     inner, heads = mixed_ref.shape[2], bias_ref.shape[1]
     pairs = inner // SPAN
-    coefs_in, x_in = [], []
-    for i in range(n):
-        pieces = blocks[2 * i : 2 * i + 2]
-        coefs_in.append(copies(halves(pieces, slice(2 * inner, None), coefs_ref.at[i]), gets, 2 * i))
-        if i:
-            x_in.append(copies(halves(pieces, slice(0, inner), x_ref.at[i - 1]), gets, 2 * (n + i)))
-    own_in = copies([(state_hbm, enter_ref.at[place_ref[0]]), (own_hbm, mixed_ref.at[0])], gets, 2 * n)
-    for i in range(n):
+    coefs_in = [
+        copies(halves(blocks[2 * i : 2 * i + 2], slice(2 * inner, None), coefs_ref.at[i]), gets, 2 * i)
+        for i in reversed(range(n))
+    ][::-1]
+    x_in = copies(halves(blocks[2 * last :], slice(0, inner), x_ref), gets, 2 * n)
+    state_in = copies([(states[i], enter_ref.at[place_ref[i]]) for i in range(last)], gets, 2 * n + 2)
+    mixed_in = copies([(given[i], mixed_ref.at[i]) for i in range(last)], gets, 3 * n + 2)
+    for i in reversed(range(n)):
         for copy in coefs_in[i]:
             copy.wait()
         place = place_ref[i]
-        if i:
+        if i == last:
+            state_ref = enter_ref.at[place]
             logs_ref[place] = local_block(
-                x_ref.at[i - 1],
-                coefs_ref.at[i],
-                bias_ref,
-                decay_ref,
-                skip_ref,
-                mixed_ref.at[i],
-                enter_ref.at[place],
-                [x_in[i - 1]],
+                x_ref, coefs_ref.at[i], bias_ref, decay_ref, skip_ref, mixed_ref.at[i], state_ref, [x_in]
             )
         else:
             logs_ref[place] = steps_of(coefs_ref[i, :heads, 2 * SPAN :], bias_ref[...], decay_ref[...])[1]
-    for copy in own_in:
+    for copy in state_in:
         copy.wait()
     for pair in range(pairs):
         lanes = slice(pair * SPAN, (pair + 1) * SPAN)
@@ -262,6 +258,8 @@
     low = first_lanes((SPAN, SPAN))
     out_copies = []
     for i in range(n):
+        if i < last:
+            mixed_in[i].wait()
         place = place_ref[i]
         cumulative = jnp.transpose(logs_ref[place])
         c = coefs_ref[i, :, SPAN : 2 * SPAN]
@@ -426,22 +424,23 @@
     place = (at_x + jnp.array([0, n_x - 1, 1, 2], jnp.int32)) % n_x
     place = jnp.concatenate([place, lax.axis_index("core").astype(jnp.int32).reshape(1)])
 
-    own_local = call(
-        local_kernel,
-        [values, jax.ShapeDtypeStruct((inner, SPAN), F32)],
-        scratch=[
-            pltpu.VMEM((tokens, inner), BF16),
-            pltpu.VMEM((tokens, 3 * SPAN), BF16),
-            pltpu.VMEM((tokens, inner), F32),
-            pltpu.VMEM((inner, SPAN), F32),
-            pltpu.SemaphoreType.DMA((10,)),
-            pltpu.SemaphoreType.DMA((8,)),
-        ],
-        flops=10**6,
-        vmem=3,
-        hbm_outs=2,
-        args=(bias, decay, skip, *own),
-    )
+    def local(block):
+        return call(
+            local_kernel,
+            [values, jax.ShapeDtypeStruct((inner, SPAN), F32)],
+            scratch=[
+                pltpu.VMEM((tokens, inner), BF16),
+                pltpu.VMEM((tokens, 3 * SPAN), BF16),
+                pltpu.VMEM((tokens, inner), F32),
+                pltpu.VMEM((inner, SPAN), F32),
+                pltpu.SemaphoreType.DMA((10,)),
+                pltpu.SemaphoreType.DMA((8,)),
+            ],
+            flops=10**6,
+            vmem=3,
+            hbm_outs=2,
+            args=(bias, decay, skip, *block),
+        )
 
     (grouped,) = call(
         group_kernel,
@@ -451,14 +450,13 @@
         args=(parts,),
     )
     parts = lax.all_to_all(grouped, GROUPS, 0, 0, tiled=True)
-    own_local, top_later, bottom_later = lax.optimization_barrier((own_local, top, bottom))
+    own_local, top_later, bottom_later = lax.optimization_barrier((local(own), top, bottom))
     left_bottom = lax.ppermute(bottom_later, "x", ring(n_x, 1))
     right_top = lax.ppermute(top_later, "x", ring(n_x, -1))
-    (mixed, fresh), parts, left_top, right_bottom, place = lax.optimization_barrier(
+    own_local, parts, left_top, right_bottom, place = lax.optimization_barrier(
         (own_local, parts, left_top, right_bottom, place)
     )
     left, right = (left_top, left_bottom), (right_top, right_bottom)
-    far = (lax.ppermute(left_top, "x", ring(n_x, 1)), lax.ppermute(right_bottom, "x", ring(n_x, -1)))
     mine = lax.axis_index(GROUPS)
     each = STATE // size
     carry = lax.dynamic_index_in_dim(
@@ -472,8 +470,11 @@
         vmem=2,
         args=(parts, carry),
     )
+    entering, onward, back = lax.optimization_barrier((entering, left_top, right_bottom))
+    far = (lax.ppermute(onward, "x", ring(n_x, 1)), lax.ppermute(back, "x", ring(n_x, -1)))
     entering = lax.all_to_all(entering, GROUPS, 0, 0, tiled=True).reshape(1, quarter, SPAN)
-    entering, left, right, far = lax.optimization_barrier((entering, left, right, far))
+    entering, left_local, right_local, far = lax.optimization_barrier((entering, local(left), local(right), far))
+    mixed, fresh = zip(own_local, left_local, right_local)
     entering = lax.all_to_all(jnp.broadcast_to(entering, (n_x, quarter, SPAN)), "x", 0, 0, tiled=True)
 
     blocks = (*own, *left, *right, *far)
@@ -481,19 +482,19 @@
         functools.partial(fold_kernel, n_x),
         [values] * n_x,
         scratch=[
-            pltpu.VMEM((n_x - 1, tokens, inner), BF16),
+            pltpu.VMEM((tokens, inner), BF16),
             pltpu.VMEM((n_x, inner, SPAN), F32),
             pltpu.VMEM((n_x, heads, SPAN), F32),
             pltpu.VMEM((n_x, tokens, inner), F32),
             pltpu.VMEM((n_x, tokens, 3 * SPAN), BF16),
-            pltpu.SemaphoreType.DMA((4 * n_x,)),
+            pltpu.SemaphoreType.DMA((4 * n_x + 2,)),
             pltpu.SemaphoreType.DMA((n_x,)),
         ],
         flops=2 * n_x * tokens * inner * STATE * 2,
         smem=1,
         vmem=3,
         hbm_outs=n_x,
-        args=(place, bias, decay, skip, fresh, mixed, *blocks),
+        args=(place, bias, decay, skip, *fresh, *mixed, *blocks),
     )
     kept, sent = call(
         functools.partial(mix_kernel, n_x),
@@ -509,6 +510,7 @@
         flops=2 * n_x * tokens * inner * (STATE * 2 + weight.shape[0]),
         smem=1,
         vmem=4,
+        limit=52 * 2**20,
         args=(
             place,
             bias,

time: 159 us -> 159 us (level)
  Pallas kernels: 36 us -> 43.9 us
  waiting for transfers between devices: 34.2 us -> 28.2 us
  starting transfers between devices: 52.4 us -> 49.3 us
  local copies, waits for them, and re-layouts: 2.94 us -> 4.91 us
    all_to_all x1, waiting for transfers between devices: 12.4 us -> 1.8 us  [on_device(): lax.all_to_all(entering, GROUPS, 0, 0, tiled=True).reshape(1, quarter, SPAN)]
    pallas_call x7 -> x9, Pallas kernels: 36 us -> 43.9 us  [call(): pl.pallas_call(kernel, out_shape=list(outs), in_specs=specs, out_specs=[p...]
    ppermute x1, starting transfers between devices: 2.65 us -> 0.08 us  [on_device(): right_top = lax.ppermute(top_later, 'x', ring(n_x, -1))]
    all_to_all x1, starting transfers between devices: 8.78 us -> 6.68 us  [on_device(): lax.all_to_all(entering, GROUPS, 0, 0, tiled=True).reshape(1, quarter, SPAN)]
    all_to_all x1, waiting for transfers between devices: 0.01 us -> 2.07 us  [on_device(): parts = lax.all_to_all(grouped, GROUPS, 0, 0, tiled=True)]
    unnamed x21 -> x39, local copies, waits for them, and re-layouts: 0.89 us -> 2.92 us
  transfers between devices with their start and end apart: 15 -> 15, of which waited for: 8 -> 10; matrix products, arithmetic and copies ran while one was open for 2% -> 2% of each run, Pallas kernels for 13% -> 18%
where the time goes in v8:
time: 159 us; the launch traced here: 158 us
  starting transfers between devices  49.3 us (31%)
  Pallas kernels  43.9 us (28%)
  waiting for transfers between devices  28.2 us (18%)
  between operations  13.7 us (9%)
  blocking collectives  13.6 us (9%)
  local copies, waits for them, and re-layouts  4.91 us (3%)
  other arithmetic  4.23 us (3%)
    pallas_call x9, Pallas kernels, call(): pl.pallas_call(kernel, out_shape=list(outs), in_specs=specs, out_specs=[p...  43.9 us
    all_to_all x1, blocking collectives, on_device(): partial = lax.all_to_all(partial, ('x', *TENSOR), 0, 0, tiled=True)  13.6 us
    all_to_all x1, starting transfers between devices, on_device(): parts = lax.all_to_all(grouped, GROUPS, 0, 0, tiled=True)  12 us
    ppermute x1, starting transfers between devices, on_device(): partial = (kept + lax.ppermute(sent, 'core', ring(2, 1))).astype(BF16)  7.98 us
    all_to_all x1, starting transfers between devices, on_device(): lax.all_to_all(entering, GROUPS, 0, 0, tiled=True).reshape(1, quarter, SPAN)  6.68 us
    all_to_all x1, waiting for transfers between devices, on_device(): parts = lax.all_to_all(states, 'x', 0, 0, tiled=True)  5.75 us
    ppermute x1, waiting for transfers between devices, on_device(): across = lax.ppermute(done, 'yl', ring(2, 1))  5.5 us
    all_to_all x1, starting transfers between devices, on_device(): parts = lax.all_to_all(states, 'x', 0, 0, tiled=True)  4.99 us
  transfers between devices with their start and end apart: 15, of which 10 were waited for; matrix products, arithmetic and copies ran while one was open for 2% of the time, Pallas kernels for 18%

profile of v8, /device:TPU:1, one launch (start us, length us, event | category | flops | bytes accessed | tf_op | source)
XLA Modules:
  0.0 157.9 jit_solution(17672307237784170023)
XLA Ops:
  6.5 3.6 %shard_map.136 = (f32[4,520,128]{2,1,0:T(8,128)}, bf16[64,4480]{1,0:T(8,128)(2,1)}, bf16[64,4480]{1,0:T(8,128)(2,1)}) custom-call(bf16[128,2048]{1,0:T(8,128)(2,1)} %x_hbm.1, bf16[128,2048]{1,0:T(8,128)(2,1)} %gate_hbm.1, bf16[128,128]{1,0:T(8,128)(2,1)} %b_hbm.1, bf16[128,128]{1,0:T(8,128)(2,1)} %c_hbm.1, bf16[32,128]{1,0:T(8,128)(2,1)} %bitcast.45, ...), custom_call_target="tpu_custom_call" | custom-call | flops 134217728 | bytes 3334400 | tf_op jit(solution)/shard_map/pallas_call | solution.py:30
  10.1 5.0 %all-to-all-start = ((f32[4,520,128]{2,1,0:T(8,128)}), f32[4,520,128]{2,1,0:T(8,128)S(1)}, u32[]{:S(2)}, u32[]{:S(2)}) async-start(f32[4,520,128]{2,1,0:T(8,128)} %get-tuple-element.45), calls=%async_computation | async-start | bytes 2129920 | tf_op jit(solution)/shard_map/all_to_all | solution.py:415
  15.1 3.0 %collective-permute-start = (bf16[64,2048]{1,0:T(8,128)(2,1)S(1)}, bf16[64,2048]{1,0:T(8,128)(2,1)S(1)}, u32[]{:S(2)}, u32[]{:S(2)}) collective-permute-start(bf16[64,2048]{1,0:T(8,128)(2,1)S(1)} %bitcast.43), channel_id=1, source_target_pairs={{0,128},{128,0},{1,129},{129,1},{2,130},{130,2},{3,131},{131,3},{4... | collective-permute-start | bytes 786440 | tf_op jit(solution)/shard_map/ppermute | solution.py:400
  18.1 4.7 %collective-permute-done = bf16[64,2048]{1,0:T(8,128)(2,1)S(1)} collective-permute-done((bf16[64,2048]{1,0:T(8,128)(2,1)S(1)}, bf16[64,2048]{1,0:T(8,128)(2,1)S(1)}, u32[]{:S(2)}, u32[]{:S(2)}) %collective-permute-start) | collective-permute-done | bytes 262176 | tf_op jit(solution)/shard_map/ppermute | solution.py:400
  22.8 5.8 %all-to-all-done.parts_ref = f32[4,520,128]{2,1,0:T(8,128)S(1)} async-done(((f32[4,520,128]{2,1,0:T(8,128)}), f32[4,520,128]{2,1,0:T(8,128)S(1)}, u32[]{:S(2)}, u32[]{:S(2)}) %all-to-all-start) | async-done | bytes 1064992 | tf_op jit(solution)/shard_map/all_to_all | solution.py:415
  32.8 12.0 %all-to-all-start.1 = ((f32[16,40,128]{2,1,0:T(8,128)}), f32[16,40,128]{2,1,0:T(8,128)}, u32[]{:S(2)}, u32[]{:S(2)}) async-start(f32[16,40,128]{2,1,0:T(8,128)} %shard_map.138), calls=%async_computation.1 | async-start | bytes 655360 | tf_op jit(solution)/shard_map/all_to_all | solution.py:452
  45.2 2.4 %collective-permute-start.2 = (bf16[64,4480]{1,0:T(8,128)(2,1)S(1)}, bf16[64,4480]{1,0:T(8,128)(2,1)}, u32[]{:S(2)}, u32[]{:S(2)}) collective-permute-start(bf16[64,4480]{1,0:T(8,128)(2,1)S(1)} %copy-done.4), channel_id=1, source_target_pairs={{0,12},{4,0},{8,4},{12,8},{1,13},{5,1},{9,5},{13,9},{2,14},{6,2},{... | collective-permute-start | bytes 1720328 | tf_op jit(solution)/shard_map/ppermute | solution.py:423
  49.2 5.3 %shard_map.137 = (f32[128,2048]{1,0:T(8,128)}, f32[2048,128]{1,0:T(8,128)}) custom-call(f32[1,32]{1,0:T(1,128)} %bitcast.26, f32[1,32]{1,0:T(1,128)} %bitcast.32, f32[1,2048]{1,0:T(1,128)} %reshape_reshape.3.skip_ref, bf16[64,4480]{1,0:T(8,128)(2,1)} %get-tuple-element.64.top_hbm.refs_6_.refs_4_, bf16[64,4480]{1,0:T(8,128)(2,1)} %get-tuple-element.61.bottom_hbm.refs_7_.refs_5_), custom_call_target="tpu_custom_call" | custom-call | flops 1000000 | bytes 3252480 | tf_op jit(solution)/shard_map/pallas_call | solution.py:30
  56.1 2.5 %collective-permute-done.1.top_hbm.refs_8_.refs_6_ = bf16[64,4480]{1,0:T(8,128)(2,1)} collective-permute-done((bf16[64,4480]{1,0:T(8,128)(2,1)S(1)}, bf16[64,4480]{1,0:T(8,128)(2,1)}, u32[]{:S(2)}, u32[]{:S(2)}) %collective-permute-start.1) | collective-permute-done | bytes 573472 | tf_op jit(solution)/shard_map/ppermute | solution.py:422
  58.6 2.1 %all-to-all-done.1.parts_ref = f32[16,40,128]{2,1,0:T(8,128)} async-done(((f32[16,40,128]{2,1,0:T(8,128)}), f32[16,40,128]{2,1,0:T(8,128)}, u32[]{:S(2)}, u32[]{:S(2)}) %all-to-all-start.1) | async-done | bytes 327712 | tf_op jit(solution)/shard_map/all_to_all | solution.py:452
  62.4 2.7 %collective-permute-start.6 = (bf16[64,4480]{1,0:T(8,128)(2,1)}, bf16[64,4480]{1,0:T(8,128)(2,1)S(1)}, u32[]{:S(2)}, u32[]{:S(2)}) collective-permute-start(bf16[64,4480]{1,0:T(8,128)(2,1)} %collective-permute-done.2.bottom_hbm.refs_11_.refs_9_), channel_id=1, source_target_pairs={{0,12},{4,0},{8,4},{12,8},{1,13},{5,1},{9,5},{13,9},{2,14},{6,2},{... | collective-permute-start | bytes 1720328 | tf_op jit(solution)/shard_map/ppermute | solution.py:474
  65.1 6.7 %all-to-all-start.2 = ((f32[16,32,128]{2,1,0:T(8,128)}), f32[16,32,128]{2,1,0:T(8,128)S(1)}, u32[]{:S(2)}, u32[]{:S(2)}) async-start(f32[16,32,128]{2,1,0:T(8,128)} %shard_map.139), calls=%async_computation.2 | async-start | bytes 524288 | tf_op jit(solution)/shard_map/all_to_all | solution.py:475
  71.8 5.3 %shard_map.141 = (f32[128,2048]{1,0:T(8,128)}, f32[2048,128]{1,0:T(8,128)}) custom-call(f32[1,32]{1,0:T(1,128)} %bitcast.27, f32[1,32]{1,0:T(1,128)} %bitcast.33, f32[1,2048]{1,0:T(1,128)} %reshape_reshape.3.skip_ref, bf16[64,4480]{1,0:T(8,128)(2,1)} %collective-permute-done.4.top_hbm.refs_10_.refs_8_, ...), custom_call_target="tpu_custom_call" | custom-call | flops 1000000 | bytes 3252480 | tf_op jit(solution)/shard_map/pallas_call | solution.py:30
  77.1 5.3 %shard_map.140 = (f32[128,2048]{1,0:T(8,128)}, f32[2048,128]{1,0:T(8,128)}) custom-call(f32[1,32]{1,0:T(1,128)} %bitcast.28, f32[1,32]{1,0:T(1,128)} %bitcast.34, f32[1,2048]{1,0:T(1,128)} %reshape_reshape.3.skip_ref, bf16[64,4480]{1,0:T(8,128)(2,1)} %collective-permute-done.1.top_hbm.refs_8_.refs_6_, ...), custom_call_target="tpu_custom_call" | custom-call | flops 1000000 | bytes 3252480 | tf_op jit(solution)/shard_map/pallas_call | solution.py:30
  82.4 1.8 %all-to-all-done.2 = f32[16,32,128]{2,1,0:T(8,128)S(1)} async-done(((f32[16,32,128]{2,1,0:T(8,128)}), f32[16,32,128]{2,1,0:T(8,128)S(1)}, u32[]{:S(2)}, u32[]{:S(2)}) %all-to-all-start.2) | async-done | bytes 262176 | tf_op jit(solution)/shard_map/all_to_all | solution.py:475
  85.5 4.3 %all-to-all-start.3 = ((f32[4,512,128]{2,1,0:T(8,128)}), f32[4,512,128]{2,1,0:T(8,128)}, u32[]{:S(2)}, u32[]{:S(2)}) async-start(f32[4,512,128]{2,1,0:T(8,128)} %broadcast_in_dim.12), calls=%async_computation.3 | async-start | bytes 2097152 | tf_op jit(solution)/shard_map/all_to_all | solution.py:478
  89.9 9.7 %shard_map.142 = (f32[128,2048]{1,0:T(8,128)}, f32[128,2048]{1,0:T(8,128)}, f32[128,2048]{1,0:T(8,128)}, f32[128,2048]{1,0:T(8,128)}) custom-call(s32[5]{0:T(128)} %pad_add_fusion.place_ref, f32[1,32]{1,0:T(1,128)} %bitcast.29, f32[1,32]{1,0:T(1,128)} %bitcast.35, f32[1,2048]{1,0:T(1,128)} %reshape_reshape.3.skip_ref, ...), custom_call_target="tpu_custom_call" | custom-call | flops 536870912 | bytes 15081748 | tf_op jit(solution)/shard_map/pallas_call | solution.py:30
  99.6 1.8 %all-gather.2.cloned.1.call-done.refs_12_ = bf16[1024,2048]{1,0:T(8,128)(2,1)} async-done(((bf16[128,2048]{1,0:T(8,128)(2,1)}), bf16[1024,2048]{1,0:T(8,128)(2,1)}) %all-gather.2.cloned.1.call-update) | async-done | bytes 4194320 | tf_op jit(solution)/shard_map/all_gather | solution.py:418
  101.4 11.6 %shard_map.143 = (f32[512,512]{1,0:T(8,128)}, f32[512,512]{1,0:T(8,128)}) custom-call(s32[5]{0:T(128)S(1)} %copy-done.13, f32[1,32]{1,0:T(1,128)S(1)} %bitcast.30, f32[1,32]{1,0:T(1,128)S(1)} %bitcast.36, f32[1,2048]{1,0:T(1,128)S(1)} %bitcast.38, f32[2048,128]{1,0:T(8,128)} %bitcast.12.enter_ref, f32[128,2048]{1,0:T(8,128)} %get-tuple-element.78.refs_0_, ...), custom_call_target="tpu_custom_call" | custom-call | flops 2684354560 | bytes 16130324 | tf_op jit(solution)/shard_map/pallas_call | solution.py:30
  113.1 8.0 %collective-permute-start.7 = (f32[512,512]{1,0:T(8,128)}, f32[512,512]{1,0:T(8,128)S(1)}, u32[]{:S(2)}, u32[]{:S(2)}) collective-permute-start(f32[512,512]{1,0:T(8,128)} %get-tuple-element.84), channel_id=1, source_target_pairs={{0,1},{1,0},{2,3},{3,2},{4,5},{5,4},{6,7},{7,6},{8,9},{9,8},{10,11... | collective-permute-start | bytes 3145736 | tf_op jit(solution)/shard_map/ppermute | solution.py:525
  121.0 2.5 %collective-permute-done.7 = f32[512,512]{1,0:T(8,128)S(1)} collective-permute-done((f32[512,512]{1,0:T(8,128)}, f32[512,512]{1,0:T(8,128)S(1)}, u32[]{:S(2)}, u32[]{:S(2)}) %collective-permute-start.7) | collective-permute-done | bytes 1048608 | tf_op jit(solution)/shard_map/ppermute | solution.py:525
  124.9 13.6 %all_to_all.29 = bf16[16,32,512]{2,1,0:T(8,128)(2,1)S(1)} all-to-all(bf16[16,32,512]{2,1,0:T(8,128)(2,1)S(1)} %bitcast.39), channel_id=1, replica_groups=mesh['yh'=2,'z'=8,'x'=4,'yl'=2,'core'=2] {'x','yl','core'}, dimensions={0} | all-to-all | bytes 1048576 | tf_op jit(solution)/shard_map/all_to_all | solution.py:526
  140.5 5.5 %collective-permute-done.8 = bf16[32,4096]{1,0:T(8,128)(2,1)S(1)} collective-permute-done((bf16[32,4096]{1,0:T(8,128)(2,1)S(1)}, bf16[32,4096]{1,0:T(8,128)(2,1)S(1)}, u32[]{:S(2)}, u32[]{:S(2)}) %collective-permute-start.8) | collective-permute-done | bytes 262176 | tf_op jit(solution)/shard_map/ppermute | solution.py:537
  146.1 2.1 %collective-permute-start.9 = (bf16[2,32,4096]{2,1,0:T(8,128)(2,1)S(1)}, bf16[2,32,4096]{2,1,0:T(8,128)(2,1)S(1)}, u32[]{:S(2)}, u32[]{:S(2)}) collective-permute-start(bf16[2,32,4096]{2,1,0:T(8,128)(2,1)S(1)} %pad_maximum_fusion.2), channel_id=1, source_target_pairs={{0,1},{1,0},{2,3},{3,2},{4,5},{5,4},{6,7},{7,6},{8,9},{9,8},{10,11... | collective-permute-start | bytes 1572872 | tf_op jit(solution)/shard_map/ppermute | solution.py:539
  (69 shorter events, 17.1 us)
Async XLA Ops:
  6.5 41.8 %copy-start = (f32[32,64,128]{2,1,0:T(8,128)S(1)}, f32[32,64,128]{2,1,0:T(8,128)}, u32[]{:S(2)}) copy-start(f32[32,64,128]{2,1,0:T(8,128)} %param.23) | copy-start | bytes 3145732
  10.1 18.4 %all-to-all-start = ((f32[4,520,128]{2,1,0:T(8,128)}), f32[4,520,128]{2,1,0:T(8,128)S(1)}, u32[]{:S(2)}, u32[]{:S(2)}) async-start(f32[4,520,128]{2,1,0:T(8,128)} %get-tuple-element.45), calls=%async_computation | async-start | bytes 2129920 | tf_op jit(solution)/shard_map/all_to_all | solution.py:415
  15.1 86.3 %all-gather.2.cloned.1.call-start = ((), (), s32[]{:S(2)}) async-start(), calls=%async_computation.5 | async-start | bytes 4718592 | tf_op jit(solution)/shard_map/all_gather | solution.py:418
  15.1 7.7 %collective-permute-start = (bf16[64,2048]{1,0:T(8,128)(2,1)S(1)}, bf16[64,2048]{1,0:T(8,128)(2,1)S(1)}, u32[]{:S(2)}, u32[]{:S(2)}) collective-permute-start(bf16[64,2048]{1,0:T(8,128)(2,1)S(1)} %bitcast.43), channel_id=1, source_target_pairs={{0,128},{128,0},{1,129},{129,1},{2,130},{130,2},{3,131},{131,3},{4... | collective-permute-start | bytes 786440 | tf_op jit(solution)/shard_map/ppermute | solution.py:400
  30.4 17.2 %copy-start.17 = (f32[32]{0:T(128)S(1)}, f32[32]{0:T(128)}, u32[]{:S(2)}) copy-start(f32[32]{0:T(128)} %param.21) | copy-start | bytes 388
  30.4 14.4 %copy-start.1 = (bf16[64,4480]{1,0:T(8,128)(2,1)S(1)}, bf16[64,4480]{1,0:T(8,128)(2,1)}, u32[]{:S(2)}) copy-start(bf16[64,4480]{1,0:T(8,128)(2,1)} %get-tuple-element.64.top_hbm.refs_6_.refs_4_) | copy-start | bytes 1720324
  30.4 14.8 %copy-start.4 = (bf16[64,4480]{1,0:T(8,128)(2,1)S(1)}, bf16[64,4480]{1,0:T(8,128)(2,1)}, u32[]{:S(2)}) copy-start(bf16[64,4480]{1,0:T(8,128)(2,1)} %get-tuple-element.61.bottom_hbm.refs_7_.refs_5_) | copy-start | bytes 1720324
  32.0 16.5 %copy-start.18 = (s32[4]{0:T(128)S(1)}, s32[4]{0:T(128)}, u32[]{:S(2)}) copy-start(s32[4]{0:T(128)} %constant.86.clone) | copy-start | bytes 52
  32.8 21.7 %copy-start.2 = (bf16[64,4480]{1,0:T(8,128)(2,1)S(1)}, bf16[64,4480]{1,0:T(8,128)(2,1)}, u32[]{:S(2)}) copy-start(bf16[64,4480]{1,0:T(8,128)(2,1)} %get-tuple-element.64.top_hbm.refs_6_.refs_4_) | copy-start | bytes 1720324
  32.8 27.9 %all-to-all-start.1 = ((f32[16,40,128]{2,1,0:T(8,128)}), f32[16,40,128]{2,1,0:T(8,128)}, u32[]{:S(2)}, u32[]{:S(2)}) async-start(f32[16,40,128]{2,1,0:T(8,128)} %shard_map.138), calls=%async_computation.1 | async-start | bytes 655360 | tf_op jit(solution)/shard_map/all_to_all | solution.py:452
  44.9 13.7 %collective-permute-start.1 = (bf16[64,4480]{1,0:T(8,128)(2,1)S(1)}, bf16[64,4480]{1,0:T(8,128)(2,1)}, u32[]{:S(2)}, u32[]{:S(2)}) collective-permute-start(bf16[64,4480]{1,0:T(8,128)(2,1)S(1)} %copy-done.1), channel_id=1, source_target_pairs={{0,4},{4,8},{8,12},{12,0},{1,5},{5,9},{9,13},{13,1},{2,6},{6,10},{... | collective-permute-start | bytes 1720328 | tf_op jit(solution)/shard_map/ppermute | solution.py:422
  45.2 13.4 %collective-permute-start.2 = (bf16[64,4480]{1,0:T(8,128)(2,1)S(1)}, bf16[64,4480]{1,0:T(8,128)(2,1)}, u32[]{:S(2)}, u32[]{:S(2)}) collective-permute-start(bf16[64,4480]{1,0:T(8,128)(2,1)S(1)} %copy-done.4), channel_id=1, source_target_pairs={{0,12},{4,0},{8,4},{12,8},{1,13},{5,1},{9,5},{13,9},{2,14},{6,2},{... | collective-permute-start | bytes 1720328 | tf_op jit(solution)/shard_map/ppermute | solution.py:423
  54.5 17.2 %collective-permute-start.4 = (bf16[64,4480]{1,0:T(8,128)(2,1)S(1)}, bf16[64,4480]{1,0:T(8,128)(2,1)}, u32[]{:S(2)}, u32[]{:S(2)}) collective-permute-start(bf16[64,4480]{1,0:T(8,128)(2,1)S(1)} %copy-done.2), channel_id=1, source_target_pairs={{0,12},{4,0},{8,4},{12,8},{1,13},{5,1},{9,5},{13,9},{2,14},{6,2},{... | collective-permute-start | bytes 1720328 | tf_op jit(solution)/shard_map/ppermute | solution.py:455
  54.6 22.4 %collective-permute-start.3 = (bf16[64,4480]{1,0:T(8,128)(2,1)}, bf16[64,4480]{1,0:T(8,128)(2,1)}, u32[]{:S(2)}, u32[]{:S(2)}) collective-permute-start(bf16[64,4480]{1,0:T(8,128)(2,1)} %get-tuple-element.61.bottom_hbm.refs_7_.refs_5_), channel_id=1, source_target_pairs={{0,4},{4,8},{8,12},{12,0},{1,5},{5,9},{9,13},{13,1},{2,6},{6,10},{... | collective-permute-start | bytes 1720328 | tf_op jit(solution)/shard_map/ppermute | solution.py:454
  62.4 21.8 %collective-permute-start.5 = (bf16[64,4480]{1,0:T(8,128)(2,1)}, bf16[64,4480]{1,0:T(8,128)(2,1)S(1)}, u32[]{:S(2)}, u32[]{:S(2)}) collective-permute-start(bf16[64,4480]{1,0:T(8,128)(2,1)} %collective-permute-done.1.top_hbm.refs_8_.refs_6_), channel_id=1, source_target_pairs={{0,4},{4,8},{8,12},{12,0},{1,5},{5,9},{9,13},{13,1},{2,6},{6,10},{... | collective-permute-start | bytes 1720328 | tf_op jit(solution)/shard_map/ppermute | solution.py:474
  62.4 21.8 %collective-permute-start.6 = (bf16[64,4480]{1,0:T(8,128)(2,1)}, bf16[64,4480]{1,0:T(8,128)(2,1)S(1)}, u32[]{:S(2)}, u32[]{:S(2)}) collective-permute-start(bf16[64,4480]{1,0:T(8,128)(2,1)} %collective-permute-done.2.bottom_hbm.refs_11_.refs_9_), channel_id=1, source_target_pairs={{0,12},{4,0},{8,4},{12,8},{1,13},{5,1},{9,5},{13,9},{2,14},{6,2},{... | collective-permute-start | bytes 1720328 | tf_op jit(solution)/shard_map/ppermute | solution.py:474
  65.1 19.1 %all-to-all-start.2 = ((f32[16,32,128]{2,1,0:T(8,128)}), f32[16,32,128]{2,1,0:T(8,128)S(1)}, u32[]{:S(2)}, u32[]{:S(2)}) async-start(f32[16,32,128]{2,1,0:T(8,128)} %shard_map.139), calls=%async_computation.2 | async-start | bytes 524288 | tf_op jit(solution)/shard_map/all_to_all | solution.py:475
  85.5 14.1 %all-to-all-start.3 = ((f32[4,512,128]{2,1,0:T(8,128)}), f32[4,512,128]{2,1,0:T(8,128)}, u32[]{:S(2)}, u32[]{:S(2)}) async-start(f32[4,512,128]{2,1,0:T(8,128)} %broadcast_in_dim.12), calls=%async_computation.3 | async-start | bytes 2097152 | tf_op jit(solution)/shard_map/all_to_all | solution.py:478
  89.8 11.6 %copy-start.3 = (bf16[64,4480]{1,0:T(8,128)(2,1)S(1)}, bf16[64,4480]{1,0:T(8,128)(2,1)}, u32[]{:S(2)}) copy-start(bf16[64,4480]{1,0:T(8,128)(2,1)} %get-tuple-element.64.top_hbm.refs_6_.refs_4_) | copy-start | bytes 1720324
  113.1 10.5 %collective-permute-start.7 = (f32[512,512]{1,0:T(8,128)}, f32[512,512]{1,0:T(8,128)S(1)}, u32[]{:S(2)}, u32[]{:S(2)}) collective-permute-start(f32[512,512]{1,0:T(8,128)} %get-tuple-element.84), channel_id=1, source_target_pairs={{0,1},{1,0},{2,3},{3,2},{4,5},{5,4},{6,7},{7,6},{8,9},{9,8},{10,11... | collective-permute-start | bytes 3145736 | tf_op jit(solution)/shard_map/ppermute | solution.py:525
  124.9 13.6 %copy-start.8 = (bf16[32,4096]{1,0:T(8,128)(2,1)S(1)}, bf16[32,4096]{1,0:T(8,128)(2,1)}, u32[]{:S(2)}) copy-start(bf16[32,4096]{1,0:T(8,128)(2,1)} %residual_ref.1) | copy-start | bytes 786436
  124.9 13.6 %copy-start.11 = (f32[4096]{0:T(1024)S(1)}, f32[4096]{0:T(1024)}, u32[]{:S(2)}) copy-start(f32[4096]{0:T(1024)} %param.26) | copy-start | bytes 49156
  139.2 6.8 %collective-permute-start.8 = (bf16[32,4096]{1,0:T(8,128)(2,1)S(1)}, bf16[32,4096]{1,0:T(8,128)(2,1)S(1)}, u32[]{:S(2)}, u32[]{:S(2)}) collective-permute-start(bf16[32,4096]{1,0:T(8,128)(2,1)S(1)} %shard_map.144), channel_id=1, source_target_pairs={{0,2},{2,0},{1,3},{3,1},{4,6},{6,4},{5,7},{7,5},{8,10},{10,8},{9,1... | collective-permute-start | bytes 786440 | tf_op jit(solution)/shard_map/ppermute | solution.py:537
  146.1 3.6 %collective-permute-start.9 = (bf16[2,32,4096]{2,1,0:T(8,128)(2,1)S(1)}, bf16[2,32,4096]{2,1,0:T(8,128)(2,1)S(1)}, u32[]{:S(2)}, u32[]{:S(2)}) collective-permute-start(bf16[2,32,4096]{2,1,0:T(8,128)(2,1)S(1)} %pad_maximum_fusion.2), channel_id=1, source_target_pairs={{0,1},{1,0},{2,3},{3,2},{4,5},{5,4},{6,7},{7,6},{8,9},{9,8},{10,11... | collective-permute-start | bytes 1572872 | tf_op jit(solution)/shard_map/ppermute | solution.py:539
  (10 other events, 67.9 us)
Sparse Core Ops, SparseCore 0:
  30.5 70.7 all-gather.1

commit v9 on v8

--- a/solution.py
+++ b/solution.py
@@ -276,7 +276,7 @@
 
 def mix_kernel(n, place_ref, bias_ref, decay_ref, gain_ref, enter_ref, *refs):
     mixed, blocks, weight_hbm = refs[:n], refs[n : 3 * n], refs[3 * n]
-    kept_ref, sent_ref, logs_ref, mixed_ref, block_ref, normed_ref, weight_ref, semaphores = refs[3 * n + 1 :]
+    kept_ref, sent_ref, logs_ref, mixed_ref, block_ref, normed_ref, weight_ref, enter_two, semaphores = refs[3 * n + 1 :]
     inner, heads = mixed_ref.shape[2], bias_ref.shape[1]
     pairs = inner // SPAN
     block_in, mixed_in = [], []
@@ -291,6 +291,9 @@
             copy.wait()
         raw_t = block_ref[i, :heads, inner + 2 * SPAN :]
         logs_ref[place_ref[i]] = steps_of(raw_t, bias_ref[...], decay_ref[...])[1]
+    for pair in range(pairs):
+        parts = split(enter_ref[pair * SPAN : (pair + 1) * SPAN, :])
+        enter_two[2 * pair * SPAN : 2 * (pair + 1) * SPAN, :] = jnp.concatenate(parts, axis=0)
     before = jnp.zeros((heads, 1), F32)
     for p in range(n):
         here = logs_ref[p]
@@ -307,7 +310,7 @@
         for pair in range(pairs):
             lanes = slice(pair * SPAN, (pair + 1) * SPAN)
             at = jnp.where(low, column(cumulative, 2 * pair), column(cumulative, 2 * pair + 1))
-            carried = dot(c_twice, jnp.concatenate(split(enter_ref[lanes, :]), axis=0))
+            carried = dot(c_twice, enter_two[2 * pair * SPAN : 2 * (pair + 1) * SPAN, :])
             mixer_out = mixed_ref[i, :, lanes] + carried * jnp.exp(at)
             gate = block_ref[i, :, lanes].astype(F32)
             gated = mixer_out * (gate / (1.0 + jnp.exp(-gate)))
@@ -505,12 +508,13 @@
             pltpu.VMEM((n_x, tokens, packed - inner), BF16),
             pltpu.VMEM((n_x * tokens, inner), BF16),
             pltpu.VMEM(weight.shape, BF16),
+            pltpu.VMEM((2 * inner, SPAN), BF16),
             pltpu.SemaphoreType.DMA((3 * n_x + 1,)),
         ],
         flops=2 * n_x * tokens * inner * (STATE * 2 + weight.shape[0]),
         smem=1,
         vmem=4,
-        limit=52 * 2**20,
+        limit=57 * 2**20,
         args=(
             place,
             bias,

time: 159 us -> 155 us (0.975)
  local copies, waits for them, and re-layouts: 4.91 us -> 2.13 us
    unnamed x39 -> x21, local copies, waits for them, and re-layouts: 2.92 us -> 0.13 us
    all_to_all x1, starting transfers between devices: 6.68 us -> 8.79 us  [on_device(): lax.all_to_all(entering, GROUPS, 0, 0, tiled=True).reshape(1, quarter, SPAN)]
    all_to_all x1, waiting for transfers between devices: 2.07 us -> 0.01 us  [on_device(): parts = lax.all_to_all(grouped, GROUPS, 0, 0, tiled=True)]
    all_gather x1, waiting for transfers between devices: 1.78 us -> 3.44 us  [on_device(): weight = lax.all_gather(weight, 'z', axis=0, tiled=True)]
where the time goes in v9:
time: 155 us
  starting transfers between devices  49.8 us (32%)
  Pallas kernels  43.1 us (28%)
  waiting for transfers between devices  28.2 us (18%)
  blocking collectives  13.6 us (9%)
  between operations  13.6 us (9%)
  other arithmetic  4.17 us (3%)
  local copies, waits for them, and re-layouts  2.13 us (1%)
    pallas_call x9, Pallas kernels, call(): pl.pallas_call(kernel, out_shape=list(outs), in_specs=specs, out_specs=[p...  43.1 us
    all_to_all x1, blocking collectives, on_device(): partial = lax.all_to_all(partial, ('x', *TENSOR), 0, 0, tiled=True)  13.6 us
    all_to_all x1, starting transfers between devices, on_device(): parts = lax.all_to_all(grouped, GROUPS, 0, 0, tiled=True)  12 us
    all_to_all x1, starting transfers between devices, on_device(): lax.all_to_all(entering, GROUPS, 0, 0, tiled=True).reshape(1, quarter, SPAN)  8.79 us
    ppermute x1, starting transfers between devices, on_device(): partial = (kept + lax.ppermute(sent, 'core', ring(2, 1))).astype(BF16)  7.15 us
    all_to_all x1, waiting for transfers between devices, on_device(): parts = lax.all_to_all(states, 'x', 0, 0, tiled=True)  5.75 us
    ppermute x1, waiting for transfers between devices, on_device(): across = lax.ppermute(done, 'yl', ring(2, 1))  5.5 us
    all_to_all x1, starting transfers between devices, on_device(): parts = lax.all_to_all(states, 'x', 0, 0, tiled=True)  4.99 us
  transfers between devices with their start and end apart: 15, of which 10 were waited for; matrix products, arithmetic and copies ran while one was open for 2% of the time, Pallas kernels for 18%

profile of v9, /device:TPU:1, one launch (start us, length us, event | category | flops | bytes accessed | tf_op | source)
XLA Modules:
  0.0 154.6 jit_solution(10556186444880131861)
XLA Ops:
  6.5 3.5 %shard_map.136 = (f32[4,520,128]{2,1,0:T(8,128)}, bf16[64,4480]{1,0:T(8,128)(2,1)}, bf16[64,4480]{1,0:T(8,128)(2,1)}) custom-call(bf16[128,2048]{1,0:T(8,128)(2,1)} %x_hbm.1, bf16[128,2048]{1,0:T(8,128)(2,1)} %gate_hbm.1, bf16[128,128]{1,0:T(8,128)(2,1)} %b_hbm.1, bf16[128,128]{1,0:T(8,128)(2,1)} %c_hbm.1, bf16[32,128]{1,0:T(8,128)(2,1)} %bitcast.45, ...), custom_call_target="tpu_custom_call" | custom-call | flops 134217728 | bytes 3334400 | tf_op jit(solution)/shard_map/pallas_call | solution.py:30
  10.1 5.0 %all-to-all-start = ((f32[4,520,128]{2,1,0:T(8,128)}), f32[4,520,128]{2,1,0:T(8,128)S(1)}, u32[]{:S(2)}, u32[]{:S(2)}) async-start(f32[4,520,128]{2,1,0:T(8,128)} %get-tuple-element.45), calls=%async_computation | async-start | bytes 2129920 | tf_op jit(solution)/shard_map/all_to_all | solution.py:418
  15.1 3.0 %collective-permute-start = (bf16[64,2048]{1,0:T(8,128)(2,1)S(1)}, bf16[64,2048]{1,0:T(8,128)(2,1)S(1)}, u32[]{:S(2)}, u32[]{:S(2)}) collective-permute-start(bf16[64,2048]{1,0:T(8,128)(2,1)S(1)} %bitcast.31), channel_id=1, source_target_pairs={{0,128},{128,0},{1,129},{129,1},{2,130},{130,2},{3,131},{131,3},{4... | collective-permute-start | bytes 786440 | tf_op jit(solution)/shard_map/ppermute | solution.py:403
  18.1 4.7 %collective-permute-done = bf16[64,2048]{1,0:T(8,128)(2,1)S(1)} collective-permute-done((bf16[64,2048]{1,0:T(8,128)(2,1)S(1)}, bf16[64,2048]{1,0:T(8,128)(2,1)S(1)}, u32[]{:S(2)}, u32[]{:S(2)}) %collective-permute-start) | collective-permute-done | bytes 262176 | tf_op jit(solution)/shard_map/ppermute | solution.py:403
  22.7 5.8 %all-to-all-done.parts_ref = f32[4,520,128]{2,1,0:T(8,128)S(1)} async-done(((f32[4,520,128]{2,1,0:T(8,128)}), f32[4,520,128]{2,1,0:T(8,128)S(1)}, u32[]{:S(2)}, u32[]{:S(2)}) %all-to-all-start) | async-done | bytes 1064992 | tf_op jit(solution)/shard_map/all_to_all | solution.py:418
  30.2 12.0 %all-to-all-start.1 = ((f32[16,40,128]{2,1,0:T(8,128)}), f32[16,40,128]{2,1,0:T(8,128)S(1)}, u32[]{:S(2)}, u32[]{:S(2)}) async-start(f32[16,40,128]{2,1,0:T(8,128)} %shard_map.138), calls=%async_computation.1 | async-start | bytes 655360 | tf_op jit(solution)/shard_map/all_to_all | solution.py:455
  42.6 2.4 %collective-permute-start.2 = (bf16[64,4480]{1,0:T(8,128)(2,1)}, bf16[64,4480]{1,0:T(8,128)(2,1)}, u32[]{:S(2)}, u32[]{:S(2)}) collective-permute-start(bf16[64,4480]{1,0:T(8,128)(2,1)} %get-tuple-element.61.bottom_hbm.refs_7_.refs_5_), channel_id=1, source_target_pairs={{0,12},{4,0},{8,4},{12,8},{1,13},{5,1},{9,5},{13,9},{2,14},{6,2},{... | collective-permute-start | bytes 1720328 | tf_op jit(solution)/shard_map/ppermute | solution.py:426
  46.5 5.3 %shard_map.137 = (f32[128,2048]{1,0:T(8,128)}, f32[2048,128]{1,0:T(8,128)}) custom-call(f32[1,32]{1,0:T(1,128)} %bitcast.34, f32[1,32]{1,0:T(1,128)} %bitcast.40, f32[1,2048]{1,0:T(1,128)} %reshape_reshape.3.skip_ref, bf16[64,4480]{1,0:T(8,128)(2,1)} %get-tuple-element.64.top_hbm.refs_6_.refs_4_, bf16[64,4480]{1,0:T(8,128)(2,1)} %get-tuple-element.61.bottom_hbm.refs_7_.refs_5_), custom_call_target="tpu_custom_call" | custom-call | flops 1000000 | bytes 3252480 | tf_op jit(solution)/shard_map/pallas_call | solution.py:30
  53.4 2.5 %collective-permute-done.1.top_hbm.refs_8_.refs_6_ = bf16[64,4480]{1,0:T(8,128)(2,1)} collective-permute-done((bf16[64,4480]{1,0:T(8,128)(2,1)S(1)}, bf16[64,4480]{1,0:T(8,128)(2,1)}, u32[]{:S(2)}, u32[]{:S(2)}) %collective-permute-start.1) | collective-permute-done | bytes 573472 | tf_op jit(solution)/shard_map/ppermute | solution.py:425
  56.7 2.7 %collective-permute-start.6 = (bf16[64,4480]{1,0:T(8,128)(2,1)}, bf16[64,4480]{1,0:T(8,128)(2,1)}, u32[]{:S(2)}, u32[]{:S(2)}) collective-permute-start(bf16[64,4480]{1,0:T(8,128)(2,1)} %collective-permute-done.2.bottom_hbm.refs_11_.refs_9_), channel_id=1, source_target_pairs={{0,12},{4,0},{8,4},{12,8},{1,13},{5,1},{9,5},{13,9},{2,14},{6,2},{... | collective-permute-start | bytes 1720328 | tf_op jit(solution)/shard_map/ppermute | solution.py:477
  59.4 8.8 %all-to-all-start.2 = ((f32[16,32,128]{2,1,0:T(8,128)}), f32[16,32,128]{2,1,0:T(8,128)S(1)}, u32[]{:S(2)}, u32[]{:S(2)}) async-start(f32[16,32,128]{2,1,0:T(8,128)} %shard_map.139), calls=%async_computation.2 | async-start | bytes 524288 | tf_op jit(solution)/shard_map/all_to_all | solution.py:478
  68.2 5.3 %shard_map.141 = (f32[128,2048]{1,0:T(8,128)}, f32[2048,128]{1,0:T(8,128)}) custom-call(f32[1,32]{1,0:T(1,128)} %bitcast.35, f32[1,32]{1,0:T(1,128)} %bitcast.41, f32[1,2048]{1,0:T(1,128)} %reshape_reshape.3.skip_ref, bf16[64,4480]{1,0:T(8,128)(2,1)} %collective-permute-done.4.top_hbm.refs_10_.refs_8_, ...), custom_call_target="tpu_custom_call" | custom-call | flops 1000000 | bytes 3252480 | tf_op jit(solution)/shard_map/pallas_call | solution.py:30
  73.5 5.3 %shard_map.140 = (f32[128,2048]{1,0:T(8,128)}, f32[2048,128]{1,0:T(8,128)}) custom-call(f32[1,32]{1,0:T(1,128)} %bitcast.36, f32[1,32]{1,0:T(1,128)} %bitcast.42, f32[1,2048]{1,0:T(1,128)} %reshape_reshape.3.skip_ref, bf16[64,4480]{1,0:T(8,128)(2,1)} %collective-permute-done.1.top_hbm.refs_8_.refs_6_, ...), custom_call_target="tpu_custom_call" | custom-call | flops 1000000 | bytes 3252480 | tf_op jit(solution)/shard_map/pallas_call | solution.py:30
  78.7 1.8 %all-to-all-done.2 = f32[16,32,128]{2,1,0:T(8,128)S(1)} async-done(((f32[16,32,128]{2,1,0:T(8,128)}), f32[16,32,128]{2,1,0:T(8,128)S(1)}, u32[]{:S(2)}, u32[]{:S(2)}) %all-to-all-start.2) | async-done | bytes 262176 | tf_op jit(solution)/shard_map/all_to_all | solution.py:478
  82.0 3.5 %all-to-all-start.3 = ((f32[4,512,128]{2,1,0:T(8,128)}), f32[4,512,128]{2,1,0:T(8,128)S(1)}, u32[]{:S(2)}, u32[]{:S(2)}) async-start(f32[4,512,128]{2,1,0:T(8,128)} %broadcast_in_dim.12), calls=%async_computation.3 | async-start | bytes 2097152 | tf_op jit(solution)/shard_map/all_to_all | solution.py:481
  85.6 9.7 %shard_map.142 = (f32[128,2048]{1,0:T(8,128)}, f32[128,2048]{1,0:T(8,128)}, f32[128,2048]{1,0:T(8,128)}, f32[128,2048]{1,0:T(8,128)}) custom-call(s32[5]{0:T(128)} %pad_add_fusion.place_ref, f32[1,32]{1,0:T(1,128)} %bitcast.37, f32[1,32]{1,0:T(1,128)} %bitcast.43, f32[1,2048]{1,0:T(1,128)} %reshape_reshape.3.skip_ref, ...), custom_call_target="tpu_custom_call" | custom-call | flops 536870912 | bytes 15081748 | tf_op jit(solution)/shard_map/pallas_call | solution.py:30
  95.3 3.4 %all-gather.2.cloned.1.call-done.refs_12_ = bf16[1024,2048]{1,0:T(8,128)(2,1)} async-done(((bf16[128,2048]{1,0:T(8,128)(2,1)}), bf16[1024,2048]{1,0:T(8,128)(2,1)}) %all-gather.2.cloned.1.call-update) | async-done | bytes 4194320 | tf_op jit(solution)/shard_map/all_gather | solution.py:421
  98.8 11.9 %shard_map.143 = (f32[512,512]{1,0:T(8,128)}, f32[512,512]{1,0:T(8,128)}) custom-call(s32[5]{0:T(128)} %pad_add_fusion.place_ref, f32[1,32]{1,0:T(1,128)} %bitcast.38, f32[1,32]{1,0:T(1,128)} %bitcast.44, f32[1,2048]{1,0:T(1,128)} %bitcast.46, f32[2048,128]{1,0:T(8,128)} %bitcast.26, f32[128,2048]{1,0:T(8,128)} %get-tuple-element.78.refs_0_, ...), custom_call_target="tpu_custom_call" | custom-call | flops 2684354560 | bytes 16130324 | tf_op jit(solution)/shard_map/pallas_call | solution.py:30
  110.6 7.1 %collective-permute-start.7 = (f32[512,512]{1,0:T(8,128)}, f32[512,512]{1,0:T(8,128)S(1)}, u32[]{:S(2)}, u32[]{:S(2)}) collective-permute-start(f32[512,512]{1,0:T(8,128)} %get-tuple-element.84), channel_id=1, source_target_pairs={{0,1},{1,0},{2,3},{3,2},{4,5},{5,4},{6,7},{7,6},{8,9},{9,8},{10,11... | collective-permute-start | bytes 3145736 | tf_op jit(solution)/shard_map/ppermute | solution.py:529
  117.8 2.5 %collective-permute-done.7 = f32[512,512]{1,0:T(8,128)S(1)} collective-permute-done((f32[512,512]{1,0:T(8,128)}, f32[512,512]{1,0:T(8,128)S(1)}, u32[]{:S(2)}, u32[]{:S(2)}) %collective-permute-start.7) | collective-permute-done | bytes 1048608 | tf_op jit(solution)/shard_map/ppermute | solution.py:529
  121.7 13.6 %all_to_all.29 = bf16[16,32,512]{2,1,0:T(8,128)(2,1)S(1)} all-to-all(bf16[16,32,512]{2,1,0:T(8,128)(2,1)S(1)} %bitcast.27), channel_id=1, replica_groups=mesh['yh'=2,'z'=8,'x'=4,'yl'=2,'core'=2] {'x','yl','core'}, dimensions={0} | all-to-all | bytes 1048576 | tf_op jit(solution)/shard_map/all_to_all | solution.py:530
  137.3 5.5 %collective-permute-done.8 = bf16[32,4096]{1,0:T(8,128)(2,1)S(1)} collective-permute-done((bf16[32,4096]{1,0:T(8,128)(2,1)S(1)}, bf16[32,4096]{1,0:T(8,128)(2,1)S(1)}, u32[]{:S(2)}, u32[]{:S(2)}) %collective-permute-start.8) | collective-permute-done | bytes 262176 | tf_op jit(solution)/shard_map/ppermute | solution.py:541
  142.8 2.1 %collective-permute-start.9 = (bf16[2,32,4096]{2,1,0:T(8,128)(2,1)S(1)}, bf16[2,32,4096]{2,1,0:T(8,128)(2,1)S(1)}, u32[]{:S(2)}, u32[]{:S(2)}) collective-permute-start(bf16[2,32,4096]{2,1,0:T(8,128)(2,1)S(1)} %pad_maximum_fusion.2), channel_id=1, source_target_pairs={{0,1},{1,0},{2,3},{3,2},{4,5},{5,4},{6,7},{7,6},{8,9},{9,8},{10,11... | collective-permute-start | bytes 1572872 | tf_op jit(solution)/shard_map/ppermute | solution.py:543
  144.9 1.5 collective-permute-done.9
  (51 shorter events, 12.1 us)
Async XLA Ops:
  6.5 39.2 %copy-start = (f32[32,64,128]{2,1,0:T(8,128)S(1)}, f32[32,64,128]{2,1,0:T(8,128)}, u32[]{:S(2)}) copy-start(f32[32,64,128]{2,1,0:T(8,128)} %param.23) | copy-start | bytes 3145732
  10.1 5.0 %copy-start.7 = (bf16[2048,64]{0,1:T(8,128)(2,1)S(1)}, bf16[2048,64]{0,1:T(8,128)(2,1)}, u32[]{:S(2)}) copy-start(bf16[2048,64]{0,1:T(8,128)(2,1)} %param.24) | copy-start | bytes 786436
  10.1 18.4 %all-to-all-start = ((f32[4,520,128]{2,1,0:T(8,128)}), f32[4,520,128]{2,1,0:T(8,128)S(1)}, u32[]{:S(2)}, u32[]{:S(2)}) async-start(f32[4,520,128]{2,1,0:T(8,128)} %get-tuple-element.45), calls=%async_computation | async-start | bytes 2129920 | tf_op jit(solution)/shard_map/all_to_all | solution.py:418
  15.1 83.7 %all-gather.2.cloned.1.call-start = ((), (), s32[]{:S(2)}) async-start(), calls=%async_computation.5 | async-start | bytes 4718592 | tf_op jit(solution)/shard_map/all_gather | solution.py:421
  15.1 7.7 %collective-permute-start = (bf16[64,2048]{1,0:T(8,128)(2,1)S(1)}, bf16[64,2048]{1,0:T(8,128)(2,1)S(1)}, u32[]{:S(2)}, u32[]{:S(2)}) collective-permute-start(bf16[64,2048]{1,0:T(8,128)(2,1)S(1)} %bitcast.31), channel_id=1, source_target_pairs={{0,128},{128,0},{1,129},{129,1},{2,130},{130,2},{3,131},{131,3},{4... | collective-permute-start | bytes 786440 | tf_op jit(solution)/shard_map/ppermute | solution.py:403
  29.3 12.9 %copy-start.3 = (bf16[64,4480]{1,0:T(8,128)(2,1)S(1)}, bf16[64,4480]{1,0:T(8,128)(2,1)}, u32[]{:S(2)}) copy-start(bf16[64,4480]{1,0:T(8,128)(2,1)} %get-tuple-element.64.top_hbm.refs_6_.refs_4_) | copy-start | bytes 1720324
  29.4 15.6 %copy-start.8 = (f32[32]{0:T(128)S(1)}, f32[32]{0:T(128)}, u32[]{:S(2)}) copy-start(f32[32]{0:T(128)} %param.21) | copy-start | bytes 388
  29.4 16.5 %copy-start.9 = (s32[4]{0:T(128)S(1)}, s32[4]{0:T(128)}, u32[]{:S(2)}) copy-start(s32[4]{0:T(128)} %constant.86.clone) | copy-start | bytes 52
  30.2 21.7 %copy-start.4 = (bf16[64,4480]{1,0:T(8,128)(2,1)S(1)}, bf16[64,4480]{1,0:T(8,128)(2,1)}, u32[]{:S(2)}) copy-start(bf16[64,4480]{1,0:T(8,128)(2,1)} %get-tuple-element.64.top_hbm.refs_6_.refs_4_) | copy-start | bytes 1720324
  30.2 25.7 %all-to-all-start.1 = ((f32[16,40,128]{2,1,0:T(8,128)}), f32[16,40,128]{2,1,0:T(8,128)S(1)}, u32[]{:S(2)}, u32[]{:S(2)}) async-start(f32[16,40,128]{2,1,0:T(8,128)} %shard_map.138), calls=%async_computation.1 | async-start | bytes 655360 | tf_op jit(solution)/shard_map/all_to_all | solution.py:455
  42.2 13.7 %collective-permute-start.1 = (bf16[64,4480]{1,0:T(8,128)(2,1)S(1)}, bf16[64,4480]{1,0:T(8,128)(2,1)}, u32[]{:S(2)}, u32[]{:S(2)}) collective-permute-start(bf16[64,4480]{1,0:T(8,128)(2,1)S(1)} %copy-done.3), channel_id=1, source_target_pairs={{0,4},{4,8},{8,12},{12,0},{1,5},{5,9},{9,13},{13,1},{2,6},{6,10},{... | collective-permute-start | bytes 1720328 | tf_op jit(solution)/shard_map/ppermute | solution.py:425
  42.6 13.4 %collective-permute-start.2 = (bf16[64,4480]{1,0:T(8,128)(2,1)}, bf16[64,4480]{1,0:T(8,128)(2,1)}, u32[]{:S(2)}, u32[]{:S(2)}) collective-permute-start(bf16[64,4480]{1,0:T(8,128)(2,1)} %get-tuple-element.61.bottom_hbm.refs_7_.refs_5_), channel_id=1, source_target_pairs={{0,12},{4,0},{8,4},{12,8},{1,13},{5,1},{9,5},{13,9},{2,14},{6,2},{... | collective-permute-start | bytes 1720328 | tf_op jit(solution)/shard_map/ppermute | solution.py:426
  51.9 16.3 %collective-permute-start.4 = (bf16[64,4480]{1,0:T(8,128)(2,1)S(1)}, bf16[64,4480]{1,0:T(8,128)(2,1)}, u32[]{:S(2)}, u32[]{:S(2)}) collective-permute-start(bf16[64,4480]{1,0:T(8,128)(2,1)S(1)} %copy-done.4), channel_id=1, source_target_pairs={{0,12},{4,0},{8,4},{12,8},{1,13},{5,1},{9,5},{13,9},{2,14},{6,2},{... | collective-permute-start | bytes 1720328 | tf_op jit(solution)/shard_map/ppermute | solution.py:458
  52.0 21.5 %collective-permute-start.3 = (bf16[64,4480]{1,0:T(8,128)(2,1)}, bf16[64,4480]{1,0:T(8,128)(2,1)}, u32[]{:S(2)}, u32[]{:S(2)}) collective-permute-start(bf16[64,4480]{1,0:T(8,128)(2,1)} %get-tuple-element.61.bottom_hbm.refs_7_.refs_5_), channel_id=1, source_target_pairs={{0,4},{4,8},{8,12},{12,0},{1,5},{5,9},{9,13},{13,1},{2,6},{6,10},{... | collective-permute-start | bytes 1720328 | tf_op jit(solution)/shard_map/ppermute | solution.py:457
  56.7 24.2 %collective-permute-start.5 = (bf16[64,4480]{1,0:T(8,128)(2,1)}, bf16[64,4480]{1,0:T(8,128)(2,1)S(1)}, u32[]{:S(2)}, u32[]{:S(2)}) collective-permute-start(bf16[64,4480]{1,0:T(8,128)(2,1)} %collective-permute-done.1.top_hbm.refs_8_.refs_6_), channel_id=1, source_target_pairs={{0,4},{4,8},{8,12},{12,0},{1,5},{5,9},{9,13},{13,1},{2,6},{6,10},{... | collective-permute-start | bytes 1720328 | tf_op jit(solution)/shard_map/ppermute | solution.py:477
  56.7 24.2 %collective-permute-start.6 = (bf16[64,4480]{1,0:T(8,128)(2,1)}, bf16[64,4480]{1,0:T(8,128)(2,1)}, u32[]{:S(2)}, u32[]{:S(2)}) collective-permute-start(bf16[64,4480]{1,0:T(8,128)(2,1)} %collective-permute-done.2.bottom_hbm.refs_11_.refs_9_), channel_id=1, source_target_pairs={{0,12},{4,0},{8,4},{12,8},{1,13},{5,1},{9,5},{13,9},{2,14},{6,2},{... | collective-permute-start | bytes 1720328 | tf_op jit(solution)/shard_map/ppermute | solution.py:477
  59.4 21.2 %all-to-all-start.2 = ((f32[16,32,128]{2,1,0:T(8,128)}), f32[16,32,128]{2,1,0:T(8,128)S(1)}, u32[]{:S(2)}, u32[]{:S(2)}) async-start(f32[16,32,128]{2,1,0:T(8,128)} %shard_map.139), calls=%async_computation.2 | async-start | bytes 524288 | tf_op jit(solution)/shard_map/all_to_all | solution.py:478
  82.0 13.3 %all-to-all-start.3 = ((f32[4,512,128]{2,1,0:T(8,128)}), f32[4,512,128]{2,1,0:T(8,128)S(1)}, u32[]{:S(2)}, u32[]{:S(2)}) async-start(f32[4,512,128]{2,1,0:T(8,128)} %broadcast_in_dim.12), calls=%async_computation.3 | async-start | bytes 2097152 | tf_op jit(solution)/shard_map/all_to_all | solution.py:481
  95.3 3.4 %copy-start.5 = (f32[4,512,128]{2,1,0:T(8,128)}, f32[4,512,128]{2,1,0:T(8,128)S(1)}, u32[]{:S(2)}) copy-start(f32[4,512,128]{2,1,0:T(8,128)S(1)} %all-to-all-done.3) | copy-start | bytes 3145732
  110.6 9.6 %collective-permute-start.7 = (f32[512,512]{1,0:T(8,128)}, f32[512,512]{1,0:T(8,128)S(1)}, u32[]{:S(2)}, u32[]{:S(2)}) collective-permute-start(f32[512,512]{1,0:T(8,128)} %get-tuple-element.84), channel_id=1, source_target_pairs={{0,1},{1,0},{2,3},{3,2},{4,5},{5,4},{6,7},{7,6},{8,9},{9,8},{10,11... | collective-permute-start | bytes 3145736 | tf_op jit(solution)/shard_map/ppermute | solution.py:529
  121.7 13.7 %copy-start.1 = (bf16[32,4096]{1,0:T(8,128)(2,1)S(1)}, bf16[32,4096]{1,0:T(8,128)(2,1)}, u32[]{:S(2)}) copy-start(bf16[32,4096]{1,0:T(8,128)(2,1)} %residual_ref.1) | copy-start | bytes 786436
  121.7 13.6 %copy-start.2 = (f32[4096]{0:T(1024)S(1)}, f32[4096]{0:T(1024)}, u32[]{:S(2)}) copy-start(f32[4096]{0:T(1024)} %param.26) | copy-start | bytes 49156
  136.0 6.8 %collective-permute-start.8 = (bf16[32,4096]{1,0:T(8,128)(2,1)S(1)}, bf16[32,4096]{1,0:T(8,128)(2,1)S(1)}, u32[]{:S(2)}, u32[]{:S(2)}) collective-permute-start(bf16[32,4096]{1,0:T(8,128)(2,1)S(1)} %shard_map.144), channel_id=1, source_target_pairs={{0,2},{2,0},{1,3},{3,1},{4,6},{6,4},{5,7},{7,5},{8,10},{10,8},{9,1... | collective-permute-start | bytes 786440 | tf_op jit(solution)/shard_map/ppermute | solution.py:541
  142.8 3.6 %collective-permute-start.9 = (bf16[2,32,4096]{2,1,0:T(8,128)(2,1)S(1)}, bf16[2,32,4096]{2,1,0:T(8,128)(2,1)S(1)}, u32[]{:S(2)}, u32[]{:S(2)}) collective-permute-start(bf16[2,32,4096]{2,1,0:T(8,128)(2,1)S(1)} %pad_maximum_fusion.2), channel_id=1, source_target_pairs={{0,1},{1,0},{2,3},{3,2},{4,5},{5,4},{6,7},{7,6},{8,9},{9,8},{10,11... | collective-permute-start | bytes 1572872 | tf_op jit(solution)/shard_map/ppermute | solution.py:543
  (1 other events, 1.1 us)
Sparse Core Ops, SparseCore 0:
  29.5 69.2 all-gather.1

commit v10 on v9

--- a/solution.py
+++ b/solution.py
@@ -279,16 +279,20 @@
     kept_ref, sent_ref, logs_ref, mixed_ref, block_ref, normed_ref, weight_ref, enter_two, semaphores = refs[3 * n + 1 :]
     inner, heads = mixed_ref.shape[2], bias_ref.shape[1]
     pairs = inner // SPAN
-    block_in, mixed_in = [], []
+    coefs_in, gate_in, mixed_in = [], [], []
     for i in range(n):
-        block_in += copies(
-            halves(blocks[2 * i : 2 * i + 2], slice(inner, None), block_ref.at[i]), semaphores, 2 * i
+        to = block_ref.at[i, :, pl.ds(inner, 3 * SPAN)]
+        coefs_in += copies(halves(blocks[2 * i : 2 * i + 2], slice(2 * inner, None), to), semaphores, 2 * i)
+    for i in range(n):
+        to = block_ref.at[i, :, pl.ds(0, inner)]
+        mixed_in += copies([(mixed[i], mixed_ref.at[i])], semaphores, 2 * n + i)
+        gate_in.append(
+            copies(halves(blocks[2 * i : 2 * i + 2], slice(inner, 2 * inner), to), semaphores, 3 * n + 2 * i)
         )
-        mixed_in += copies([(mixed[i], mixed_ref.at[i])], semaphores, 2 * n + i)
-    (weight_in,) = copies([(weight_hbm, weight_ref)], semaphores, 3 * n)
+    (weight_in,) = copies([(weight_hbm, weight_ref)], semaphores, 5 * n)
+    for copy in coefs_in:
+        copy.wait()
     for i in range(n):
-        for copy in block_in[2 * i : 2 * i + 2]:
-            copy.wait()
         raw_t = block_ref[i, :heads, inner + 2 * SPAN :]
         logs_ref[place_ref[i]] = steps_of(raw_t, bias_ref[...], decay_ref[...])[1]
     for pair in range(pairs):
@@ -301,7 +305,8 @@
         before = before + here[:, SPAN - 1 :]
     low = first_lanes((SPAN, SPAN))
     for i in range(n):
-        mixed_in[i].wait()
+        for copy in (mixed_in[i], *gate_in[i]):
+            copy.wait()
         place = place_ref[i]
         cumulative = jnp.transpose(logs_ref[place])
         c = block_ref[i, :, inner + SPAN : inner + 2 * SPAN]
@@ -509,7 +514,7 @@
             pltpu.VMEM((n_x * tokens, inner), BF16),
             pltpu.VMEM(weight.shape, BF16),
             pltpu.VMEM((2 * inner, SPAN), BF16),
-            pltpu.SemaphoreType.DMA((3 * n_x + 1,)),
+            pltpu.SemaphoreType.DMA((5 * n_x + 1,)),
         ],
         flops=2 * n_x * tokens * inner * (STATE * 2 + weight.shape[0]),
         smem=1,

time: 155 us -> 154 us (level)
  no operation moved by 1% of the time
where the time goes in v10:
time: 154 us; the launch traced here: 153 us
  starting transfers between devices  49.8 us (32%)
  Pallas kernels  41.7 us (27%)
  waiting for transfers between devices  28.2 us (18%)
  blocking collectives  13.6 us (9%)
  between operations  13.6 us (9%)
  other arithmetic  4.17 us (3%)
  local copies, waits for them, and re-layouts  2.13 us (1%)
    pallas_call x9, Pallas kernels, call(): pl.pallas_call(kernel, out_shape=list(outs), in_specs=specs, out_specs=[p...  41.7 us
    all_to_all x1, blocking collectives, on_device(): partial = lax.all_to_all(partial, ('x', *TENSOR), 0, 0, tiled=True)  13.6 us
    all_to_all x1, starting transfers between devices, on_device(): parts = lax.all_to_all(grouped, GROUPS, 0, 0, tiled=True)  12 us
    all_to_all x1, starting transfers between devices, on_device(): lax.all_to_all(entering, GROUPS, 0, 0, tiled=True).reshape(1, quarter, SPAN)  8.79 us
    ppermute x1, starting transfers between devices, on_device(): partial = (kept + lax.ppermute(sent, 'core', ring(2, 1))).astype(BF16)  7.15 us
    all_to_all x1, waiting for transfers between devices, on_device(): parts = lax.all_to_all(states, 'x', 0, 0, tiled=True)  5.75 us
    ppermute x1, waiting for transfers between devices, on_device(): across = lax.ppermute(done, 'yl', ring(2, 1))  5.5 us
    all_to_all x1, starting transfers between devices, on_device(): parts = lax.all_to_all(states, 'x', 0, 0, tiled=True)  4.99 us
  transfers between devices with their start and end apart: 15, of which 10 were waited for; matrix products, arithmetic and copies ran while one was open for 2% of the time, Pallas kernels for 18%

profile of v10, /device:TPU:1, one launch (start us, length us, event | category | flops | bytes accessed | tf_op | source)
XLA Modules:
  0.0 153.2 jit_solution(636732045664750666)
XLA Ops:
  6.5 3.5 %shard_map.136 = (f32[4,520,128]{2,1,0:T(8,128)}, bf16[64,4480]{1,0:T(8,128)(2,1)}, bf16[64,4480]{1,0:T(8,128)(2,1)}) custom-call(bf16[128,2048]{1,0:T(8,128)(2,1)} %x_hbm.1, bf16[128,2048]{1,0:T(8,128)(2,1)} %gate_hbm.1, bf16[128,128]{1,0:T(8,128)(2,1)} %b_hbm.1, bf16[128,128]{1,0:T(8,128)(2,1)} %c_hbm.1, bf16[32,128]{1,0:T(8,128)(2,1)} %bitcast.45, ...), custom_call_target="tpu_custom_call" | custom-call | flops 134217728 | bytes 3334400 | tf_op jit(solution)/shard_map/pallas_call | solution.py:30
  10.1 5.0 %all-to-all-start = ((f32[4,520,128]{2,1,0:T(8,128)}), f32[4,520,128]{2,1,0:T(8,128)S(1)}, u32[]{:S(2)}, u32[]{:S(2)}) async-start(f32[4,520,128]{2,1,0:T(8,128)} %get-tuple-element.45), calls=%async_computation | async-start | bytes 2129920 | tf_op jit(solution)/shard_map/all_to_all | solution.py:423
  15.1 3.0 %collective-permute-start = (bf16[64,2048]{1,0:T(8,128)(2,1)S(1)}, bf16[64,2048]{1,0:T(8,128)(2,1)S(1)}, u32[]{:S(2)}, u32[]{:S(2)}) collective-permute-start(bf16[64,2048]{1,0:T(8,128)(2,1)S(1)} %bitcast.31), channel_id=1, source_target_pairs={{0,128},{128,0},{1,129},{129,1},{2,130},{130,2},{3,131},{131,3},{4... | collective-permute-start | bytes 786440 | tf_op jit(solution)/shard_map/ppermute | solution.py:408
  18.1 4.7 %collective-permute-done = bf16[64,2048]{1,0:T(8,128)(2,1)S(1)} collective-permute-done((bf16[64,2048]{1,0:T(8,128)(2,1)S(1)}, bf16[64,2048]{1,0:T(8,128)(2,1)S(1)}, u32[]{:S(2)}, u32[]{:S(2)}) %collective-permute-start) | collective-permute-done | bytes 262176 | tf_op jit(solution)/shard_map/ppermute | solution.py:408
  22.7 5.8 %all-to-all-done.parts_ref = f32[4,520,128]{2,1,0:T(8,128)S(1)} async-done(((f32[4,520,128]{2,1,0:T(8,128)}), f32[4,520,128]{2,1,0:T(8,128)S(1)}, u32[]{:S(2)}, u32[]{:S(2)}) %all-to-all-start) | async-done | bytes 1064992 | tf_op jit(solution)/shard_map/all_to_all | solution.py:423
  30.2 12.0 %all-to-all-start.1 = ((f32[16,40,128]{2,1,0:T(8,128)}), f32[16,40,128]{2,1,0:T(8,128)S(1)}, u32[]{:S(2)}, u32[]{:S(2)}) async-start(f32[16,40,128]{2,1,0:T(8,128)} %shard_map.138), calls=%async_computation.1 | async-start | bytes 655360 | tf_op jit(solution)/shard_map/all_to_all | solution.py:460
  42.6 2.4 %collective-permute-start.2 = (bf16[64,4480]{1,0:T(8,128)(2,1)}, bf16[64,4480]{1,0:T(8,128)(2,1)}, u32[]{:S(2)}, u32[]{:S(2)}) collective-permute-start(bf16[64,4480]{1,0:T(8,128)(2,1)} %get-tuple-element.61.bottom_hbm.refs_7_.refs_5_), channel_id=1, source_target_pairs={{0,12},{4,0},{8,4},{12,8},{1,13},{5,1},{9,5},{13,9},{2,14},{6,2},{... | collective-permute-start | bytes 1720328 | tf_op jit(solution)/shard_map/ppermute | solution.py:431
  46.5 5.3 %shard_map.137 = (f32[128,2048]{1,0:T(8,128)}, f32[2048,128]{1,0:T(8,128)}) custom-call(f32[1,32]{1,0:T(1,128)} %bitcast.34, f32[1,32]{1,0:T(1,128)} %bitcast.40, f32[1,2048]{1,0:T(1,128)} %reshape_reshape.3.skip_ref, bf16[64,4480]{1,0:T(8,128)(2,1)} %get-tuple-element.64.top_hbm.refs_6_.refs_4_, bf16[64,4480]{1,0:T(8,128)(2,1)} %get-tuple-element.61.bottom_hbm.refs_7_.refs_5_), custom_call_target="tpu_custom_call" | custom-call | flops 1000000 | bytes 3252480 | tf_op jit(solution)/shard_map/pallas_call | solution.py:30
  53.4 2.5 %collective-permute-done.1.top_hbm.refs_8_.refs_6_ = bf16[64,4480]{1,0:T(8,128)(2,1)} collective-permute-done((bf16[64,4480]{1,0:T(8,128)(2,1)S(1)}, bf16[64,4480]{1,0:T(8,128)(2,1)}, u32[]{:S(2)}, u32[]{:S(2)}) %collective-permute-start.1) | collective-permute-done | bytes 573472 | tf_op jit(solution)/shard_map/ppermute | solution.py:430
  56.7 2.7 %collective-permute-start.6 = (bf16[64,4480]{1,0:T(8,128)(2,1)}, bf16[64,4480]{1,0:T(8,128)(2,1)}, u32[]{:S(2)}, u32[]{:S(2)}) collective-permute-start(bf16[64,4480]{1,0:T(8,128)(2,1)} %collective-permute-done.2.bottom_hbm.refs_11_.refs_9_), channel_id=1, source_target_pairs={{0,12},{4,0},{8,4},{12,8},{1,13},{5,1},{9,5},{13,9},{2,14},{6,2},{... | collective-permute-start | bytes 1720328 | tf_op jit(solution)/shard_map/ppermute | solution.py:482
  59.4 8.8 %all-to-all-start.2 = ((f32[16,32,128]{2,1,0:T(8,128)}), f32[16,32,128]{2,1,0:T(8,128)S(1)}, u32[]{:S(2)}, u32[]{:S(2)}) async-start(f32[16,32,128]{2,1,0:T(8,128)} %shard_map.139), calls=%async_computation.2 | async-start | bytes 524288 | tf_op jit(solution)/shard_map/all_to_all | solution.py:483
  68.2 5.3 %shard_map.141 = (f32[128,2048]{1,0:T(8,128)}, f32[2048,128]{1,0:T(8,128)}) custom-call(f32[1,32]{1,0:T(1,128)} %bitcast.35, f32[1,32]{1,0:T(1,128)} %bitcast.41, f32[1,2048]{1,0:T(1,128)} %reshape_reshape.3.skip_ref, bf16[64,4480]{1,0:T(8,128)(2,1)} %collective-permute-done.4.top_hbm.refs_10_.refs_8_, ...), custom_call_target="tpu_custom_call" | custom-call | flops 1000000 | bytes 3252480 | tf_op jit(solution)/shard_map/pallas_call | solution.py:30
  73.5 5.3 %shard_map.140 = (f32[128,2048]{1,0:T(8,128)}, f32[2048,128]{1,0:T(8,128)}) custom-call(f32[1,32]{1,0:T(1,128)} %bitcast.36, f32[1,32]{1,0:T(1,128)} %bitcast.42, f32[1,2048]{1,0:T(1,128)} %reshape_reshape.3.skip_ref, bf16[64,4480]{1,0:T(8,128)(2,1)} %collective-permute-done.1.top_hbm.refs_8_.refs_6_, ...), custom_call_target="tpu_custom_call" | custom-call | flops 1000000 | bytes 3252480 | tf_op jit(solution)/shard_map/pallas_call | solution.py:30
  78.7 1.8 %all-to-all-done.2 = f32[16,32,128]{2,1,0:T(8,128)S(1)} async-done(((f32[16,32,128]{2,1,0:T(8,128)}), f32[16,32,128]{2,1,0:T(8,128)S(1)}, u32[]{:S(2)}, u32[]{:S(2)}) %all-to-all-start.2) | async-done | bytes 262176 | tf_op jit(solution)/shard_map/all_to_all | solution.py:483
  82.0 3.5 %all-to-all-start.3 = ((f32[4,512,128]{2,1,0:T(8,128)}), f32[4,512,128]{2,1,0:T(8,128)S(1)}, u32[]{:S(2)}, u32[]{:S(2)}) async-start(f32[4,512,128]{2,1,0:T(8,128)} %broadcast_in_dim.12), calls=%async_computation.3 | async-start | bytes 2097152 | tf_op jit(solution)/shard_map/all_to_all | solution.py:486
  85.6 9.7 %shard_map.142 = (f32[128,2048]{1,0:T(8,128)}, f32[128,2048]{1,0:T(8,128)}, f32[128,2048]{1,0:T(8,128)}, f32[128,2048]{1,0:T(8,128)}) custom-call(s32[5]{0:T(128)} %pad_add_fusion.place_ref, f32[1,32]{1,0:T(1,128)} %bitcast.37, f32[1,32]{1,0:T(1,128)} %bitcast.43, f32[1,2048]{1,0:T(1,128)} %reshape_reshape.3.skip_ref, ...), custom_call_target="tpu_custom_call" | custom-call | flops 536870912 | bytes 15081748 | tf_op jit(solution)/shard_map/pallas_call | solution.py:30
  95.3 3.4 %all-gather.2.cloned.1.call-done.refs_12_ = bf16[1024,2048]{1,0:T(8,128)(2,1)} async-done(((bf16[128,2048]{1,0:T(8,128)(2,1)}), bf16[1024,2048]{1,0:T(8,128)(2,1)}) %all-gather.2.cloned.1.call-update) | async-done | bytes 4194320 | tf_op jit(solution)/shard_map/all_gather | solution.py:426
  98.8 10.5 %shard_map.143 = (f32[512,512]{1,0:T(8,128)}, f32[512,512]{1,0:T(8,128)}) custom-call(s32[5]{0:T(128)} %pad_add_fusion.place_ref, f32[1,32]{1,0:T(1,128)} %bitcast.38, f32[1,32]{1,0:T(1,128)} %bitcast.44, f32[1,2048]{1,0:T(1,128)} %bitcast.46, f32[2048,128]{1,0:T(8,128)} %bitcast.26, f32[128,2048]{1,0:T(8,128)} %get-tuple-element.78.refs_0_, ...), custom_call_target="tpu_custom_call" | custom-call | flops 2684354560 | bytes 16130324 | tf_op jit(solution)/shard_map/pallas_call | solution.py:30
  109.2 7.1 %collective-permute-start.7 = (f32[512,512]{1,0:T(8,128)}, f32[512,512]{1,0:T(8,128)S(1)}, u32[]{:S(2)}, u32[]{:S(2)}) collective-permute-start(f32[512,512]{1,0:T(8,128)} %get-tuple-element.84), channel_id=1, source_target_pairs={{0,1},{1,0},{2,3},{3,2},{4,5},{5,4},{6,7},{7,6},{8,9},{9,8},{10,11... | collective-permute-start | bytes 3145736 | tf_op jit(solution)/shard_map/ppermute | solution.py:534
  116.4 2.5 %collective-permute-done.7 = f32[512,512]{1,0:T(8,128)S(1)} collective-permute-done((f32[512,512]{1,0:T(8,128)}, f32[512,512]{1,0:T(8,128)S(1)}, u32[]{:S(2)}, u32[]{:S(2)}) %collective-permute-start.7) | collective-permute-done | bytes 1048608 | tf_op jit(solution)/shard_map/ppermute | solution.py:534
  120.3 13.6 %all_to_all.29 = bf16[16,32,512]{2,1,0:T(8,128)(2,1)S(1)} all-to-all(bf16[16,32,512]{2,1,0:T(8,128)(2,1)S(1)} %bitcast.27), channel_id=1, replica_groups=mesh['yh'=2,'z'=8,'x'=4,'yl'=2,'core'=2] {'x','yl','core'}, dimensions={0} | all-to-all | bytes 1048576 | tf_op jit(solution)/shard_map/all_to_all | solution.py:535
  135.9 5.5 %collective-permute-done.8 = bf16[32,4096]{1,0:T(8,128)(2,1)S(1)} collective-permute-done((bf16[32,4096]{1,0:T(8,128)(2,1)S(1)}, bf16[32,4096]{1,0:T(8,128)(2,1)S(1)}, u32[]{:S(2)}, u32[]{:S(2)}) %collective-permute-start.8) | collective-permute-done | bytes 262176 | tf_op jit(solution)/shard_map/ppermute | solution.py:546
  141.4 2.1 %collective-permute-start.9 = (bf16[2,32,4096]{2,1,0:T(8,128)(2,1)S(1)}, bf16[2,32,4096]{2,1,0:T(8,128)(2,1)S(1)}, u32[]{:S(2)}, u32[]{:S(2)}) collective-permute-start(bf16[2,32,4096]{2,1,0:T(8,128)(2,1)S(1)} %pad_maximum_fusion.2), channel_id=1, source_target_pairs={{0,1},{1,0},{2,3},{3,2},{4,5},{5,4},{6,7},{7,6},{8,9},{9,8},{10,11... | collective-permute-start | bytes 1572872 | tf_op jit(solution)/shard_map/ppermute | solution.py:548
  143.5 1.5 %collective-permute-done.9 = bf16[2,32,4096]{2,1,0:T(8,128)(2,1)S(1)} collective-permute-done((bf16[2,32,4096]{2,1,0:T(8,128)(2,1)S(1)}, bf16[2,32,4096]{2,1,0:T(8,128)(2,1)S(1)}, u32[]{:S(2)}, u32[]{:S(2)}) %collective-permute-start.9) | collective-permute-done | bytes 524320 | tf_op jit(solution)/shard_map/ppermute | solution.py:548
  (51 shorter events, 12.1 us)
Async XLA Ops:
  6.5 39.2 %copy-start = (f32[32,64,128]{2,1,0:T(8,128)S(1)}, f32[32,64,128]{2,1,0:T(8,128)}, u32[]{:S(2)}) copy-start(f32[32,64,128]{2,1,0:T(8,128)} %param.23) | copy-start | bytes 3145732
  10.1 5.0 %copy-start.7 = (bf16[2048,64]{0,1:T(8,128)(2,1)S(1)}, bf16[2048,64]{0,1:T(8,128)(2,1)}, u32[]{:S(2)}) copy-start(bf16[2048,64]{0,1:T(8,128)(2,1)} %param.24) | copy-start | bytes 786436
  10.1 18.4 %all-to-all-start = ((f32[4,520,128]{2,1,0:T(8,128)}), f32[4,520,128]{2,1,0:T(8,128)S(1)}, u32[]{:S(2)}, u32[]{:S(2)}) async-start(f32[4,520,128]{2,1,0:T(8,128)} %get-tuple-element.45), calls=%async_computation | async-start | bytes 2129920 | tf_op jit(solution)/shard_map/all_to_all | solution.py:423
  15.1 83.7 %all-gather.2.cloned.1.call-start = ((), (), s32[]{:S(2)}) async-start(), calls=%async_computation.5 | async-start | bytes 4718592 | tf_op jit(solution)/shard_map/all_gather | solution.py:426
  15.1 7.7 %collective-permute-start = (bf16[64,2048]{1,0:T(8,128)(2,1)S(1)}, bf16[64,2048]{1,0:T(8,128)(2,1)S(1)}, u32[]{:S(2)}, u32[]{:S(2)}) collective-permute-start(bf16[64,2048]{1,0:T(8,128)(2,1)S(1)} %bitcast.31), channel_id=1, source_target_pairs={{0,128},{128,0},{1,129},{129,1},{2,130},{130,2},{3,131},{131,3},{4... | collective-permute-start | bytes 786440 | tf_op jit(solution)/shard_map/ppermute | solution.py:408
  29.3 12.9 %copy-start.3 = (bf16[64,4480]{1,0:T(8,128)(2,1)S(1)}, bf16[64,4480]{1,0:T(8,128)(2,1)}, u32[]{:S(2)}) copy-start(bf16[64,4480]{1,0:T(8,128)(2,1)} %get-tuple-element.64.top_hbm.refs_6_.refs_4_) | copy-start | bytes 1720324
  29.4 15.6 %copy-start.8 = (f32[32]{0:T(128)S(1)}, f32[32]{0:T(128)}, u32[]{:S(2)}) copy-start(f32[32]{0:T(128)} %param.21) | copy-start | bytes 388
  29.4 16.5 %copy-start.9 = (s32[4]{0:T(128)S(1)}, s32[4]{0:T(128)}, u32[]{:S(2)}) copy-start(s32[4]{0:T(128)} %constant.86.clone) | copy-start | bytes 52
  30.2 21.7 %copy-start.4 = (bf16[64,4480]{1,0:T(8,128)(2,1)S(1)}, bf16[64,4480]{1,0:T(8,128)(2,1)}, u32[]{:S(2)}) copy-start(bf16[64,4480]{1,0:T(8,128)(2,1)} %get-tuple-element.64.top_hbm.refs_6_.refs_4_) | copy-start | bytes 1720324
  30.2 25.7 %all-to-all-start.1 = ((f32[16,40,128]{2,1,0:T(8,128)}), f32[16,40,128]{2,1,0:T(8,128)S(1)}, u32[]{:S(2)}, u32[]{:S(2)}) async-start(f32[16,40,128]{2,1,0:T(8,128)} %shard_map.138), calls=%async_computation.1 | async-start | bytes 655360 | tf_op jit(solution)/shard_map/all_to_all | solution.py:460
  42.2 13.7 %collective-permute-start.1 = (bf16[64,4480]{1,0:T(8,128)(2,1)S(1)}, bf16[64,4480]{1,0:T(8,128)(2,1)}, u32[]{:S(2)}, u32[]{:S(2)}) collective-permute-start(bf16[64,4480]{1,0:T(8,128)(2,1)S(1)} %copy-done.3), channel_id=1, source_target_pairs={{0,4},{4,8},{8,12},{12,0},{1,5},{5,9},{9,13},{13,1},{2,6},{6,10},{... | collective-permute-start | bytes 1720328 | tf_op jit(solution)/shard_map/ppermute | solution.py:430
  42.6 13.4 %collective-permute-start.2 = (bf16[64,4480]{1,0:T(8,128)(2,1)}, bf16[64,4480]{1,0:T(8,128)(2,1)}, u32[]{:S(2)}, u32[]{:S(2)}) collective-permute-start(bf16[64,4480]{1,0:T(8,128)(2,1)} %get-tuple-element.61.bottom_hbm.refs_7_.refs_5_), channel_id=1, source_target_pairs={{0,12},{4,0},{8,4},{12,8},{1,13},{5,1},{9,5},{13,9},{2,14},{6,2},{... | collective-permute-start | bytes 1720328 | tf_op jit(solution)/shard_map/ppermute | solution.py:431
  51.9 16.3 %collective-permute-start.4 = (bf16[64,4480]{1,0:T(8,128)(2,1)S(1)}, bf16[64,4480]{1,0:T(8,128)(2,1)}, u32[]{:S(2)}, u32[]{:S(2)}) collective-permute-start(bf16[64,4480]{1,0:T(8,128)(2,1)S(1)} %copy-done.4), channel_id=1, source_target_pairs={{0,12},{4,0},{8,4},{12,8},{1,13},{5,1},{9,5},{13,9},{2,14},{6,2},{... | collective-permute-start | bytes 1720328 | tf_op jit(solution)/shard_map/ppermute | solution.py:463
  52.0 21.5 %collective-permute-start.3 = (bf16[64,4480]{1,0:T(8,128)(2,1)}, bf16[64,4480]{1,0:T(8,128)(2,1)}, u32[]{:S(2)}, u32[]{:S(2)}) collective-permute-start(bf16[64,4480]{1,0:T(8,128)(2,1)} %get-tuple-element.61.bottom_hbm.refs_7_.refs_5_), channel_id=1, source_target_pairs={{0,4},{4,8},{8,12},{12,0},{1,5},{5,9},{9,13},{13,1},{2,6},{6,10},{... | collective-permute-start | bytes 1720328 | tf_op jit(solution)/shard_map/ppermute | solution.py:462
  56.7 24.2 %collective-permute-start.5 = (bf16[64,4480]{1,0:T(8,128)(2,1)}, bf16[64,4480]{1,0:T(8,128)(2,1)S(1)}, u32[]{:S(2)}, u32[]{:S(2)}) collective-permute-start(bf16[64,4480]{1,0:T(8,128)(2,1)} %collective-permute-done.1.top_hbm.refs_8_.refs_6_), channel_id=1, source_target_pairs={{0,4},{4,8},{8,12},{12,0},{1,5},{5,9},{9,13},{13,1},{2,6},{6,10},{... | collective-permute-start | bytes 1720328 | tf_op jit(solution)/shard_map/ppermute | solution.py:482
  56.7 24.2 %collective-permute-start.6 = (bf16[64,4480]{1,0:T(8,128)(2,1)}, bf16[64,4480]{1,0:T(8,128)(2,1)}, u32[]{:S(2)}, u32[]{:S(2)}) collective-permute-start(bf16[64,4480]{1,0:T(8,128)(2,1)} %collective-permute-done.2.bottom_hbm.refs_11_.refs_9_), channel_id=1, source_target_pairs={{0,12},{4,0},{8,4},{12,8},{1,13},{5,1},{9,5},{13,9},{2,14},{6,2},{... | collective-permute-start | bytes 1720328 | tf_op jit(solution)/shard_map/ppermute | solution.py:482
  59.4 21.2 %all-to-all-start.2 = ((f32[16,32,128]{2,1,0:T(8,128)}), f32[16,32,128]{2,1,0:T(8,128)S(1)}, u32[]{:S(2)}, u32[]{:S(2)}) async-start(f32[16,32,128]{2,1,0:T(8,128)} %shard_map.139), calls=%async_computation.2 | async-start | bytes 524288 | tf_op jit(solution)/shard_map/all_to_all | solution.py:483
  82.0 13.3 %all-to-all-start.3 = ((f32[4,512,128]{2,1,0:T(8,128)}), f32[4,512,128]{2,1,0:T(8,128)S(1)}, u32[]{:S(2)}, u32[]{:S(2)}) async-start(f32[4,512,128]{2,1,0:T(8,128)} %broadcast_in_dim.12), calls=%async_computation.3 | async-start | bytes 2097152 | tf_op jit(solution)/shard_map/all_to_all | solution.py:486
  95.3 3.4 %copy-start.5 = (f32[4,512,128]{2,1,0:T(8,128)}, f32[4,512,128]{2,1,0:T(8,128)S(1)}, u32[]{:S(2)}) copy-start(f32[4,512,128]{2,1,0:T(8,128)S(1)} %all-to-all-done.3) | copy-start | bytes 3145732
  109.2 9.6 %collective-permute-start.7 = (f32[512,512]{1,0:T(8,128)}, f32[512,512]{1,0:T(8,128)S(1)}, u32[]{:S(2)}, u32[]{:S(2)}) collective-permute-start(f32[512,512]{1,0:T(8,128)} %get-tuple-element.84), channel_id=1, source_target_pairs={{0,1},{1,0},{2,3},{3,2},{4,5},{5,4},{6,7},{7,6},{8,9},{9,8},{10,11... | collective-permute-start | bytes 3145736 | tf_op jit(solution)/shard_map/ppermute | solution.py:534
  120.3 13.7 %copy-start.1 = (bf16[32,4096]{1,0:T(8,128)(2,1)S(1)}, bf16[32,4096]{1,0:T(8,128)(2,1)}, u32[]{:S(2)}) copy-start(bf16[32,4096]{1,0:T(8,128)(2,1)} %residual_ref.1) | copy-start | bytes 786436
  120.3 13.6 %copy-start.2 = (f32[4096]{0:T(1024)S(1)}, f32[4096]{0:T(1024)}, u32[]{:S(2)}) copy-start(f32[4096]{0:T(1024)} %param.26) | copy-start | bytes 49156
  134.6 6.8 %collective-permute-start.8 = (bf16[32,4096]{1,0:T(8,128)(2,1)S(1)}, bf16[32,4096]{1,0:T(8,128)(2,1)S(1)}, u32[]{:S(2)}, u32[]{:S(2)}) collective-permute-start(bf16[32,4096]{1,0:T(8,128)(2,1)S(1)} %shard_map.144), channel_id=1, source_target_pairs={{0,2},{2,0},{1,3},{3,1},{4,6},{6,4},{5,7},{7,5},{8,10},{10,8},{9,1... | collective-permute-start | bytes 786440 | tf_op jit(solution)/shard_map/ppermute | solution.py:546
  141.4 3.6 %collective-permute-start.9 = (bf16[2,32,4096]{2,1,0:T(8,128)(2,1)S(1)}, bf16[2,32,4096]{2,1,0:T(8,128)(2,1)S(1)}, u32[]{:S(2)}, u32[]{:S(2)}) collective-permute-start(bf16[2,32,4096]{2,1,0:T(8,128)(2,1)S(1)} %pad_maximum_fusion.2), channel_id=1, source_target_pairs={{0,1},{1,0},{2,3},{3,2},{4,5},{5,4},{6,7},{7,6},{8,9},{9,8},{10,11... | collective-permute-start | bytes 1572872 | tf_op jit(solution)/shard_map/ppermute | solution.py:548
  (1 other events, 1.1 us)
Sparse Core Ops, SparseCore 0:
  29.5 69.2 all-gather.1

commit v11 on v10

--- a/solution.py
+++ b/solution.py
@@ -289,12 +289,12 @@
         gate_in.append(
             copies(halves(blocks[2 * i : 2 * i + 2], slice(inner, 2 * inner), to), semaphores, 3 * n + 2 * i)
         )
-    (weight_in,) = copies([(weight_hbm, weight_ref)], semaphores, 5 * n)
     for copy in coefs_in:
         copy.wait()
     for i in range(n):
         raw_t = block_ref[i, :heads, inner + 2 * SPAN :]
         logs_ref[place_ref[i]] = steps_of(raw_t, bias_ref[...], decay_ref[...])[1]
+    (weight_in,) = copies([(weight_hbm, weight_ref)], semaphores, 5 * n)
     for pair in range(pairs):
         parts = split(enter_ref[pair * SPAN : (pair + 1) * SPAN, :])
         enter_two[2 * pair * SPAN : 2 * (pair + 1) * SPAN, :] = jnp.concatenate(parts, axis=0)

time: 154 us -> 154 us (level)
  no operation moved by 1% of the time
where the time goes in v11:
time: 154 us; the launch traced here: 153 us
  starting transfers between devices  49.8 us (32%)
  Pallas kernels  41.7 us (27%)
  waiting for transfers between devices  28.2 us (18%)
  blocking collectives  13.6 us (9%)
  between operations  13.6 us (9%)
  other arithmetic  4.17 us (3%)
  local copies, waits for them, and re-layouts  2.13 us (1%)
    pallas_call x9, Pallas kernels, call(): pl.pallas_call(kernel, out_shape=list(outs), in_specs=specs, out_specs=[p...  41.7 us
    all_to_all x1, blocking collectives, on_device(): partial = lax.all_to_all(partial, ('x', *TENSOR), 0, 0, tiled=True)  13.6 us
    all_to_all x1, starting transfers between devices, on_device(): parts = lax.all_to_all(grouped, GROUPS, 0, 0, tiled=True)  12 us
    all_to_all x1, starting transfers between devices, on_device(): lax.all_to_all(entering, GROUPS, 0, 0, tiled=True).reshape(1, quarter, SPAN)  8.79 us
    ppermute x1, starting transfers between devices, on_device(): partial = (kept + lax.ppermute(sent, 'core', ring(2, 1))).astype(BF16)  7.15 us
    all_to_all x1, waiting for transfers between devices, on_device(): parts = lax.all_to_all(states, 'x', 0, 0, tiled=True)  5.75 us
    ppermute x1, waiting for transfers between devices, on_device(): across = lax.ppermute(done, 'yl', ring(2, 1))  5.5 us
    all_to_all x1, starting transfers between devices, on_device(): parts = lax.all_to_all(states, 'x', 0, 0, tiled=True)  4.99 us
  transfers between devices with their start and end apart: 15, of which 10 were waited for; matrix products, arithmetic and copies ran while one was open for 2% of the time, Pallas kernels for 18%

profile of v11, /device:TPU:1, one launch (start us, length us, event | category | flops | bytes accessed | tf_op | source)
XLA Modules:
  0.0 153.2 jit_solution(10011904010734510770)
XLA Ops:
  6.5 3.5 %shard_map.136 = (f32[4,520,128]{2,1,0:T(8,128)}, bf16[64,4480]{1,0:T(8,128)(2,1)}, bf16[64,4480]{1,0:T(8,128)(2,1)}) custom-call(bf16[128,2048]{1,0:T(8,128)(2,1)} %x_hbm.1, bf16[128,2048]{1,0:T(8,128)(2,1)} %gate_hbm.1, bf16[128,128]{1,0:T(8,128)(2,1)} %b_hbm.1, bf16[128,128]{1,0:T(8,128)(2,1)} %c_hbm.1, bf16[32,128]{1,0:T(8,128)(2,1)} %bitcast.45, ...), custom_call_target="tpu_custom_call" | custom-call | flops 134217728 | bytes 3334400 | tf_op jit(solution)/shard_map/pallas_call | solution.py:30
  10.1 5.0 %all-to-all-start = ((f32[4,520,128]{2,1,0:T(8,128)}), f32[4,520,128]{2,1,0:T(8,128)S(1)}, u32[]{:S(2)}, u32[]{:S(2)}) async-start(f32[4,520,128]{2,1,0:T(8,128)} %get-tuple-element.45), calls=%async_computation | async-start | bytes 2129920 | tf_op jit(solution)/shard_map/all_to_all | solution.py:423
  15.1 3.0 %collective-permute-start = (bf16[64,2048]{1,0:T(8,128)(2,1)S(1)}, bf16[64,2048]{1,0:T(8,128)(2,1)S(1)}, u32[]{:S(2)}, u32[]{:S(2)}) collective-permute-start(bf16[64,2048]{1,0:T(8,128)(2,1)S(1)} %bitcast.31), channel_id=1, source_target_pairs={{0,128},{128,0},{1,129},{129,1},{2,130},{130,2},{3,131},{131,3},{4... | collective-permute-start | bytes 786440 | tf_op jit(solution)/shard_map/ppermute | solution.py:408
  18.1 4.7 %collective-permute-done = bf16[64,2048]{1,0:T(8,128)(2,1)S(1)} collective-permute-done((bf16[64,2048]{1,0:T(8,128)(2,1)S(1)}, bf16[64,2048]{1,0:T(8,128)(2,1)S(1)}, u32[]{:S(2)}, u32[]{:S(2)}) %collective-permute-start) | collective-permute-done | bytes 262176 | tf_op jit(solution)/shard_map/ppermute | solution.py:408
  22.7 5.8 %all-to-all-done.parts_ref = f32[4,520,128]{2,1,0:T(8,128)S(1)} async-done(((f32[4,520,128]{2,1,0:T(8,128)}), f32[4,520,128]{2,1,0:T(8,128)S(1)}, u32[]{:S(2)}, u32[]{:S(2)}) %all-to-all-start) | async-done | bytes 1064992 | tf_op jit(solution)/shard_map/all_to_all | solution.py:423
  30.2 12.0 %all-to-all-start.1 = ((f32[16,40,128]{2,1,0:T(8,128)}), f32[16,40,128]{2,1,0:T(8,128)S(1)}, u32[]{:S(2)}, u32[]{:S(2)}) async-start(f32[16,40,128]{2,1,0:T(8,128)} %shard_map.138), calls=%async_computation.1 | async-start | bytes 655360 | tf_op jit(solution)/shard_map/all_to_all | solution.py:460
  42.6 2.4 %collective-permute-start.2 = (bf16[64,4480]{1,0:T(8,128)(2,1)}, bf16[64,4480]{1,0:T(8,128)(2,1)}, u32[]{:S(2)}, u32[]{:S(2)}) collective-permute-start(bf16[64,4480]{1,0:T(8,128)(2,1)} %get-tuple-element.61.bottom_hbm.refs_7_.refs_5_), channel_id=1, source_target_pairs={{0,12},{4,0},{8,4},{12,8},{1,13},{5,1},{9,5},{13,9},{2,14},{6,2},{... | collective-permute-start | bytes 1720328 | tf_op jit(solution)/shard_map/ppermute | solution.py:431
  46.5 5.3 %shard_map.137 = (f32[128,2048]{1,0:T(8,128)}, f32[2048,128]{1,0:T(8,128)}) custom-call(f32[1,32]{1,0:T(1,128)} %bitcast.34, f32[1,32]{1,0:T(1,128)} %bitcast.40, f32[1,2048]{1,0:T(1,128)} %reshape_reshape.3.skip_ref, bf16[64,4480]{1,0:T(8,128)(2,1)} %get-tuple-element.64.top_hbm.refs_6_.refs_4_, bf16[64,4480]{1,0:T(8,128)(2,1)} %get-tuple-element.61.bottom_hbm.refs_7_.refs_5_), custom_call_target="tpu_custom_call" | custom-call | flops 1000000 | bytes 3252480 | tf_op jit(solution)/shard_map/pallas_call | solution.py:30
  53.4 2.5 %collective-permute-done.1.top_hbm.refs_8_.refs_6_ = bf16[64,4480]{1,0:T(8,128)(2,1)} collective-permute-done((bf16[64,4480]{1,0:T(8,128)(2,1)S(1)}, bf16[64,4480]{1,0:T(8,128)(2,1)}, u32[]{:S(2)}, u32[]{:S(2)}) %collective-permute-start.1) | collective-permute-done | bytes 573472 | tf_op jit(solution)/shard_map/ppermute | solution.py:430
  56.7 2.7 %collective-permute-start.6 = (bf16[64,4480]{1,0:T(8,128)(2,1)}, bf16[64,4480]{1,0:T(8,128)(2,1)}, u32[]{:S(2)}, u32[]{:S(2)}) collective-permute-start(bf16[64,4480]{1,0:T(8,128)(2,1)} %collective-permute-done.2.bottom_hbm.refs_11_.refs_9_), channel_id=1, source_target_pairs={{0,12},{4,0},{8,4},{12,8},{1,13},{5,1},{9,5},{13,9},{2,14},{6,2},{... | collective-permute-start | bytes 1720328 | tf_op jit(solution)/shard_map/ppermute | solution.py:482
  59.4 8.8 %all-to-all-start.2 = ((f32[16,32,128]{2,1,0:T(8,128)}), f32[16,32,128]{2,1,0:T(8,128)S(1)}, u32[]{:S(2)}, u32[]{:S(2)}) async-start(f32[16,32,128]{2,1,0:T(8,128)} %shard_map.139), calls=%async_computation.2 | async-start | bytes 524288 | tf_op jit(solution)/shard_map/all_to_all | solution.py:483
  68.2 5.3 %shard_map.141 = (f32[128,2048]{1,0:T(8,128)}, f32[2048,128]{1,0:T(8,128)}) custom-call(f32[1,32]{1,0:T(1,128)} %bitcast.35, f32[1,32]{1,0:T(1,128)} %bitcast.41, f32[1,2048]{1,0:T(1,128)} %reshape_reshape.3.skip_ref, bf16[64,4480]{1,0:T(8,128)(2,1)} %collective-permute-done.4.top_hbm.refs_10_.refs_8_, ...), custom_call_target="tpu_custom_call" | custom-call | flops 1000000 | bytes 3252480 | tf_op jit(solution)/shard_map/pallas_call | solution.py:30
  73.5 5.3 %shard_map.140 = (f32[128,2048]{1,0:T(8,128)}, f32[2048,128]{1,0:T(8,128)}) custom-call(f32[1,32]{1,0:T(1,128)} %bitcast.36, f32[1,32]{1,0:T(1,128)} %bitcast.42, f32[1,2048]{1,0:T(1,128)} %reshape_reshape.3.skip_ref, bf16[64,4480]{1,0:T(8,128)(2,1)} %collective-permute-done.1.top_hbm.refs_8_.refs_6_, ...), custom_call_target="tpu_custom_call" | custom-call | flops 1000000 | bytes 3252480 | tf_op jit(solution)/shard_map/pallas_call | solution.py:30
  78.7 1.8 %all-to-all-done.2 = f32[16,32,128]{2,1,0:T(8,128)S(1)} async-done(((f32[16,32,128]{2,1,0:T(8,128)}), f32[16,32,128]{2,1,0:T(8,128)S(1)}, u32[]{:S(2)}, u32[]{:S(2)}) %all-to-all-start.2) | async-done | bytes 262176 | tf_op jit(solution)/shard_map/all_to_all | solution.py:483
  82.0 3.5 %all-to-all-start.3 = ((f32[4,512,128]{2,1,0:T(8,128)}), f32[4,512,128]{2,1,0:T(8,128)S(1)}, u32[]{:S(2)}, u32[]{:S(2)}) async-start(f32[4,512,128]{2,1,0:T(8,128)} %broadcast_in_dim.12), calls=%async_computation.3 | async-start | bytes 2097152 | tf_op jit(solution)/shard_map/all_to_all | solution.py:486
  85.6 9.7 %shard_map.142 = (f32[128,2048]{1,0:T(8,128)}, f32[128,2048]{1,0:T(8,128)}, f32[128,2048]{1,0:T(8,128)}, f32[128,2048]{1,0:T(8,128)}) custom-call(s32[5]{0:T(128)} %pad_add_fusion.place_ref, f32[1,32]{1,0:T(1,128)} %bitcast.37, f32[1,32]{1,0:T(1,128)} %bitcast.43, f32[1,2048]{1,0:T(1,128)} %reshape_reshape.3.skip_ref, ...), custom_call_target="tpu_custom_call" | custom-call | flops 536870912 | bytes 15081748 | tf_op jit(solution)/shard_map/pallas_call | solution.py:30
  95.3 3.4 %all-gather.2.cloned.1.call-done.refs_12_ = bf16[1024,2048]{1,0:T(8,128)(2,1)} async-done(((bf16[128,2048]{1,0:T(8,128)(2,1)}), bf16[1024,2048]{1,0:T(8,128)(2,1)}) %all-gather.2.cloned.1.call-update) | async-done | bytes 4194320 | tf_op jit(solution)/shard_map/all_gather | solution.py:426
  98.8 10.5 %shard_map.143 = (f32[512,512]{1,0:T(8,128)}, f32[512,512]{1,0:T(8,128)}) custom-call(s32[5]{0:T(128)} %pad_add_fusion.place_ref, f32[1,32]{1,0:T(1,128)} %bitcast.38, f32[1,32]{1,0:T(1,128)} %bitcast.44, f32[1,2048]{1,0:T(1,128)} %bitcast.46, f32[2048,128]{1,0:T(8,128)} %bitcast.26, f32[128,2048]{1,0:T(8,128)} %get-tuple-element.78.refs_0_, ...), custom_call_target="tpu_custom_call" | custom-call | flops 2684354560 | bytes 16130324 | tf_op jit(solution)/shard_map/pallas_call | solution.py:30
  109.2 7.1 %collective-permute-start.7 = (f32[512,512]{1,0:T(8,128)}, f32[512,512]{1,0:T(8,128)S(1)}, u32[]{:S(2)}, u32[]{:S(2)}) collective-permute-start(f32[512,512]{1,0:T(8,128)} %get-tuple-element.84), channel_id=1, source_target_pairs={{0,1},{1,0},{2,3},{3,2},{4,5},{5,4},{6,7},{7,6},{8,9},{9,8},{10,11... | collective-permute-start | bytes 3145736 | tf_op jit(solution)/shard_map/ppermute | solution.py:534
  116.4 2.5 %collective-permute-done.7 = f32[512,512]{1,0:T(8,128)S(1)} collective-permute-done((f32[512,512]{1,0:T(8,128)}, f32[512,512]{1,0:T(8,128)S(1)}, u32[]{:S(2)}, u32[]{:S(2)}) %collective-permute-start.7) | collective-permute-done | bytes 1048608 | tf_op jit(solution)/shard_map/ppermute | solution.py:534
  120.3 13.6 %all_to_all.29 = bf16[16,32,512]{2,1,0:T(8,128)(2,1)S(1)} all-to-all(bf16[16,32,512]{2,1,0:T(8,128)(2,1)S(1)} %bitcast.27), channel_id=1, replica_groups=mesh['yh'=2,'z'=8,'x'=4,'yl'=2,'core'=2] {'x','yl','core'}, dimensions={0} | all-to-all | bytes 1048576 | tf_op jit(solution)/shard_map/all_to_all | solution.py:535
  135.9 5.5 %collective-permute-done.8 = bf16[32,4096]{1,0:T(8,128)(2,1)S(1)} collective-permute-done((bf16[32,4096]{1,0:T(8,128)(2,1)S(1)}, bf16[32,4096]{1,0:T(8,128)(2,1)S(1)}, u32[]{:S(2)}, u32[]{:S(2)}) %collective-permute-start.8) | collective-permute-done | bytes 262176 | tf_op jit(solution)/shard_map/ppermute | solution.py:546
  141.4 2.1 %collective-permute-start.9 = (bf16[2,32,4096]{2,1,0:T(8,128)(2,1)S(1)}, bf16[2,32,4096]{2,1,0:T(8,128)(2,1)S(1)}, u32[]{:S(2)}, u32[]{:S(2)}) collective-permute-start(bf16[2,32,4096]{2,1,0:T(8,128)(2,1)S(1)} %pad_maximum_fusion.2), channel_id=1, source_target_pairs={{0,1},{1,0},{2,3},{3,2},{4,5},{5,4},{6,7},{7,6},{8,9},{9,8},{10,11... | collective-permute-start | bytes 1572872 | tf_op jit(solution)/shard_map/ppermute | solution.py:548
  143.5 1.5 %collective-permute-done.9 = bf16[2,32,4096]{2,1,0:T(8,128)(2,1)S(1)} collective-permute-done((bf16[2,32,4096]{2,1,0:T(8,128)(2,1)S(1)}, bf16[2,32,4096]{2,1,0:T(8,128)(2,1)S(1)}, u32[]{:S(2)}, u32[]{:S(2)}) %collective-permute-start.9) | collective-permute-done | bytes 524320 | tf_op jit(solution)/shard_map/ppermute | solution.py:548
  (51 shorter events, 12.1 us)
Async XLA Ops:
  6.5 39.2 %copy-start = (f32[32,64,128]{2,1,0:T(8,128)S(1)}, f32[32,64,128]{2,1,0:T(8,128)}, u32[]{:S(2)}) copy-start(f32[32,64,128]{2,1,0:T(8,128)} %param.23) | copy-start | bytes 3145732
  10.1 5.0 %copy-start.7 = (bf16[2048,64]{0,1:T(8,128)(2,1)S(1)}, bf16[2048,64]{0,1:T(8,128)(2,1)}, u32[]{:S(2)}) copy-start(bf16[2048,64]{0,1:T(8,128)(2,1)} %param.24) | copy-start | bytes 786436
  10.1 18.4 %all-to-all-start = ((f32[4,520,128]{2,1,0:T(8,128)}), f32[4,520,128]{2,1,0:T(8,128)S(1)}, u32[]{:S(2)}, u32[]{:S(2)}) async-start(f32[4,520,128]{2,1,0:T(8,128)} %get-tuple-element.45), calls=%async_computation | async-start | bytes 2129920 | tf_op jit(solution)/shard_map/all_to_all | solution.py:423
  15.1 83.7 %all-gather.2.cloned.1.call-start = ((), (), s32[]{:S(2)}) async-start(), calls=%async_computation.5 | async-start | bytes 4718592 | tf_op jit(solution)/shard_map/all_gather | solution.py:426
  15.1 7.7 %collective-permute-start = (bf16[64,2048]{1,0:T(8,128)(2,1)S(1)}, bf16[64,2048]{1,0:T(8,128)(2,1)S(1)}, u32[]{:S(2)}, u32[]{:S(2)}) collective-permute-start(bf16[64,2048]{1,0:T(8,128)(2,1)S(1)} %bitcast.31), channel_id=1, source_target_pairs={{0,128},{128,0},{1,129},{129,1},{2,130},{130,2},{3,131},{131,3},{4... | collective-permute-start | bytes 786440 | tf_op jit(solution)/shard_map/ppermute | solution.py:408
  29.3 12.9 %copy-start.3 = (bf16[64,4480]{1,0:T(8,128)(2,1)S(1)}, bf16[64,4480]{1,0:T(8,128)(2,1)}, u32[]{:S(2)}) copy-start(bf16[64,4480]{1,0:T(8,128)(2,1)} %get-tuple-element.64.top_hbm.refs_6_.refs_4_) | copy-start | bytes 1720324
  29.4 15.6 %copy-start.8 = (f32[32]{0:T(128)S(1)}, f32[32]{0:T(128)}, u32[]{:S(2)}) copy-start(f32[32]{0:T(128)} %param.21) | copy-start | bytes 388
  29.4 16.5 %copy-start.9 = (s32[4]{0:T(128)S(1)}, s32[4]{0:T(128)}, u32[]{:S(2)}) copy-start(s32[4]{0:T(128)} %constant.86.clone) | copy-start | bytes 52
  30.2 21.7 %copy-start.4 = (bf16[64,4480]{1,0:T(8,128)(2,1)S(1)}, bf16[64,4480]{1,0:T(8,128)(2,1)}, u32[]{:S(2)}) copy-start(bf16[64,4480]{1,0:T(8,128)(2,1)} %get-tuple-element.64.top_hbm.refs_6_.refs_4_) | copy-start | bytes 1720324
  30.2 25.7 %all-to-all-start.1 = ((f32[16,40,128]{2,1,0:T(8,128)}), f32[16,40,128]{2,1,0:T(8,128)S(1)}, u32[]{:S(2)}, u32[]{:S(2)}) async-start(f32[16,40,128]{2,1,0:T(8,128)} %shard_map.138), calls=%async_computation.1 | async-start | bytes 655360 | tf_op jit(solution)/shard_map/all_to_all | solution.py:460
  42.2 13.7 %collective-permute-start.1 = (bf16[64,4480]{1,0:T(8,128)(2,1)S(1)}, bf16[64,4480]{1,0:T(8,128)(2,1)}, u32[]{:S(2)}, u32[]{:S(2)}) collective-permute-start(bf16[64,4480]{1,0:T(8,128)(2,1)S(1)} %copy-done.3), channel_id=1, source_target_pairs={{0,4},{4,8},{8,12},{12,0},{1,5},{5,9},{9,13},{13,1},{2,6},{6,10},{... | collective-permute-start | bytes 1720328 | tf_op jit(solution)/shard_map/ppermute | solution.py:430
  42.6 13.4 %collective-permute-start.2 = (bf16[64,4480]{1,0:T(8,128)(2,1)}, bf16[64,4480]{1,0:T(8,128)(2,1)}, u32[]{:S(2)}, u32[]{:S(2)}) collective-permute-start(bf16[64,4480]{1,0:T(8,128)(2,1)} %get-tuple-element.61.bottom_hbm.refs_7_.refs_5_), channel_id=1, source_target_pairs={{0,12},{4,0},{8,4},{12,8},{1,13},{5,1},{9,5},{13,9},{2,14},{6,2},{... | collective-permute-start | bytes 1720328 | tf_op jit(solution)/shard_map/ppermute | solution.py:431
  51.9 16.3 %collective-permute-start.4 = (bf16[64,4480]{1,0:T(8,128)(2,1)S(1)}, bf16[64,4480]{1,0:T(8,128)(2,1)}, u32[]{:S(2)}, u32[]{:S(2)}) collective-permute-start(bf16[64,4480]{1,0:T(8,128)(2,1)S(1)} %copy-done.4), channel_id=1, source_target_pairs={{0,12},{4,0},{8,4},{12,8},{1,13},{5,1},{9,5},{13,9},{2,14},{6,2},{... | collective-permute-start | bytes 1720328 | tf_op jit(solution)/shard_map/ppermute | solution.py:463
  52.0 21.5 %collective-permute-start.3 = (bf16[64,4480]{1,0:T(8,128)(2,1)}, bf16[64,4480]{1,0:T(8,128)(2,1)}, u32[]{:S(2)}, u32[]{:S(2)}) collective-permute-start(bf16[64,4480]{1,0:T(8,128)(2,1)} %get-tuple-element.61.bottom_hbm.refs_7_.refs_5_), channel_id=1, source_target_pairs={{0,4},{4,8},{8,12},{12,0},{1,5},{5,9},{9,13},{13,1},{2,6},{6,10},{... | collective-permute-start | bytes 1720328 | tf_op jit(solution)/shard_map/ppermute | solution.py:462
  56.7 24.2 %collective-permute-start.5 = (bf16[64,4480]{1,0:T(8,128)(2,1)}, bf16[64,4480]{1,0:T(8,128)(2,1)S(1)}, u32[]{:S(2)}, u32[]{:S(2)}) collective-permute-start(bf16[64,4480]{1,0:T(8,128)(2,1)} %collective-permute-done.1.top_hbm.refs_8_.refs_6_), channel_id=1, source_target_pairs={{0,4},{4,8},{8,12},{12,0},{1,5},{5,9},{9,13},{13,1},{2,6},{6,10},{... | collective-permute-start | bytes 1720328 | tf_op jit(solution)/shard_map/ppermute | solution.py:482
  56.7 24.2 %collective-permute-start.6 = (bf16[64,4480]{1,0:T(8,128)(2,1)}, bf16[64,4480]{1,0:T(8,128)(2,1)}, u32[]{:S(2)}, u32[]{:S(2)}) collective-permute-start(bf16[64,4480]{1,0:T(8,128)(2,1)} %collective-permute-done.2.bottom_hbm.refs_11_.refs_9_), channel_id=1, source_target_pairs={{0,12},{4,0},{8,4},{12,8},{1,13},{5,1},{9,5},{13,9},{2,14},{6,2},{... | collective-permute-start | bytes 1720328 | tf_op jit(solution)/shard_map/ppermute | solution.py:482
  59.4 21.2 %all-to-all-start.2 = ((f32[16,32,128]{2,1,0:T(8,128)}), f32[16,32,128]{2,1,0:T(8,128)S(1)}, u32[]{:S(2)}, u32[]{:S(2)}) async-start(f32[16,32,128]{2,1,0:T(8,128)} %shard_map.139), calls=%async_computation.2 | async-start | bytes 524288 | tf_op jit(solution)/shard_map/all_to_all | solution.py:483
  82.0 13.3 %all-to-all-start.3 = ((f32[4,512,128]{2,1,0:T(8,128)}), f32[4,512,128]{2,1,0:T(8,128)S(1)}, u32[]{:S(2)}, u32[]{:S(2)}) async-start(f32[4,512,128]{2,1,0:T(8,128)} %broadcast_in_dim.12), calls=%async_computation.3 | async-start | bytes 2097152 | tf_op jit(solution)/shard_map/all_to_all | solution.py:486
  95.3 3.4 %copy-start.5 = (f32[4,512,128]{2,1,0:T(8,128)}, f32[4,512,128]{2,1,0:T(8,128)S(1)}, u32[]{:S(2)}) copy-start(f32[4,512,128]{2,1,0:T(8,128)S(1)} %all-to-all-done.3) | copy-start | bytes 3145732
  109.2 9.6 %collective-permute-start.7 = (f32[512,512]{1,0:T(8,128)}, f32[512,512]{1,0:T(8,128)S(1)}, u32[]{:S(2)}, u32[]{:S(2)}) collective-permute-start(f32[512,512]{1,0:T(8,128)} %get-tuple-element.84), channel_id=1, source_target_pairs={{0,1},{1,0},{2,3},{3,2},{4,5},{5,4},{6,7},{7,6},{8,9},{9,8},{10,11... | collective-permute-start | bytes 3145736 | tf_op jit(solution)/shard_map/ppermute | solution.py:534
  120.3 13.7 %copy-start.1 = (bf16[32,4096]{1,0:T(8,128)(2,1)S(1)}, bf16[32,4096]{1,0:T(8,128)(2,1)}, u32[]{:S(2)}) copy-start(bf16[32,4096]{1,0:T(8,128)(2,1)} %residual_ref.1) | copy-start | bytes 786436
  120.3 13.6 %copy-start.2 = (f32[4096]{0:T(1024)S(1)}, f32[4096]{0:T(1024)}, u32[]{:S(2)}) copy-start(f32[4096]{0:T(1024)} %param.26) | copy-start | bytes 49156
  134.6 6.8 %collective-permute-start.8 = (bf16[32,4096]{1,0:T(8,128)(2,1)S(1)}, bf16[32,4096]{1,0:T(8,128)(2,1)S(1)}, u32[]{:S(2)}, u32[]{:S(2)}) collective-permute-start(bf16[32,4096]{1,0:T(8,128)(2,1)S(1)} %shard_map.144), channel_id=1, source_target_pairs={{0,2},{2,0},{1,3},{3,1},{4,6},{6,4},{5,7},{7,5},{8,10},{10,8},{9,1... | collective-permute-start | bytes 786440 | tf_op jit(solution)/shard_map/ppermute | solution.py:546
  141.4 3.6 %collective-permute-start.9 = (bf16[2,32,4096]{2,1,0:T(8,128)(2,1)S(1)}, bf16[2,32,4096]{2,1,0:T(8,128)(2,1)S(1)}, u32[]{:S(2)}, u32[]{:S(2)}) collective-permute-start(bf16[2,32,4096]{2,1,0:T(8,128)(2,1)S(1)} %pad_maximum_fusion.2), channel_id=1, source_target_pairs={{0,1},{1,0},{2,3},{3,2},{4,5},{5,4},{6,7},{7,6},{8,9},{9,8},{10,11... | collective-permute-start | bytes 1572872 | tf_op jit(solution)/shard_map/ppermute | solution.py:548
  (1 other events, 1.1 us)
Sparse Core Ops, SparseCore 0:
  29.5 69.2 all-gather.1
